TPU v7x, 32 devices: a whole 2x2x4 slice. The times are simulated.
32 devices in a mesh: elem: 32 (over z, y, x, core).
Axes of the slice: x: 2, y: 2, z: 4, core: 2. Of those that a mesh axis runs over, the one named last changes fastest.
Arguments:
- moment_fields: float32 [3, 512, 4096], P(None, None, 'elem'), may hold values from -6 to 6
- adjoint_fields: float32 [3, 512, 4096], P(None, None, 'elem'), may hold values from -6 to 6
- velocity: float32 [3, 512, 4096], P(None, None, 'elem'), may hold values from -12 to 12
- mass_weights: float32 [512, 4096], P(None, 'elem'), may hold values from 0.5 to 2
- diffusivity: float32 [3], replicated, may hold values from 0.1 to 0.5
- numbering: int32 [4096], P('elem'), may hold values from 0 to 4095, as said below
Outputs:
- moments: float32 [3, 512, 4096], P(None, None, 'elem')
- sensitivities: float32 [3, 512, 4096], P(None, None, 'elem')
Inputs may be any that keep to these rules, and one draw needn't show every extreme that they name: `numbering`: rows d * 128 to (d + 1) * 128 - 1 hold, in some order, each of the numbers c * 128 to (c + 1) * 128 - 1 once, where c = (d + 4) % 32.
All inputs are finite; a program needn't handle non-finite values.
Results may differ from a plain program's by a relative error of at most 0.0001.
Values sent between devices are 32-bit elements; how exact they have to be, the bound alone decides.
No kernel may reach another device: no remote copies, remote signals or barrier semaphores. Data moves between devices by JAX's collectives and lax.ppermute only.
A program may use at most 64 MiB of HBM per device.

v0:
```python
import functools

import jax
import jax.numpy as jnp
import numpy as np
from jax import lax
from jax.experimental import pallas as pl
from jax.experimental.pallas import tpu as pltpu
from jax.sharding import PartitionSpec as P

DA = 4
DT = 0.001
F32 = jnp.float32
BF16 = jnp.bfloat16


def gll_tables():
    points = [
        -1.0,
        -0.8717401485096066,
        -0.5917001814331423,
        -0.2092992179024789,
        0.2092992179024789,
        0.5917001814331423,
        0.8717401485096066,
        1.0,
    ]
    weights = [
        0.03571428571428571,
        0.21070422714350603,
        0.3411226924835044,
        0.4124587946587038,
        0.4124587946587038,
        0.3411226924835044,
        0.21070422714350603,
        0.03571428571428571,
    ]
    barycentric = []
    for left_index in range(8):
        product = 1.0
        for right_index in range(8):
            if right_index != left_index:
                product = product * (points[left_index] - points[right_index])
        barycentric.append(1.0 / product)
    derivative = np.zeros((8, 8))
    for left_index in range(8):
        row_total = 0.0
        for right_index in range(8):
            if left_index != right_index:
                entry = (
                    barycentric[right_index]
                    / barycentric[left_index]
                    / (points[left_index] - points[right_index])
                )
                derivative[left_index, right_index] = entry
                row_total = row_total + entry
        derivative[left_index, left_index] = -row_total
    return derivative, np.asarray(weights)


DM, WEIGHTS = gll_tables()


def line(table, values):
    sums = [values[q] + values[7 - q] for q in range(4)]
    differences = [values[q] - values[7 - q] for q in range(4)]
    out = [None] * 8
    for i in range(4):
        even = odd = None
        for q in range(4):
            on_sum = float(table[i, q] + table[i, 7 - q]) / 2
            on_difference = float(table[i, q] - table[i, 7 - q]) / 2
            even = sums[q] * on_sum if even is None else even + sums[q] * on_sum
            odd = (
                differences[q] * on_difference
                if odd is None
                else odd + differences[q] * on_difference
            )
        out[i] = odd + even
        out[7 - i] = odd - even
    return out


def rows(i, j):
    return pl.ds((8 * i + j) * 8, 8)


def along_k(table_ref, block):
    wide = jnp.concatenate([block[:256], block[256:]], axis=1)
    high = wide.astype(BF16)
    low = (wide - high.astype(F32)).astype(BF16)
    both = jnp.dot(table_ref[...], high, preferred_element_type=F32)
    rest = jnp.dot(table_ref[:256], low, preferred_element_type=F32)
    out = both[:256] + (both[256:] + rest)
    return jnp.concatenate([out[:, :128], out[:, 128:]], axis=0)


def lanes(block, index):
    wide = jnp.broadcast_to(index[None], (block.shape[0] // 8, 8, 128)).reshape(block.shape)
    return jnp.take_along_axis(block, wide, axis=1, mode="promise_in_bounds")


def set_mass(weight_ref, mass_ref):
    sub = lax.broadcasted_iota(jnp.int32, (8, 128), 0)
    along = jnp.zeros((8, 128), F32)
    for k in range(8):
        along = jnp.where(sub == k, float(WEIGHTS[k]), along)
    for i in range(8):
        for j in range(8):
            r = rows(i, j)
            mass_ref[r] = weight_ref[r] * (along * float(WEIGHTS[i] * WEIGHTS[j]))


def forward(f, source, flow_ref, mass_ref, diff, table_ref, turned_ref, work, target):
    slope = along_k(table_ref, source[...])
    flux = slope * mass_ref[...]
    work[...] = flow_ref[2] * flux + diff * along_k(turned_ref, flux)
    for j in range(8):
        slopes = line(DM, [source[rows(i, j)] for i in range(8)])
        fluxes = [slopes[i] * mass_ref[rows(i, j)] for i in range(8)]
        back = line(DM.T, fluxes)
        for i in range(8):
            r = rows(i, j)
            target[r] = flow_ref[0, r] * fluxes[i] + diff * back[i]
    for i in range(8):
        slopes = line(DM, [source[rows(i, j)] for j in range(8)])
        fluxes = [slopes[j] * mass_ref[rows(i, j)] for j in range(8)]
        back = line(DM.T, fluxes)
        for j in range(8):
            r = rows(i, j)
            target[r] = -(target[r] + work[r] + (flow_ref[1, r] * fluxes[j] + diff * back[j]))


def adjoint(f, source, base, flow_ref, mass_ref, diff, table_ref, turned_ref, work, target):
    slope = along_k(table_ref, source[...])
    flux = (flow_ref[2] * source[...] + diff * slope) * mass_ref[...]
    work[...] = along_k(turned_ref, flux)
    for j in range(8):
        values = [source[rows(i, j)] for i in range(8)]
        slopes = line(DM, values)
        fluxes = [
            (flow_ref[0, rows(i, j)] * values[i] + diff * slopes[i]) * mass_ref[rows(i, j)]
            for i in range(8)
        ]
        back = line(DM.T, fluxes)
        for i in range(8):
            target[rows(i, j)] = back[i]
    for i in range(8):
        values = [source[rows(i, j)] for j in range(8)]
        slopes = line(DM, values)
        fluxes = [
            (flow_ref[1, rows(i, j)] * values[j] + diff * slopes[j]) * mass_ref[rows(i, j)]
            for j in range(8)
        ]
        back = line(DM.T, fluxes)
        for j in range(8):
            r = rows(i, j)
            target[r] = base[r] - DT * (target[r] + work[r] + back[j])


def join_heights(ref, index):
    height, _, below, above = index
    lower = ref[pl.ds(0, 64, stride=8)]
    upper = ref[pl.ds(7, 64, stride=8)]
    tall = jnp.broadcast_to(height[None], (8, 8, 128)).reshape(64, 128)
    ref[pl.ds(0, 64, stride=8)] = lower + jnp.where(tall > 0, lanes(upper, below), 0.0)
    ref[pl.ds(7, 64, stride=8)] = upper + jnp.where(tall < 127, lanes(lower, above), 0.0)


def send_faces(c, ref, index, ends, out):
    inverse = index[1]
    for way in range(2):
        i_face = ref[pl.ds(pl.multiple_of(ends[0][way] * 64, 64), 64)]
        out[way][c] = lanes(i_face, inverse)
        for i in range(8):
            j_face = ref[pl.ds(pl.multiple_of(ends[1][way] * 8 + i * 64, 8), 8)]
            out[2 + way][c, pl.ds(i * 8, 8)] = lanes(j_face, inverse)


def add_faces(c, ref, index, ends, got):
    height = index[0]
    for way in range(2):
        r = pl.ds(pl.multiple_of(ends[0][way] * 64, 64), 64)
        ref[r] = ref[r] + lanes(got[way][c], height)
    for way in range(2):
        for i in range(8):
            r = pl.ds(pl.multiple_of(ends[1][way] * 8 + i * 64, 8), 8)
            ref[r] = ref[r] + lanes(got[2 + way][c, pl.ds(i * 8, 8)], height)


def ends_of(number_ref, columns):
    column = lax.shift_right_logical(number_ref[0], 7)
    row_odd = lax.rem(lax.div(column, columns), 2)
    place_odd = lax.rem(lax.rem(column, columns), 2)
    return ((7 - 7 * row_odd, 7 * row_odd), (7 - 7 * place_odd, 7 * place_odd))


def index_of(index_ref):
    return tuple(index_ref[n] for n in range(4))


def first_kernel(
    columns,
    moment_ref,
    state_ref,
    flow_ref,
    weight_ref,
    diff_ref,
    number_ref,
    numbers_ref,
    table_ref,
    turned_ref,
    index_ref,
    joined_ref,
    ie_ref,
    io_ref,
    je_ref,
    jo_ref,
    mass_ref,
    work_ref,
):
    ends = ends_of(number_ref, columns)
    height = jnp.broadcast_to(numbers_ref[...] & 127, (8, 128))
    square = jnp.broadcast_to(height[:1].astype(F32), (128, 128)).T
    lane = lax.broadcasted_iota(jnp.int32, (128, 128), 1).astype(F32)
    row = lax.broadcasted_iota(jnp.int32, (128, 128), 0).astype(F32)
    inverse = jnp.sum(jnp.where(square == lane, row, 0.0), axis=0, keepdims=True)
    inverse = jnp.broadcast_to(inverse, (8, 128)).astype(jnp.int32)
    index = (
        height,
        inverse,
        lanes(inverse, (height - 1) & 127),
        lanes(inverse, (height + 1) & 127),
    )
    for n in range(4):
        index_ref[n] = index[n]
    set_mass(weight_ref, mass_ref)
    out = (ie_ref, io_ref, je_ref, jo_ref)

    joined_ref[6] = mass_ref[...]
    join_heights(joined_ref.at[6], index)
    send_faces(6, joined_ref.at[6], index, ends, out)

    def one_field(f, carry):
        joined_ref[3 + f] = state_ref[f]
        forward(
            f,
            moment_ref.at[f],
            flow_ref,
            mass_ref,
            diff_ref[f],
            table_ref,
            turned_ref,
            work_ref,
            joined_ref.at[f],
        )
        for c in (f, 3 + f):
            join_heights(joined_ref.at[c], index)
            send_faces(c, joined_ref.at[c], index, ends, out)
        return carry

    lax.fori_loop(0, 3, one_field, 0)


def edge_kernel(columns, count, number_ref, ie_ref, io_ref, je_ref, jo_ref, out_e, out_o):
    ends = ends_of(number_ref, columns)
    for way, (face, out) in enumerate(((je_ref, out_e), (jo_ref, out_o))):
        out[...] = face[...]
        r = pl.ds(pl.multiple_of(ends[1][way] * 8, 8), 8)
        for other, got in enumerate((ie_ref, io_ref)):
            w = pl.ds(pl.multiple_of(ends[0][other] * 8, 8), 8)
            out[:, w] = out[:, w] + got[:, r]


def second_kernel(
    columns,
    moment_ref,
    state_ref,
    flow_ref,
    weight_ref,
    diff_ref,
    number_ref,
    table_ref,
    turned_ref,
    index_ref,
    joined_ref,
    gie_ref,
    gio_ref,
    gje_ref,
    gjo_ref,
    moment_out,
    state_out,
    inverse_out,
    joined_out,
    ie_ref,
    io_ref,
    je_ref,
    jo_ref,
    mass_ref,
    work_ref,
    hold_ref,
):
    ends = ends_of(number_ref, columns)
    index = index_of(index_ref)
    set_mass(weight_ref, mass_ref)
    out = (ie_ref, io_ref, je_ref, jo_ref)
    got = (gie_ref, gio_ref, gje_ref, gjo_ref)
    hold_ref[...] = joined_ref[6]
    add_faces(6, hold_ref, index, ends, got)
    inverse_out[...] = 1.0 / hold_ref[...]

    def one_field(f, carry):
        hold_ref[...] = joined_ref[f]
        add_faces(f, hold_ref, index, ends, got)
        moment_out[f] = moment_ref[f] + DT * (hold_ref[...] * inverse_out[...])
        forward(
            f,
            moment_out.at[f],
            flow_ref,
            mass_ref,
            diff_ref[f],
            table_ref,
            turned_ref,
            work_ref,
            joined_out.at[f],
        )
        hold_ref[...] = joined_ref[3 + f]
        add_faces(3 + f, hold_ref, index, ends, got)
        hold_ref[...] = hold_ref[...] * inverse_out[...]
        adjoint(
            f,
            hold_ref,
            state_ref.at[f],
            flow_ref,
            mass_ref,
            diff_ref[f],
            table_ref,
            turned_ref,
            work_ref,
            state_out.at[f],
        )
        joined_out[3 + f] = state_out[f]
        for c in (f, 3 + f):
            join_heights(joined_out.at[c], index)
            send_faces(c, joined_out.at[c], index, ends, out)
        return carry

    lax.fori_loop(0, 3, one_field, 0)


def third_kernel(
    columns,
    moment_ref,
    state_ref,
    flow_ref,
    weight_ref,
    diff_ref,
    number_ref,
    table_ref,
    turned_ref,
    index_ref,
    inverse_ref,
    joined_ref,
    gie_ref,
    gio_ref,
    gje_ref,
    gjo_ref,
    moment_out,
    state_out,
    mass_ref,
    work_ref,
    hold_ref,
):
    ends = ends_of(number_ref, columns)
    index = index_of(index_ref)
    set_mass(weight_ref, mass_ref)
    got = (gie_ref, gio_ref, gje_ref, gjo_ref)

    def one_field(f, carry):
        hold_ref[...] = joined_ref[f]
        add_faces(f, hold_ref, index, ends, got)
        moment_out[f] = moment_ref[f] + DT * (hold_ref[...] * inverse_ref[...])
        hold_ref[...] = joined_ref[3 + f]
        add_faces(3 + f, hold_ref, index, ends, got)
        hold_ref[...] = hold_ref[...] * inverse_ref[...]
        adjoint(
            f,
            hold_ref,
            state_ref.at[f],
            flow_ref,
            mass_ref,
            diff_ref[f],
            table_ref,
            turned_ref,
            work_ref,
            state_out.at[f],
        )
        return carry

    lax.fori_loop(0, 3, one_field, 0)


VMEM = pl.BlockSpec(memory_space=pltpu.VMEM)
SMEM = pl.BlockSpec(memory_space=pltpu.SMEM)


def call(kernel, specs, shapes, scratch, flops, *operands):
    moved = sum(o.size * 4 for o in operands) + sum(int(np.prod(s)) * 4 for s, _ in shapes)
    return pl.pallas_call(
        kernel,
        out_shape=[jax.ShapeDtypeStruct(s, t) for s, t in shapes],
        in_specs=specs,
        out_specs=[VMEM] * len(shapes),
        scratch_shapes=[pltpu.VMEM(s, F32) for s in scratch],
        compiler_params=pltpu.CompilerParams(vmem_limit_bytes=32 * 1024 * 1024),
        cost_estimate=pl.CostEstimate(flops=flops, bytes_accessed=moved, transcendentals=0),
    )(*operands)


def pairings(devices):
    columns = devices // DA
    device = lambda row, place: (row * columns + place - columns // 2) % devices

    def both(pairs):
        return [(a, b) for a, b in pairs] + [(b, a) for a, b in pairs]

    along_i = [
        both([(device(r, s), device(r + 1, s)) for r in range(way, DA - 1, 2) for s in range(columns)])
        for way in range(2)
    ]
    along_j = [
        both([(device(r, s), device(r, s + 1)) for r in range(DA) for s in range(way, columns - 1, 2)])
        for way in range(2)
    ]
    return along_i, along_j


def split_table(table):
    wide = np.kron(np.eye(32), table).astype(np.float32)
    high = wide.astype(jnp.bfloat16)
    low = (wide - high.astype(np.float32)).astype(jnp.bfloat16)
    return jnp.asarray(np.concatenate([high, low], axis=0))


def shards(moment_fields, adjoint_fields, velocity, mass_weights, diffusivity, numbering):
    devices = lax.axis_size("elem")
    columns = devices // DA
    along_i, along_j = pairings(devices)
    table, turned = split_table(DM), split_table(DM.T)
    numbers = numbering.reshape(1, 128)
    whole = (3, 512, 128)

    def exchange(blocks, pairs):
        return [lax.ppermute(b, "elem", p) for b, p in zip(blocks, pairs)]

    def meet(count, faces):
        got_i = exchange(faces[:2], along_i)
        faces_j = call(
            functools.partial(edge_kernel, columns, count),
            [SMEM] + [VMEM] * 4,
            [((count, 64, 128), F32)] * 2,
            [],
            count * 64 * 128,
            numbering,
            *got_i,
            *faces[2:],
        )
        return got_i + exchange(faces_j, along_j)

    def faces_shape(count):
        return [((count, 64, 128), F32)] * 4

    index, joined, *faces = call(
        functools.partial(first_kernel, columns),
        [VMEM] * 4 + [SMEM] * 2 + [VMEM] * 3,
        [((4, 8, 128), jnp.int32), ((7, 512, 128), F32)] + faces_shape(7),
        [(512, 128)] * 2,
        20_000_000,
        moment_fields,
        adjoint_fields,
        velocity,
        mass_weights,
        diffusivity,
        numbering,
        numbers,
        table,
        turned,
    )
    got = meet(7, faces)
    moment_one, state_one, inverse, joined, *faces = call(
        functools.partial(second_kernel, columns),
        [VMEM] * 4 + [SMEM] * 2 + [VMEM] * 8,
        [(whole, F32), (whole, F32), ((512, 128), F32), ((6, 512, 128), F32)] + faces_shape(6),
        [(512, 128)] * 3,
        40_000_000,
        moment_fields,
        adjoint_fields,
        velocity,
        mass_weights,
        diffusivity,
        numbering,
        table,
        turned,
        index,
        joined,
        *got,
    )
    got = meet(6, faces)
    return tuple(
        call(
            functools.partial(third_kernel, columns),
            [VMEM] * 4 + [SMEM] * 2 + [VMEM] * 9,
            [(whole, F32), (whole, F32)],
            [(512, 128)] * 3,
            20_000_000,
            moment_one,
            state_one,
            velocity,
            mass_weights,
            diffusivity,
            numbering,
            table,
            turned,
            index,
            inverse,
            joined,
            *got,
        )
    )


def solution(mesh):
    in_specs = (
        P(None, None, "elem"),
        P(None, None, "elem"),
        P(None, None, "elem"),
        P(None, "elem"),
        P(),
        P("elem"),
    )
    out_specs = (P(None, None, "elem"), P(None, None, "elem"))
    return jax.shard_map(shards, mesh=mesh, in_specs=in_specs, out_specs=out_specs, check_vma=False)
```

profile of v0, /device:TPU:7, one launch (start us, length us, event | category | flops | bytes accessed | tf_op | source)
XLA Modules:
  0.0 69.0 jit_solution(1590896851011871415)
XLA Ops:
  0.6 0.0 copy-start
  0.6 1.1 %copy-done = f32[3,512,128]{2,1,0:T(8,128)S(1)} copy-done((f32[3,512,128]{2,1,0:T(8,128)S(1)}, f32[3,512,128]{2,1,0:T(8,128)}, u32[]{:S(2)}) %copy-start) | copy-done | bytes 786456
  1.8 0.0 copy-start.2
  1.8 1.1 %copy-done.2 = f32[3,512,128]{2,1,0:T(8,128)S(1)} copy-done((f32[3,512,128]{2,1,0:T(8,128)S(1)}, f32[3,512,128]{2,1,0:T(8,128)}, u32[]{:S(2)}) %copy-start.2) | copy-done | bytes 786456
  2.9 0.0 copy-start.4
  2.9 1.1 %copy-done.4 = f32[3,512,128]{2,1,0:T(8,128)S(1)} copy-done((f32[3,512,128]{2,1,0:T(8,128)S(1)}, f32[3,512,128]{2,1,0:T(8,128)}, u32[]{:S(2)}) %copy-start.4) | copy-done | bytes 786456
  4.0 0.0 copy-start.6
  4.0 0.9 %copy-done.6 = f32[512,128]{1,0:T(8,128)S(1)} copy-done((f32[512,128]{1,0:T(8,128)S(1)}, f32[512,128]{1,0:T(8,128)}, u32[]{:S(2)}) %copy-start.6) | copy-done | bytes 262168
  5.0 0.0 copy-start.8
  5.0 0.9 %copy-done.8 = bf16[512,256]{1,0:T(8,128)(2,1)S(1)} copy-done((bf16[512,256]{1,0:T(8,128)(2,1)S(1)}, bf16[512,256]{1,0:T(8,128)(2,1)}, u32[]{:S(2)}) %copy-start.8) | copy-done | bytes 262168
  5.9 0.0 copy-start.10
  5.9 0.9 %copy-done.10 = bf16[512,256]{1,0:T(8,128)(2,1)S(1)} copy-done((bf16[512,256]{1,0:T(8,128)(2,1)S(1)}, bf16[512,256]{1,0:T(8,128)(2,1)}, u32[]{:S(2)}) %copy-start.10) | copy-done | bytes 262168
  6.9 0.0 copy-start.12
  6.9 0.7 copy-done.12
  7.5 0.0 copy-start.13
  7.5 0.7 copy-done.13
  8.2 0.0 copy-start.3
  8.2 4.5 %shard_map.95 = (s32[4,8,128]{2,1,0:T(8,128)S(1)}, f32[7,512,128]{2,1,0:T(8,128)S(1)}, f32[7,64,128]{2,1,0:T(8,128)S(1)}, f32[7,64,128]{2,1,0:T(8,128)S(1)}, f32...) custom-call(f32[3,512,128]{2,1,0:T(8,128)S(1)} %copy-done.2, f32[3,512,128]{2,1,0:T(8,128)S(1)} %copy-done.4, ...), custom_call_target="tpu_custom_call" | custom-call | flops 20000000 | bytes 6439948 | tf_op jit(solution)/shard_map/pallas_call | solution.py:409
  12.7 3.4 %collective-permute-start = (f32[7,64,128]{2,1,0:T(8,128)S(1)}, f32[7,64,128]{2,1,0:T(8,128)S(1)}, u32[]{:S(2)}, u32[]{:S(2)}) collective-permute-start(f32[7,64,128]{2,1,0:T(8,128)S(1)} %get-tuple-element.22), channel_id=1, source_target_pairs={{28,4},{29,5},{30,6},{31,7},{0,8},{1,9},{2,10},{3,11},{12,20},{13,... | collective-permute-start | bytes 688136 | tf_op jit(solution)/shard_map/ppermute | solution.py:454
  16.1 1.9 %collective-permute-start.1 = (f32[7,64,128]{2,1,0:T(8,128)S(1)}, f32[7,64,128]{2,1,0:T(8,128)S(1)}, u32[]{:S(2)}, u32[]{:S(2)}) collective-permute-start(f32[7,64,128]{2,1,0:T(8,128)S(1)} %get-tuple-element.23), channel_id=1, source_target_pairs={{4,12},{5,13},{6,14},{7,15},{8,16},{9,17},{10,18},{11,19},{12,4},{... | collective-permute-start | bytes 688136 | tf_op jit(solution)/shard_map/ppermute | solution.py:454
  18.0 3.3 %collective-permute-done.ie_ref.gie_ref = f32[7,64,128]{2,1,0:T(8,128)S(1)} collective-permute-done((f32[7,64,128]{2,1,0:T(8,128)S(1)}, f32[7,64,128]{2,1,0:T(8,128)S(1)}, u32[]{:S(2)}, u32[]{:S(2)}) %collective-permute-start) | collective-permute-done | bytes 229408 | tf_op jit(solution)/shard_map/ppermute | solution.py:454
  21.3 5.9 %collective-permute-done.1.io_ref.gio_ref = f32[7,64,128]{2,1,0:T(8,128)S(1)} collective-permute-done((f32[7,64,128]{2,1,0:T(8,128)S(1)}, f32[7,64,128]{2,1,0:T(8,128)S(1)}, u32[]{:S(2)}, u32[]{:S(2)}) %collective-permute-start.1) | collective-permute-done | bytes 229408 | tf_op jit(solution)/shard_map/ppermute | solution.py:454
  27.2 0.6 shard_map.96
  27.8 0.6 collective-permute-start.2
  28.3 1.9 %collective-permute-start.3 = (f32[7,64,128]{2,1,0:T(8,128)S(1)}, f32[7,64,128]{2,1,0:T(8,128)S(1)}, u32[]{:S(2)}, u32[]{:S(2)}) collective-permute-start(f32[7,64,128]{2,1,0:T(8,128)S(1)} %get-tuple-element.27), channel_id=1, source_target_pairs={{29,30},{31,0},{1,2},{5,6},{7,8},{9,10},{13,14},{15,16},{17,18},{2... | collective-permute-start | bytes 688136 | tf_op jit(solution)/shard_map/ppermute | solution.py:454
  30.3 0.0 collective-permute-done.2.gje_ref
  30.3 7.2 %collective-permute-done.3.gjo_ref = f32[7,64,128]{2,1,0:T(8,128)S(1)} collective-permute-done((f32[7,64,128]{2,1,0:T(8,128)S(1)}, f32[7,64,128]{2,1,0:T(8,128)S(1)}, u32[]{:S(2)}, u32[]{:S(2)}) %collective-permute-start.3) | collective-permute-done | bytes 229408 | tf_op jit(solution)/shard_map/ppermute | solution.py:454
  37.5 0.0 copy-done.3
  37.5 0.0 copy-done.5
  37.5 0.0 copy-start.1
  37.5 0.0 copy-start.7
  37.5 0.0 copy-start.9
  37.5 0.0 copy-start.11
  37.5 5.6 %shard_map.97 = (f32[3,512,128]{2,1,0:T(8,128)S(1)}, f32[3,512,128]{2,1,0:T(8,128)S(1)}, f32[512,128]{1,0:T(8,128)S(1)}, f32[6,512,128]{2,1,0:T(8,128)S(1)}, f32...) custom-call(f32[3,512,128]{2,1,0:T(8,128)S(1)} %copy-done.3, ...), custom_call_target="tpu_custom_call" | custom-call | flops 40000000 | bytes 10633740 | tf_op jit(solution)/shard_map/pallas_call | solution.py:409
  43.1 1.3 %collective-permute-start.4 = (f32[6,64,128]{2,1,0:T(8,128)S(1)}, f32[6,64,128]{2,1,0:T(8,128)S(1)}, u32[]{:S(2)}, u32[]{:S(2)}) collective-permute-start(f32[6,64,128]{2,1,0:T(8,128)S(1)} %get-tuple-element.32), channel_id=1, source_target_pairs={{28,4},{29,5},{30,6},{31,7},{0,8},{1,9},{2,10},{3,11},{12,20},{13,... | collective-permute-start | bytes 589832 | tf_op jit(solution)/shard_map/ppermute | solution.py:454
  44.4 2.1 %collective-permute-start.5 = (f32[6,64,128]{2,1,0:T(8,128)S(1)}, f32[6,64,128]{2,1,0:T(8,128)S(1)}, u32[]{:S(2)}, u32[]{:S(2)}) collective-permute-start(f32[6,64,128]{2,1,0:T(8,128)S(1)} %get-tuple-element.33), channel_id=1, source_target_pairs={{4,12},{5,13},{6,14},{7,15},{8,16},{9,17},{10,18},{11,19},{12,4},{... | collective-permute-start | bytes 589832 | tf_op jit(solution)/shard_map/ppermute | solution.py:454
  46.5 4.0 %collective-permute-done.4.ie_ref.gie_ref = f32[6,64,128]{2,1,0:T(8,128)S(1)} collective-permute-done((f32[6,64,128]{2,1,0:T(8,128)S(1)}, f32[6,64,128]{2,1,0:T(8,128)S(1)}, u32[]{:S(2)}, u32[]{:S(2)}) %collective-permute-start.4) | collective-permute-done | bytes 196640 | tf_op jit(solution)/shard_map/ppermute | solution.py:454
  50.5 4.3 %collective-permute-done.5.io_ref.gio_ref = f32[6,64,128]{2,1,0:T(8,128)S(1)} collective-permute-done((f32[6,64,128]{2,1,0:T(8,128)S(1)}, f32[6,64,128]{2,1,0:T(8,128)S(1)}, u32[]{:S(2)}, u32[]{:S(2)}) %collective-permute-start.5) | collective-permute-done | bytes 196640 | tf_op jit(solution)/shard_map/ppermute | solution.py:454
  54.8 0.6 shard_map.98
  55.4 0.5 collective-permute-start.6
  55.9 1.9 %collective-permute-start.7 = (f32[6,64,128]{2,1,0:T(8,128)S(1)}, f32[6,64,128]{2,1,0:T(8,128)S(1)}, u32[]{:S(2)}, u32[]{:S(2)}) collective-permute-start(f32[6,64,128]{2,1,0:T(8,128)S(1)} %get-tuple-element.37), channel_id=1, source_target_pairs={{29,30},{31,0},{1,2},{5,6},{7,8},{9,10},{13,14},{15,16},{17,18},{2... | collective-permute-start | bytes 589832 | tf_op jit(solution)/shard_map/ppermute | solution.py:454
  57.8 0.0 collective-permute-done.6.gje_ref
  57.8 6.8 %collective-permute-done.7.gjo_ref = f32[6,64,128]{2,1,0:T(8,128)S(1)} collective-permute-done((f32[6,64,128]{2,1,0:T(8,128)S(1)}, f32[6,64,128]{2,1,0:T(8,128)S(1)}, u32[]{:S(2)}, u32[]{:S(2)}) %collective-permute-start.7) | collective-permute-done | bytes 196640 | tf_op jit(solution)/shard_map/ppermute | solution.py:454
  64.7 0.0 copy-done.1
  64.7 0.0 copy-done.7
  64.7 0.0 copy-done.9
  64.7 0.0 copy-done.11
  64.7 4.4 %shard_map.99 = (f32[3,512,128]{2,1,0:T(8,128)}, f32[3,512,128]{2,1,0:T(8,128)}) custom-call(f32[3,512,128]{2,1,0:T(8,128)S(1)} %get-tuple-element.28.moment_ref, f32[3,512,128]{2,1,0:T(8,128)S(1)} %get-tuple-element.29.state_ref, f32[3,512,128]{2,1,0:T(8,128)S(1)} %copy-done.1, f32[512,128]{1,0:T(8,128)S(1)} %copy-done.7, f32[3]{0:T(128)S(1)} %copy-done.13, ...), custom_call_target="tpu_custom_call" | custom-call | flops 20000000 | bytes 7881228 | tf_op jit(solution)/shard_map/pallas_call | solution.py:409
  (1 shorter events, 0.0 us)
Async XLA Ops:
  0.6 1.1 %copy-start = (f32[3,512,128]{2,1,0:T(8,128)S(1)}, f32[3,512,128]{2,1,0:T(8,128)}, u32[]{:S(2)}) copy-start(f32[3,512,128]{2,1,0:T(8,128)} %flow_ref.5) | copy-start | bytes 2359300
  1.8 1.1 %copy-start.2 = (f32[3,512,128]{2,1,0:T(8,128)S(1)}, f32[3,512,128]{2,1,0:T(8,128)}, u32[]{:S(2)}) copy-start(f32[3,512,128]{2,1,0:T(8,128)} %moment_ref.3) | copy-start | bytes 2359300
  2.9 1.1 %copy-start.4 = (f32[3,512,128]{2,1,0:T(8,128)S(1)}, f32[3,512,128]{2,1,0:T(8,128)}, u32[]{:S(2)}) copy-start(f32[3,512,128]{2,1,0:T(8,128)} %state_ref.3) | copy-start | bytes 2359300
  4.0 0.9 %copy-start.6 = (f32[512,128]{1,0:T(8,128)S(1)}, f32[512,128]{1,0:T(8,128)}, u32[]{:S(2)}) copy-start(f32[512,128]{1,0:T(8,128)} %weight_ref.5) | copy-start | bytes 786436
  5.0 0.9 %copy-start.8 = (bf16[512,256]{1,0:T(8,128)(2,1)S(1)}, bf16[512,256]{1,0:T(8,128)(2,1)}, u32[]{:S(2)}) copy-start(bf16[512,256]{1,0:T(8,128)(2,1)} %constant.5.clone.turned_ref) | copy-start | bytes 786436
  5.9 0.9 %copy-start.10 = (bf16[512,256]{1,0:T(8,128)(2,1)S(1)}, bf16[512,256]{1,0:T(8,128)(2,1)}, u32[]{:S(2)}) copy-start(bf16[512,256]{1,0:T(8,128)(2,1)} %constant.4.clone.table_ref) | copy-start | bytes 786436
  6.9 0.7 copy-start.12
  7.5 0.7 copy-start.13
  8.2 29.3 %copy-start.3 = (f32[3,512,128]{2,1,0:T(8,128)S(1)}, f32[3,512,128]{2,1,0:T(8,128)}, u32[]{:S(2)}) copy-start(f32[3,512,128]{2,1,0:T(8,128)} %moment_ref.3) | copy-start | bytes 2359300
  8.2 29.3 %copy-start.5 = (f32[3,512,128]{2,1,0:T(8,128)S(1)}, f32[3,512,128]{2,1,0:T(8,128)}, u32[]{:S(2)}) copy-start(f32[3,512,128]{2,1,0:T(8,128)} %state_ref.3) | copy-start | bytes 2359300
  12.7 8.6 %collective-permute-start = (f32[7,64,128]{2,1,0:T(8,128)S(1)}, f32[7,64,128]{2,1,0:T(8,128)S(1)}, u32[]{:S(2)}, u32[]{:S(2)}) collective-permute-start(f32[7,64,128]{2,1,0:T(8,128)S(1)} %get-tuple-element.22), channel_id=1, source_target_pairs={{28,4},{29,5},{30,6},{31,7},{0,8},{1,9},{2,10},{3,11},{12,20},{13,... | collective-permute-start | bytes 688136 | tf_op jit(solution)/shard_map/ppermute | solution.py:454
  16.1 11.1 %collective-permute-start.1 = (f32[7,64,128]{2,1,0:T(8,128)S(1)}, f32[7,64,128]{2,1,0:T(8,128)S(1)}, u32[]{:S(2)}, u32[]{:S(2)}) collective-permute-start(f32[7,64,128]{2,1,0:T(8,128)S(1)} %get-tuple-element.23), channel_id=1, source_target_pairs={{4,12},{5,13},{6,14},{7,15},{8,16},{9,17},{10,18},{11,19},{12,4},{... | collective-permute-start | bytes 688136 | tf_op jit(solution)/shard_map/ppermute | solution.py:454
  27.8 2.5 %collective-permute-start.2 = (f32[7,64,128]{2,1,0:T(8,128)S(1)}, f32[7,64,128]{2,1,0:T(8,128)S(1)}, u32[]{:S(2)}, u32[]{:S(2)}) collective-permute-start(f32[7,64,128]{2,1,0:T(8,128)S(1)} %get-tuple-element.26), channel_id=1, source_target_pairs={{28,29},{30,31},{0,1},{2,3},{4,5},{6,7},{8,9},{10,11},{12,13},{14,... | collective-permute-start | bytes 688136 | tf_op jit(solution)/shard_map/ppermute | solution.py:454
  28.3 9.1 %collective-permute-start.3 = (f32[7,64,128]{2,1,0:T(8,128)S(1)}, f32[7,64,128]{2,1,0:T(8,128)S(1)}, u32[]{:S(2)}, u32[]{:S(2)}) collective-permute-start(f32[7,64,128]{2,1,0:T(8,128)S(1)} %get-tuple-element.27), channel_id=1, source_target_pairs={{29,30},{31,0},{1,2},{5,6},{7,8},{9,10},{13,14},{15,16},{17,18},{2... | collective-permute-start | bytes 688136 | tf_op jit(solution)/shard_map/ppermute | solution.py:454
  37.5 27.2 %copy-start.1 = (f32[3,512,128]{2,1,0:T(8,128)S(1)}, f32[3,512,128]{2,1,0:T(8,128)}, u32[]{:S(2)}) copy-start(f32[3,512,128]{2,1,0:T(8,128)} %flow_ref.5) | copy-start | bytes 2359300
  37.5 27.2 %copy-start.7 = (f32[512,128]{1,0:T(8,128)S(1)}, f32[512,128]{1,0:T(8,128)}, u32[]{:S(2)}) copy-start(f32[512,128]{1,0:T(8,128)} %weight_ref.5) | copy-start | bytes 786436
  37.5 27.2 %copy-start.9 = (bf16[512,256]{1,0:T(8,128)(2,1)S(1)}, bf16[512,256]{1,0:T(8,128)(2,1)}, u32[]{:S(2)}) copy-start(bf16[512,256]{1,0:T(8,128)(2,1)} %constant.5.clone.turned_ref) | copy-start | bytes 786436
  37.5 27.2 %copy-start.11 = (bf16[512,256]{1,0:T(8,128)(2,1)S(1)}, bf16[512,256]{1,0:T(8,128)(2,1)}, u32[]{:S(2)}) copy-start(bf16[512,256]{1,0:T(8,128)(2,1)} %constant.4.clone.table_ref) | copy-start | bytes 786436
  43.1 7.4 %collective-permute-start.4 = (f32[6,64,128]{2,1,0:T(8,128)S(1)}, f32[6,64,128]{2,1,0:T(8,128)S(1)}, u32[]{:S(2)}, u32[]{:S(2)}) collective-permute-start(f32[6,64,128]{2,1,0:T(8,128)S(1)} %get-tuple-element.32), channel_id=1, source_target_pairs={{28,4},{29,5},{30,6},{31,7},{0,8},{1,9},{2,10},{3,11},{12,20},{13,... | collective-permute-start | bytes 589832 | tf_op jit(solution)/shard_map/ppermute | solution.py:454
  44.4 10.4 %collective-permute-start.5 = (f32[6,64,128]{2,1,0:T(8,128)S(1)}, f32[6,64,128]{2,1,0:T(8,128)S(1)}, u32[]{:S(2)}, u32[]{:S(2)}) collective-permute-start(f32[6,64,128]{2,1,0:T(8,128)S(1)} %get-tuple-element.33), channel_id=1, source_target_pairs={{4,12},{5,13},{6,14},{7,15},{8,16},{9,17},{10,18},{11,19},{12,4},{... | collective-permute-start | bytes 589832 | tf_op jit(solution)/shard_map/ppermute | solution.py:454
  55.4 2.4 %collective-permute-start.6 = (f32[6,64,128]{2,1,0:T(8,128)S(1)}, f32[6,64,128]{2,1,0:T(8,128)S(1)}, u32[]{:S(2)}, u32[]{:S(2)}) collective-permute-start(f32[6,64,128]{2,1,0:T(8,128)S(1)} %get-tuple-element.36), channel_id=1, source_target_pairs={{28,29},{30,31},{0,1},{2,3},{4,5},{6,7},{8,9},{10,11},{12,13},{14,... | collective-permute-start | bytes 589832 | tf_op jit(solution)/shard_map/ppermute | solution.py:454
  55.9 8.8 %collective-permute-start.7 = (f32[6,64,128]{2,1,0:T(8,128)S(1)}, f32[6,64,128]{2,1,0:T(8,128)S(1)}, u32[]{:S(2)}, u32[]{:S(2)}) collective-permute-start(f32[6,64,128]{2,1,0:T(8,128)S(1)} %get-tuple-element.37), channel_id=1, source_target_pairs={{29,30},{31,0},{1,2},{5,6},{7,8},{9,10},{13,14},{15,16},{17,18},{2... | collective-permute-start | bytes 589832 | tf_op jit(solution)/shard_map/ppermute | solution.py:454
where the time goes:
time: 69.5 us; the launch traced here: 69 us
  waiting for transfers between devices  31.5 us (45%)
  Pallas kernels  15.7 us (23%)
  starting transfers between devices  13.5 us (19%)
  local copies, waits for them, and re-layouts  7.58 us (11%)
  between operations  0.76 us (1%)
    ppermute x8, waiting for transfers between devices, exchange(): return [lax.ppermute(b, 'elem', p) for b, p in zip(blocks, pairs)]  31.5 us
    pallas_call x5, Pallas kernels, call(): pl.pallas_call(kernel, out_shape=[jax.ShapeDtypeStruct(s, t) for s, t in...  15.7 us
    ppermute x8, starting transfers between devices, exchange(): return [lax.ppermute(b, 'elem', p) for b, p in zip(blocks, pairs)]  13.5 us
    unnamed x28, local copies, waits for them, and re-layouts  7.58 us
  transfers between devices with their start and end apart: 8, of which 6 were waited for; matrix products, arithmetic and copies ran while one was open for 0% of the time, Pallas kernels for 0%

commit v1 on v0

--- a/solution.py
+++ b/solution.py
@@ -95,6 +95,27 @@
     return jnp.concatenate([out[:, :128], out[:, 128:]], axis=0)
 
 
+def write_table(table, table_ref):
+    sub = lax.broadcasted_iota(jnp.int32, (8, 128), 0)
+    lane = lax.broadcasted_iota(jnp.int32, (8, 128), 1)
+    base = jnp.zeros((8, 128), F32)
+    for i in range(8):
+        one_row = jnp.zeros((8, 128), F32)
+        for q in range(8):
+            one_row = jnp.where((lane & 7) == q, float(table[i, q]), one_row)
+        base = jnp.where(sub == i, one_row, base)
+    high = base.astype(BF16).astype(F32)
+    block = lax.shift_right_logical(lane, 3)
+    zero = jnp.zeros((8, 128), F32)
+    for part, values in enumerate((high, base - high)):
+        for a in range(0, 32, 2):
+            pair = [jnp.where(block == (a + n) % 16, values, zero) for n in range(2)]
+            pair = jnp.concatenate(pair, axis=0)
+            wide = [pair, jnp.zeros((16, 128), F32)]
+            wide = jnp.concatenate(wide if a < 16 else wide[::-1], axis=1)
+            table_ref[pl.ds(256 * part + 8 * a, 16)] = wide.astype(BF16)
+
+
 def lanes(block, index):
     wide = jnp.broadcast_to(index[None], (block.shape[0] // 8, 8, 128)).reshape(block.shape)
     return jnp.take_along_axis(block, wide, axis=1, mode="promise_in_bounds")
@@ -177,22 +198,36 @@
             out[2 + way][c, pl.ds(i * 8, 8)] = lanes(j_face, inverse)
 
 
+def partner(ends, axis, way):
+    odd, inside = ends[2 + axis]
+    return (odd, inside) if way else (1 - odd, 1.0)
+
+
 def add_faces(c, ref, index, ends, got):
     height = index[0]
     for way in range(2):
+        slot, weight = partner(ends, 0, way)
         r = pl.ds(pl.multiple_of(ends[0][way] * 64, 64), 64)
-        ref[r] = ref[r] + lanes(got[way][c], height)
+        ref[r] = ref[r] + lanes(got[way][slot, c], height) * weight
     for way in range(2):
+        slot, weight = partner(ends, 1, way)
         for i in range(8):
             r = pl.ds(pl.multiple_of(ends[1][way] * 8 + i * 64, 8), 8)
-            ref[r] = ref[r] + lanes(got[2 + way][c, pl.ds(i * 8, 8)], height)
-
-
-def ends_of(number_ref, columns):
-    column = lax.shift_right_logical(number_ref[0], 7)
-    row_odd = lax.rem(lax.div(column, columns), 2)
-    place_odd = lax.rem(lax.rem(column, columns), 2)
-    return ((7 - 7 * row_odd, 7 * row_odd), (7 - 7 * place_odd, 7 * place_odd))
+            ref[r] = ref[r] + lanes(got[2 + way][slot, c, pl.ds(i * 8, 8)], height) * weight
+
+
+def ends_of(columns):
+    column = lax.rem(lax.axis_index("elem") + columns // 2, columns * DA)
+    row, place = lax.div(column, columns), lax.rem(column, columns)
+    row_odd, place_odd = lax.rem(row, 2), lax.rem(place, 2)
+    row_inside = jnp.where((row > 0) & (row < DA - 1), 1.0, 0.0)
+    place_inside = jnp.where((place > 0) & (place < columns - 1), 1.0, 0.0)
+    return (
+        (7 - 7 * row_odd, 7 * row_odd),
+        (7 - 7 * place_odd, 7 * place_odd),
+        (row_odd, row_inside),
+        (place_odd, place_inside),
+    )
 
 
 def index_of(index_ref):
@@ -201,13 +236,12 @@
 
 def first_kernel(
     columns,
-    moment_ref,
-    state_ref,
-    flow_ref,
-    weight_ref,
-    diff_ref,
-    number_ref,
-    numbers_ref,
+    moment_far,
+    state_far,
+    flow_far,
+    weight_far,
+    diff_far,
+    numbers_far,
     table_ref,
     turned_ref,
     index_ref,
@@ -218,8 +252,23 @@
     jo_ref,
     mass_ref,
     work_ref,
+    moment_ref,
+    state_ref,
+    flow_ref,
+    weight_ref,
+    numbers_ref,
+    diff_ref,
+    arrived,
 ):
-    ends = ends_of(number_ref, columns)
+    far = (numbers_far, weight_far, state_far, moment_far, flow_far, diff_far)
+    near = (numbers_ref, weight_ref, state_ref, moment_ref, flow_ref, diff_ref)
+    copies = [pltpu.make_async_copy(a, b, arrived.at[n]) for n, (a, b) in enumerate(zip(far, near))]
+    for copy in copies:
+        copy.start()
+    write_table(DM, table_ref)
+    write_table(DM.T, turned_ref)
+    ends = ends_of(columns)
+    copies[0].wait()
     height = jnp.broadcast_to(numbers_ref[...] & 127, (8, 128))
     square = jnp.broadcast_to(height[:1].astype(F32), (128, 128)).T
     lane = lax.broadcasted_iota(jnp.int32, (128, 128), 1).astype(F32)
@@ -234,12 +283,15 @@
     )
     for n in range(4):
         index_ref[n] = index[n]
+    copies[1].wait()
     set_mass(weight_ref, mass_ref)
     out = (ie_ref, io_ref, je_ref, jo_ref)
 
     joined_ref[6] = mass_ref[...]
     join_heights(joined_ref.at[6], index)
     send_faces(6, joined_ref.at[6], index, ends, out)
+    for copy in copies[2:]:
+        copy.wait()
 
     def one_field(f, carry):
         joined_ref[3 + f] = state_ref[f]
@@ -262,14 +314,15 @@
     lax.fori_loop(0, 3, one_field, 0)
 
 
-def edge_kernel(columns, count, number_ref, ie_ref, io_ref, je_ref, jo_ref, out_e, out_o):
-    ends = ends_of(number_ref, columns)
+def edge_kernel(columns, ie_ref, io_ref, je_ref, jo_ref, out_e, out_o):
+    ends = ends_of(columns)
     for way, (face, out) in enumerate(((je_ref, out_e), (jo_ref, out_o))):
         out[...] = face[...]
         r = pl.ds(pl.multiple_of(ends[1][way] * 8, 8), 8)
         for other, got in enumerate((ie_ref, io_ref)):
             w = pl.ds(pl.multiple_of(ends[0][other] * 8, 8), 8)
-            out[:, w] = out[:, w] + got[:, r]
+            slot, weight = partner(ends, 0, other)
+            out[:, w] = out[:, w] + got[slot, :, r] * weight
 
 
 def second_kernel(
@@ -279,7 +332,6 @@
     flow_ref,
     weight_ref,
     diff_ref,
-    number_ref,
     table_ref,
     turned_ref,
     index_ref,
@@ -300,7 +352,7 @@
     work_ref,
     hold_ref,
 ):
-    ends = ends_of(number_ref, columns)
+    ends = ends_of(columns)
     index = index_of(index_ref)
     set_mass(weight_ref, mass_ref)
     out = (ie_ref, io_ref, je_ref, jo_ref)
@@ -355,7 +407,6 @@
     flow_ref,
     weight_ref,
     diff_ref,
-    number_ref,
     table_ref,
     turned_ref,
     index_ref,
@@ -371,7 +422,7 @@
     work_ref,
     hold_ref,
 ):
-    ends = ends_of(number_ref, columns)
+    ends = ends_of(columns)
     index = index_of(index_ref)
     set_mass(weight_ref, mass_ref)
     got = (gie_ref, gio_ref, gje_ref, gjo_ref)
@@ -402,6 +453,7 @@
 
 VMEM = pl.BlockSpec(memory_space=pltpu.VMEM)
 SMEM = pl.BlockSpec(memory_space=pltpu.SMEM)
+FAR = pl.BlockSpec(memory_space=pltpu.HBM)
 
 
 def call(kernel, specs, shapes, scratch, flops, *operands):
@@ -411,7 +463,7 @@
         out_shape=[jax.ShapeDtypeStruct(s, t) for s, t in shapes],
         in_specs=specs,
         out_specs=[VMEM] * len(shapes),
-        scratch_shapes=[pltpu.VMEM(s, F32) for s in scratch],
+        scratch_shapes=scratch,
         compiler_params=pltpu.CompilerParams(vmem_limit_bytes=32 * 1024 * 1024),
         cost_estimate=pl.CostEstimate(flops=flops, bytes_accessed=moved, transcendentals=0),
     )(*operands)
@@ -421,84 +473,76 @@
     columns = devices // DA
     device = lambda row, place: (row * columns + place - columns // 2) % devices
 
-    def both(pairs):
-        return [(a, b) for a, b in pairs] + [(b, a) for a, b in pairs]
-
     along_i = [
-        both([(device(r, s), device(r + 1, s)) for r in range(way, DA - 1, 2) for s in range(columns)])
+        [(device(r, s), device((r + 1) % DA, s)) for r in range(way, DA, 2) for s in range(columns)]
         for way in range(2)
     ]
     along_j = [
-        both([(device(r, s), device(r, s + 1)) for r in range(DA) for s in range(way, columns - 1, 2)])
+        [
+            (device(r, s), device(r, (s + 1) % columns))
+            for r in range(DA)
+            for s in range(way, columns, 2)
+        ]
         for way in range(2)
     ]
     return along_i, along_j
-
-
-def split_table(table):
-    wide = np.kron(np.eye(32), table).astype(np.float32)
-    high = wide.astype(jnp.bfloat16)
-    low = (wide - high.astype(np.float32)).astype(jnp.bfloat16)
-    return jnp.asarray(np.concatenate([high, low], axis=0))
 
 
 def shards(moment_fields, adjoint_fields, velocity, mass_weights, diffusivity, numbering):
     devices = lax.axis_size("elem")
     columns = devices // DA
     along_i, along_j = pairings(devices)
-    table, turned = split_table(DM), split_table(DM.T)
     numbers = numbering.reshape(1, 128)
     whole = (3, 512, 128)
 
     def exchange(blocks, pairs):
-        return [lax.ppermute(b, "elem", p) for b, p in zip(blocks, pairs)]
+        return [
+            lax.all_gather(b, "elem", axis_index_groups=p) for b, p in zip(blocks, pairs)
+        ]
 
     def meet(count, faces):
         got_i = exchange(faces[:2], along_i)
         faces_j = call(
-            functools.partial(edge_kernel, columns, count),
-            [SMEM] + [VMEM] * 4,
+            functools.partial(edge_kernel, columns),
+            [VMEM] * 4,
             [((count, 64, 128), F32)] * 2,
             [],
             count * 64 * 128,
-            numbering,
             *got_i,
             *faces[2:],
         )
         return got_i + exchange(faces_j, along_j)
 
+    def far(array):
+        return pltpu.with_memory_space_constraint(array, pltpu.HBM)
+
     def faces_shape(count):
         return [((count, 64, 128), F32)] * 4
 
-    index, joined, *faces = call(
+    table, turned, index, joined, *faces = call(
         functools.partial(first_kernel, columns),
-        [VMEM] * 4 + [SMEM] * 2 + [VMEM] * 3,
-        [((4, 8, 128), jnp.int32), ((7, 512, 128), F32)] + faces_shape(7),
-        [(512, 128)] * 2,
+        [FAR] * 6,
+        [((512, 256), BF16)] * 2 + [((4, 8, 128), jnp.int32), ((7, 512, 128), F32)] + faces_shape(7),
+        [pltpu.VMEM((512, 128), F32)] * 2
+        + [pltpu.VMEM(whole, F32)] * 3
+        + [pltpu.VMEM((512, 128), F32), pltpu.VMEM((1, 128), jnp.int32)]
+        + [pltpu.SMEM((3,), F32), pltpu.SemaphoreType.DMA((6,))],
         20_000_000,
-        moment_fields,
-        adjoint_fields,
-        velocity,
-        mass_weights,
-        diffusivity,
-        numbering,
-        numbers,
-        table,
-        turned,
+        *map(far, (moment_fields, adjoint_fields, velocity, mass_weights)),
+        *map(far, (diffusivity, numbers)),
     )
     got = meet(7, faces)
     moment_one, state_one, inverse, joined, *faces = call(
         functools.partial(second_kernel, columns),
-        [VMEM] * 4 + [SMEM] * 2 + [VMEM] * 8,
+        [VMEM] * 4 + [SMEM] + [VMEM] * 8,
         [(whole, F32), (whole, F32), ((512, 128), F32), ((6, 512, 128), F32)] + faces_shape(6),
-        [(512, 128)] * 3,
+        [pltpu.VMEM((512, 128), F32)] * 3,
         40_000_000,
         moment_fields,
         adjoint_fields,
         velocity,
         mass_weights,
         diffusivity,
-        numbering,
         table,
         turned,
         index,
@@ -509,16 +553,15 @@
     return tuple(
         call(
             functools.partial(third_kernel, columns),
-            [VMEM] * 4 + [SMEM] * 2 + [VMEM] * 9,
+            [VMEM] * 4 + [SMEM] + [VMEM] * 9,
             [(whole, F32), (whole, F32)],
-            [(512, 128)] * 3,
+            [pltpu.VMEM((512, 128), F32)] * 3,
             20_000_000,
             moment_one,
             state_one,
             velocity,
             mass_weights,
             diffusivity,
-            numbering,
             table,
             turned,
             index,

time: 69.5 us -> 76.9 us (1.11)
  the two profiles are of different devices: /device:TPU:7 before, /device:TPU:0 now
where the time goes in v1:
time: 76.9 us; the launch traced here: 76.3 us
  blocking collectives  60.1 us (78%)
  Pallas kernels  15.5 us (20%)
    all_gather x8, blocking collectives, exchange(): lax.all_gather(b, 'elem', axis_index_groups=p)  60.1 us
    pallas_call x5, Pallas kernels, call(): pl.pallas_call(kernel, out_shape=[jax.ShapeDtypeStruct(s, t) for s, t in...  15.5 us

profile of v1, /device:TPU:0, one launch (start us, length us, event | category | flops | bytes accessed | tf_op | source)
XLA Modules:
  0.0 76.3 jit_solution(7164338280855135146)
XLA Ops:
  0.6 5.4 %shard_map.77 = (bf16[512,256]{1,0:T(8,128)(2,1)S(1)}, bf16[512,256]{1,0:T(8,128)(2,1)S(1)}, s32[4,8,128]{2,1,0:T(8,128)S(1)}, f32[7,512,128]{2,1,0:T(8,128)S(1)...) custom-call(f32[3,512,128]{2,1,0:T(8,128)} %moment_ref.1, ...), custom_call_target="tpu_custom_call" | custom-call | flops 20000000 | bytes 6439436 | tf_op jit(solution)/shard_map/pallas_call | solution.py:461
  6.0 9.3 %all-gather = f32[14,64,128]{2,1,0:T(8,128)S(1)} all-gather(f32[7,64,128]{2,1,0:T(8,128)S(1)} %get-tuple-element.26), channel_id=2, replica_groups={{28,4},{29,5},{30,6},{31,7},{0,8},{1,9},{2,10},{3,11},{12,20},{13,21},{..., dimensions={0}, use_global_device_ids=true | all-gather | bytes 688128 | tf_op jit(solution)/shard_map/all_gather | solution.py:500
  15.3 0.0 copy-start
  15.3 0.0 copy-start.1
  15.3 0.0 copy-start.2
  15.3 0.0 copy-start.3
  15.3 0.0 copy-start.4
  15.3 9.5 %all-gather.1 = f32[14,64,128]{2,1,0:T(8,128)S(1)} all-gather(f32[7,64,128]{2,1,0:T(8,128)S(1)} %get-tuple-element.27), channel_id=3, replica_groups={{4,12},{5,13},{6,14},{7,15},{8,16},{9,17},{10,18},{11,19},{20,28},{21,2..., dimensions={0}, use_global_device_ids=true | all-gather | bytes 688128 | tf_op jit(solution)/shard_map/all_gather | solution.py:500
  24.8 0.1 shard_map.78
  24.9 2.1 %all-gather.2 = f32[14,64,128]{2,1,0:T(8,128)S(1)} all-gather(f32[7,64,128]{2,1,0:T(8,128)S(1)} %get-tuple-element.30), channel_id=4, replica_groups={{28,29},{30,31},{0,1},{2,3},{4,5},{6,7},{8,9},{10,11},{12,13},{14,15},{..., dimensions={0}, use_global_device_ids=true | all-gather | bytes 688128 | tf_op jit(solution)/shard_map/all_gather | solution.py:500
  27.0 11.2 %all-gather.3 = f32[14,64,128]{2,1,0:T(8,128)S(1)} all-gather(f32[7,64,128]{2,1,0:T(8,128)S(1)} %get-tuple-element.31), channel_id=5, replica_groups={{29,30},{31,0},{1,2},{3,28},{5,6},{7,8},{9,10},{11,4},{13,14},{15,16},{..., dimensions={0}, use_global_device_ids=true | all-gather | bytes 688128 | tf_op jit(solution)/shard_map/all_gather | solution.py:500
  38.2 0.0 copy-done
  38.2 0.0 copy-done.1
  38.3 0.0 copy-done.2
  38.3 0.0 copy-done.3
  38.3 0.0 copy-done.4
  38.3 5.6 %shard_map.79 = (f32[3,512,128]{2,1,0:T(8,128)S(1)}, f32[3,512,128]{2,1,0:T(8,128)S(1)}, f32[512,128]{1,0:T(8,128)S(1)}, f32[6,512,128]{2,1,0:T(8,128)S(1)}, f32...) custom-call(f32[3,512,128]{2,1,0:T(8,128)S(1)} %copy-done.1, ...), custom_call_target="tpu_custom_call" | custom-call | flops 40000000 | bytes 11550732 | tf_op jit(solution)/shard_map/pallas_call | solution.py:461
  43.9 7.6 %all-gather.4 = f32[12,64,128]{2,1,0:T(8,128)S(1)} all-gather(f32[6,64,128]{2,1,0:T(8,128)S(1)} %get-tuple-element.36), channel_id=6, replica_groups={{28,4},{29,5},{30,6},{31,7},{0,8},{1,9},{2,10},{3,11},{12,20},{13,21},{..., dimensions={0}, use_global_device_ids=true | all-gather | bytes 589824 | tf_op jit(solution)/shard_map/all_gather | solution.py:500
  51.5 8.7 %all-gather.5 = f32[12,64,128]{2,1,0:T(8,128)S(1)} all-gather(f32[6,64,128]{2,1,0:T(8,128)S(1)} %get-tuple-element.37), channel_id=7, replica_groups={{4,12},{5,13},{6,14},{7,15},{8,16},{9,17},{10,18},{11,19},{20,28},{21,2..., dimensions={0}, use_global_device_ids=true | all-gather | bytes 589824 | tf_op jit(solution)/shard_map/all_gather | solution.py:500
  60.2 0.1 shard_map.80
  60.3 2.1 %all-gather.6 = f32[12,64,128]{2,1,0:T(8,128)S(1)} all-gather(f32[6,64,128]{2,1,0:T(8,128)S(1)} %get-tuple-element.40), channel_id=8, replica_groups={{28,29},{30,31},{0,1},{2,3},{4,5},{6,7},{8,9},{10,11},{12,13},{14,15},{..., dimensions={0}, use_global_device_ids=true | all-gather | bytes 589824 | tf_op jit(solution)/shard_map/all_gather | solution.py:500
  62.3 9.6 %all-gather.7 = f32[12,64,128]{2,1,0:T(8,128)S(1)} all-gather(f32[6,64,128]{2,1,0:T(8,128)S(1)} %get-tuple-element.41), channel_id=9, replica_groups={{29,30},{31,0},{1,2},{3,28},{5,6},{7,8},{9,10},{11,4},{13,14},{15,16},{..., dimensions={0}, use_global_device_ids=true | all-gather | bytes 589824 | tf_op jit(solution)/shard_map/all_gather | solution.py:500
  71.9 4.4 %shard_map.81 = (f32[3,512,128]{2,1,0:T(8,128)}, f32[3,512,128]{2,1,0:T(8,128)}) custom-call(f32[3,512,128]{2,1,0:T(8,128)S(1)} %get-tuple-element.32.moment_ref, f32[3,512,128]{2,1,0:T(8,128)S(1)} %get-tuple-element.33.state_ref, f32[3,512,128]{2,1,0:T(8,128)S(1)} %copy-done, f32[512,128]{1,0:T(8,128)S(1)} %copy-done.3, f32[3]{0:T(128)S(1)} %copy-done.4, ...), custom_call_target="tpu_custom_call" | custom-call | flops 20000000 | bytes 8667148 | tf_op jit(solution)/shard_map/pallas_call | solution.py:461
Async XLA Ops:
  15.3 23.0 %copy-start = (f32[3,512,128]{2,1,0:T(8,128)S(1)}, f32[3,512,128]{2,1,0:T(8,128)}, u32[]{:S(2)}) copy-start(f32[3,512,128]{2,1,0:T(8,128)} %flow_ref.3) | copy-start | bytes 2359300
  15.3 23.0 %copy-start.1 = (f32[3,512,128]{2,1,0:T(8,128)S(1)}, f32[3,512,128]{2,1,0:T(8,128)}, u32[]{:S(2)}) copy-start(f32[3,512,128]{2,1,0:T(8,128)} %moment_ref.1) | copy-start | bytes 2359300
  15.3 23.0 %copy-start.2 = (f32[3,512,128]{2,1,0:T(8,128)S(1)}, f32[3,512,128]{2,1,0:T(8,128)}, u32[]{:S(2)}) copy-start(f32[3,512,128]{2,1,0:T(8,128)} %state_ref.1) | copy-start | bytes 2359300
  15.3 23.0 %copy-start.3 = (f32[512,128]{1,0:T(8,128)S(1)}, f32[512,128]{1,0:T(8,128)}, u32[]{:S(2)}) copy-start(f32[512,128]{1,0:T(8,128)} %weight_ref.3) | copy-start | bytes 786436
  15.3 23.0 %copy-start.4 = (f32[3]{0:T(128)S(1)}, f32[3]{0:T(128)}, u32[]{:S(2)}) copy-start(f32[3]{0:T(128)} %diff_ref.3) | copy-start | bytes 40

commit v2 on v1

--- a/solution.py
+++ b/solution.py
@@ -132,7 +132,7 @@
             mass_ref[r] = weight_ref[r] * (along * float(WEIGHTS[i] * WEIGHTS[j]))
 
 
-def forward(f, source, flow_ref, mass_ref, diff, table_ref, turned_ref, work, target):
+def forward(source, flow_ref, mass_ref, diff, table_ref, turned_ref, work, target):
     slope = along_k(table_ref, source[...])
     flux = slope * mass_ref[...]
     work[...] = flow_ref[2] * flux + diff * along_k(turned_ref, flux)
@@ -152,7 +152,7 @@
             target[r] = -(target[r] + work[r] + (flow_ref[1, r] * fluxes[j] + diff * back[j]))
 
 
-def adjoint(f, source, base, flow_ref, mass_ref, diff, table_ref, turned_ref, work, target):
+def adjoint(source, base, flow_ref, mass_ref, diff, table_ref, turned_ref, work, target):
     slope = along_k(table_ref, source[...])
     flux = (flow_ref[2] * source[...] + diff * slope) * mass_ref[...]
     work[...] = along_k(turned_ref, flux)
@@ -198,70 +198,48 @@
             out[2 + way][c, pl.ds(i * 8, 8)] = lanes(j_face, inverse)
 
 
-def partner(ends, axis, way):
-    odd, inside = ends[2 + axis]
-    return (odd, inside) if way else (1 - odd, 1.0)
-
-
 def add_faces(c, ref, index, ends, got):
     height = index[0]
     for way in range(2):
-        slot, weight = partner(ends, 0, way)
         r = pl.ds(pl.multiple_of(ends[0][way] * 64, 64), 64)
-        ref[r] = ref[r] + lanes(got[way][slot, c], height) * weight
+        ref[r] = ref[r] + lanes(got[way][c], height)
     for way in range(2):
-        slot, weight = partner(ends, 1, way)
         for i in range(8):
             r = pl.ds(pl.multiple_of(ends[1][way] * 8 + i * 64, 8), 8)
-            ref[r] = ref[r] + lanes(got[2 + way][slot, c, pl.ds(i * 8, 8)], height) * weight
+            ref[r] = ref[r] + lanes(got[2 + way][c, pl.ds(i * 8, 8)], height)
 
 
 def ends_of(columns):
     column = lax.rem(lax.axis_index("elem") + columns // 2, columns * DA)
-    row, place = lax.div(column, columns), lax.rem(column, columns)
-    row_odd, place_odd = lax.rem(row, 2), lax.rem(place, 2)
-    row_inside = jnp.where((row > 0) & (row < DA - 1), 1.0, 0.0)
-    place_inside = jnp.where((place > 0) & (place < columns - 1), 1.0, 0.0)
-    return (
-        (7 - 7 * row_odd, 7 * row_odd),
-        (7 - 7 * place_odd, 7 * place_odd),
-        (row_odd, row_inside),
-        (place_odd, place_inside),
-    )
+    row_odd = lax.rem(lax.div(column, columns), 2)
+    place_odd = lax.rem(lax.rem(column, columns), 2)
+    return ((7 - 7 * row_odd, 7 * row_odd), (7 - 7 * place_odd, 7 * place_odd))
 
 
 def index_of(index_ref):
     return tuple(index_ref[n] for n in range(4))
 
 
-def first_kernel(
+def index_kernel(
     columns,
-    moment_far,
     state_far,
-    flow_far,
     weight_far,
-    diff_far,
     numbers_far,
     table_ref,
     turned_ref,
     index_ref,
+    mass_ref,
     joined_ref,
     ie_ref,
     io_ref,
     je_ref,
     jo_ref,
-    mass_ref,
-    work_ref,
-    moment_ref,
-    state_ref,
-    flow_ref,
     weight_ref,
     numbers_ref,
-    diff_ref,
     arrived,
 ):
-    far = (numbers_far, weight_far, state_far, moment_far, flow_far, diff_far)
-    near = (numbers_ref, weight_ref, state_ref, moment_ref, flow_ref, diff_ref)
+    far = (numbers_far, weight_far, state_far)
+    near = (numbers_ref, weight_ref, joined_ref.at[pl.ds(0, 3)])
     copies = [pltpu.make_async_copy(a, b, arrived.at[n]) for n, (a, b) in enumerate(zip(far, near))]
     for copy in copies:
         copy.start()
@@ -285,18 +263,36 @@
         index_ref[n] = index[n]
     copies[1].wait()
     set_mass(weight_ref, mass_ref)
+    joined_ref[3] = mass_ref[...]
+    copies[2].wait()
     out = (ie_ref, io_ref, je_ref, jo_ref)
-
-    joined_ref[6] = mass_ref[...]
-    join_heights(joined_ref.at[6], index)
-    send_faces(6, joined_ref.at[6], index, ends, out)
-    for copy in copies[2:]:
-        copy.wait()
+    for c in range(4):
+        join_heights(joined_ref.at[c], index)
+        send_faces(c, joined_ref.at[c], index, ends, out)
+
+
+def moment_kernel(
+    columns,
+    moment_ref,
+    flow_ref,
+    diff_ref,
+    table_ref,
+    turned_ref,
+    index_ref,
+    mass_ref,
+    joined_ref,
+    ie_ref,
+    io_ref,
+    je_ref,
+    jo_ref,
+    work_ref,
+):
+    ends = ends_of(columns)
+    index = index_of(index_ref)
+    out = (ie_ref, io_ref, je_ref, jo_ref)
 
     def one_field(f, carry):
-        joined_ref[3 + f] = state_ref[f]
         forward(
-            f,
             moment_ref.at[f],
             flow_ref,
             mass_ref,
@@ -306,9 +302,8 @@
             work_ref,
             joined_ref.at[f],
         )
-        for c in (f, 3 + f):
-            join_heights(joined_ref.at[c], index)
-            send_faces(c, joined_ref.at[c], index, ends, out)
+        join_heights(joined_ref.at[f], index)
+        send_faces(f, joined_ref.at[f], index, ends, out)
         return carry
 
     lax.fori_loop(0, 3, one_field, 0)
@@ -321,66 +316,39 @@
         r = pl.ds(pl.multiple_of(ends[1][way] * 8, 8), 8)
         for other, got in enumerate((ie_ref, io_ref)):
             w = pl.ds(pl.multiple_of(ends[0][other] * 8, 8), 8)
-            slot, weight = partner(ends, 0, other)
-            out[:, w] = out[:, w] + got[slot, :, r] * weight
-
-
-def second_kernel(
+            out[:, w] = out[:, w] + got[:, r]
+
+
+def state_kernel(
     columns,
-    moment_ref,
+    first,
     state_ref,
     flow_ref,
-    weight_ref,
     diff_ref,
     table_ref,
     turned_ref,
     index_ref,
+    mass_ref,
     joined_ref,
-    gie_ref,
-    gio_ref,
-    gje_ref,
-    gjo_ref,
-    moment_out,
-    state_out,
-    inverse_out,
-    joined_out,
-    ie_ref,
-    io_ref,
-    je_ref,
-    jo_ref,
-    mass_ref,
-    work_ref,
-    hold_ref,
+    *refs,
 ):
     ends = ends_of(columns)
     index = index_of(index_ref)
-    set_mass(weight_ref, mass_ref)
-    out = (ie_ref, io_ref, je_ref, jo_ref)
-    got = (gie_ref, gio_ref, gje_ref, gjo_ref)
-    hold_ref[...] = joined_ref[6]
-    add_faces(6, hold_ref, index, ends, got)
-    inverse_out[...] = 1.0 / hold_ref[...]
+    if first:
+        got, (inverse_ref, state_out, joined_out), refs = refs[:4], refs[4:7], refs[7:]
+        out, (work_ref, hold_ref) = refs[:4], refs[4:]
+        hold_ref[...] = joined_ref[3]
+        add_faces(3, hold_ref, index, ends, got)
+        inverse_ref[...] = 1.0 / hold_ref[...]
+    else:
+        inverse_ref, *got = refs[:5]
+        state_out, work_ref, hold_ref = refs[5:]
 
     def one_field(f, carry):
         hold_ref[...] = joined_ref[f]
         add_faces(f, hold_ref, index, ends, got)
-        moment_out[f] = moment_ref[f] + DT * (hold_ref[...] * inverse_out[...])
-        forward(
-            f,
-            moment_out.at[f],
-            flow_ref,
-            mass_ref,
-            diff_ref[f],
-            table_ref,
-            turned_ref,
-            work_ref,
-            joined_out.at[f],
-        )
-        hold_ref[...] = joined_ref[3 + f]
-        add_faces(3 + f, hold_ref, index, ends, got)
-        hold_ref[...] = hold_ref[...] * inverse_out[...]
+        hold_ref[...] = hold_ref[...] * inverse_ref[...]
         adjoint(
-            f,
             hold_ref,
             state_ref.at[f],
             flow_ref,
@@ -391,24 +359,72 @@
             work_ref,
             state_out.at[f],
         )
-        joined_out[3 + f] = state_out[f]
-        for c in (f, 3 + f):
-            join_heights(joined_out.at[c], index)
-            send_faces(c, joined_out.at[c], index, ends, out)
+        if first:
+            joined_out[f] = state_out[f]
+            join_heights(joined_out.at[f], index)
+            send_faces(f, joined_out.at[f], index, ends, out)
         return carry
 
     lax.fori_loop(0, 3, one_field, 0)
 
 
-def third_kernel(
+def moment_step(f, ends, index, moment_ref, joined_ref, inverse_ref, got, hold_ref, moment_out):
+    hold_ref[...] = joined_ref[f]
+    add_faces(f, hold_ref, index, ends, got)
+    moment_out[f] = moment_ref[f] + DT * (hold_ref[...] * inverse_ref[...])
+
+
+def middle_kernel(
     columns,
     moment_ref,
-    state_ref,
     flow_ref,
-    weight_ref,
     diff_ref,
     table_ref,
     turned_ref,
+    index_ref,
+    mass_ref,
+    inverse_ref,
+    joined_ref,
+    gie_ref,
+    gio_ref,
+    gje_ref,
+    gjo_ref,
+    moment_out,
+    joined_out,
+    ie_ref,
+    io_ref,
+    je_ref,
+    jo_ref,
+    work_ref,
+    hold_ref,
+):
+    ends = ends_of(columns)
+    index = index_of(index_ref)
+    out = (ie_ref, io_ref, je_ref, jo_ref)
+    got = (gie_ref, gio_ref, gje_ref, gjo_ref)
+
+    def one_field(f, carry):
+        moment_step(f, ends, index, moment_ref, joined_ref, inverse_ref, got, hold_ref, moment_out)
+        forward(
+            moment_out.at[f],
+            flow_ref,
+            mass_ref,
+            diff_ref[f],
+            table_ref,
+            turned_ref,
+            work_ref,
+            joined_out.at[f],
+        )
+        join_heights(joined_out.at[f], index)
+        send_faces(f, joined_out.at[f], index, ends, out)
+        return carry
+
+    lax.fori_loop(0, 3, one_field, 0)
+
+
+def last_kernel(
+    columns,
+    moment_ref,
     index_ref,
     inverse_ref,
     joined_ref,
@@ -417,35 +433,14 @@
     gje_ref,
     gjo_ref,
     moment_out,
-    state_out,
-    mass_ref,
-    work_ref,
     hold_ref,
 ):
     ends = ends_of(columns)
     index = index_of(index_ref)
-    set_mass(weight_ref, mass_ref)
     got = (gie_ref, gio_ref, gje_ref, gjo_ref)
 
     def one_field(f, carry):
-        hold_ref[...] = joined_ref[f]
-        add_faces(f, hold_ref, index, ends, got)
-        moment_out[f] = moment_ref[f] + DT * (hold_ref[...] * inverse_ref[...])
-        hold_ref[...] = joined_ref[3 + f]
-        add_faces(3 + f, hold_ref, index, ends, got)
-        hold_ref[...] = hold_ref[...] * inverse_ref[...]
-        adjoint(
-            f,
-            hold_ref,
-            state_ref.at[f],
-            flow_ref,
-            mass_ref,
-            diff_ref[f],
-            table_ref,
-            turned_ref,
-            work_ref,
-            state_out.at[f],
-        )
+        moment_step(f, ends, index, moment_ref, joined_ref, inverse_ref, got, hold_ref, moment_out)
         return carry
 
     lax.fori_loop(0, 3, one_field, 0)
@@ -473,16 +468,15 @@
     columns = devices // DA
     device = lambda row, place: (row * columns + place - columns // 2) % devices
 
+    def both(pairs):
+        return [(a, b) for a, b in pairs] + [(b, a) for a, b in pairs]
+
     along_i = [
-        [(device(r, s), device((r + 1) % DA, s)) for r in range(way, DA, 2) for s in range(columns)]
+        both([(device(r, s), device(r + 1, s)) for r in range(way, DA - 1, 2) for s in range(columns)])
         for way in range(2)
     ]
     along_j = [
-        [
-            (device(r, s), device(r, (s + 1) % columns))
-            for r in range(DA)
-            for s in range(way, columns, 2)
-        ]
+        both([(device(r, s), device(r, s + 1)) for r in range(DA) for s in range(way, columns - 1, 2)])
         for way in range(2)
     ]
     return along_i, along_j
@@ -492,13 +486,11 @@
     devices = lax.axis_size("elem")
     columns = devices // DA
     along_i, along_j = pairings(devices)
-    numbers = numbering.reshape(1, 128)
-    whole = (3, 512, 128)
+    whole, block = ((3, 512, 128), F32), ((512, 128), F32)
+    work = pltpu.VMEM((512, 128), F32)
 
     def exchange(blocks, pairs):
-        return [
-            lax.all_gather(b, "elem", axis_index_groups=p) for b, p in zip(blocks, pairs)
-        ]
+        return [lax.ppermute(b, "elem", p) for b, p in zip(blocks, pairs)]
 
     def meet(count, faces):
         got_i = exchange(faces[:2], along_i)
@@ -519,57 +511,86 @@
     def faces_shape(count):
         return [((count, 64, 128), F32)] * 4
 
-    table, turned, index, joined, *faces = call(
-        functools.partial(first_kernel, columns),
-        [FAR] * 6,
-        [((512, 256), BF16)] * 2 + [((4, 8, 128), jnp.int32), ((7, 512, 128), F32)] + faces_shape(7),
-        [pltpu.VMEM((512, 128), F32)] * 2
-        + [pltpu.VMEM(whole, F32)] * 3
-        + [pltpu.VMEM((512, 128), F32), pltpu.VMEM((1, 128), jnp.int32)]
-        + [pltpu.SMEM((3,), F32), pltpu.SemaphoreType.DMA((6,))],
+    table, turned, index, mass, joined_state, *faces_state = call(
+        functools.partial(index_kernel, columns),
+        [FAR] * 3,
+        [((512, 256), BF16)] * 2
+        + [((4, 8, 128), jnp.int32), block, ((4, 512, 128), F32)]
+        + faces_shape(4),
+        [
+            work,
+            pltpu.VMEM((1, 128), jnp.int32),
+            pltpu.SemaphoreType.DMA((3,)),
+        ],
+        1_000_000,
+        *map(far, (adjoint_fields, mass_weights, numbering.reshape(1, 128))),
+    )
+    tables = (diffusivity, table, turned, index, mass)
+    got_state = meet(4, faces_state)
+    joined_moment, *faces_moment = call(
+        functools.partial(moment_kernel, columns),
+        [VMEM] * 2 + [SMEM] + [VMEM] * 4,
+        [whole] + faces_shape(3),
+        [work],
         20_000_000,
-        *map(far, (moment_fields, adjoint_fields, velocity, mass_weights)),
-        *map(far, (diffusivity, numbers)),
-    )
-    got = meet(7, faces)
-    moment_one, state_one, inverse, joined, *faces = call(
-        functools.partial(second_kernel, columns),
-        [VMEM] * 4 + [SMEM] + [VMEM] * 8,
-        [(whole, F32), (whole, F32), ((512, 128), F32), ((6, 512, 128), F32)] + faces_shape(6),
-        [pltpu.VMEM((512, 128), F32)] * 3,
-        40_000_000,
         moment_fields,
+        velocity,
+        *tables,
+    )
+    got_moment = meet(3, faces_moment)
+    inverse, state, joined_state, *faces_state = call(
+        functools.partial(state_kernel, columns, True),
+        [VMEM] * 2 + [SMEM] + [VMEM] * 9,
+        [block, whole, whole] + faces_shape(3),
+        [work] * 2,
+        20_000_000,
         adjoint_fields,
         velocity,
-        mass_weights,
-        diffusivity,
-        table,
-        turned,
+        *tables,
+        joined_state,
+        *got_state,
+    )
+    got_state = meet(3, faces_state)
+    moment, joined_moment, *faces_moment = call(
+        functools.partial(middle_kernel, columns),
+        [VMEM] * 2 + [SMEM] + [VMEM] * 10,
+        [whole, whole] + faces_shape(3),
+        [work] * 2,
+        20_000_000,
+        moment_fields,
+        velocity,
+        *tables,
+        inverse,
+        joined_moment,
+        *got_moment,
+    )
+    got_moment = meet(3, faces_moment)
+    (state,) = call(
+        functools.partial(state_kernel, columns, False),
+        [VMEM] * 2 + [SMEM] + [VMEM] * 10,
+        [whole],
+        [work] * 2,
+        20_000_000,
+        state,
+        velocity,
+        *tables,
+        joined_state,
+        inverse,
+        *got_state,
+    )
+    (moment,) = call(
+        functools.partial(last_kernel, columns),
+        [VMEM] * 8,
+        [whole],
+        [work],
+        1_000_000,
+        moment,
         index,
-        joined,
-        *got,
-    )
-    got = meet(6, faces)
-    return tuple(
-        call(
-            functools.partial(third_kernel, columns),
-            [VMEM] * 4 + [SMEM] + [VMEM] * 9,
-            [(whole, F32), (whole, F32)],
-            [pltpu.VMEM((512, 128), F32)] * 3,
-            20_000_000,
-            moment_one,
-            state_one,
-            velocity,
-            mass_weights,
-            diffusivity,
-            table,
-            turned,
-            index,
-            inverse,
-            joined,
-            *got,
-        )
-    )
+        inverse,
+        joined_moment,
+        *got_moment,
+    )
+    return moment, state
 
 
 def solution(mesh):

time: 76.9 us -> 59.2 us (0.77)
  blocking collectives: 60.1 us -> 0 us
  starting transfers between devices: 0 us -> 33.2 us
  waiting for transfers between devices: 0 us -> 3.74 us
  Pallas kernels: 15.5 us -> 19.2 us
  local copies, waits for them, and re-layouts: 0.02 us -> 1.79 us
    all_gather x8 -> x0, blocking collectives: 60.1 us -> none  [exchange(): lax.all_gather(b, 'elem', axis_index_groups=p)]
    ppermute x0 -> x16, starting transfers between devices: none -> 33.2 us  [exchange(): return [lax.ppermute(b, 'elem', p) for b, p in zip(blocks, pairs)]]
    ppermute x0 -> x16, waiting for transfers between devices: none -> 3.74 us  [exchange(): return [lax.ppermute(b, 'elem', p) for b, p in zip(blocks, pairs)]]
    pallas_call x5 -> x10, Pallas kernels: 15.5 us -> 19.2 us  [call(): pl.pallas_call(kernel, out_shape=[jax.ShapeDtypeStruct(s, t) for s, t in...]
    unnamed x10, local copies, waits for them, and re-layouts: 0.02 us -> 1.79 us
  transfers between devices with their start and end apart: 0 -> 16, of which waited for: 0 -> 3; matrix products, arithmetic and copies ran while one was open for 0% -> 0% of each run, Pallas kernels for 0% -> 27%
where the time goes in v2:
time: 59.2 us; the launch traced here: 58.9 us
  starting transfers between devices  33.2 us (56%)
  Pallas kernels  19.2 us (32%)
  waiting for transfers between devices  3.74 us (6%)
  local copies, waits for them, and re-layouts  1.79 us (3%)
  between operations  0.93 us (2%)
    ppermute x16, starting transfers between devices, exchange(): return [lax.ppermute(b, 'elem', p) for b, p in zip(blocks, pairs)]  33.2 us
    pallas_call x10, Pallas kernels, call(): pl.pallas_call(kernel, out_shape=[jax.ShapeDtypeStruct(s, t) for s, t in...  19.2 us
    ppermute x16, waiting for transfers between devices, exchange(): return [lax.ppermute(b, 'elem', p) for b, p in zip(blocks, pairs)]  3.74 us
    unnamed x10, local copies, waits for them, and re-layouts  1.79 us
  transfers between devices with their start and end apart: 16, of which 3 were waited for; matrix products, arithmetic and copies ran while one was open for 0% of the time, Pallas kernels for 27%

profile of v2, /device:TPU:0, one launch (start us, length us, event | category | flops | bytes accessed | tf_op | source)
XLA Modules:
  0.0 58.9 jit_solution(8405143366451934942)
XLA Ops:
  0.6 0.0 copy-start
  0.6 1.9 %shard_map.77 = (bf16[512,256]{1,0:T(8,128)(2,1)S(1)}, bf16[512,256]{1,0:T(8,128)(2,1)S(1)}, s32[4,8,128]{2,1,0:T(8,128)S(1)}, f32[512,128]{1,0:T(8,128)S(1)}, f...) custom-call(f32[3,512,128]{2,1,0:T(8,128)} %state_ref.1, ...), custom_call_target="tpu_custom_call" | custom-call | flops 1000000 | bytes 3949056 | tf_op jit(solution)/shard_map/pallas_call | solution.py:456
  2.5 3.1 %collective-permute-start = (f32[4,64,128]{2,1,0:T(8,128)S(1)}, f32[4,64,128]{2,1,0:T(8,128)S(1)}, u32[]{:S(2)}, u32[]{:S(2)}) collective-permute-start(f32[4,64,128]{2,1,0:T(8,128)S(1)} %get-tuple-element.42), channel_id=1, source_target_pairs={{28,4},{29,5},{30,6},{31,7},{0,8},{1,9},{2,10},{3,11},{12,20},{13,... | collective-permute-start | bytes 393224 | tf_op jit(solution)/shard_map/ppermute | solution.py:493
  5.6 0.7 %collective-permute-start.1 = (f32[4,64,128]{2,1,0:T(8,128)S(1)}, f32[4,64,128]{2,1,0:T(8,128)S(1)}, u32[]{:S(2)}, u32[]{:S(2)}) collective-permute-start(f32[4,64,128]{2,1,0:T(8,128)S(1)} %get-tuple-element.43), channel_id=1, source_target_pairs={{4,12},{5,13},{6,14},{7,15},{8,16},{9,17},{10,18},{11,19},{12,4},{... | collective-permute-start | bytes 393224 | tf_op jit(solution)/shard_map/ppermute | solution.py:493
  6.3 0.0 copy-start.4
  6.3 0.0 copy-done
  6.3 0.6 %copy-done.4 = f32[3]{0:T(128)S(1)} copy-done((f32[3]{0:T(128)S(1)}, f32[3]{0:T(128)}, u32[]{:S(2)}) %copy-start.4) | copy-done | bytes 36
  6.9 0.0 copy-start.2
  6.9 1.1 %copy-done.2 = f32[3,512,128]{2,1,0:T(8,128)S(1)} copy-done((f32[3,512,128]{2,1,0:T(8,128)S(1)}, f32[3,512,128]{2,1,0:T(8,128)}, u32[]{:S(2)}) %copy-start.2) | copy-done | bytes 786456
  8.1 4.0 %shard_map.80 = (f32[3,512,128]{2,1,0:T(8,128)S(1)}, f32[3,64,128]{2,1,0:T(8,128)S(1)}, f32[3,64,128]{2,1,0:T(8,128)S(1)}, f32[3,64,128]{2,1,0:T(8,128)S(1)}, f32[3,64,128]{2,1,0:T(8,128)S(1)}) custom-call(f32[3,512,128]{2,1,0:T(8,128)S(1)} %copy-done.2, f32[3,512,128]{2,1,0:T(8,128)S(1)} %copy-done, f32[3]{0:T(128)S(1)} %copy-done.4, ...), custom_call_target="tpu_custom_call" | custom-call | flops 20000000 | bytes 4079628 | tf_op jit(solution)/shard_map/pallas_call | solution.py:456
  12.1 0.0 copy-start.1
  12.1 4.5 %collective-permute-start.4 = (f32[3,64,128]{2,1,0:T(8,128)S(1)}, f32[3,64,128]{2,1,0:T(8,128)S(1)}, u32[]{:S(2)}, u32[]{:S(2)}) collective-permute-start(f32[3,64,128]{2,1,0:T(8,128)S(1)} %get-tuple-element.50), channel_id=1, source_target_pairs={{28,4},{29,5},{30,6},{31,7},{0,8},{1,9},{2,10},{3,11},{12,20},{13,... | collective-permute-start | bytes 294920 | tf_op jit(solution)/shard_map/ppermute | solution.py:493
  16.6 0.7 %collective-permute-start.5 = (f32[3,64,128]{2,1,0:T(8,128)S(1)}, f32[3,64,128]{2,1,0:T(8,128)S(1)}, u32[]{:S(2)}, u32[]{:S(2)}) collective-permute-start(f32[3,64,128]{2,1,0:T(8,128)S(1)} %get-tuple-element.51), channel_id=1, source_target_pairs={{4,12},{5,13},{6,14},{7,15},{8,16},{9,17},{10,18},{11,19},{12,4},{... | collective-permute-start | bytes 294920 | tf_op jit(solution)/shard_map/ppermute | solution.py:493
  17.2 0.0 collective-permute-done.ie_ref.refs_0_
  17.3 0.0 collective-permute-done.1.io_ref.refs_1_
  17.3 0.1 collective-permute-start.2
  17.4 6.6 %collective-permute-start.3 = (f32[4,64,128]{2,1,0:T(8,128)S(1)}, f32[4,64,128]{2,1,0:T(8,128)S(1)}, u32[]{:S(2)}, u32[]{:S(2)}) collective-permute-start(f32[4,64,128]{2,1,0:T(8,128)S(1)} %get-tuple-element.47), channel_id=1, source_target_pairs={{29,30},{31,0},{1,2},{5,6},{7,8},{9,10},{13,14},{15,16},{17,18},{2... | collective-permute-start | bytes 393224 | tf_op jit(solution)/shard_map/ppermute | solution.py:493
  24.0 0.0 collective-permute-done.4.ie_ref.gie_ref
  24.0 0.0 collective-permute-done.5.io_ref.gio_ref
  24.1 0.1 collective-permute-start.6
  24.1 2.6 %collective-permute-start.7 = (f32[3,64,128]{2,1,0:T(8,128)S(1)}, f32[3,64,128]{2,1,0:T(8,128)S(1)}, u32[]{:S(2)}, u32[]{:S(2)}) collective-permute-start(f32[3,64,128]{2,1,0:T(8,128)S(1)} %get-tuple-element.55), channel_id=1, source_target_pairs={{29,30},{31,0},{1,2},{5,6},{7,8},{9,10},{13,14},{15,16},{17,18},{2... | collective-permute-start | bytes 294920 | tf_op jit(solution)/shard_map/ppermute | solution.py:493
  26.7 0.0 collective-permute-done.2.refs_2_
  26.7 0.7 %collective-permute-done.3.refs_3_ = f32[4,64,128]{2,1,0:T(8,128)S(1)} collective-permute-done((f32[4,64,128]{2,1,0:T(8,128)S(1)}, f32[4,64,128]{2,1,0:T(8,128)S(1)}, u32[]{:S(2)}, u32[]{:S(2)}) %collective-permute-start.3) | collective-permute-done | bytes 131104 | tf_op jit(solution)/shard_map/ppermute | solution.py:493
  27.4 0.0 copy-done.1
  27.4 0.0 copy-start.3
  27.4 3.9 %shard_map.79 = (f32[512,128]{1,0:T(8,128)S(1)}, f32[3,512,128]{2,1,0:T(8,128)S(1)}, f32[3,512,128]{2,1,0:T(8,128)S(1)}, f32[3,64,128]{2,1,0:T(8,128)S(1)}, f32[...) custom-call(f32[3,512,128]{2,1,0:T(8,128)S(1)} %copy-done.1, ...), custom_call_target="tpu_custom_call" | custom-call | flops 20000000 | bytes 6701068 | tf_op jit(solution)/shard_map/pallas_call | solution.py:456
  31.3 2.5 %collective-permute-start.12 = (f32[3,64,128]{2,1,0:T(8,128)S(1)}, f32[3,64,128]{2,1,0:T(8,128)S(1)}, u32[]{:S(2)}, u32[]{:S(2)}) collective-permute-start(f32[3,64,128]{2,1,0:T(8,128)S(1)} %get-tuple-element.66), channel_id=1, source_target_pairs={{28,4},{29,5},{30,6},{31,7},{0,8},{1,9},{2,10},{3,11},{12,20},{13,... | collective-permute-start | bytes 294920 | tf_op jit(solution)/shard_map/ppermute | solution.py:493
  33.8 0.7 %collective-permute-start.13 = (f32[3,64,128]{2,1,0:T(8,128)S(1)}, f32[3,64,128]{2,1,0:T(8,128)S(1)}, u32[]{:S(2)}, u32[]{:S(2)}) collective-permute-start(f32[3,64,128]{2,1,0:T(8,128)S(1)} %get-tuple-element.67), channel_id=1, source_target_pairs={{4,12},{5,13},{6,14},{7,15},{8,16},{9,17},{10,18},{11,19},{12,4},{... | collective-permute-start | bytes 294920 | tf_op jit(solution)/shard_map/ppermute | solution.py:493
  34.5 0.0 collective-permute-done.6.gje_ref
  34.5 0.0 collective-permute-done.7.gjo_ref
  34.5 0.0 copy-done.3
  34.5 3.7 %shard_map.82 = (f32[3,512,128]{2,1,0:T(8,128)S(1)}, f32[3,512,128]{2,1,0:T(8,128)S(1)}, f32[3,64,128]{2,1,0:T(8,128)S(1)}, f32[3,64,128]{2,1,0:T(8,128)S(1)}, f...) custom-call(f32[3,512,128]{2,1,0:T(8,128)S(1)} %copy-done.3, f32[3,512,128]{2,1,0:T(8,128)S(1)} %copy-done, ...), custom_call_target="tpu_custom_call" | custom-call | flops 20000000 | bytes 6307852 | tf_op jit(solution)/shard_map/pallas_call | solution.py:456
  38.2 1.8 %collective-permute-start.8 = (f32[3,64,128]{2,1,0:T(8,128)S(1)}, f32[3,64,128]{2,1,0:T(8,128)S(1)}, u32[]{:S(2)}, u32[]{:S(2)}) collective-permute-start(f32[3,64,128]{2,1,0:T(8,128)S(1)} %get-tuple-element.58), channel_id=1, source_target_pairs={{28,4},{29,5},{30,6},{31,7},{0,8},{1,9},{2,10},{3,11},{12,20},{13,... | collective-permute-start | bytes 294920 | tf_op jit(solution)/shard_map/ppermute | solution.py:493
  40.0 0.7 %collective-permute-start.9 = (f32[3,64,128]{2,1,0:T(8,128)S(1)}, f32[3,64,128]{2,1,0:T(8,128)S(1)}, u32[]{:S(2)}, u32[]{:S(2)}) collective-permute-start(f32[3,64,128]{2,1,0:T(8,128)S(1)} %get-tuple-element.59), channel_id=1, source_target_pairs={{4,12},{5,13},{6,14},{7,15},{8,16},{9,17},{10,18},{11,19},{12,4},{... | collective-permute-start | bytes 294920 | tf_op jit(solution)/shard_map/ppermute | solution.py:493
  40.6 0.0 collective-permute-done.12.ie_ref.refs_1_
  40.7 0.0 collective-permute-done.13.io_ref.refs_2_
  40.7 0.1 collective-permute-start.14
  40.8 7.0 %collective-permute-start.15 = (f32[3,64,128]{2,1,0:T(8,128)S(1)}, f32[3,64,128]{2,1,0:T(8,128)S(1)}, u32[]{:S(2)}, u32[]{:S(2)}) collective-permute-start(f32[3,64,128]{2,1,0:T(8,128)S(1)} %get-tuple-element.71), channel_id=1, source_target_pairs={{29,30},{31,0},{1,2},{5,6},{7,8},{9,10},{13,14},{15,16},{17,18},{2... | collective-permute-start | bytes 294920 | tf_op jit(solution)/shard_map/ppermute | solution.py:493
  47.8 0.0 collective-permute-done.8.ie_ref.gie_ref
  47.8 0.0 collective-permute-done.9.io_ref.gio_ref
  47.9 0.1 collective-permute-start.10
  47.9 2.4 %collective-permute-start.11 = (f32[3,64,128]{2,1,0:T(8,128)S(1)}, f32[3,64,128]{2,1,0:T(8,128)S(1)}, u32[]{:S(2)}, u32[]{:S(2)}) collective-permute-start(f32[3,64,128]{2,1,0:T(8,128)S(1)} %get-tuple-element.63), channel_id=1, source_target_pairs={{29,30},{31,0},{1,2},{5,6},{7,8},{9,10},{13,14},{15,16},{17,18},{2... | collective-permute-start | bytes 294920 | tf_op jit(solution)/shard_map/ppermute | solution.py:493
  50.3 0.0 collective-permute-done.14.refs_3_
  50.3 0.1 collective-permute-done.15.refs_4_
  50.4 4.1 %shard_map.86 = f32[3,512,128]{2,1,0:T(8,128)} custom-call(f32[3,512,128]{2,1,0:T(8,128)S(1)} %get-tuple-element.64.state_ref, f32[3,512,128]{2,1,0:T(8,128)S(1)} %copy-done, f32[3]{0:T(128)S(1)} %copy-done.4, bf16[512,256]{1,0:T(8,128)(2,1)S(1)} %get-tuple-element.37.table_ref, bf16[512,256]{1,0:T(8,128)(2,1)S(1)} %get-tuple-element.38.turned_ref, ...), custom_call_target="tpu_custom_call" | custom-call | flops 20000000 | bytes 5128204 | tf_op jit(solution)/shard_map/pallas_call | solution.py:456
  54.5 0.0 collective-permute-done.10.gje_ref
  54.5 3.0 %collective-permute-done.11.gjo_ref = f32[3,64,128]{2,1,0:T(8,128)S(1)} collective-permute-done((f32[3,64,128]{2,1,0:T(8,128)S(1)}, f32[3,64,128]{2,1,0:T(8,128)S(1)}, u32[]{:S(2)}, u32[]{:S(2)}) %collective-permute-start.11) | collective-permute-done | bytes 98336 | tf_op jit(solution)/shard_map/ppermute | solution.py:493
  57.5 1.4 %shard_map.84 = f32[3,512,128]{2,1,0:T(8,128)} custom-call(f32[3,512,128]{2,1,0:T(8,128)S(1)} %get-tuple-element.56.moment_ref, s32[4,8,128]{2,1,0:T(8,128)S(1)} %get-tuple-element.39.index_ref, f32[512,128]{1,0:T(8,128)S(1)} %get-tuple-element.48.inverse_ref.refs_0_, f32[3,512,128]{2,1,0:T(8,128)S(1)} %get-tuple-element.57.joined_ref, ...), custom_call_target="tpu_custom_call" | custom-call | flops 1000000 | bytes 3031040 | tf_op jit(solution)/shard_map/pallas_call | solution.py:456
  (4 shorter events, 0.1 us)
Async XLA Ops:
  0.6 5.7 %copy-start = (f32[3,512,128]{2,1,0:T(8,128)S(1)}, f32[3,512,128]{2,1,0:T(8,128)}, u32[]{:S(2)}) copy-start(f32[3,512,128]{2,1,0:T(8,128)} %flow_ref.7) | copy-start | bytes 2359300
  2.5 14.7 %collective-permute-start = (f32[4,64,128]{2,1,0:T(8,128)S(1)}, f32[4,64,128]{2,1,0:T(8,128)S(1)}, u32[]{:S(2)}, u32[]{:S(2)}) collective-permute-start(f32[4,64,128]{2,1,0:T(8,128)S(1)} %get-tuple-element.42), channel_id=1, source_target_pairs={{28,4},{29,5},{30,6},{31,7},{0,8},{1,9},{2,10},{3,11},{12,20},{13,... | collective-permute-start | bytes 393224 | tf_op jit(solution)/shard_map/ppermute | solution.py:493
  5.6 11.7 %collective-permute-start.1 = (f32[4,64,128]{2,1,0:T(8,128)S(1)}, f32[4,64,128]{2,1,0:T(8,128)S(1)}, u32[]{:S(2)}, u32[]{:S(2)}) collective-permute-start(f32[4,64,128]{2,1,0:T(8,128)S(1)} %get-tuple-element.43), channel_id=1, source_target_pairs={{4,12},{5,13},{6,14},{7,15},{8,16},{9,17},{10,18},{11,19},{12,4},{... | collective-permute-start | bytes 393224 | tf_op jit(solution)/shard_map/ppermute | solution.py:493
  6.3 0.7 %copy-start.4 = (f32[3]{0:T(128)S(1)}, f32[3]{0:T(128)}, u32[]{:S(2)}) copy-start(f32[3]{0:T(128)} %diff_ref.7) | copy-start | bytes 40
  6.9 1.1 %copy-start.2 = (f32[3,512,128]{2,1,0:T(8,128)S(1)}, f32[3,512,128]{2,1,0:T(8,128)}, u32[]{:S(2)}) copy-start(f32[3,512,128]{2,1,0:T(8,128)} %moment_ref.3) | copy-start | bytes 2359300
  12.1 15.3 %copy-start.1 = (f32[3,512,128]{2,1,0:T(8,128)S(1)}, f32[3,512,128]{2,1,0:T(8,128)}, u32[]{:S(2)}) copy-start(f32[3,512,128]{2,1,0:T(8,128)} %state_ref.1) | copy-start | bytes 2359300
  12.1 11.9 %collective-permute-start.4 = (f32[3,64,128]{2,1,0:T(8,128)S(1)}, f32[3,64,128]{2,1,0:T(8,128)S(1)}, u32[]{:S(2)}, u32[]{:S(2)}) collective-permute-start(f32[3,64,128]{2,1,0:T(8,128)S(1)} %get-tuple-element.50), channel_id=1, source_target_pairs={{28,4},{29,5},{30,6},{31,7},{0,8},{1,9},{2,10},{3,11},{12,20},{13,... | collective-permute-start | bytes 294920 | tf_op jit(solution)/shard_map/ppermute | solution.py:493
  16.6 7.4 %collective-permute-start.5 = (f32[3,64,128]{2,1,0:T(8,128)S(1)}, f32[3,64,128]{2,1,0:T(8,128)S(1)}, u32[]{:S(2)}, u32[]{:S(2)}) collective-permute-start(f32[3,64,128]{2,1,0:T(8,128)S(1)} %get-tuple-element.51), channel_id=1, source_target_pairs={{4,12},{5,13},{6,14},{7,15},{8,16},{9,17},{10,18},{11,19},{12,4},{... | collective-permute-start | bytes 294920 | tf_op jit(solution)/shard_map/ppermute | solution.py:493
  17.3 9.4 %collective-permute-start.2 = (f32[4,64,128]{2,1,0:T(8,128)S(1)}, f32[4,64,128]{2,1,0:T(8,128)S(1)}, u32[]{:S(2)}, u32[]{:S(2)}) collective-permute-start(f32[4,64,128]{2,1,0:T(8,128)S(1)} %get-tuple-element.46), channel_id=1, source_target_pairs={{28,29},{30,31},{0,1},{2,3},{4,5},{6,7},{8,9},{10,11},{12,13},{14,... | collective-permute-start | bytes 393224 | tf_op jit(solution)/shard_map/ppermute | solution.py:493
  17.4 10.0 %collective-permute-start.3 = (f32[4,64,128]{2,1,0:T(8,128)S(1)}, f32[4,64,128]{2,1,0:T(8,128)S(1)}, u32[]{:S(2)}, u32[]{:S(2)}) collective-permute-start(f32[4,64,128]{2,1,0:T(8,128)S(1)} %get-tuple-element.47), channel_id=1, source_target_pairs={{29,30},{31,0},{1,2},{5,6},{7,8},{9,10},{13,14},{15,16},{17,18},{2... | collective-permute-start | bytes 393224 | tf_op jit(solution)/shard_map/ppermute | solution.py:493
  24.1 10.4 %collective-permute-start.6 = (f32[3,64,128]{2,1,0:T(8,128)S(1)}, f32[3,64,128]{2,1,0:T(8,128)S(1)}, u32[]{:S(2)}, u32[]{:S(2)}) collective-permute-start(f32[3,64,128]{2,1,0:T(8,128)S(1)} %get-tuple-element.54), channel_id=1, source_target_pairs={{28,29},{30,31},{0,1},{2,3},{4,5},{6,7},{8,9},{10,11},{12,13},{14,... | collective-permute-start | bytes 294920 | tf_op jit(solution)/shard_map/ppermute | solution.py:493
  24.1 10.4 %collective-permute-start.7 = (f32[3,64,128]{2,1,0:T(8,128)S(1)}, f32[3,64,128]{2,1,0:T(8,128)S(1)}, u32[]{:S(2)}, u32[]{:S(2)}) collective-permute-start(f32[3,64,128]{2,1,0:T(8,128)S(1)} %get-tuple-element.55), channel_id=1, source_target_pairs={{29,30},{31,0},{1,2},{5,6},{7,8},{9,10},{13,14},{15,16},{17,18},{2... | collective-permute-start | bytes 294920 | tf_op jit(solution)/shard_map/ppermute | solution.py:493
  27.4 7.1 %copy-start.3 = (f32[3,512,128]{2,1,0:T(8,128)S(1)}, f32[3,512,128]{2,1,0:T(8,128)}, u32[]{:S(2)}) copy-start(f32[3,512,128]{2,1,0:T(8,128)} %moment_ref.3) | copy-start | bytes 2359300
  31.3 9.3 %collective-permute-start.12 = (f32[3,64,128]{2,1,0:T(8,128)S(1)}, f32[3,64,128]{2,1,0:T(8,128)S(1)}, u32[]{:S(2)}, u32[]{:S(2)}) collective-permute-start(f32[3,64,128]{2,1,0:T(8,128)S(1)} %get-tuple-element.66), channel_id=1, source_target_pairs={{28,4},{29,5},{30,6},{31,7},{0,8},{1,9},{2,10},{3,11},{12,20},{13,... | collective-permute-start | bytes 294920 | tf_op jit(solution)/shard_map/ppermute | solution.py:493
  33.8 6.8 %collective-permute-start.13 = (f32[3,64,128]{2,1,0:T(8,128)S(1)}, f32[3,64,128]{2,1,0:T(8,128)S(1)}, u32[]{:S(2)}, u32[]{:S(2)}) collective-permute-start(f32[3,64,128]{2,1,0:T(8,128)S(1)} %get-tuple-element.67), channel_id=1, source_target_pairs={{4,12},{5,13},{6,14},{7,15},{8,16},{9,17},{10,18},{11,19},{12,4},{... | collective-permute-start | bytes 294920 | tf_op jit(solution)/shard_map/ppermute | solution.py:493
  38.2 9.6 %collective-permute-start.8 = (f32[3,64,128]{2,1,0:T(8,128)S(1)}, f32[3,64,128]{2,1,0:T(8,128)S(1)}, u32[]{:S(2)}, u32[]{:S(2)}) collective-permute-start(f32[3,64,128]{2,1,0:T(8,128)S(1)} %get-tuple-element.58), channel_id=1, source_target_pairs={{28,4},{29,5},{30,6},{31,7},{0,8},{1,9},{2,10},{3,11},{12,20},{13,... | collective-permute-start | bytes 294920 | tf_op jit(solution)/shard_map/ppermute | solution.py:493
  40.0 7.8 %collective-permute-start.9 = (f32[3,64,128]{2,1,0:T(8,128)S(1)}, f32[3,64,128]{2,1,0:T(8,128)S(1)}, u32[]{:S(2)}, u32[]{:S(2)}) collective-permute-start(f32[3,64,128]{2,1,0:T(8,128)S(1)} %get-tuple-element.59), channel_id=1, source_target_pairs={{4,12},{5,13},{6,14},{7,15},{8,16},{9,17},{10,18},{11,19},{12,4},{... | collective-permute-start | bytes 294920 | tf_op jit(solution)/shard_map/ppermute | solution.py:493
  40.7 9.6 %collective-permute-start.14 = (f32[3,64,128]{2,1,0:T(8,128)S(1)}, f32[3,64,128]{2,1,0:T(8,128)S(1)}, u32[]{:S(2)}, u32[]{:S(2)}) collective-permute-start(f32[3,64,128]{2,1,0:T(8,128)S(1)} %get-tuple-element.70), channel_id=1, source_target_pairs={{28,29},{30,31},{0,1},{2,3},{4,5},{6,7},{8,9},{10,11},{12,13},{14,... | collective-permute-start | bytes 294920 | tf_op jit(solution)/shard_map/ppermute | solution.py:493
  40.8 9.6 %collective-permute-start.15 = (f32[3,64,128]{2,1,0:T(8,128)S(1)}, f32[3,64,128]{2,1,0:T(8,128)S(1)}, u32[]{:S(2)}, u32[]{:S(2)}) collective-permute-start(f32[3,64,128]{2,1,0:T(8,128)S(1)} %get-tuple-element.71), channel_id=1, source_target_pairs={{29,30},{31,0},{1,2},{5,6},{7,8},{9,10},{13,14},{15,16},{17,18},{2... | collective-permute-start | bytes 294920 | tf_op jit(solution)/shard_map/ppermute | solution.py:493
  47.9 6.6 %collective-permute-start.10 = (f32[3,64,128]{2,1,0:T(8,128)S(1)}, f32[3,64,128]{2,1,0:T(8,128)S(1)}, u32[]{:S(2)}, u32[]{:S(2)}) collective-permute-start(f32[3,64,128]{2,1,0:T(8,128)S(1)} %get-tuple-element.62), channel_id=1, source_target_pairs={{28,29},{30,31},{0,1},{2,3},{4,5},{6,7},{8,9},{10,11},{12,13},{14,... | collective-permute-start | bytes 294920 | tf_op jit(solution)/shard_map/ppermute | solution.py:493
  47.9 9.5 %collective-permute-start.11 = (f32[3,64,128]{2,1,0:T(8,128)S(1)}, f32[3,64,128]{2,1,0:T(8,128)S(1)}, u32[]{:S(2)}, u32[]{:S(2)}) collective-permute-start(f32[3,64,128]{2,1,0:T(8,128)S(1)} %get-tuple-element.63), channel_id=1, source_target_pairs={{29,30},{31,0},{1,2},{5,6},{7,8},{9,10},{13,14},{15,16},{17,18},{2... | collective-permute-start | bytes 294920 | tf_op jit(solution)/shard_map/ppermute | solution.py:493

commit v3 on v2

--- a/solution.py
+++ b/solution.py
@@ -116,6 +116,10 @@
             table_ref[pl.ds(256 * part + 8 * a, 16)] = wide.astype(BF16)
 
 
+def spread(diff, block):
+    return (diff[None] * block.reshape(-1, 8, 128)).reshape(block.shape)
+
+
 def lanes(block, index):
     wide = jnp.broadcast_to(index[None], (block.shape[0] // 8, 8, 128)).reshape(block.shape)
     return jnp.take_along_axis(block, wide, axis=1, mode="promise_in_bounds")
@@ -132,10 +136,18 @@
             mass_ref[r] = weight_ref[r] * (along * float(WEIGHTS[i] * WEIGHTS[j]))
 
 
-def forward(source, flow_ref, mass_ref, diff, table_ref, turned_ref, work, target):
+def forward_k(source, flow_ref, mass_ref, diff, table_ref, turned_ref, work):
+    flux = along_k(table_ref, source[...]) * mass_ref[...]
+    work[...] = flow_ref[2] * flux + spread(diff, along_k(turned_ref, flux))
+
+
+def adjoint_k(source, flow_ref, mass_ref, diff, table_ref, turned_ref, work):
     slope = along_k(table_ref, source[...])
-    flux = slope * mass_ref[...]
-    work[...] = flow_ref[2] * flux + diff * along_k(turned_ref, flux)
+    flux = (flow_ref[2] * source[...] + spread(diff, slope)) * mass_ref[...]
+    work[...] = along_k(turned_ref, flux)
+
+
+def forward(source, flow_ref, mass_ref, diff, work, target):
     for j in range(8):
         slopes = line(DM, [source[rows(i, j)] for i in range(8)])
         fluxes = [slopes[i] * mass_ref[rows(i, j)] for i in range(8)]
@@ -152,10 +164,7 @@
             target[r] = -(target[r] + work[r] + (flow_ref[1, r] * fluxes[j] + diff * back[j]))
 
 
-def adjoint(source, base, flow_ref, mass_ref, diff, table_ref, turned_ref, work, target):
-    slope = along_k(table_ref, source[...])
-    flux = (flow_ref[2] * source[...] + diff * slope) * mass_ref[...]
-    work[...] = along_k(turned_ref, flux)
+def adjoint(source, base, flow_ref, mass_ref, diff, work, target):
     for j in range(8):
         values = [source[rows(i, j)] for i in range(8)]
         slopes = line(DM, values)
@@ -202,18 +211,26 @@
     height = index[0]
     for way in range(2):
         r = pl.ds(pl.multiple_of(ends[0][way] * 64, 64), 64)
-        ref[r] = ref[r] + lanes(got[way][c], height)
+        part = lanes(got[way][c], height)
+        ref[r] = ref[r] + (part * ends[2][0] if way else part)
     for way in range(2):
         for i in range(8):
             r = pl.ds(pl.multiple_of(ends[1][way] * 8 + i * 64, 8), 8)
-            ref[r] = ref[r] + lanes(got[2 + way][c, pl.ds(i * 8, 8)], height)
+            part = lanes(got[2 + way][c, pl.ds(i * 8, 8)], height)
+            ref[r] = ref[r] + (part * ends[2][1] if way else part)
 
 
 def ends_of(columns):
     column = lax.rem(lax.axis_index("elem") + columns // 2, columns * DA)
-    row_odd = lax.rem(lax.div(column, columns), 2)
-    place_odd = lax.rem(lax.rem(column, columns), 2)
-    return ((7 - 7 * row_odd, 7 * row_odd), (7 - 7 * place_odd, 7 * place_odd))
+    row, place = lax.div(column, columns), lax.rem(column, columns)
+    row_odd, place_odd = lax.rem(row, 2), lax.rem(place, 2)
+    row_inside = jnp.where((row > 0) & (row < DA - 1), 1.0, 0.0)
+    place_inside = jnp.where((place > 0) & (place < columns - 1), 1.0, 0.0)
+    return (
+        (7 - 7 * row_odd, 7 * row_odd),
+        (7 - 7 * place_odd, 7 * place_odd),
+        (row_inside, place_inside),
+    )
 
 
 def index_of(index_ref):
@@ -222,9 +239,16 @@
 
 def index_kernel(
     columns,
+    moment_far,
     state_far,
+    flow_far,
     weight_far,
+    diff_far,
     numbers_far,
+    moment_ref,
+    state_ref,
+    flow_ref,
+    diff_ref,
     table_ref,
     turned_ref,
     index_ref,
@@ -236,10 +260,11 @@
     jo_ref,
     weight_ref,
     numbers_ref,
+    scalar_ref,
     arrived,
 ):
-    far = (numbers_far, weight_far, state_far)
-    near = (numbers_ref, weight_ref, joined_ref.at[pl.ds(0, 3)])
+    far = (numbers_far, weight_far, state_far, diff_far, moment_far, flow_far)
+    near = (numbers_ref, weight_ref, state_ref, scalar_ref, moment_ref, flow_ref)
     copies = [pltpu.make_async_copy(a, b, arrived.at[n]) for n, (a, b) in enumerate(zip(far, near))]
     for copy in copies:
         copy.start()
@@ -266,9 +291,16 @@
     joined_ref[3] = mass_ref[...]
     copies[2].wait()
     out = (ie_ref, io_ref, je_ref, jo_ref)
+    for c in range(3):
+        joined_ref[c] = state_ref[c]
     for c in range(4):
         join_heights(joined_ref.at[c], index)
         send_faces(c, joined_ref.at[c], index, ends, out)
+    copies[3].wait()
+    for f in range(3):
+        diff_ref[f] = jnp.full((8, 128), scalar_ref[f], F32)
+    copies[4].wait()
+    copies[5].wait()
 
 
 def moment_kernel(
@@ -291,22 +323,14 @@
     index = index_of(index_ref)
     out = (ie_ref, io_ref, je_ref, jo_ref)
 
-    def one_field(f, carry):
-        forward(
-            moment_ref.at[f],
-            flow_ref,
-            mass_ref,
-            diff_ref[f],
-            table_ref,
-            turned_ref,
-            work_ref,
-            joined_ref.at[f],
-        )
+    for f in range(3):
+        at = (flow_ref, mass_ref, diff_ref[f])
+        forward_k(moment_ref.at[f], *at, table_ref, turned_ref, work_ref.at[f])
+    for f in range(3):
+        at = (flow_ref, mass_ref, diff_ref[f])
+        forward(moment_ref.at[f], *at, work_ref.at[f], joined_ref.at[f])
         join_heights(joined_ref.at[f], index)
         send_faces(f, joined_ref.at[f], index, ends, out)
-        return carry
-
-    lax.fori_loop(0, 3, one_field, 0)
 
 
 def edge_kernel(columns, ie_ref, io_ref, je_ref, jo_ref, out_e, out_o):
@@ -316,7 +340,8 @@
         r = pl.ds(pl.multiple_of(ends[1][way] * 8, 8), 8)
         for other, got in enumerate((ie_ref, io_ref)):
             w = pl.ds(pl.multiple_of(ends[0][other] * 8, 8), 8)
-            out[:, w] = out[:, w] + got[:, r]
+            part = got[:, r]
+            out[:, w] = out[:, w] + (part * ends[2][0] if other else part)
 
 
 def state_kernel(
@@ -337,41 +362,35 @@
     if first:
         got, (inverse_ref, state_out, joined_out), refs = refs[:4], refs[4:7], refs[7:]
         out, (work_ref, hold_ref) = refs[:4], refs[4:]
-        hold_ref[...] = joined_ref[3]
-        add_faces(3, hold_ref, index, ends, got)
-        inverse_ref[...] = 1.0 / hold_ref[...]
+        held = hold_ref.at[0]
+        held[...] = joined_ref[3]
+        add_faces(3, held, index, ends, got)
+        inverse_ref[...] = 1.0 / held[...]
     else:
         inverse_ref, *got = refs[:5]
         state_out, work_ref, hold_ref = refs[5:]
 
-    def one_field(f, carry):
-        hold_ref[...] = joined_ref[f]
-        add_faces(f, hold_ref, index, ends, got)
-        hold_ref[...] = hold_ref[...] * inverse_ref[...]
-        adjoint(
-            hold_ref,
-            state_ref.at[f],
-            flow_ref,
-            mass_ref,
-            diff_ref[f],
-            table_ref,
-            turned_ref,
-            work_ref,
-            state_out.at[f],
-        )
+    for f in range(3):
+        held = hold_ref.at[f]
+        held[...] = joined_ref[f]
+        add_faces(f, held, index, ends, got)
+        held[...] = held[...] * inverse_ref[...]
+        at = (flow_ref, mass_ref, diff_ref[f])
+        adjoint_k(held, *at, table_ref, turned_ref, work_ref.at[f])
+    for f in range(3):
+        at = (flow_ref, mass_ref, diff_ref[f])
+        adjoint(hold_ref.at[f], state_ref.at[f], *at, work_ref.at[f], state_out.at[f])
         if first:
             joined_out[f] = state_out[f]
             join_heights(joined_out.at[f], index)
             send_faces(f, joined_out.at[f], index, ends, out)
-        return carry
-
-    lax.fori_loop(0, 3, one_field, 0)
 
 
 def moment_step(f, ends, index, moment_ref, joined_ref, inverse_ref, got, hold_ref, moment_out):
-    hold_ref[...] = joined_ref[f]
-    add_faces(f, hold_ref, index, ends, got)
-    moment_out[f] = moment_ref[f] + DT * (hold_ref[...] * inverse_ref[...])
+    held = hold_ref.at[f]
+    held[...] = joined_ref[f]
+    add_faces(f, held, index, ends, got)
+    moment_out[f] = moment_ref[f] + DT * (held[...] * inverse_ref[...])
 
 
 def middle_kernel(
@@ -403,23 +422,15 @@
     out = (ie_ref, io_ref, je_ref, jo_ref)
     got = (gie_ref, gio_ref, gje_ref, gjo_ref)
 
-    def one_field(f, carry):
+    for f in range(3):
         moment_step(f, ends, index, moment_ref, joined_ref, inverse_ref, got, hold_ref, moment_out)
-        forward(
-            moment_out.at[f],
-            flow_ref,
-            mass_ref,
-            diff_ref[f],
-            table_ref,
-            turned_ref,
-            work_ref,
-            joined_out.at[f],
-        )
+        at = (flow_ref, mass_ref, diff_ref[f])
+        forward_k(moment_out.at[f], *at, table_ref, turned_ref, work_ref.at[f])
+    for f in range(3):
+        at = (flow_ref, mass_ref, diff_ref[f])
+        forward(moment_out.at[f], *at, work_ref.at[f], joined_out.at[f])
         join_heights(joined_out.at[f], index)
         send_faces(f, joined_out.at[f], index, ends, out)
-        return carry
-
-    lax.fori_loop(0, 3, one_field, 0)
 
 
 def last_kernel(
@@ -439,15 +450,11 @@
     index = index_of(index_ref)
     got = (gie_ref, gio_ref, gje_ref, gjo_ref)
 
-    def one_field(f, carry):
+    for f in range(3):
         moment_step(f, ends, index, moment_ref, joined_ref, inverse_ref, got, hold_ref, moment_out)
-        return carry
-
-    lax.fori_loop(0, 3, one_field, 0)
 
 
 VMEM = pl.BlockSpec(memory_space=pltpu.VMEM)
-SMEM = pl.BlockSpec(memory_space=pltpu.SMEM)
 FAR = pl.BlockSpec(memory_space=pltpu.HBM)
 
 
@@ -469,7 +476,9 @@
     device = lambda row, place: (row * columns + place - columns // 2) % devices
 
     def both(pairs):
-        return [(a, b) for a, b in pairs] + [(b, a) for a, b in pairs]
+        paired = {device for pair in pairs for device in pair}
+        alone = [(device, device) for device in range(devices) if device not in paired]
+        return pairs + [(b, a) for a, b in pairs] + alone
 
     along_i = [
         both([(device(r, s), device(r + 1, s)) for r in range(way, DA - 1, 2) for s in range(columns)])
@@ -487,7 +496,7 @@
     columns = devices // DA
     along_i, along_j = pairings(devices)
     whole, block = ((3, 512, 128), F32), ((512, 128), F32)
-    work = pltpu.VMEM((512, 128), F32)
+    work = pltpu.VMEM((3, 512, 128), F32)
 
     def exchange(blocks, pairs):
         return [lax.ppermute(b, "elem", p) for b, p in zip(blocks, pairs)]
@@ -511,41 +520,43 @@
     def faces_shape(count):
         return [((count, 64, 128), F32)] * 4
 
-    table, turned, index, mass, joined_state, *faces_state = call(
+    moment, state, flow, diff, table, turned, index, mass, joined_state, *faces_state = call(
         functools.partial(index_kernel, columns),
-        [FAR] * 3,
-        [((512, 256), BF16)] * 2
+        [FAR] * 6,
+        [whole] * 3
+        + [((3, 8, 128), F32)]
+        + [((512, 256), BF16)] * 2
         + [((4, 8, 128), jnp.int32), block, ((4, 512, 128), F32)]
         + faces_shape(4),
         [
-            work,
+            pltpu.VMEM((512, 128), F32),
             pltpu.VMEM((1, 128), jnp.int32),
-            pltpu.SemaphoreType.DMA((3,)),
+            pltpu.SMEM((3,), F32),
+            pltpu.SemaphoreType.DMA((6,)),
         ],
         1_000_000,
-        *map(far, (adjoint_fields, mass_weights, numbering.reshape(1, 128))),
-    )
-    tables = (diffusivity, table, turned, index, mass)
+        *map(far, (moment_fields, adjoint_fields, velocity, mass_weights)),
+        *map(far, (diffusivity, numbering.reshape(1, 128))),
+    )
+    tables = (flow, diff, table, turned, index, mass)
     got_state = meet(4, faces_state)
     joined_moment, *faces_moment = call(
         functools.partial(moment_kernel, columns),
-        [VMEM] * 2 + [SMEM] + [VMEM] * 4,
+        [VMEM] * 7,
         [whole] + faces_shape(3),
         [work],
         20_000_000,
-        moment_fields,
-        velocity,
+        moment,
         *tables,
     )
     got_moment = meet(3, faces_moment)
     inverse, state, joined_state, *faces_state = call(
         functools.partial(state_kernel, columns, True),
-        [VMEM] * 2 + [SMEM] + [VMEM] * 9,
+        [VMEM] * 12,
         [block, whole, whole] + faces_shape(3),
         [work] * 2,
         20_000_000,
-        adjoint_fields,
-        velocity,
+        state,
         *tables,
         joined_state,
         *got_state,
@@ -553,12 +564,11 @@
     got_state = meet(3, faces_state)
     moment, joined_moment, *faces_moment = call(
         functools.partial(middle_kernel, columns),
-        [VMEM] * 2 + [SMEM] + [VMEM] * 10,
+        [VMEM] * 13,
         [whole, whole] + faces_shape(3),
         [work] * 2,
         20_000_000,
-        moment_fields,
-        velocity,
+        moment,
         *tables,
         inverse,
         joined_moment,
@@ -567,12 +577,11 @@
     got_moment = meet(3, faces_moment)
     (state,) = call(
         functools.partial(state_kernel, columns, False),
-        [VMEM] * 2 + [SMEM] + [VMEM] * 10,
+        [VMEM] * 13,
         [whole],
         [work] * 2,
         20_000_000,
         state,
-        velocity,
         *tables,
         joined_state,
         inverse,

time: 59.2 us -> 52.6 us (0.89)
  Pallas kernels: 19.2 us -> 13.4 us
  local copies, waits for them, and re-layouts: 1.79 us -> 0 us
  waiting for transfers between devices: 3.74 us -> 4.73 us
    pallas_call x10, Pallas kernels: 19.2 us -> 13.4 us  [call(): pl.pallas_call(kernel, out_shape=[jax.ShapeDtypeStruct(s, t) for s, t in...]
    unnamed x10 -> x0, local copies, waits for them, and re-layouts: 1.79 us -> none
    ppermute x16, waiting for transfers between devices: 3.74 us -> 4.73 us  [exchange(): return [lax.ppermute(b, 'elem', p) for b, p in zip(blocks, pairs)]]
  transfers between devices with their start and end apart: 16 -> 16, of which waited for: 3 -> 2; matrix products, arithmetic and copies ran while one was open for 0% -> 0% of each run, Pallas kernels for 27% -> 20%
where the time goes in v3:
time: 52.6 us; the launch traced here: 52.2 us
  starting transfers between devices  33.2 us (63%)
  Pallas kernels  13.4 us (25%)
  waiting for transfers between devices  4.73 us (9%)
  between operations  0.89 us (2%)
    ppermute x16, starting transfers between devices, exchange(): return [lax.ppermute(b, 'elem', p) for b, p in zip(blocks, pairs)]  33.2 us
    pallas_call x10, Pallas kernels, call(): pl.pallas_call(kernel, out_shape=[jax.ShapeDtypeStruct(s, t) for s, t in...  13.4 us
    ppermute x16, waiting for transfers between devices, exchange(): return [lax.ppermute(b, 'elem', p) for b, p in zip(blocks, pairs)]  4.73 us
  transfers between devices with their start and end apart: 16, of which 2 were waited for; matrix products, arithmetic and copies ran while one was open for 0% of the time, Pallas kernels for 20%

profile of v3, /device:TPU:0, one launch (start us, length us, event | category | flops | bytes accessed | tf_op | source)
XLA Modules:
  0.0 52.2 jit_solution(4030141242425971775)
XLA Ops:
  0.6 1.9 %shard_map.77 = (f32[3,512,128]{2,1,0:T(8,128)S(1)}, f32[3,512,128]{2,1,0:T(8,128)S(1)}, f32[3,512,128]{2,1,0:T(8,128)S(1)}, f32[3,8,128]{2,1,0:T(8,128)S(1)}, b...) custom-call(f32[3,512,128]{2,1,0:T(8,128)} %moment_far.1, ...), custom_call_target="tpu_custom_call" | custom-call | flops 1000000 | bytes 7893516 | tf_op jit(solution)/shard_map/pallas_call | solution.py:463
  2.5 3.1 %collective-permute-start = (f32[4,64,128]{2,1,0:T(8,128)S(1)}, f32[4,64,128]{2,1,0:T(8,128)S(1)}, u32[]{:S(2)}, u32[]{:S(2)}) collective-permute-start(f32[4,64,128]{2,1,0:T(8,128)S(1)} %get-tuple-element.50), channel_id=1, source_target_pairs={{28,4},{29,5},{30,6},{31,7},{0,8},{1,9},{2,10},{3,11},{12,20},{13,... | collective-permute-start | bytes 393224 | tf_op jit(solution)/shard_map/ppermute | solution.py:502
  5.6 0.7 %collective-permute-start.1 = (f32[4,64,128]{2,1,0:T(8,128)S(1)}, f32[4,64,128]{2,1,0:T(8,128)S(1)}, u32[]{:S(2)}, u32[]{:S(2)}) collective-permute-start(f32[4,64,128]{2,1,0:T(8,128)S(1)} %get-tuple-element.51), channel_id=1, source_target_pairs={{4,12},{5,13},{6,14},{7,15},{8,16},{9,17},{10,18},{11,19},{12,4},{... | collective-permute-start | bytes 393224 | tf_op jit(solution)/shard_map/ppermute | solution.py:502
  6.3 2.3 %shard_map.80 = (f32[3,512,128]{2,1,0:T(8,128)S(1)}, f32[3,64,128]{2,1,0:T(8,128)S(1)}, f32[3,64,128]{2,1,0:T(8,128)S(1)}, f32[3,64,128]{2,1,0:T(8,128)S(1)}, f32[3,64,128]{2,1,0:T(8,128)S(1)}) custom-call(f32[3,512,128]{2,1,0:T(8,128)S(1)} %get-tuple-element.41.moment_ref, f32[3,512,128]{2,1,0:T(8,128)S(1)} %get-tuple-element.42.flow_ref, ...), custom_call_target="tpu_custom_call" | custom-call | flops 20000000 | bytes 4091904 | tf_op jit(solution)/shard_map/pallas_call | solution.py:463
  8.5 4.5 %collective-permute-start.4 = (f32[3,64,128]{2,1,0:T(8,128)S(1)}, f32[3,64,128]{2,1,0:T(8,128)S(1)}, u32[]{:S(2)}, u32[]{:S(2)}) collective-permute-start(f32[3,64,128]{2,1,0:T(8,128)S(1)} %get-tuple-element.58), channel_id=1, source_target_pairs={{28,4},{29,5},{30,6},{31,7},{0,8},{1,9},{2,10},{3,11},{12,20},{13,... | collective-permute-start | bytes 294920 | tf_op jit(solution)/shard_map/ppermute | solution.py:502
  13.0 0.7 %collective-permute-start.5 = (f32[3,64,128]{2,1,0:T(8,128)S(1)}, f32[3,64,128]{2,1,0:T(8,128)S(1)}, u32[]{:S(2)}, u32[]{:S(2)}) collective-permute-start(f32[3,64,128]{2,1,0:T(8,128)S(1)} %get-tuple-element.59), channel_id=1, source_target_pairs={{4,12},{5,13},{6,14},{7,15},{8,16},{9,17},{10,18},{11,19},{12,4},{... | collective-permute-start | bytes 294920 | tf_op jit(solution)/shard_map/ppermute | solution.py:502
  13.7 0.0 collective-permute-done.ie_ref.refs_0_
  13.7 0.0 collective-permute-done.1.io_ref.refs_1_
  13.7 0.1 collective-permute-start.2
  13.8 6.6 %collective-permute-start.3 = (f32[4,64,128]{2,1,0:T(8,128)S(1)}, f32[4,64,128]{2,1,0:T(8,128)S(1)}, u32[]{:S(2)}, u32[]{:S(2)}) collective-permute-start(f32[4,64,128]{2,1,0:T(8,128)S(1)} %get-tuple-element.55), channel_id=1, source_target_pairs={{29,30},{31,0},{1,2},{5,6},{7,8},{9,10},{13,14},{15,16},{17,18},{2... | collective-permute-start | bytes 393224 | tf_op jit(solution)/shard_map/ppermute | solution.py:502
  20.4 0.0 collective-permute-done.4.ie_ref.gie_ref
  20.4 0.0 collective-permute-done.5.io_ref.gio_ref
  20.5 0.1 collective-permute-start.6
  20.5 3.2 %collective-permute-start.7 = (f32[3,64,128]{2,1,0:T(8,128)S(1)}, f32[3,64,128]{2,1,0:T(8,128)S(1)}, u32[]{:S(2)}, u32[]{:S(2)}) collective-permute-start(f32[3,64,128]{2,1,0:T(8,128)S(1)} %get-tuple-element.63), channel_id=1, source_target_pairs={{29,30},{31,0},{1,2},{5,6},{7,8},{9,10},{13,14},{15,16},{17,18},{2... | collective-permute-start | bytes 294920 | tf_op jit(solution)/shard_map/ppermute | solution.py:502
  23.8 0.0 collective-permute-done.2.refs_2_
  23.8 0.0 collective-permute-done.3.refs_3_
  23.8 2.5 %shard_map.79 = (f32[512,128]{1,0:T(8,128)S(1)}, f32[3,512,128]{2,1,0:T(8,128)S(1)}, f32[3,512,128]{2,1,0:T(8,128)S(1)}, f32[3,64,128]{2,1,0:T(8,128)S(1)}, f32[...) custom-call(f32[3,512,128]{2,1,0:T(8,128)S(1)} %get-tuple-element.48.state_ref, ...), custom_call_target="tpu_custom_call" | custom-call | flops 20000000 | bytes 6713344 | tf_op jit(solution)/shard_map/pallas_call | solution.py:463
  26.3 2.4 %collective-permute-start.12 = (f32[3,64,128]{2,1,0:T(8,128)S(1)}, f32[3,64,128]{2,1,0:T(8,128)S(1)}, u32[]{:S(2)}, u32[]{:S(2)}) collective-permute-start(f32[3,64,128]{2,1,0:T(8,128)S(1)} %get-tuple-element.74), channel_id=1, source_target_pairs={{28,4},{29,5},{30,6},{31,7},{0,8},{1,9},{2,10},{3,11},{12,20},{13,... | collective-permute-start | bytes 294920 | tf_op jit(solution)/shard_map/ppermute | solution.py:502
  28.8 0.7 %collective-permute-start.13 = (f32[3,64,128]{2,1,0:T(8,128)S(1)}, f32[3,64,128]{2,1,0:T(8,128)S(1)}, u32[]{:S(2)}, u32[]{:S(2)}) collective-permute-start(f32[3,64,128]{2,1,0:T(8,128)S(1)} %get-tuple-element.75), channel_id=1, source_target_pairs={{4,12},{5,13},{6,14},{7,15},{8,16},{9,17},{10,18},{11,19},{12,4},{... | collective-permute-start | bytes 294920 | tf_op jit(solution)/shard_map/ppermute | solution.py:502
  29.4 0.0 collective-permute-done.6.gje_ref
  29.4 0.6 %collective-permute-done.7.gjo_ref = f32[3,64,128]{2,1,0:T(8,128)S(1)} collective-permute-done((f32[3,64,128]{2,1,0:T(8,128)S(1)}, f32[3,64,128]{2,1,0:T(8,128)S(1)}, u32[]{:S(2)}, u32[]{:S(2)}) %collective-permute-start.7) | collective-permute-done | bytes 98336 | tf_op jit(solution)/shard_map/ppermute | solution.py:502
  30.1 2.3 %shard_map.82 = (f32[3,512,128]{2,1,0:T(8,128)S(1)}, f32[3,512,128]{2,1,0:T(8,128)S(1)}, f32[3,64,128]{2,1,0:T(8,128)S(1)}, f32[3,64,128]{2,1,0:T(8,128)S(1)}, f...) custom-call(f32[3,512,128]{2,1,0:T(8,128)S(1)} %get-tuple-element.41.moment_ref, ...), custom_call_target="tpu_custom_call" | custom-call | flops 20000000 | bytes 6320128 | tf_op jit(solution)/shard_map/pallas_call | solution.py:463
  32.4 1.0 %collective-permute-start.8 = (f32[3,64,128]{2,1,0:T(8,128)S(1)}, f32[3,64,128]{2,1,0:T(8,128)S(1)}, u32[]{:S(2)}, u32[]{:S(2)}) collective-permute-start(f32[3,64,128]{2,1,0:T(8,128)S(1)} %get-tuple-element.66), channel_id=1, source_target_pairs={{28,4},{29,5},{30,6},{31,7},{0,8},{1,9},{2,10},{3,11},{12,20},{13,... | collective-permute-start | bytes 294920 | tf_op jit(solution)/shard_map/ppermute | solution.py:502
  33.4 0.7 %collective-permute-start.9 = (f32[3,64,128]{2,1,0:T(8,128)S(1)}, f32[3,64,128]{2,1,0:T(8,128)S(1)}, u32[]{:S(2)}, u32[]{:S(2)}) collective-permute-start(f32[3,64,128]{2,1,0:T(8,128)S(1)} %get-tuple-element.67), channel_id=1, source_target_pairs={{4,12},{5,13},{6,14},{7,15},{8,16},{9,17},{10,18},{11,19},{12,4},{... | collective-permute-start | bytes 294920 | tf_op jit(solution)/shard_map/ppermute | solution.py:502
  34.0 0.0 collective-permute-done.12.ie_ref.refs_1_
  34.0 0.0 collective-permute-done.13.io_ref.refs_2_
  34.1 0.1 collective-permute-start.14
  34.2 7.2 %collective-permute-start.15 = (f32[3,64,128]{2,1,0:T(8,128)S(1)}, f32[3,64,128]{2,1,0:T(8,128)S(1)}, u32[]{:S(2)}, u32[]{:S(2)}) collective-permute-start(f32[3,64,128]{2,1,0:T(8,128)S(1)} %get-tuple-element.79), channel_id=1, source_target_pairs={{29,30},{31,0},{1,2},{5,6},{7,8},{9,10},{13,14},{15,16},{17,18},{2... | collective-permute-start | bytes 294920 | tf_op jit(solution)/shard_map/ppermute | solution.py:502
  41.3 0.0 collective-permute-done.8.ie_ref.gie_ref
  41.3 0.0 collective-permute-done.9.io_ref.gio_ref
  41.4 0.1 collective-permute-start.10
  41.5 2.4 %collective-permute-start.11 = (f32[3,64,128]{2,1,0:T(8,128)S(1)}, f32[3,64,128]{2,1,0:T(8,128)S(1)}, u32[]{:S(2)}, u32[]{:S(2)}) collective-permute-start(f32[3,64,128]{2,1,0:T(8,128)S(1)} %get-tuple-element.71), channel_id=1, source_target_pairs={{29,30},{31,0},{1,2},{5,6},{7,8},{9,10},{13,14},{15,16},{17,18},{2... | collective-permute-start | bytes 294920 | tf_op jit(solution)/shard_map/ppermute | solution.py:502
  43.9 0.0 collective-permute-done.14.refs_3_
  43.9 0.0 collective-permute-done.15.refs_4_
  43.9 3.1 %shard_map.86 = f32[3,512,128]{2,1,0:T(8,128)} custom-call(f32[3,512,128]{2,1,0:T(8,128)S(1)} %get-tuple-element.72.state_ref, f32[3,512,128]{2,1,0:T(8,128)S(1)} %get-tuple-element.42.flow_ref, f32[3,8,128]{2,1,0:T(8,128)S(1)} %get-tuple-element.43.diff_ref, bf16[512,256]{1,0:T(8,128)(2,1)S(1)} %get-tuple-element.44.table_ref, ...), custom_call_target="tpu_custom_call" | custom-call | flops 20000000 | bytes 5140480 | tf_op jit(solution)/shard_map/pallas_call | solution.py:463
  47.0 0.0 collective-permute-done.10.gje_ref
  47.0 4.0 %collective-permute-done.11.gjo_ref = f32[3,64,128]{2,1,0:T(8,128)S(1)} collective-permute-done((f32[3,64,128]{2,1,0:T(8,128)S(1)}, f32[3,64,128]{2,1,0:T(8,128)S(1)}, u32[]{:S(2)}, u32[]{:S(2)}) %collective-permute-start.11) | collective-permute-done | bytes 98336 | tf_op jit(solution)/shard_map/ppermute | solution.py:502
  51.0 1.2 %shard_map.84 = f32[3,512,128]{2,1,0:T(8,128)} custom-call(f32[3,512,128]{2,1,0:T(8,128)S(1)} %get-tuple-element.64.moment_ref, s32[4,8,128]{2,1,0:T(8,128)S(1)} %get-tuple-element.46.index_ref, f32[512,128]{1,0:T(8,128)S(1)} %get-tuple-element.56.inverse_ref.refs_0_, f32[3,512,128]{2,1,0:T(8,128)S(1)} %get-tuple-element.65.joined_ref, ...), custom_call_target="tpu_custom_call" | custom-call | flops 1000000 | bytes 3031040 | tf_op jit(solution)/shard_map/pallas_call | solution.py:463
  (4 shorter events, 0.1 us)
Async XLA Ops:
  2.5 11.1 %collective-permute-start = (f32[4,64,128]{2,1,0:T(8,128)S(1)}, f32[4,64,128]{2,1,0:T(8,128)S(1)}, u32[]{:S(2)}, u32[]{:S(2)}) collective-permute-start(f32[4,64,128]{2,1,0:T(8,128)S(1)} %get-tuple-element.50), channel_id=1, source_target_pairs={{28,4},{29,5},{30,6},{31,7},{0,8},{1,9},{2,10},{3,11},{12,20},{13,... | collective-permute-start | bytes 393224 | tf_op jit(solution)/shard_map/ppermute | solution.py:502
  5.6 8.1 %collective-permute-start.1 = (f32[4,64,128]{2,1,0:T(8,128)S(1)}, f32[4,64,128]{2,1,0:T(8,128)S(1)}, u32[]{:S(2)}, u32[]{:S(2)}) collective-permute-start(f32[4,64,128]{2,1,0:T(8,128)S(1)} %get-tuple-element.51), channel_id=1, source_target_pairs={{4,12},{5,13},{6,14},{7,15},{8,16},{9,17},{10,18},{11,19},{12,4},{... | collective-permute-start | bytes 393224 | tf_op jit(solution)/shard_map/ppermute | solution.py:502
  8.5 11.9 %collective-permute-start.4 = (f32[3,64,128]{2,1,0:T(8,128)S(1)}, f32[3,64,128]{2,1,0:T(8,128)S(1)}, u32[]{:S(2)}, u32[]{:S(2)}) collective-permute-start(f32[3,64,128]{2,1,0:T(8,128)S(1)} %get-tuple-element.58), channel_id=1, source_target_pairs={{28,4},{29,5},{30,6},{31,7},{0,8},{1,9},{2,10},{3,11},{12,20},{13,... | collective-permute-start | bytes 294920 | tf_op jit(solution)/shard_map/ppermute | solution.py:502
  13.0 7.4 %collective-permute-start.5 = (f32[3,64,128]{2,1,0:T(8,128)S(1)}, f32[3,64,128]{2,1,0:T(8,128)S(1)}, u32[]{:S(2)}, u32[]{:S(2)}) collective-permute-start(f32[3,64,128]{2,1,0:T(8,128)S(1)} %get-tuple-element.59), channel_id=1, source_target_pairs={{4,12},{5,13},{6,14},{7,15},{8,16},{9,17},{10,18},{11,19},{12,4},{... | collective-permute-start | bytes 294920 | tf_op jit(solution)/shard_map/ppermute | solution.py:502
  13.7 10.1 %collective-permute-start.2 = (f32[4,64,128]{2,1,0:T(8,128)S(1)}, f32[4,64,128]{2,1,0:T(8,128)S(1)}, u32[]{:S(2)}, u32[]{:S(2)}) collective-permute-start(f32[4,64,128]{2,1,0:T(8,128)S(1)} %get-tuple-element.54), channel_id=1, source_target_pairs={{28,29},{30,31},{0,1},{2,3},{4,5},{6,7},{8,9},{10,11},{12,13},{14,... | collective-permute-start | bytes 393224 | tf_op jit(solution)/shard_map/ppermute | solution.py:502
  13.8 10.0 %collective-permute-start.3 = (f32[4,64,128]{2,1,0:T(8,128)S(1)}, f32[4,64,128]{2,1,0:T(8,128)S(1)}, u32[]{:S(2)}, u32[]{:S(2)}) collective-permute-start(f32[4,64,128]{2,1,0:T(8,128)S(1)} %get-tuple-element.55), channel_id=1, source_target_pairs={{29,30},{31,0},{1,2},{5,6},{7,8},{9,10},{13,14},{15,16},{17,18},{2... | collective-permute-start | bytes 393224 | tf_op jit(solution)/shard_map/ppermute | solution.py:502
  20.5 9.0 %collective-permute-start.6 = (f32[3,64,128]{2,1,0:T(8,128)S(1)}, f32[3,64,128]{2,1,0:T(8,128)S(1)}, u32[]{:S(2)}, u32[]{:S(2)}) collective-permute-start(f32[3,64,128]{2,1,0:T(8,128)S(1)} %get-tuple-element.62), channel_id=1, source_target_pairs={{28,29},{30,31},{0,1},{2,3},{4,5},{6,7},{8,9},{10,11},{12,13},{14,... | collective-permute-start | bytes 294920 | tf_op jit(solution)/shard_map/ppermute | solution.py:502
  20.5 9.5 %collective-permute-start.7 = (f32[3,64,128]{2,1,0:T(8,128)S(1)}, f32[3,64,128]{2,1,0:T(8,128)S(1)}, u32[]{:S(2)}, u32[]{:S(2)}) collective-permute-start(f32[3,64,128]{2,1,0:T(8,128)S(1)} %get-tuple-element.63), channel_id=1, source_target_pairs={{29,30},{31,0},{1,2},{5,6},{7,8},{9,10},{13,14},{15,16},{17,18},{2... | collective-permute-start | bytes 294920 | tf_op jit(solution)/shard_map/ppermute | solution.py:502
  26.3 7.7 %collective-permute-start.12 = (f32[3,64,128]{2,1,0:T(8,128)S(1)}, f32[3,64,128]{2,1,0:T(8,128)S(1)}, u32[]{:S(2)}, u32[]{:S(2)}) collective-permute-start(f32[3,64,128]{2,1,0:T(8,128)S(1)} %get-tuple-element.74), channel_id=1, source_target_pairs={{28,4},{29,5},{30,6},{31,7},{0,8},{1,9},{2,10},{3,11},{12,20},{13,... | collective-permute-start | bytes 294920 | tf_op jit(solution)/shard_map/ppermute | solution.py:502
  28.8 5.3 %collective-permute-start.13 = (f32[3,64,128]{2,1,0:T(8,128)S(1)}, f32[3,64,128]{2,1,0:T(8,128)S(1)}, u32[]{:S(2)}, u32[]{:S(2)}) collective-permute-start(f32[3,64,128]{2,1,0:T(8,128)S(1)} %get-tuple-element.75), channel_id=1, source_target_pairs={{4,12},{5,13},{6,14},{7,15},{8,16},{9,17},{10,18},{11,19},{12,4},{... | collective-permute-start | bytes 294920 | tf_op jit(solution)/shard_map/ppermute | solution.py:502
  32.4 9.0 %collective-permute-start.8 = (f32[3,64,128]{2,1,0:T(8,128)S(1)}, f32[3,64,128]{2,1,0:T(8,128)S(1)}, u32[]{:S(2)}, u32[]{:S(2)}) collective-permute-start(f32[3,64,128]{2,1,0:T(8,128)S(1)} %get-tuple-element.66), channel_id=1, source_target_pairs={{28,4},{29,5},{30,6},{31,7},{0,8},{1,9},{2,10},{3,11},{12,20},{13,... | collective-permute-start | bytes 294920 | tf_op jit(solution)/shard_map/ppermute | solution.py:502
  33.4 8.0 %collective-permute-start.9 = (f32[3,64,128]{2,1,0:T(8,128)S(1)}, f32[3,64,128]{2,1,0:T(8,128)S(1)}, u32[]{:S(2)}, u32[]{:S(2)}) collective-permute-start(f32[3,64,128]{2,1,0:T(8,128)S(1)} %get-tuple-element.67), channel_id=1, source_target_pairs={{4,12},{5,13},{6,14},{7,15},{8,16},{9,17},{10,18},{11,19},{12,4},{... | collective-permute-start | bytes 294920 | tf_op jit(solution)/shard_map/ppermute | solution.py:502
  34.1 9.8 %collective-permute-start.14 = (f32[3,64,128]{2,1,0:T(8,128)S(1)}, f32[3,64,128]{2,1,0:T(8,128)S(1)}, u32[]{:S(2)}, u32[]{:S(2)}) collective-permute-start(f32[3,64,128]{2,1,0:T(8,128)S(1)} %get-tuple-element.78), channel_id=1, source_target_pairs={{28,29},{30,31},{0,1},{2,3},{4,5},{6,7},{8,9},{10,11},{12,13},{14,... | collective-permute-start | bytes 294920 | tf_op jit(solution)/shard_map/ppermute | solution.py:502
  34.2 9.7 %collective-permute-start.15 = (f32[3,64,128]{2,1,0:T(8,128)S(1)}, f32[3,64,128]{2,1,0:T(8,128)S(1)}, u32[]{:S(2)}, u32[]{:S(2)}) collective-permute-start(f32[3,64,128]{2,1,0:T(8,128)S(1)} %get-tuple-element.79), channel_id=1, source_target_pairs={{29,30},{31,0},{1,2},{5,6},{7,8},{9,10},{13,14},{15,16},{17,18},{2... | collective-permute-start | bytes 294920 | tf_op jit(solution)/shard_map/ppermute | solution.py:502
  41.4 5.6 %collective-permute-start.10 = (f32[3,64,128]{2,1,0:T(8,128)S(1)}, f32[3,64,128]{2,1,0:T(8,128)S(1)}, u32[]{:S(2)}, u32[]{:S(2)}) collective-permute-start(f32[3,64,128]{2,1,0:T(8,128)S(1)} %get-tuple-element.70), channel_id=1, source_target_pairs={{28,29},{30,31},{0,1},{2,3},{4,5},{6,7},{8,9},{10,11},{12,13},{14,... | collective-permute-start | bytes 294920 | tf_op jit(solution)/shard_map/ppermute | solution.py:502
  41.5 9.5 %collective-permute-start.11 = (f32[3,64,128]{2,1,0:T(8,128)S(1)}, f32[3,64,128]{2,1,0:T(8,128)S(1)}, u32[]{:S(2)}, u32[]{:S(2)}) collective-permute-start(f32[3,64,128]{2,1,0:T(8,128)S(1)} %get-tuple-element.71), channel_id=1, source_target_pairs={{29,30},{31,0},{1,2},{5,6},{7,8},{9,10},{13,14},{15,16},{17,18},{2... | collective-permute-start | bytes 294920 | tf_op jit(solution)/shard_map/ppermute | solution.py:502

commit v4 on v3

--- a/solution.py
+++ b/solution.py
@@ -473,22 +473,23 @@
 
 def pairings(devices):
     columns = devices // DA
-    device = lambda row, place: (row * columns + place - columns // 2) % devices
+    device = lambda row, place: (row % DA * columns + place - columns // 2) % devices
 
     def both(pairs):
-        paired = {device for pair in pairs for device in pair}
-        alone = [(device, device) for device in range(devices) if device not in paired]
-        return pairs + [(b, a) for a, b in pairs] + alone
-
+        return pairs + [(b, a) for a, b in pairs]
+
+    places, halves = range(columns), range(0, columns, 2)
     along_i = [
-        both([(device(r, s), device(r + 1, s)) for r in range(way, DA - 1, 2) for s in range(columns)])
-        for way in range(2)
+        [(device(r, s), device(r + 1, s)) for r in range(0, DA, 2) for s in places],
+        [(device(r, s), device(r + 1, s)) for r in range(1, DA - 1, 2) for s in places]
+        + [(device(r, s), device(r, s + 1)) for r in (0, DA - 1) for s in halves],
     ]
     along_j = [
-        both([(device(r, s), device(r, s + 1)) for r in range(DA) for s in range(way, columns - 1, 2)])
-        for way in range(2)
+        [(device(r, s), device(r, s + 1)) for r in range(DA) for s in halves],
+        [(device(r, s - 1), device(r, s)) for r in range(DA) for s in halves if s]
+        + [(device(r, columns - 1), device(r + 1, 0)) for r in range(DA)],
     ]
-    return along_i, along_j
+    return [both(p) for p in along_i], [both(p) for p in along_j]
 
 
 def shards(moment_fields, adjoint_fields, velocity, mass_weights, diffusivity, numbering):

time: 52.6 us -> 44.8 us (0.85)
  waiting for transfers between devices: 4.73 us -> 0.04 us
  starting transfers between devices: 33.2 us -> 30.5 us
    ppermute x16, waiting for transfers between devices: 4.73 us -> 0.04 us  [exchange(): return [lax.ppermute(b, 'elem', p) for b, p in zip(blocks, pairs)]]
    ppermute x16, starting transfers between devices: 33.2 us -> 30.5 us  [exchange(): return [lax.ppermute(b, 'elem', p) for b, p in zip(blocks, pairs)]]
  transfers between devices with their start and end apart: 16 -> 16, of which waited for: 2 -> 0; matrix products, arithmetic and copies ran while one was open for 0% -> 0% of each run, Pallas kernels for 20% -> 23%
where the time goes in v4:
time: 44.8 us; the launch traced here: 44.6 us
  starting transfers between devices  30.5 us (68%)
  Pallas kernels  13.4 us (30%)
  between operations  0.73 us (2%)
    ppermute x16, starting transfers between devices, exchange(): return [lax.ppermute(b, 'elem', p) for b, p in zip(blocks, pairs)]  30.5 us
    pallas_call x10, Pallas kernels, call(): pl.pallas_call(kernel, out_shape=[jax.ShapeDtypeStruct(s, t) for s, t in...  13.4 us
  transfers between devices with their start and end apart: 16, of which 0 were waited for; matrix products, arithmetic and copies ran while one was open for 0% of the time, Pallas kernels for 23%

profile of v4, /device:TPU:0, one launch (start us, length us, event | category | flops | bytes accessed | tf_op | source)
XLA Modules:
  0.0 44.6 jit_solution(3479268157967417055)
XLA Ops:
  0.6 1.9 %shard_map.77 = (f32[3,512,128]{2,1,0:T(8,128)S(1)}, f32[3,512,128]{2,1,0:T(8,128)S(1)}, f32[3,512,128]{2,1,0:T(8,128)S(1)}, f32[3,8,128]{2,1,0:T(8,128)S(1)}, b...) custom-call(f32[3,512,128]{2,1,0:T(8,128)} %moment_far.1, ...), custom_call_target="tpu_custom_call" | custom-call | flops 1000000 | bytes 7893516 | tf_op jit(solution)/shard_map/pallas_call | solution.py:463
  2.5 3.1 %collective-permute-start = (f32[4,64,128]{2,1,0:T(8,128)S(1)}, f32[4,64,128]{2,1,0:T(8,128)S(1)}, u32[]{:S(2)}, u32[]{:S(2)}) collective-permute-start(f32[4,64,128]{2,1,0:T(8,128)S(1)} %get-tuple-element.50), channel_id=1, source_target_pairs={{28,4},{29,5},{30,6},{31,7},{0,8},{1,9},{2,10},{3,11},{12,20},{13,... | collective-permute-start | bytes 393224 | tf_op jit(solution)/shard_map/ppermute | solution.py:503
  5.6 0.0 collective-permute-start.1
  5.6 2.3 %shard_map.80 = (f32[3,512,128]{2,1,0:T(8,128)S(1)}, f32[3,64,128]{2,1,0:T(8,128)S(1)}, f32[3,64,128]{2,1,0:T(8,128)S(1)}, f32[3,64,128]{2,1,0:T(8,128)S(1)}, f32[3,64,128]{2,1,0:T(8,128)S(1)}) custom-call(f32[3,512,128]{2,1,0:T(8,128)S(1)} %get-tuple-element.41.moment_ref, f32[3,512,128]{2,1,0:T(8,128)S(1)} %get-tuple-element.42.flow_ref, ...), custom_call_target="tpu_custom_call" | custom-call | flops 20000000 | bytes 4091904 | tf_op jit(solution)/shard_map/pallas_call | solution.py:463
  7.9 3.2 %collective-permute-start.4 = (f32[3,64,128]{2,1,0:T(8,128)S(1)}, f32[3,64,128]{2,1,0:T(8,128)S(1)}, u32[]{:S(2)}, u32[]{:S(2)}) collective-permute-start(f32[3,64,128]{2,1,0:T(8,128)S(1)} %get-tuple-element.58), channel_id=1, source_target_pairs={{28,4},{29,5},{30,6},{31,7},{0,8},{1,9},{2,10},{3,11},{12,20},{13,... | collective-permute-start | bytes 294920 | tf_op jit(solution)/shard_map/ppermute | solution.py:503
  11.1 0.0 collective-permute-start.5
  11.1 0.0 collective-permute-done.ie_ref.refs_0_
  11.1 0.0 collective-permute-done.1.io_ref.refs_1_
  11.1 0.6 %collective-permute-start.2 = (f32[4,64,128]{2,1,0:T(8,128)S(1)}, f32[4,64,128]{2,1,0:T(8,128)S(1)}, u32[]{:S(2)}, u32[]{:S(2)}) collective-permute-start(f32[4,64,128]{2,1,0:T(8,128)S(1)} %get-tuple-element.54), channel_id=1, source_target_pairs={{28,29},{30,31},{0,1},{2,3},{4,5},{6,7},{8,9},{10,11},{12,13},{14,... | collective-permute-start | bytes 393224 | tf_op jit(solution)/shard_map/ppermute | solution.py:503
  11.7 6.2 %collective-permute-start.3 = (f32[4,64,128]{2,1,0:T(8,128)S(1)}, f32[4,64,128]{2,1,0:T(8,128)S(1)}, u32[]{:S(2)}, u32[]{:S(2)}) collective-permute-start(f32[4,64,128]{2,1,0:T(8,128)S(1)} %get-tuple-element.55), channel_id=1, source_target_pairs={{29,30},{31,0},{1,2},{5,6},{7,8},{9,10},{13,14},{15,16},{17,18},{2... | collective-permute-start | bytes 393224 | tf_op jit(solution)/shard_map/ppermute | solution.py:503
  17.9 0.0 collective-permute-done.4.ie_ref.gie_ref
  17.9 0.0 collective-permute-done.5.io_ref.gio_ref
  18.0 0.1 collective-permute-start.6
  18.1 4.8 %collective-permute-start.7 = (f32[3,64,128]{2,1,0:T(8,128)S(1)}, f32[3,64,128]{2,1,0:T(8,128)S(1)}, u32[]{:S(2)}, u32[]{:S(2)}) collective-permute-start(f32[3,64,128]{2,1,0:T(8,128)S(1)} %get-tuple-element.63), channel_id=1, source_target_pairs={{29,30},{31,0},{1,2},{5,6},{7,8},{9,10},{13,14},{15,16},{17,18},{2... | collective-permute-start | bytes 294920 | tf_op jit(solution)/shard_map/ppermute | solution.py:503
  22.8 0.0 collective-permute-done.2.refs_2_
  22.8 0.0 collective-permute-done.3.refs_3_
  22.9 2.5 %shard_map.79 = (f32[512,128]{1,0:T(8,128)S(1)}, f32[3,512,128]{2,1,0:T(8,128)S(1)}, f32[3,512,128]{2,1,0:T(8,128)S(1)}, f32[3,64,128]{2,1,0:T(8,128)S(1)}, f32[...) custom-call(f32[3,512,128]{2,1,0:T(8,128)S(1)} %get-tuple-element.48.state_ref, ...), custom_call_target="tpu_custom_call" | custom-call | flops 20000000 | bytes 6713344 | tf_op jit(solution)/shard_map/pallas_call | solution.py:463
  25.4 1.0 %collective-permute-start.12 = (f32[3,64,128]{2,1,0:T(8,128)S(1)}, f32[3,64,128]{2,1,0:T(8,128)S(1)}, u32[]{:S(2)}, u32[]{:S(2)}) collective-permute-start(f32[3,64,128]{2,1,0:T(8,128)S(1)} %get-tuple-element.74), channel_id=1, source_target_pairs={{28,4},{29,5},{30,6},{31,7},{0,8},{1,9},{2,10},{3,11},{12,20},{13,... | collective-permute-start | bytes 294920 | tf_op jit(solution)/shard_map/ppermute | solution.py:503
  26.4 0.0 collective-permute-start.13
  26.4 0.0 collective-permute-done.6.gje_ref
  26.4 0.0 collective-permute-done.7.gjo_ref
  26.4 2.3 %shard_map.82 = (f32[3,512,128]{2,1,0:T(8,128)S(1)}, f32[3,512,128]{2,1,0:T(8,128)S(1)}, f32[3,64,128]{2,1,0:T(8,128)S(1)}, f32[3,64,128]{2,1,0:T(8,128)S(1)}, f...) custom-call(f32[3,512,128]{2,1,0:T(8,128)S(1)} %get-tuple-element.41.moment_ref, ...), custom_call_target="tpu_custom_call" | custom-call | flops 20000000 | bytes 6320128 | tf_op jit(solution)/shard_map/pallas_call | solution.py:463
  28.7 1.5 %collective-permute-start.8 = (f32[3,64,128]{2,1,0:T(8,128)S(1)}, f32[3,64,128]{2,1,0:T(8,128)S(1)}, u32[]{:S(2)}, u32[]{:S(2)}) collective-permute-start(f32[3,64,128]{2,1,0:T(8,128)S(1)} %get-tuple-element.66), channel_id=1, source_target_pairs={{28,4},{29,5},{30,6},{31,7},{0,8},{1,9},{2,10},{3,11},{12,20},{13,... | collective-permute-start | bytes 294920 | tf_op jit(solution)/shard_map/ppermute | solution.py:503
  30.2 0.0 collective-permute-start.9
  30.2 0.0 collective-permute-done.12.ie_ref.refs_1_
  30.2 0.0 collective-permute-done.13.io_ref.refs_2_
  30.2 0.6 %collective-permute-start.14 = (f32[3,64,128]{2,1,0:T(8,128)S(1)}, f32[3,64,128]{2,1,0:T(8,128)S(1)}, u32[]{:S(2)}, u32[]{:S(2)}) collective-permute-start(f32[3,64,128]{2,1,0:T(8,128)S(1)} %get-tuple-element.78), channel_id=1, source_target_pairs={{28,29},{30,31},{0,1},{2,3},{4,5},{6,7},{8,9},{10,11},{12,13},{14,... | collective-permute-start | bytes 294920 | tf_op jit(solution)/shard_map/ppermute | solution.py:503
  30.8 3.9 %collective-permute-start.15 = (f32[3,64,128]{2,1,0:T(8,128)S(1)}, f32[3,64,128]{2,1,0:T(8,128)S(1)}, u32[]{:S(2)}, u32[]{:S(2)}) collective-permute-start(f32[3,64,128]{2,1,0:T(8,128)S(1)} %get-tuple-element.79), channel_id=1, source_target_pairs={{29,30},{31,0},{1,2},{5,6},{7,8},{9,10},{13,14},{15,16},{17,18},{2... | collective-permute-start | bytes 294920 | tf_op jit(solution)/shard_map/ppermute | solution.py:503
  34.7 0.0 collective-permute-done.8.ie_ref.gie_ref
  34.8 0.0 collective-permute-done.9.io_ref.gio_ref
  34.8 0.1 collective-permute-start.10
  34.9 5.4 %collective-permute-start.11 = (f32[3,64,128]{2,1,0:T(8,128)S(1)}, f32[3,64,128]{2,1,0:T(8,128)S(1)}, u32[]{:S(2)}, u32[]{:S(2)}) collective-permute-start(f32[3,64,128]{2,1,0:T(8,128)S(1)} %get-tuple-element.71), channel_id=1, source_target_pairs={{29,30},{31,0},{1,2},{5,6},{7,8},{9,10},{13,14},{15,16},{17,18},{2... | collective-permute-start | bytes 294920 | tf_op jit(solution)/shard_map/ppermute | solution.py:503
  40.3 0.0 collective-permute-done.14.refs_3_
  40.3 0.0 collective-permute-done.15.refs_4_
  40.3 3.1 %shard_map.86 = f32[3,512,128]{2,1,0:T(8,128)} custom-call(f32[3,512,128]{2,1,0:T(8,128)S(1)} %get-tuple-element.72.state_ref, f32[3,512,128]{2,1,0:T(8,128)S(1)} %get-tuple-element.42.flow_ref, f32[3,8,128]{2,1,0:T(8,128)S(1)} %get-tuple-element.43.diff_ref, bf16[512,256]{1,0:T(8,128)(2,1)S(1)} %get-tuple-element.44.table_ref, ...), custom_call_target="tpu_custom_call" | custom-call | flops 20000000 | bytes 5140480 | tf_op jit(solution)/shard_map/pallas_call | solution.py:463
  43.4 0.0 collective-permute-done.10.gje_ref
  43.4 0.0 collective-permute-done.11.gjo_ref
  43.4 1.2 %shard_map.84 = f32[3,512,128]{2,1,0:T(8,128)} custom-call(f32[3,512,128]{2,1,0:T(8,128)S(1)} %get-tuple-element.64.moment_ref, s32[4,8,128]{2,1,0:T(8,128)S(1)} %get-tuple-element.46.index_ref, f32[512,128]{1,0:T(8,128)S(1)} %get-tuple-element.56.inverse_ref.refs_0_, f32[3,512,128]{2,1,0:T(8,128)S(1)} %get-tuple-element.65.joined_ref, ...), custom_call_target="tpu_custom_call" | custom-call | flops 1000000 | bytes 3031040 | tf_op jit(solution)/shard_map/pallas_call | solution.py:463
  (4 shorter events, 0.1 us)
Async XLA Ops:
  2.5 8.6 %collective-permute-start = (f32[4,64,128]{2,1,0:T(8,128)S(1)}, f32[4,64,128]{2,1,0:T(8,128)S(1)}, u32[]{:S(2)}, u32[]{:S(2)}) collective-permute-start(f32[4,64,128]{2,1,0:T(8,128)S(1)} %get-tuple-element.50), channel_id=1, source_target_pairs={{28,4},{29,5},{30,6},{31,7},{0,8},{1,9},{2,10},{3,11},{12,20},{13,... | collective-permute-start | bytes 393224 | tf_op jit(solution)/shard_map/ppermute | solution.py:503
  5.6 5.5 %collective-permute-start.1 = (f32[4,64,128]{2,1,0:T(8,128)S(1)}, f32[4,64,128]{2,1,0:T(8,128)S(1)}, u32[]{:S(2)}, u32[]{:S(2)}) collective-permute-start(f32[4,64,128]{2,1,0:T(8,128)S(1)} %get-tuple-element.51), channel_id=1, source_target_pairs={{4,12},{5,13},{6,14},{7,15},{8,16},{9,17},{10,18},{11,19},{28,29},... | collective-permute-start | bytes 393224 | tf_op jit(solution)/shard_map/ppermute | solution.py:503
  7.9 10.1 %collective-permute-start.4 = (f32[3,64,128]{2,1,0:T(8,128)S(1)}, f32[3,64,128]{2,1,0:T(8,128)S(1)}, u32[]{:S(2)}, u32[]{:S(2)}) collective-permute-start(f32[3,64,128]{2,1,0:T(8,128)S(1)} %get-tuple-element.58), channel_id=1, source_target_pairs={{28,4},{29,5},{30,6},{31,7},{0,8},{1,9},{2,10},{3,11},{12,20},{13,... | collective-permute-start | bytes 294920 | tf_op jit(solution)/shard_map/ppermute | solution.py:503
  11.1 6.9 %collective-permute-start.5 = (f32[3,64,128]{2,1,0:T(8,128)S(1)}, f32[3,64,128]{2,1,0:T(8,128)S(1)}, u32[]{:S(2)}, u32[]{:S(2)}) collective-permute-start(f32[3,64,128]{2,1,0:T(8,128)S(1)} %get-tuple-element.59), channel_id=1, source_target_pairs={{4,12},{5,13},{6,14},{7,15},{8,16},{9,17},{10,18},{11,19},{28,29},... | collective-permute-start | bytes 294920 | tf_op jit(solution)/shard_map/ppermute | solution.py:503
  11.1 11.7 %collective-permute-start.2 = (f32[4,64,128]{2,1,0:T(8,128)S(1)}, f32[4,64,128]{2,1,0:T(8,128)S(1)}, u32[]{:S(2)}, u32[]{:S(2)}) collective-permute-start(f32[4,64,128]{2,1,0:T(8,128)S(1)} %get-tuple-element.54), channel_id=1, source_target_pairs={{28,29},{30,31},{0,1},{2,3},{4,5},{6,7},{8,9},{10,11},{12,13},{14,... | collective-permute-start | bytes 393224 | tf_op jit(solution)/shard_map/ppermute | solution.py:503
  11.7 11.1 %collective-permute-start.3 = (f32[4,64,128]{2,1,0:T(8,128)S(1)}, f32[4,64,128]{2,1,0:T(8,128)S(1)}, u32[]{:S(2)}, u32[]{:S(2)}) collective-permute-start(f32[4,64,128]{2,1,0:T(8,128)S(1)} %get-tuple-element.55), channel_id=1, source_target_pairs={{29,30},{31,0},{1,2},{5,6},{7,8},{9,10},{13,14},{15,16},{17,18},{2... | collective-permute-start | bytes 393224 | tf_op jit(solution)/shard_map/ppermute | solution.py:503
  18.0 8.4 %collective-permute-start.6 = (f32[3,64,128]{2,1,0:T(8,128)S(1)}, f32[3,64,128]{2,1,0:T(8,128)S(1)}, u32[]{:S(2)}, u32[]{:S(2)}) collective-permute-start(f32[3,64,128]{2,1,0:T(8,128)S(1)} %get-tuple-element.62), channel_id=1, source_target_pairs={{28,29},{30,31},{0,1},{2,3},{4,5},{6,7},{8,9},{10,11},{12,13},{14,... | collective-permute-start | bytes 294920 | tf_op jit(solution)/shard_map/ppermute | solution.py:503
  18.1 8.3 %collective-permute-start.7 = (f32[3,64,128]{2,1,0:T(8,128)S(1)}, f32[3,64,128]{2,1,0:T(8,128)S(1)}, u32[]{:S(2)}, u32[]{:S(2)}) collective-permute-start(f32[3,64,128]{2,1,0:T(8,128)S(1)} %get-tuple-element.63), channel_id=1, source_target_pairs={{29,30},{31,0},{1,2},{5,6},{7,8},{9,10},{13,14},{15,16},{17,18},{2... | collective-permute-start | bytes 294920 | tf_op jit(solution)/shard_map/ppermute | solution.py:503
  25.4 4.8 %collective-permute-start.12 = (f32[3,64,128]{2,1,0:T(8,128)S(1)}, f32[3,64,128]{2,1,0:T(8,128)S(1)}, u32[]{:S(2)}, u32[]{:S(2)}) collective-permute-start(f32[3,64,128]{2,1,0:T(8,128)S(1)} %get-tuple-element.74), channel_id=1, source_target_pairs={{28,4},{29,5},{30,6},{31,7},{0,8},{1,9},{2,10},{3,11},{12,20},{13,... | collective-permute-start | bytes 294920 | tf_op jit(solution)/shard_map/ppermute | solution.py:503
  26.4 3.8 %collective-permute-start.13 = (f32[3,64,128]{2,1,0:T(8,128)S(1)}, f32[3,64,128]{2,1,0:T(8,128)S(1)}, u32[]{:S(2)}, u32[]{:S(2)}) collective-permute-start(f32[3,64,128]{2,1,0:T(8,128)S(1)} %get-tuple-element.75), channel_id=1, source_target_pairs={{4,12},{5,13},{6,14},{7,15},{8,16},{9,17},{10,18},{11,19},{28,29},... | collective-permute-start | bytes 294920 | tf_op jit(solution)/shard_map/ppermute | solution.py:503
  28.7 6.1 %collective-permute-start.8 = (f32[3,64,128]{2,1,0:T(8,128)S(1)}, f32[3,64,128]{2,1,0:T(8,128)S(1)}, u32[]{:S(2)}, u32[]{:S(2)}) collective-permute-start(f32[3,64,128]{2,1,0:T(8,128)S(1)} %get-tuple-element.66), channel_id=1, source_target_pairs={{28,4},{29,5},{30,6},{31,7},{0,8},{1,9},{2,10},{3,11},{12,20},{13,... | collective-permute-start | bytes 294920 | tf_op jit(solution)/shard_map/ppermute | solution.py:503
  30.2 4.6 %collective-permute-start.9 = (f32[3,64,128]{2,1,0:T(8,128)S(1)}, f32[3,64,128]{2,1,0:T(8,128)S(1)}, u32[]{:S(2)}, u32[]{:S(2)}) collective-permute-start(f32[3,64,128]{2,1,0:T(8,128)S(1)} %get-tuple-element.67), channel_id=1, source_target_pairs={{4,12},{5,13},{6,14},{7,15},{8,16},{9,17},{10,18},{11,19},{28,29},... | collective-permute-start | bytes 294920 | tf_op jit(solution)/shard_map/ppermute | solution.py:503
  30.2 10.1 %collective-permute-start.14 = (f32[3,64,128]{2,1,0:T(8,128)S(1)}, f32[3,64,128]{2,1,0:T(8,128)S(1)}, u32[]{:S(2)}, u32[]{:S(2)}) collective-permute-start(f32[3,64,128]{2,1,0:T(8,128)S(1)} %get-tuple-element.78), channel_id=1, source_target_pairs={{28,29},{30,31},{0,1},{2,3},{4,5},{6,7},{8,9},{10,11},{12,13},{14,... | collective-permute-start | bytes 294920 | tf_op jit(solution)/shard_map/ppermute | solution.py:503
  30.8 9.5 %collective-permute-start.15 = (f32[3,64,128]{2,1,0:T(8,128)S(1)}, f32[3,64,128]{2,1,0:T(8,128)S(1)}, u32[]{:S(2)}, u32[]{:S(2)}) collective-permute-start(f32[3,64,128]{2,1,0:T(8,128)S(1)} %get-tuple-element.79), channel_id=1, source_target_pairs={{29,30},{31,0},{1,2},{5,6},{7,8},{9,10},{13,14},{15,16},{17,18},{2... | collective-permute-start | bytes 294920 | tf_op jit(solution)/shard_map/ppermute | solution.py:503
  34.8 8.6 %collective-permute-start.10 = (f32[3,64,128]{2,1,0:T(8,128)S(1)}, f32[3,64,128]{2,1,0:T(8,128)S(1)}, u32[]{:S(2)}, u32[]{:S(2)}) collective-permute-start(f32[3,64,128]{2,1,0:T(8,128)S(1)} %get-tuple-element.70), channel_id=1, source_target_pairs={{28,29},{30,31},{0,1},{2,3},{4,5},{6,7},{8,9},{10,11},{12,13},{14,... | collective-permute-start | bytes 294920 | tf_op jit(solution)/shard_map/ppermute | solution.py:503
  34.9 8.5 %collective-permute-start.11 = (f32[3,64,128]{2,1,0:T(8,128)S(1)}, f32[3,64,128]{2,1,0:T(8,128)S(1)}, u32[]{:S(2)}, u32[]{:S(2)}) collective-permute-start(f32[3,64,128]{2,1,0:T(8,128)S(1)} %get-tuple-element.71), channel_id=1, source_target_pairs={{29,30},{31,0},{1,2},{5,6},{7,8},{9,10},{13,14},{15,16},{17,18},{2... | collective-permute-start | bytes 294920 | tf_op jit(solution)/shard_map/ppermute | solution.py:503

commit v5 on v4

--- a/solution.py
+++ b/solution.py
@@ -89,9 +89,8 @@
     wide = jnp.concatenate([block[:256], block[256:]], axis=1)
     high = wide.astype(BF16)
     low = (wide - high.astype(F32)).astype(BF16)
-    both = jnp.dot(table_ref[...], high, preferred_element_type=F32)
-    rest = jnp.dot(table_ref[:256], low, preferred_element_type=F32)
-    out = both[:256] + (both[256:] + rest)
+    parts = jnp.concatenate([high, high, low], axis=0)
+    out = jnp.dot(table_ref[...], parts, preferred_element_type=F32)
     return jnp.concatenate([out[:, :128], out[:, 128:]], axis=0)
 
 
@@ -107,17 +106,15 @@
     high = base.astype(BF16).astype(F32)
     block = lax.shift_right_logical(lane, 3)
     zero = jnp.zeros((8, 128), F32)
-    for part, values in enumerate((high, base - high)):
-        for a in range(0, 32, 2):
+    empty = jnp.zeros((16, 128), F32)
+    for a in range(0, 32, 2):
+        parts = []
+        for values in (high, base - high):
             pair = [jnp.where(block == (a + n) % 16, values, zero) for n in range(2)]
             pair = jnp.concatenate(pair, axis=0)
-            wide = [pair, jnp.zeros((16, 128), F32)]
-            wide = jnp.concatenate(wide if a < 16 else wide[::-1], axis=1)
-            table_ref[pl.ds(256 * part + 8 * a, 16)] = wide.astype(BF16)
-
-
-def spread(diff, block):
-    return (diff[None] * block.reshape(-1, 8, 128)).reshape(block.shape)
+            parts.append([pair, empty] if a < 16 else [empty, pair])
+        wide = jnp.concatenate(parts[0] + parts[1] + parts[0], axis=1)
+        table_ref[pl.ds(8 * a, 16)] = wide.astype(BF16)
 
 
 def lanes(block, index):
@@ -136,56 +133,52 @@
             mass_ref[r] = weight_ref[r] * (along * float(WEIGHTS[i] * WEIGHTS[j]))
 
 
-def forward_k(source, flow_ref, mass_ref, diff, table_ref, turned_ref, work):
-    flux = along_k(table_ref, source[...]) * mass_ref[...]
-    work[...] = flow_ref[2] * flux + spread(diff, along_k(turned_ref, flux))
-
-
-def adjoint_k(source, flow_ref, mass_ref, diff, table_ref, turned_ref, work):
+def forward_k(source, carry_ref, weigh, table_ref, turned_ref, work):
     slope = along_k(table_ref, source[...])
-    flux = (flow_ref[2] * source[...] + spread(diff, slope)) * mass_ref[...]
-    work[...] = along_k(turned_ref, flux)
-
-
-def forward(source, flow_ref, mass_ref, diff, work, target):
+    work[...] = carry_ref[2] * slope + along_k(turned_ref, weigh[...] * slope)
+
+
+def adjoint_k(source, carry_ref, weigh, table_ref, turned_ref, work):
+    slope = along_k(table_ref, source[...])
+    work[...] = along_k(turned_ref, carry_ref[2] * source[...] + weigh[...] * slope)
+
+
+def forward(source, carry_ref, weigh, work, target):
     for j in range(8):
         slopes = line(DM, [source[rows(i, j)] for i in range(8)])
-        fluxes = [slopes[i] * mass_ref[rows(i, j)] for i in range(8)]
-        back = line(DM.T, fluxes)
+        back = line(DM.T, [weigh[rows(i, j)] * slopes[i] for i in range(8)])
         for i in range(8):
             r = rows(i, j)
-            target[r] = flow_ref[0, r] * fluxes[i] + diff * back[i]
+            target[r] = work[r] + (carry_ref[0, r] * slopes[i] + back[i])
     for i in range(8):
         slopes = line(DM, [source[rows(i, j)] for j in range(8)])
-        fluxes = [slopes[j] * mass_ref[rows(i, j)] for j in range(8)]
-        back = line(DM.T, fluxes)
+        back = line(DM.T, [weigh[rows(i, j)] * slopes[j] for j in range(8)])
         for j in range(8):
             r = rows(i, j)
-            target[r] = -(target[r] + work[r] + (flow_ref[1, r] * fluxes[j] + diff * back[j]))
-
-
-def adjoint(source, base, flow_ref, mass_ref, diff, work, target):
+            target[r] = target[r] + (carry_ref[1, r] * slopes[j] + back[j])
+
+
+def adjoint(source, base, carry_ref, weigh, work, target):
     for j in range(8):
         values = [source[rows(i, j)] for i in range(8)]
         slopes = line(DM, values)
         fluxes = [
-            (flow_ref[0, rows(i, j)] * values[i] + diff * slopes[i]) * mass_ref[rows(i, j)]
-            for i in range(8)
+            carry_ref[0, rows(i, j)] * values[i] + weigh[rows(i, j)] * slopes[i] for i in range(8)
         ]
         back = line(DM.T, fluxes)
         for i in range(8):
-            target[rows(i, j)] = back[i]
+            r = rows(i, j)
+            target[r] = base[r] - (work[r] + back[i])
     for i in range(8):
         values = [source[rows(i, j)] for j in range(8)]
         slopes = line(DM, values)
         fluxes = [
-            (flow_ref[1, rows(i, j)] * values[j] + diff * slopes[j]) * mass_ref[rows(i, j)]
-            for j in range(8)
+            carry_ref[1, rows(i, j)] * values[j] + weigh[rows(i, j)] * slopes[j] for j in range(8)
         ]
         back = line(DM.T, fluxes)
         for j in range(8):
             r = rows(i, j)
-            target[r] = base[r] - DT * (target[r] + work[r] + back[j])
+            target[r] = target[r] - back[j]
 
 
 def join_heights(ref, index):
@@ -247,24 +240,25 @@
     numbers_far,
     moment_ref,
     state_ref,
-    flow_ref,
-    diff_ref,
+    carry_ref,
+    weigh_ref,
     table_ref,
     turned_ref,
     index_ref,
-    mass_ref,
     joined_ref,
     ie_ref,
     io_ref,
     je_ref,
     jo_ref,
     weight_ref,
+    mass_ref,
+    flow_ref,
     numbers_ref,
-    scalar_ref,
+    diff_ref,
     arrived,
 ):
     far = (numbers_far, weight_far, state_far, diff_far, moment_far, flow_far)
-    near = (numbers_ref, weight_ref, state_ref, scalar_ref, moment_ref, flow_ref)
+    near = (numbers_ref, weight_ref, state_ref, diff_ref, moment_ref, flow_ref)
     copies = [pltpu.make_async_copy(a, b, arrived.at[n]) for n, (a, b) in enumerate(zip(far, near))]
     for copy in copies:
         copy.start()
@@ -298,20 +292,21 @@
         send_faces(c, joined_ref.at[c], index, ends, out)
     copies[3].wait()
     for f in range(3):
-        diff_ref[f] = jnp.full((8, 128), scalar_ref[f], F32)
+        weigh_ref[f] = mass_ref[...] * (DT * diff_ref[f])
+    copies[5].wait()
+    for d in range(3):
+        carry_ref[d] = mass_ref[...] * (DT * flow_ref[d])
     copies[4].wait()
-    copies[5].wait()
 
 
 def moment_kernel(
     columns,
     moment_ref,
-    flow_ref,
-    diff_ref,
+    carry_ref,
+    weigh_ref,
     table_ref,
     turned_ref,
     index_ref,
-    mass_ref,
     joined_ref,
     ie_ref,
     io_ref,
@@ -324,10 +319,10 @@
     out = (ie_ref, io_ref, je_ref, jo_ref)
 
     for f in range(3):
-        at = (flow_ref, mass_ref, diff_ref[f])
+        at = (carry_ref, weigh_ref.at[f])
         forward_k(moment_ref.at[f], *at, table_ref, turned_ref, work_ref.at[f])
     for f in range(3):
-        at = (flow_ref, mass_ref, diff_ref[f])
+        at = (carry_ref, weigh_ref.at[f])
         forward(moment_ref.at[f], *at, work_ref.at[f], joined_ref.at[f])
         join_heights(joined_ref.at[f], index)
         send_faces(f, joined_ref.at[f], index, ends, out)
@@ -348,12 +343,11 @@
     columns,
     first,
     state_ref,
-    flow_ref,
-    diff_ref,
+    carry_ref,
+    weigh_ref,
     table_ref,
     turned_ref,
     index_ref,
-    mass_ref,
     joined_ref,
     *refs,
 ):
@@ -368,40 +362,48 @@
         inverse_ref[...] = 1.0 / held[...]
     else:
         inverse_ref, *got = refs[:5]
-        state_out, work_ref, hold_ref = refs[5:]
+        state_far, work_ref, hold_ref, state_out, sent = refs[5:]
 
     for f in range(3):
         held = hold_ref.at[f]
         held[...] = joined_ref[f]
         add_faces(f, held, index, ends, got)
         held[...] = held[...] * inverse_ref[...]
-        at = (flow_ref, mass_ref, diff_ref[f])
+        at = (carry_ref, weigh_ref.at[f])
         adjoint_k(held, *at, table_ref, turned_ref, work_ref.at[f])
     for f in range(3):
-        at = (flow_ref, mass_ref, diff_ref[f])
+        at = (carry_ref, weigh_ref.at[f])
         adjoint(hold_ref.at[f], state_ref.at[f], *at, work_ref.at[f], state_out.at[f])
         if first:
             joined_out[f] = state_out[f]
             join_heights(joined_out.at[f], index)
             send_faces(f, joined_out.at[f], index, ends, out)
+        else:
+            send_out(f, state_out, state_far, sent).start()
+    if not first:
+        for f in range(3):
+            send_out(f, state_out, state_far, sent).wait()
+
+
+def send_out(f, near, far, sent):
+    return pltpu.make_async_copy(near.at[f], far.at[f], sent.at[f])
 
 
 def moment_step(f, ends, index, moment_ref, joined_ref, inverse_ref, got, hold_ref, moment_out):
     held = hold_ref.at[f]
     held[...] = joined_ref[f]
     add_faces(f, held, index, ends, got)
-    moment_out[f] = moment_ref[f] + DT * (held[...] * inverse_ref[...])
+    moment_out[f] = moment_ref[f] - held[...] * inverse_ref[...]
 
 
 def middle_kernel(
     columns,
     moment_ref,
-    flow_ref,
-    diff_ref,
+    carry_ref,
+    weigh_ref,
     table_ref,
     turned_ref,
     index_ref,
-    mass_ref,
     inverse_ref,
     joined_ref,
     gie_ref,
@@ -424,10 +426,10 @@
 
     for f in range(3):
         moment_step(f, ends, index, moment_ref, joined_ref, inverse_ref, got, hold_ref, moment_out)
-        at = (flow_ref, mass_ref, diff_ref[f])
+        at = (carry_ref, weigh_ref.at[f])
         forward_k(moment_out.at[f], *at, table_ref, turned_ref, work_ref.at[f])
     for f in range(3):
-        at = (flow_ref, mass_ref, diff_ref[f])
+        at = (carry_ref, weigh_ref.at[f])
         forward(moment_out.at[f], *at, work_ref.at[f], joined_out.at[f])
         join_heights(joined_out.at[f], index)
         send_faces(f, joined_out.at[f], index, ends, out)
@@ -443,8 +445,10 @@
     gio_ref,
     gje_ref,
     gjo_ref,
+    moment_far,
+    hold_ref,
     moment_out,
-    hold_ref,
+    sent,
 ):
     ends = ends_of(columns)
     index = index_of(index_ref)
@@ -452,19 +456,22 @@
 
     for f in range(3):
         moment_step(f, ends, index, moment_ref, joined_ref, inverse_ref, got, hold_ref, moment_out)
+        send_out(f, moment_out, moment_far, sent).start()
+    for f in range(3):
+        send_out(f, moment_out, moment_far, sent).wait()
 
 
 VMEM = pl.BlockSpec(memory_space=pltpu.VMEM)
 FAR = pl.BlockSpec(memory_space=pltpu.HBM)
 
 
-def call(kernel, specs, shapes, scratch, flops, *operands):
+def call(kernel, specs, shapes, scratch, flops, *operands, out=VMEM):
     moved = sum(o.size * 4 for o in operands) + sum(int(np.prod(s)) * 4 for s, _ in shapes)
     return pl.pallas_call(
         kernel,
         out_shape=[jax.ShapeDtypeStruct(s, t) for s, t in shapes],
         in_specs=specs,
-        out_specs=[VMEM] * len(shapes),
+        out_specs=[out] * len(shapes),
         scratch_shapes=scratch,
         compiler_params=pltpu.CompilerParams(vmem_limit_bytes=32 * 1024 * 1024),
         cost_estimate=pl.CostEstimate(flops=flops, bytes_accessed=moved, transcendentals=0),
@@ -513,7 +520,7 @@
             *got_i,
             *faces[2:],
         )
-        return got_i + exchange(faces_j, along_j)
+        return got_i + exchange(faces_j[::-1], along_j[::-1])[::-1]
 
     def far(array):
         return pltpu.with_memory_space_constraint(array, pltpu.HBM)
@@ -521,16 +528,17 @@
     def faces_shape(count):
         return [((count, 64, 128), F32)] * 4
 
-    moment, state, flow, diff, table, turned, index, mass, joined_state, *faces_state = call(
+    moment, state, carry, weigh, table, turned, index, joined_state, *faces_state = call(
         functools.partial(index_kernel, columns),
         [FAR] * 6,
-        [whole] * 3
-        + [((3, 8, 128), F32)]
-        + [((512, 256), BF16)] * 2
-        + [((4, 8, 128), jnp.int32), block, ((4, 512, 128), F32)]
+        [whole] * 4
+        + [((256, 768), BF16)] * 2
+        + [((4, 8, 128), jnp.int32), ((4, 512, 128), F32)]
         + faces_shape(4),
         [
             pltpu.VMEM((512, 128), F32),
+            pltpu.VMEM((512, 128), F32),
+            work,
             pltpu.VMEM((1, 128), jnp.int32),
             pltpu.SMEM((3,), F32),
             pltpu.SemaphoreType.DMA((6,)),
@@ -539,11 +547,11 @@
         *map(far, (moment_fields, adjoint_fields, velocity, mass_weights)),
         *map(far, (diffusivity, numbering.reshape(1, 128))),
     )
-    tables = (flow, diff, table, turned, index, mass)
+    tables = (carry, weigh, table, turned, index)
     got_state = meet(4, faces_state)
     joined_moment, *faces_moment = call(
         functools.partial(moment_kernel, columns),
-        [VMEM] * 7,
+        [VMEM] * 6,
         [whole] + faces_shape(3),
         [work],
         20_000_000,
@@ -553,7 +561,7 @@
     got_moment = meet(3, faces_moment)
     inverse, state, joined_state, *faces_state = call(
         functools.partial(state_kernel, columns, True),
-        [VMEM] * 12,
+        [VMEM] * 11,
         [block, whole, whole] + faces_shape(3),
         [work] * 2,
         20_000_000,
@@ -565,7 +573,7 @@
     got_state = meet(3, faces_state)
     moment, joined_moment, *faces_moment = call(
         functools.partial(middle_kernel, columns),
-        [VMEM] * 13,
+        [VMEM] * 12,
         [whole, whole] + faces_shape(3),
         [work] * 2,
         20_000_000,
@@ -578,27 +586,29 @@
     got_moment = meet(3, faces_moment)
     (state,) = call(
         functools.partial(state_kernel, columns, False),
-        [VMEM] * 13,
+        [VMEM] * 12,
         [whole],
-        [work] * 2,
+        [work] * 3 + [pltpu.SemaphoreType.DMA((3,))],
         20_000_000,
         state,
         *tables,
         joined_state,
         inverse,
         *got_state,
+        out=FAR,
     )
     (moment,) = call(
         functools.partial(last_kernel, columns),
         [VMEM] * 8,
         [whole],
-        [work],
+        [work] * 2 + [pltpu.SemaphoreType.DMA((3,))],
         1_000_000,
         moment,
         index,
         inverse,
         joined_moment,
         *got_moment,
+        out=FAR,
     )
     return moment, state
 

time: 44.8 us -> 44 us (0.982)
  Pallas kernels: 13.4 us -> 12.3 us
    pallas_call x10, Pallas kernels: 13.4 us -> 12.3 us  [call(): pl.pallas_call(kernel, out_shape=[jax.ShapeDtypeStruct(s, t) for s, t in...]
  transfers between devices with their start and end apart: 16 -> 16, of which waited for: 0 -> 1; matrix products, arithmetic and copies ran while one was open for 0% -> 0% of each run, Pallas kernels for 23% -> 21%
where the time goes in v5:
time: 44 us; the launch traced here: 43.8 us
  starting transfers between devices  30.6 us (70%)
  Pallas kernels  12.3 us (28%)
  between operations  0.75 us (2%)
    ppermute x16, starting transfers between devices, exchange(): return [lax.ppermute(b, 'elem', p) for b, p in zip(blocks, pairs)]  30.6 us
    pallas_call x10, Pallas kernels, call(): pl.pallas_call(kernel, out_shape=[jax.ShapeDtypeStruct(s, t) for s, t in...  12.3 us
  transfers between devices with their start and end apart: 16, of which 1 were waited for; matrix products, arithmetic and copies ran while one was open for 0% of the time, Pallas kernels for 21%

profile of v5, /device:TPU:0, one launch (start us, length us, event | category | flops | bytes accessed | tf_op | source)
XLA Modules:
  0.0 43.8 jit_solution(16775840915071639322)
XLA Ops:
  0.6 2.0 %shard_map.77 = (f32[3,512,128]{2,1,0:T(8,128)S(1)}, f32[3,512,128]{2,1,0:T(8,128)S(1)}, f32[3,512,128]{2,1,0:T(8,128)S(1)}, f32[3,512,128]{2,1,0:T(8,128)S(1)},...) custom-call(f32[3,512,128]{2,1,0:T(8,128)} %moment_far.1, ...), custom_call_target="tpu_custom_call" | custom-call | flops 1000000 | bytes 8929804 | tf_op jit(solution)/shard_map/pallas_call | solution.py:470
  2.6 3.1 %collective-permute-start = (f32[4,64,128]{2,1,0:T(8,128)S(1)}, f32[4,64,128]{2,1,0:T(8,128)S(1)}, u32[]{:S(2)}, u32[]{:S(2)}) collective-permute-start(f32[4,64,128]{2,1,0:T(8,128)S(1)} %get-tuple-element.48), channel_id=1, source_target_pairs={{28,4},{29,5},{30,6},{31,7},{0,8},{1,9},{2,10},{3,11},{12,20},{13,... | collective-permute-start | bytes 393224 | tf_op jit(solution)/shard_map/ppermute | solution.py:510
  5.7 0.0 collective-permute-start.1
  5.7 2.1 %shard_map.80 = (f32[3,512,128]{2,1,0:T(8,128)S(1)}, f32[3,64,128]{2,1,0:T(8,128)S(1)}, f32[3,64,128]{2,1,0:T(8,128)S(1)}, f32[3,64,128]{2,1,0:T(8,128)S(1)}, f32[3,64,128]{2,1,0:T(8,128)S(1)}) custom-call(f32[3,512,128]{2,1,0:T(8,128)S(1)} %get-tuple-element.40.moment_ref, f32[3,512,128]{2,1,0:T(8,128)S(1)} %get-tuple-element.41.carry_ref, ...), custom_call_target="tpu_custom_call" | custom-call | flops 20000000 | bytes 5128192 | tf_op jit(solution)/shard_map/pallas_call | solution.py:470
  7.9 3.2 %collective-permute-start.4 = (f32[3,64,128]{2,1,0:T(8,128)S(1)}, f32[3,64,128]{2,1,0:T(8,128)S(1)}, u32[]{:S(2)}, u32[]{:S(2)}) collective-permute-start(f32[3,64,128]{2,1,0:T(8,128)S(1)} %get-tuple-element.56), channel_id=1, source_target_pairs={{28,4},{29,5},{30,6},{31,7},{0,8},{1,9},{2,10},{3,11},{12,20},{13,... | collective-permute-start | bytes 294920 | tf_op jit(solution)/shard_map/ppermute | solution.py:510
  11.1 0.0 collective-permute-start.5
  11.1 0.0 collective-permute-done.ie_ref.refs_0_
  11.1 0.0 collective-permute-done.1.io_ref.refs_1_
  11.1 0.6 %collective-permute-start.2 = (f32[4,64,128]{2,1,0:T(8,128)S(1)}, f32[4,64,128]{2,1,0:T(8,128)S(1)}, u32[]{:S(2)}, u32[]{:S(2)}) collective-permute-start(f32[4,64,128]{2,1,0:T(8,128)S(1)} %get-tuple-element.52), channel_id=1, source_target_pairs={{28,29},{30,31},{0,1},{2,3},{4,5},{6,7},{8,9},{10,11},{12,13},{14,... | collective-permute-start | bytes 393224 | tf_op jit(solution)/shard_map/ppermute | solution.py:510
  11.7 6.4 %collective-permute-start.3 = (f32[4,64,128]{2,1,0:T(8,128)S(1)}, f32[4,64,128]{2,1,0:T(8,128)S(1)}, u32[]{:S(2)}, u32[]{:S(2)}) collective-permute-start(f32[4,64,128]{2,1,0:T(8,128)S(1)} %get-tuple-element.53), channel_id=1, source_target_pairs={{29,30},{31,0},{1,2},{5,6},{7,8},{9,10},{13,14},{15,16},{17,18},{2... | collective-permute-start | bytes 393224 | tf_op jit(solution)/shard_map/ppermute | solution.py:510
  18.1 0.0 collective-permute-done.4.ie_ref.gie_ref
  18.1 0.0 collective-permute-done.5.io_ref.gio_ref
  18.1 0.1 collective-permute-start.6
  18.2 4.8 %collective-permute-start.7 = (f32[3,64,128]{2,1,0:T(8,128)S(1)}, f32[3,64,128]{2,1,0:T(8,128)S(1)}, u32[]{:S(2)}, u32[]{:S(2)}) collective-permute-start(f32[3,64,128]{2,1,0:T(8,128)S(1)} %get-tuple-element.61), channel_id=1, source_target_pairs={{29,30},{31,0},{1,2},{5,6},{7,8},{9,10},{13,14},{15,16},{17,18},{2... | collective-permute-start | bytes 294920 | tf_op jit(solution)/shard_map/ppermute | solution.py:510
  23.0 0.0 collective-permute-done.2.refs_2_
  23.0 0.0 collective-permute-done.3.refs_3_
  23.0 2.3 %shard_map.79 = (f32[512,128]{1,0:T(8,128)S(1)}, f32[3,512,128]{2,1,0:T(8,128)S(1)}, f32[3,512,128]{2,1,0:T(8,128)S(1)}, f32[3,64,128]{2,1,0:T(8,128)S(1)}, f32[...) custom-call(f32[3,512,128]{2,1,0:T(8,128)S(1)} %get-tuple-element.46.state_ref, ...), custom_call_target="tpu_custom_call" | custom-call | flops 20000000 | bytes 7749632 | tf_op jit(solution)/shard_map/pallas_call | solution.py:470
  25.3 1.0 %collective-permute-start.12 = (f32[3,64,128]{2,1,0:T(8,128)S(1)}, f32[3,64,128]{2,1,0:T(8,128)S(1)}, u32[]{:S(2)}, u32[]{:S(2)}) collective-permute-start(f32[3,64,128]{2,1,0:T(8,128)S(1)} %get-tuple-element.72), channel_id=1, source_target_pairs={{28,4},{29,5},{30,6},{31,7},{0,8},{1,9},{2,10},{3,11},{12,20},{13,... | collective-permute-start | bytes 294920 | tf_op jit(solution)/shard_map/ppermute | solution.py:510
  26.3 0.0 collective-permute-start.13
  26.3 0.0 collective-permute-done.6.gje_ref
  26.3 0.0 collective-permute-done.7.gjo_ref
  26.3 2.0 %shard_map.82 = (f32[3,512,128]{2,1,0:T(8,128)S(1)}, f32[3,512,128]{2,1,0:T(8,128)S(1)}, f32[3,64,128]{2,1,0:T(8,128)S(1)}, f32[3,64,128]{2,1,0:T(8,128)S(1)}, f...) custom-call(f32[3,512,128]{2,1,0:T(8,128)S(1)} %get-tuple-element.40.moment_ref, ...), custom_call_target="tpu_custom_call" | custom-call | flops 20000000 | bytes 7356416 | tf_op jit(solution)/shard_map/pallas_call | solution.py:470
  28.3 1.5 %collective-permute-start.8 = (f32[3,64,128]{2,1,0:T(8,128)S(1)}, f32[3,64,128]{2,1,0:T(8,128)S(1)}, u32[]{:S(2)}, u32[]{:S(2)}) collective-permute-start(f32[3,64,128]{2,1,0:T(8,128)S(1)} %get-tuple-element.64), channel_id=1, source_target_pairs={{28,4},{29,5},{30,6},{31,7},{0,8},{1,9},{2,10},{3,11},{12,20},{13,... | collective-permute-start | bytes 294920 | tf_op jit(solution)/shard_map/ppermute | solution.py:510
  29.9 0.0 collective-permute-start.9
  29.9 0.1 collective-permute-done.12.ie_ref.refs_1_
  30.0 0.0 collective-permute-done.13.io_ref.refs_2_
  30.0 0.5 %collective-permute-start.14 = (f32[3,64,128]{2,1,0:T(8,128)S(1)}, f32[3,64,128]{2,1,0:T(8,128)S(1)}, u32[]{:S(2)}, u32[]{:S(2)}) collective-permute-start(f32[3,64,128]{2,1,0:T(8,128)S(1)} %get-tuple-element.76), channel_id=1, source_target_pairs={{28,29},{30,31},{0,1},{2,3},{4,5},{6,7},{8,9},{10,11},{12,13},{14,... | collective-permute-start | bytes 294920 | tf_op jit(solution)/shard_map/ppermute | solution.py:510
  30.5 3.9 %collective-permute-start.15 = (f32[3,64,128]{2,1,0:T(8,128)S(1)}, f32[3,64,128]{2,1,0:T(8,128)S(1)}, u32[]{:S(2)}, u32[]{:S(2)}) collective-permute-start(f32[3,64,128]{2,1,0:T(8,128)S(1)} %get-tuple-element.77), channel_id=1, source_target_pairs={{29,30},{31,0},{1,2},{5,6},{7,8},{9,10},{13,14},{15,16},{17,18},{2... | collective-permute-start | bytes 294920 | tf_op jit(solution)/shard_map/ppermute | solution.py:510
  34.4 0.0 collective-permute-done.8.ie_ref.gie_ref
  34.4 0.0 collective-permute-done.9.io_ref.gio_ref
  34.5 0.1 collective-permute-start.10
  34.5 5.5 %collective-permute-start.11 = (f32[3,64,128]{2,1,0:T(8,128)S(1)}, f32[3,64,128]{2,1,0:T(8,128)S(1)}, u32[]{:S(2)}, u32[]{:S(2)}) collective-permute-start(f32[3,64,128]{2,1,0:T(8,128)S(1)} %get-tuple-element.69), channel_id=1, source_target_pairs={{29,30},{31,0},{1,2},{5,6},{7,8},{9,10},{13,14},{15,16},{17,18},{2... | collective-permute-start | bytes 294920 | tf_op jit(solution)/shard_map/ppermute | solution.py:510
  40.0 0.0 collective-permute-done.14.refs_3_
  40.0 0.0 collective-permute-done.15.refs_4_
  40.0 2.7 %shard_map.86 = f32[3,512,128]{2,1,0:T(8,128)} custom-call(f32[3,512,128]{2,1,0:T(8,128)S(1)} %get-tuple-element.70.state_ref, f32[3,512,128]{2,1,0:T(8,128)S(1)} %get-tuple-element.41.carry_ref, f32[3,512,128]{2,1,0:T(8,128)S(1)} %get-tuple-element.42.weigh_ref, bf16[256,768]{1,0:T(8,128)(2,1)S(1)} %get-tuple-element.43.table_ref, ...), custom_call_target="tpu_custom_call" | custom-call | flops 20000000 | bytes 6176768 | tf_op jit(solution)/shard_map/pallas_call | solution.py:470
  42.7 0.0 collective-permute-done.10.gje_ref
  42.7 0.0 collective-permute-done.11.gjo_ref
  42.7 1.1 %shard_map.84 = f32[3,512,128]{2,1,0:T(8,128)} custom-call(f32[3,512,128]{2,1,0:T(8,128)S(1)} %get-tuple-element.62.moment_ref, s32[4,8,128]{2,1,0:T(8,128)S(1)} %get-tuple-element.45.index_ref, f32[512,128]{1,0:T(8,128)S(1)} %get-tuple-element.54.inverse_ref.refs_0_, f32[3,512,128]{2,1,0:T(8,128)S(1)} %get-tuple-element.63.joined_ref, ...), custom_call_target="tpu_custom_call" | custom-call | flops 1000000 | bytes 3031040 | tf_op jit(solution)/shard_map/pallas_call | solution.py:470
  (4 shorter events, 0.1 us)
Async XLA Ops:
  2.6 8.4 %collective-permute-start = (f32[4,64,128]{2,1,0:T(8,128)S(1)}, f32[4,64,128]{2,1,0:T(8,128)S(1)}, u32[]{:S(2)}, u32[]{:S(2)}) collective-permute-start(f32[4,64,128]{2,1,0:T(8,128)S(1)} %get-tuple-element.48), channel_id=1, source_target_pairs={{28,4},{29,5},{30,6},{31,7},{0,8},{1,9},{2,10},{3,11},{12,20},{13,... | collective-permute-start | bytes 393224 | tf_op jit(solution)/shard_map/ppermute | solution.py:510
  5.7 5.3 %collective-permute-start.1 = (f32[4,64,128]{2,1,0:T(8,128)S(1)}, f32[4,64,128]{2,1,0:T(8,128)S(1)}, u32[]{:S(2)}, u32[]{:S(2)}) collective-permute-start(f32[4,64,128]{2,1,0:T(8,128)S(1)} %get-tuple-element.49), channel_id=1, source_target_pairs={{4,12},{5,13},{6,14},{7,15},{8,16},{9,17},{10,18},{11,19},{28,29},... | collective-permute-start | bytes 393224 | tf_op jit(solution)/shard_map/ppermute | solution.py:510
  7.9 10.2 %collective-permute-start.4 = (f32[3,64,128]{2,1,0:T(8,128)S(1)}, f32[3,64,128]{2,1,0:T(8,128)S(1)}, u32[]{:S(2)}, u32[]{:S(2)}) collective-permute-start(f32[3,64,128]{2,1,0:T(8,128)S(1)} %get-tuple-element.56), channel_id=1, source_target_pairs={{28,4},{29,5},{30,6},{31,7},{0,8},{1,9},{2,10},{3,11},{12,20},{13,... | collective-permute-start | bytes 294920 | tf_op jit(solution)/shard_map/ppermute | solution.py:510
  11.1 7.0 %collective-permute-start.5 = (f32[3,64,128]{2,1,0:T(8,128)S(1)}, f32[3,64,128]{2,1,0:T(8,128)S(1)}, u32[]{:S(2)}, u32[]{:S(2)}) collective-permute-start(f32[3,64,128]{2,1,0:T(8,128)S(1)} %get-tuple-element.57), channel_id=1, source_target_pairs={{4,12},{5,13},{6,14},{7,15},{8,16},{9,17},{10,18},{11,19},{28,29},... | collective-permute-start | bytes 294920 | tf_op jit(solution)/shard_map/ppermute | solution.py:510
  11.1 11.8 %collective-permute-start.2 = (f32[4,64,128]{2,1,0:T(8,128)S(1)}, f32[4,64,128]{2,1,0:T(8,128)S(1)}, u32[]{:S(2)}, u32[]{:S(2)}) collective-permute-start(f32[4,64,128]{2,1,0:T(8,128)S(1)} %get-tuple-element.52), channel_id=1, source_target_pairs={{28,29},{30,31},{0,1},{2,3},{4,5},{6,7},{8,9},{10,11},{12,13},{14,... | collective-permute-start | bytes 393224 | tf_op jit(solution)/shard_map/ppermute | solution.py:510
  11.7 11.3 %collective-permute-start.3 = (f32[4,64,128]{2,1,0:T(8,128)S(1)}, f32[4,64,128]{2,1,0:T(8,128)S(1)}, u32[]{:S(2)}, u32[]{:S(2)}) collective-permute-start(f32[4,64,128]{2,1,0:T(8,128)S(1)} %get-tuple-element.53), channel_id=1, source_target_pairs={{29,30},{31,0},{1,2},{5,6},{7,8},{9,10},{13,14},{15,16},{17,18},{2... | collective-permute-start | bytes 393224 | tf_op jit(solution)/shard_map/ppermute | solution.py:510
  18.1 8.2 %collective-permute-start.6 = (f32[3,64,128]{2,1,0:T(8,128)S(1)}, f32[3,64,128]{2,1,0:T(8,128)S(1)}, u32[]{:S(2)}, u32[]{:S(2)}) collective-permute-start(f32[3,64,128]{2,1,0:T(8,128)S(1)} %get-tuple-element.60), channel_id=1, source_target_pairs={{28,29},{30,31},{0,1},{2,3},{4,5},{6,7},{8,9},{10,11},{12,13},{14,... | collective-permute-start | bytes 294920 | tf_op jit(solution)/shard_map/ppermute | solution.py:510
  18.2 8.1 %collective-permute-start.7 = (f32[3,64,128]{2,1,0:T(8,128)S(1)}, f32[3,64,128]{2,1,0:T(8,128)S(1)}, u32[]{:S(2)}, u32[]{:S(2)}) collective-permute-start(f32[3,64,128]{2,1,0:T(8,128)S(1)} %get-tuple-element.61), channel_id=1, source_target_pairs={{29,30},{31,0},{1,2},{5,6},{7,8},{9,10},{13,14},{15,16},{17,18},{2... | collective-permute-start | bytes 294920 | tf_op jit(solution)/shard_map/ppermute | solution.py:510
  25.3 4.7 %collective-permute-start.12 = (f32[3,64,128]{2,1,0:T(8,128)S(1)}, f32[3,64,128]{2,1,0:T(8,128)S(1)}, u32[]{:S(2)}, u32[]{:S(2)}) collective-permute-start(f32[3,64,128]{2,1,0:T(8,128)S(1)} %get-tuple-element.72), channel_id=1, source_target_pairs={{28,4},{29,5},{30,6},{31,7},{0,8},{1,9},{2,10},{3,11},{12,20},{13,... | collective-permute-start | bytes 294920 | tf_op jit(solution)/shard_map/ppermute | solution.py:510
  26.3 3.7 %collective-permute-start.13 = (f32[3,64,128]{2,1,0:T(8,128)S(1)}, f32[3,64,128]{2,1,0:T(8,128)S(1)}, u32[]{:S(2)}, u32[]{:S(2)}) collective-permute-start(f32[3,64,128]{2,1,0:T(8,128)S(1)} %get-tuple-element.73), channel_id=1, source_target_pairs={{4,12},{5,13},{6,14},{7,15},{8,16},{9,17},{10,18},{11,19},{28,29},... | collective-permute-start | bytes 294920 | tf_op jit(solution)/shard_map/ppermute | solution.py:510
  28.3 6.1 %collective-permute-start.8 = (f32[3,64,128]{2,1,0:T(8,128)S(1)}, f32[3,64,128]{2,1,0:T(8,128)S(1)}, u32[]{:S(2)}, u32[]{:S(2)}) collective-permute-start(f32[3,64,128]{2,1,0:T(8,128)S(1)} %get-tuple-element.64), channel_id=1, source_target_pairs={{28,4},{29,5},{30,6},{31,7},{0,8},{1,9},{2,10},{3,11},{12,20},{13,... | collective-permute-start | bytes 294920 | tf_op jit(solution)/shard_map/ppermute | solution.py:510
  29.9 4.6 %collective-permute-start.9 = (f32[3,64,128]{2,1,0:T(8,128)S(1)}, f32[3,64,128]{2,1,0:T(8,128)S(1)}, u32[]{:S(2)}, u32[]{:S(2)}) collective-permute-start(f32[3,64,128]{2,1,0:T(8,128)S(1)} %get-tuple-element.65), channel_id=1, source_target_pairs={{4,12},{5,13},{6,14},{7,15},{8,16},{9,17},{10,18},{11,19},{28,29},... | collective-permute-start | bytes 294920 | tf_op jit(solution)/shard_map/ppermute | solution.py:510
  30.0 10.0 %collective-permute-start.14 = (f32[3,64,128]{2,1,0:T(8,128)S(1)}, f32[3,64,128]{2,1,0:T(8,128)S(1)}, u32[]{:S(2)}, u32[]{:S(2)}) collective-permute-start(f32[3,64,128]{2,1,0:T(8,128)S(1)} %get-tuple-element.76), channel_id=1, source_target_pairs={{28,29},{30,31},{0,1},{2,3},{4,5},{6,7},{8,9},{10,11},{12,13},{14,... | collective-permute-start | bytes 294920 | tf_op jit(solution)/shard_map/ppermute | solution.py:510
  30.5 9.5 %collective-permute-start.15 = (f32[3,64,128]{2,1,0:T(8,128)S(1)}, f32[3,64,128]{2,1,0:T(8,128)S(1)}, u32[]{:S(2)}, u32[]{:S(2)}) collective-permute-start(f32[3,64,128]{2,1,0:T(8,128)S(1)} %get-tuple-element.77), channel_id=1, source_target_pairs={{29,30},{31,0},{1,2},{5,6},{7,8},{9,10},{13,14},{15,16},{17,18},{2... | collective-permute-start | bytes 294920 | tf_op jit(solution)/shard_map/ppermute | solution.py:510
  34.5 8.2 %collective-permute-start.10 = (f32[3,64,128]{2,1,0:T(8,128)S(1)}, f32[3,64,128]{2,1,0:T(8,128)S(1)}, u32[]{:S(2)}, u32[]{:S(2)}) collective-permute-start(f32[3,64,128]{2,1,0:T(8,128)S(1)} %get-tuple-element.68), channel_id=1, source_target_pairs={{28,29},{30,31},{0,1},{2,3},{4,5},{6,7},{8,9},{10,11},{12,13},{14,... | collective-permute-start | bytes 294920 | tf_op jit(solution)/shard_map/ppermute | solution.py:510
  34.5 8.2 %collective-permute-start.11 = (f32[3,64,128]{2,1,0:T(8,128)S(1)}, f32[3,64,128]{2,1,0:T(8,128)S(1)}, u32[]{:S(2)}, u32[]{:S(2)}) collective-permute-start(f32[3,64,128]{2,1,0:T(8,128)S(1)} %get-tuple-element.69), channel_id=1, source_target_pairs={{29,30},{31,0},{1,2},{5,6},{7,8},{9,10},{13,14},{15,16},{17,18},{2... | collective-permute-start | bytes 294920 | tf_op jit(solution)/shard_map/ppermute | solution.py:510

commit v6 on v5

--- a/solution.py
+++ b/solution.py
@@ -133,52 +133,80 @@
             mass_ref[r] = weight_ref[r] * (along * float(WEIGHTS[i] * WEIGHTS[j]))
 
 
-def forward_k(source, carry_ref, weigh, table_ref, turned_ref, work):
-    slope = along_k(table_ref, source[...])
-    work[...] = carry_ref[2] * slope + along_k(turned_ref, weigh[...] * slope)
-
-
-def adjoint_k(source, carry_ref, weigh, table_ref, turned_ref, work):
-    slope = along_k(table_ref, source[...])
-    work[...] = along_k(turned_ref, carry_ref[2] * source[...] + weigh[...] * slope)
-
-
-def forward(source, carry_ref, weigh, work, target):
+def slope_k(source, table_ref, slope):
+    slope[...] = along_k(table_ref, source[...])
+
+
+def forward_k(carry_ref, weigh, turned_ref, slope, work):
+    work[...] = carry_ref[2] * slope[...] + along_k(turned_ref, weigh[...] * slope[...])
+
+
+def adjoint_k(source, carry_ref, weigh, turned_ref, slope, work):
+    work[...] = along_k(turned_ref, carry_ref[2] * source[...] + weigh[...] * slope[...])
+
+
+def forward_i(source, carry_ref, weigh, target):
     for j in range(8):
         slopes = line(DM, [source[rows(i, j)] for i in range(8)])
         back = line(DM.T, [weigh[rows(i, j)] * slopes[i] for i in range(8)])
         for i in range(8):
             r = rows(i, j)
-            target[r] = work[r] + (carry_ref[0, r] * slopes[i] + back[i])
+            target[r] = carry_ref[0, r] * slopes[i] + back[i]
+
+
+def forward_j(source, carry_ref, weigh, work, target):
     for i in range(8):
         slopes = line(DM, [source[rows(i, j)] for j in range(8)])
         back = line(DM.T, [weigh[rows(i, j)] * slopes[j] for j in range(8)])
         for j in range(8):
             r = rows(i, j)
-            target[r] = target[r] + (carry_ref[1, r] * slopes[j] + back[j])
-
-
-def adjoint(source, base, carry_ref, weigh, work, target):
-    for j in range(8):
-        values = [source[rows(i, j)] for i in range(8)]
+            target[r] = target[r] + (carry_ref[1, r] * slopes[j] + (back[j] + work[r]))
+
+
+def adjoint_lines(d, source, carry_ref, weigh, line_rows):
+    for these in line_rows:
+        values = [source[r] for r in these]
         slopes = line(DM, values)
-        fluxes = [
-            carry_ref[0, rows(i, j)] * values[i] + weigh[rows(i, j)] * slopes[i] for i in range(8)
-        ]
-        back = line(DM.T, fluxes)
-        for i in range(8):
-            r = rows(i, j)
-            target[r] = base[r] - (work[r] + back[i])
-    for i in range(8):
-        values = [source[rows(i, j)] for j in range(8)]
-        slopes = line(DM, values)
-        fluxes = [
-            carry_ref[1, rows(i, j)] * values[j] + weigh[rows(i, j)] * slopes[j] for j in range(8)
-        ]
-        back = line(DM.T, fluxes)
-        for j in range(8):
-            r = rows(i, j)
-            target[r] = target[r] - back[j]
+        fluxes = [carry_ref[d, r] * v + weigh[r] * g for r, v, g in zip(these, values, slopes)]
+        yield from zip(these, line(DM.T, fluxes))
+
+
+def adjoint_i(source, base, carry_ref, weigh, target):
+    lines = [[rows(i, j) for i in range(8)] for j in range(8)]
+    for r, back in adjoint_lines(0, source, carry_ref, weigh, lines):
+        target[r] = base[r] - back
+
+
+def adjoint_j(source, carry_ref, weigh, work, target):
+    lines = [[rows(i, j) for j in range(8)] for i in range(8)]
+    for r, back in adjoint_lines(1, source, carry_ref, weigh, lines):
+        target[r] = target[r] - (back + work[r])
+
+
+def forward(sources, carry_ref, weigh_ref, table_ref, turned_ref, slope_ref, work_ref, target, finish):
+    slope_k(sources.at[0], table_ref, slope_ref.at[0])
+    for f in range(3):
+        at = (carry_ref, weigh_ref.at[f])
+        forward_i(sources.at[f], *at, target.at[f])
+        forward_k(*at, turned_ref, slope_ref.at[f], work_ref.at[f])
+        if f < 2:
+            slope_k(sources.at[f + 1], table_ref, slope_ref.at[f + 1])
+        forward_j(sources.at[f], *at, work_ref.at[f], target.at[f])
+        finish(f)
+
+
+def adjoint(
+    sources, base, carry_ref, weigh_ref, table_ref, turned_ref, slope_ref, work_ref, target, finish
+):
+    slope_k(sources.at[0], table_ref, slope_ref.at[0])
+    for f in range(3):
+        at = (carry_ref, weigh_ref.at[f])
+        adjoint_i(sources.at[f], base.at[f], *at, target.at[f])
+        adjoint_k(sources.at[f], *at, turned_ref, slope_ref.at[f], work_ref.at[f])
+        if f < 2:
+            slope_k(sources.at[f + 1], table_ref, slope_ref.at[f + 1])
+        adjoint_j(sources.at[f], *at, work_ref.at[f], target.at[f])
+        finish(f)
 
 
 def join_heights(ref, index):
@@ -209,7 +237,7 @@
     for way in range(2):
         for i in range(8):
             r = pl.ds(pl.multiple_of(ends[1][way] * 8 + i * 64, 8), 8)
-            part = lanes(got[2 + way][c, pl.ds(i * 8, 8)], height)
+            part = lanes(got[3 - way][c, pl.ds(i * 8, 8)], height)
             ref[r] = ref[r] + (part * ends[2][1] if way else part)
 
 
@@ -312,31 +340,29 @@
     io_ref,
     je_ref,
     jo_ref,
+    slope_ref,
     work_ref,
 ):
     ends = ends_of(columns)
     index = index_of(index_ref)
     out = (ie_ref, io_ref, je_ref, jo_ref)
 
-    for f in range(3):
-        at = (carry_ref, weigh_ref.at[f])
-        forward_k(moment_ref.at[f], *at, table_ref, turned_ref, work_ref.at[f])
-    for f in range(3):
-        at = (carry_ref, weigh_ref.at[f])
-        forward(moment_ref.at[f], *at, work_ref.at[f], joined_ref.at[f])
+    def finish(f):
         join_heights(joined_ref.at[f], index)
         send_faces(f, joined_ref.at[f], index, ends, out)
 
-
-def edge_kernel(columns, ie_ref, io_ref, je_ref, jo_ref, out_e, out_o):
-    ends = ends_of(columns)
-    for way, (face, out) in enumerate(((je_ref, out_e), (jo_ref, out_o))):
-        out[...] = face[...]
-        r = pl.ds(pl.multiple_of(ends[1][way] * 8, 8), 8)
-        for other, got in enumerate((ie_ref, io_ref)):
-            w = pl.ds(pl.multiple_of(ends[0][other] * 8, 8), 8)
-            part = got[:, r]
-            out[:, w] = out[:, w] + (part * ends[2][0] if other else part)
+    at = (carry_ref, weigh_ref, table_ref, turned_ref, slope_ref, work_ref)
+    forward(moment_ref, *at, joined_ref, finish)
+
+
+def edge_kernel(columns, way, ie_ref, io_ref, face, *refs):
+    ends, out = ends_of(columns), refs[-1]
+    out[...] = face[...]
+    r = pl.ds(pl.multiple_of(ends[1][way] * 8, 8), 8)
+    for other, got in enumerate((ie_ref, io_ref)):
+        w = pl.ds(pl.multiple_of(ends[0][other] * 8, 8), 8)
+        part = got[:, r]
+        out[:, w] = out[:, w] + (part * ends[2][0] if other else part)
 
 
 def state_kernel(
@@ -355,31 +381,31 @@
     index = index_of(index_ref)
     if first:
         got, (inverse_ref, state_out, joined_out), refs = refs[:4], refs[4:7], refs[7:]
-        out, (work_ref, hold_ref) = refs[:4], refs[4:]
+        out, (slope_ref, work_ref, hold_ref) = refs[:4], refs[4:]
         held = hold_ref.at[0]
         held[...] = joined_ref[3]
         add_faces(3, held, index, ends, got)
         inverse_ref[...] = 1.0 / held[...]
     else:
         inverse_ref, *got = refs[:5]
-        state_far, work_ref, hold_ref, state_out, sent = refs[5:]
-
+        state_far, token_ref, slope_ref, work_ref, hold_ref, state_out, sent = refs[5:]
+        token_ref[...] = jnp.zeros_like(token_ref)
     for f in range(3):
         held = hold_ref.at[f]
         held[...] = joined_ref[f]
         add_faces(f, held, index, ends, got)
         held[...] = held[...] * inverse_ref[...]
-        at = (carry_ref, weigh_ref.at[f])
-        adjoint_k(held, *at, table_ref, turned_ref, work_ref.at[f])
-    for f in range(3):
-        at = (carry_ref, weigh_ref.at[f])
-        adjoint(hold_ref.at[f], state_ref.at[f], *at, work_ref.at[f], state_out.at[f])
+
+    def finish(f):
         if first:
             joined_out[f] = state_out[f]
             join_heights(joined_out.at[f], index)
             send_faces(f, joined_out.at[f], index, ends, out)
         else:
             send_out(f, state_out, state_far, sent).start()
+
+    at = (carry_ref, weigh_ref, table_ref, turned_ref, slope_ref, work_ref)
+    adjoint(hold_ref, state_ref, *at, state_out, finish)
     if not first:
         for f in range(3):
             send_out(f, state_out, state_far, sent).wait()
@@ -408,31 +434,31 @@
     joined_ref,
     gie_ref,
     gio_ref,
+    gjo_ref,
     gje_ref,
-    gjo_ref,
     moment_out,
     joined_out,
     ie_ref,
     io_ref,
     je_ref,
     jo_ref,
+    slope_ref,
     work_ref,
     hold_ref,
 ):
     ends = ends_of(columns)
     index = index_of(index_ref)
     out = (ie_ref, io_ref, je_ref, jo_ref)
-    got = (gie_ref, gio_ref, gje_ref, gjo_ref)
-
+    got = (gie_ref, gio_ref, gjo_ref, gje_ref)
     for f in range(3):
         moment_step(f, ends, index, moment_ref, joined_ref, inverse_ref, got, hold_ref, moment_out)
-        at = (carry_ref, weigh_ref.at[f])
-        forward_k(moment_out.at[f], *at, table_ref, turned_ref, work_ref.at[f])
-    for f in range(3):
-        at = (carry_ref, weigh_ref.at[f])
-        forward(moment_out.at[f], *at, work_ref.at[f], joined_out.at[f])
+
+    def finish(f):
         join_heights(joined_out.at[f], index)
         send_faces(f, joined_out.at[f], index, ends, out)
+
+    at = (carry_ref, weigh_ref, table_ref, turned_ref, slope_ref, work_ref)
+    forward(moment_out, *at, joined_out, finish)
 
 
 def last_kernel(
@@ -443,8 +469,8 @@
     joined_ref,
     gie_ref,
     gio_ref,
+    gjo_ref,
     gje_ref,
-    gjo_ref,
     moment_far,
     hold_ref,
     moment_out,
@@ -452,7 +478,7 @@
 ):
     ends = ends_of(columns)
     index = index_of(index_ref)
-    got = (gie_ref, gio_ref, gje_ref, gjo_ref)
+    got = (gie_ref, gio_ref, gjo_ref, gje_ref)
 
     for f in range(3):
         moment_step(f, ends, index, moment_ref, joined_ref, inverse_ref, got, hold_ref, moment_out)
@@ -465,13 +491,13 @@
 FAR = pl.BlockSpec(memory_space=pltpu.HBM)
 
 
-def call(kernel, specs, shapes, scratch, flops, *operands, out=VMEM):
+def call(kernel, specs, shapes, scratch, flops, *operands, first_out=VMEM):
     moved = sum(o.size * 4 for o in operands) + sum(int(np.prod(s)) * 4 for s, _ in shapes)
     return pl.pallas_call(
         kernel,
         out_shape=[jax.ShapeDtypeStruct(s, t) for s, t in shapes],
         in_specs=specs,
-        out_specs=[out] * len(shapes),
+        out_specs=[first_out] + [VMEM] * (len(shapes) - 1),
         scratch_shapes=scratch,
         compiler_params=pltpu.CompilerParams(vmem_limit_bytes=32 * 1024 * 1024),
         cost_estimate=pl.CostEstimate(flops=flops, bytes_accessed=moved, transcendentals=0),
@@ -506,21 +532,37 @@
     whole, block = ((3, 512, 128), F32), ((512, 128), F32)
     work = pltpu.VMEM((3, 512, 128), F32)
 
-    def exchange(blocks, pairs):
-        return [lax.ppermute(b, "elem", p) for b, p in zip(blocks, pairs)]
-
-    def meet(count, faces):
-        got_i = exchange(faces[:2], along_i)
-        faces_j = call(
-            functools.partial(edge_kernel, columns),
-            [VMEM] * 4,
-            [((count, 64, 128), F32)] * 2,
+    def exchange(block, pairs):
+        return lax.ppermute(block, "elem", pairs)
+
+    def settle(block, *after):
+        anywhere = pl.BlockSpec(memory_space=pl.ANY)
+        return pl.pallas_call(
+            lambda *refs: None,
+            out_shape=jax.ShapeDtypeStruct(block.shape, block.dtype),
+            in_specs=[anywhere] * (1 + len(after)),
+            out_specs=anywhere,
+            input_output_aliases={0: 0},
+        )(block, *after)
+
+    def edge(count, way, *operands):
+        return call(
+            functools.partial(edge_kernel, columns, way),
+            [VMEM] * len(operands),
+            [((count, 64, 128), F32)],
             [],
             count * 64 * 128,
-            *got_i,
-            *faces[2:],
-        )
-        return got_i + exchange(faces_j[::-1], along_j[::-1])[::-1]
+            *operands,
+        )[0]
+
+    def meet(count, faces):
+        got_i = [exchange(faces[way], along_i[way]) for way in range(2)]
+        far_face = edge(count, 1, *got_i, faces[3])
+        near_face = edge(count, 0, *got_i, faces[2], far_face)
+        return got_i + [exchange(far_face, along_j[1]), exchange(near_face, along_j[0])]
+
+    def settled(got, *after):
+        return got[:2] + [settle(got[2], *after), got[3]]
 
     def far(array):
         return pltpu.with_memory_space_constraint(array, pltpu.HBM)
@@ -553,7 +595,7 @@
         functools.partial(moment_kernel, columns),
         [VMEM] * 6,
         [whole] + faces_shape(3),
-        [work],
+        [work] * 2,
         20_000_000,
         moment,
         *tables,
@@ -563,39 +605,39 @@
         functools.partial(state_kernel, columns, True),
         [VMEM] * 11,
         [block, whole, whole] + faces_shape(3),
-        [work] * 2,
+        [work] * 3,
         20_000_000,
         state,
         *tables,
         joined_state,
-        *got_state,
+        *settled(got_state),
     )
     got_state = meet(3, faces_state)
     moment, joined_moment, *faces_moment = call(
         functools.partial(middle_kernel, columns),
         [VMEM] * 12,
         [whole, whole] + faces_shape(3),
-        [work] * 2,
+        [work] * 3,
         20_000_000,
         moment,
         *tables,
         inverse,
         joined_moment,
-        *got_moment,
+        *settled(got_moment, inverse),
     )
     got_moment = meet(3, faces_moment)
-    (state,) = call(
+    state, token = call(
         functools.partial(state_kernel, columns, False),
         [VMEM] * 12,
-        [whole],
-        [work] * 3 + [pltpu.SemaphoreType.DMA((3,))],
+        [whole, ((8, 128), F32)],
+        [work] * 4 + [pltpu.SemaphoreType.DMA((3,))],
         20_000_000,
         state,
         *tables,
         joined_state,
         inverse,
-        *got_state,
-        out=FAR,
+        *settled(got_state),
+        first_out=FAR,
     )
     (moment,) = call(
         functools.partial(last_kernel, columns),
@@ -607,8 +649,8 @@
         index,
         inverse,
         joined_moment,
-        *got_moment,
-        out=FAR,
+        *settled(got_moment, token),
+        first_out=FAR,
     )
     return moment, state
 

time: 44 us -> 65.4 us (1.49)
  local copies, waits for them, and re-layouts: 0 us -> 17.3 us
  Pallas kernels: 12.3 us -> 20.8 us
  starting transfers between devices: 30.6 us -> 24.7 us
  waiting for transfers between devices: 0.13 us -> 1.05 us
    unnamed x0 -> x54, local copies, waits for them, and re-layouts: none -> 17.3 us
    pallas_call x10 -> x14, Pallas kernels: 12.3 us -> 20.8 us  [call(): pl.pallas_call(kernel, out_shape=[jax.ShapeDtypeStruct(s, t) for s, t in...]
    ppermute x16, starting transfers between devices: 30.6 us -> 24.7 us  [exchange(): return lax.ppermute(block, 'elem', pairs)]
    ppermute x16, waiting for transfers between devices: 0.13 us -> 1.05 us  [exchange(): return lax.ppermute(block, 'elem', pairs)]
  transfers between devices with their start and end apart: 16 -> 16, of which waited for: 1 -> 1; matrix products, arithmetic and copies ran while one was open for 0% -> 0% of each run, Pallas kernels for 21% -> 27%
where the time goes in v6:
time: 65.4 us; the launch traced here: 64.7 us
  starting transfers between devices  24.7 us (38%)
  Pallas kernels  20.8 us (32%)
  local copies, waits for them, and re-layouts  17.3 us (26%)
  waiting for transfers between devices  1.05 us (2%)
  between operations  0.86 us (1%)
    ppermute x16, starting transfers between devices, exchange(): return lax.ppermute(block, 'elem', pairs)  24.7 us
    pallas_call x14, Pallas kernels, call(): pl.pallas_call(kernel, out_shape=[jax.ShapeDtypeStruct(s, t) for s, t in...  20.8 us
    unnamed x54, local copies, waits for them, and re-layouts  17.3 us
  transfers between devices with their start and end apart: 16, of which 1 were waited for; matrix products, arithmetic and copies ran while one was open for 0% of the time, Pallas kernels for 27%

profile of v6, /device:TPU:0, one launch (start us, length us, event | category | flops | bytes accessed | tf_op | source)
XLA Modules:
  0.0 64.7 jit_solution(12522540333314408391)
XLA Ops:
  0.6 2.0 %shard_map.77 = (f32[3,512,128]{2,1,0:T(8,128)S(1)}, f32[3,512,128]{2,1,0:T(8,128)S(1)}, f32[3,512,128]{2,1,0:T(8,128)S(1)}, f32[3,512,128]{2,1,0:T(8,128)S(1)},...) custom-call(f32[3,512,128]{2,1,0:T(8,128)} %moment_far.1, ...), custom_call_target="tpu_custom_call" | custom-call | flops 1000000 | bytes 8929804 | tf_op jit(solution)/shard_map/pallas_call | solution.py:496
  2.7 1.0 %copy-done.2 = f32[4,512,128]{2,1,0:T(8,128)} copy-done((f32[4,512,128]{2,1,0:T(8,128)}, f32[4,512,128]{2,1,0:T(8,128)S(1)}, u32[]{:S(2)}) %copy-start.2) | copy-done | bytes 1048600
  3.7 3.0 %collective-permute-start = (f32[4,64,128]{2,1,0:T(8,128)S(1)}, f32[4,64,128]{2,1,0:T(8,128)S(1)}, u32[]{:S(2)}, u32[]{:S(2)}) collective-permute-start(f32[4,64,128]{2,1,0:T(8,128)S(1)} %get-tuple-element.42), channel_id=1, source_target_pairs={{28,4},{29,5},{30,6},{31,7},{0,8},{1,9},{2,10},{3,11},{12,20},{13,... | collective-permute-start | bytes 393224 | tf_op jit(solution)/shard_map/ppermute | solution.py:536
  6.7 0.0 collective-permute-start.1
  6.7 2.1 %shard_map.82 = (f32[3,512,128]{2,1,0:T(8,128)S(1)}, f32[3,64,128]{2,1,0:T(8,128)S(1)}, f32[3,64,128]{2,1,0:T(8,128)S(1)}, f32[3,64,128]{2,1,0:T(8,128)S(1)}, f32[3,64,128]{2,1,0:T(8,128)S(1)}) custom-call(f32[3,512,128]{2,1,0:T(8,128)S(1)} %get-tuple-element.34.moment_ref, f32[3,512,128]{2,1,0:T(8,128)S(1)} %get-tuple-element.35.carry_ref, ...), custom_call_target="tpu_custom_call" | custom-call | flops 20000000 | bytes 5128192 | tf_op jit(solution)/shard_map/pallas_call | solution.py:496
  8.8 0.0 copy-start.10
  8.8 3.2 %collective-permute-start.4 = (f32[3,64,128]{2,1,0:T(8,128)S(1)}, f32[3,64,128]{2,1,0:T(8,128)S(1)}, u32[]{:S(2)}, u32[]{:S(2)}) collective-permute-start(f32[3,64,128]{2,1,0:T(8,128)S(1)} %get-tuple-element.48), channel_id=1, source_target_pairs={{28,4},{29,5},{30,6},{31,7},{0,8},{1,9},{2,10},{3,11},{12,20},{13,... | collective-permute-start | bytes 294920 | tf_op jit(solution)/shard_map/ppermute | solution.py:536
  12.0 0.0 collective-permute-start.5
  12.0 0.0 collective-permute-done.ie_ref.refs_0_
  12.1 4.8 %collective-permute-start.2 = (f32[4,64,128]{2,1,0:T(8,128)S(1)}, f32[4,64,128]{2,1,0:T(8,128)}, u32[]{:S(2)}, u32[]{:S(2)}) collective-permute-start(f32[4,64,128]{2,1,0:T(8,128)S(1)} %shard_map.78.refs_0_), channel_id=1, source_target_pairs={{29,30},{31,0},{1,2},{5,6},{7,8},{9,10},{13,14},{15,16},{17,18},{2... | collective-permute-start | bytes 393224 | tf_op jit(solution)/shard_map/ppermute | solution.py:536
  16.9 0.7 %shard_map.80 = f32[4,64,128]{2,1,0:T(8,128)} custom-call(f32[4,64,128]{2,1,0:T(8,128)S(1)} %collective-permute-done.ie_ref.refs_0_, f32[4,64,128]{2,1,0:T(8,128)S(1)} %collective-permute-done.1.io_ref.refs_1_, f32[4,64,128]{2,1,0:T(8,128)S(1)} %get-tuple-element.45.face, f32[4,64,128]{2,1,0:T(8,128)S(1)} %shard_map.78.refs_0_), custom_call_target="tpu_custom_call" | custom-call | flops 32768 | bytes 655360 | tf_op jit(solution)/shard_map/pallas_call | solution.py:496
  17.6 0.7 %shard_map.83.refs_0_ = f32[3,64,128]{2,1,0:T(8,128)} custom-call(f32[3,64,128]{2,1,0:T(8,128)S(1)} %collective-permute-done.4.ie_ref.gie_ref, f32[3,64,128]{2,1,0:T(8,128)S(1)} %collective-permute-done.5.io_ref.gio_ref, f32[3,64,128]{2,1,0:T(8,128)S(1)} %get-tuple-element.50.face), custom_call_target="tpu_custom_call" | custom-call | flops 24576 | bytes 393216 | tf_op jit(solution)/shard_map/pallas_call | solution.py:496
  18.2 3.4 %collective-permute-start.6 = (f32[3,64,128]{2,1,0:T(8,128)}, f32[3,64,128]{2,1,0:T(8,128)}, u32[]{:S(2)}, u32[]{:S(2)}) collective-permute-start(f32[3,64,128]{2,1,0:T(8,128)} %shard_map.83.refs_0_), channel_id=1, source_target_pairs={{29,30},{31,0},{1,2},{5,6},{7,8},{9,10},{13,14},{15,16},{17,18},{2... | collective-permute-start | bytes 294920 | tf_op jit(solution)/shard_map/ppermute | solution.py:536
  21.6 1.6 %shard_map.85 = f32[3,64,128]{2,1,0:T(8,128)} custom-call(f32[3,64,128]{2,1,0:T(8,128)S(1)} %collective-permute-done.4.ie_ref.gie_ref, f32[3,64,128]{2,1,0:T(8,128)S(1)} %collective-permute-done.5.io_ref.gio_ref, f32[3,64,128]{2,1,0:T(8,128)S(1)} %get-tuple-element.51.face, f32[3,64,128]{2,1,0:T(8,128)} %shard_map.83.refs_0_), custom_call_target="tpu_custom_call" | custom-call | flops 24576 | bytes 491520 | tf_op jit(solution)/shard_map/pallas_call | solution.py:496
  23.2 1.2 %copy-done.3 = f32[4,512,128]{2,1,0:T(8,128)S(1)} copy-done((f32[4,512,128]{2,1,0:T(8,128)S(1)}, f32[4,512,128]{2,1,0:T(8,128)}, u32[]{:S(2)}) %copy-start.3) | copy-done | bytes 1048600
  24.4 1.1 %copy-done.13 = f32[3,512,128]{2,1,0:T(8,128)S(1)} copy-done((f32[3,512,128]{2,1,0:T(8,128)S(1)}, f32[3,512,128]{2,1,0:T(8,128)}, u32[]{:S(2)}) %copy-start.13) | copy-done | bytes 786456
  25.6 3.9 %shard_map.81 = (f32[512,128]{1,0:T(8,128)S(1)}, f32[3,512,128]{2,1,0:T(8,128)S(1)}, f32[3,512,128]{2,1,0:T(8,128)S(1)}, f32[3,64,128]{2,1,0:T(8,128)}, f32[3,64...) custom-call(f32[3,512,128]{2,1,0:T(8,128)S(1)} %copy-done.13, ...), custom_call_target="tpu_custom_call" | custom-call | flops 20000000 | bytes 7749632 | tf_op jit(solution)/shard_map/pallas_call | solution.py:496
  29.5 0.7 %copy-done = f32[512,128]{1,0:T(8,128)} copy-done((f32[512,128]{1,0:T(8,128)}, f32[512,128]{1,0:T(8,128)S(1)}, u32[]{:S(2)}) %copy-start) | copy-done | bytes 262168
  30.2 0.9 %copy-done.6 = f32[3,512,128]{2,1,0:T(8,128)} copy-done((f32[3,512,128]{2,1,0:T(8,128)}, f32[3,512,128]{2,1,0:T(8,128)S(1)}, u32[]{:S(2)}) %copy-start.6) | copy-done | bytes 786456
  31.1 0.9 %copy-done.8 = f32[3,512,128]{2,1,0:T(8,128)} copy-done((f32[3,512,128]{2,1,0:T(8,128)}, f32[3,512,128]{2,1,0:T(8,128)S(1)}, u32[]{:S(2)}) %copy-start.8) | copy-done | bytes 786456
  32.0 0.6 copy-done.22
  32.6 0.6 copy-done.24
  33.3 3.4 %collective-permute-start.11 = (f32[3,64,128]{2,1,0:T(8,128)}, f32[3,64,128]{2,1,0:T(8,128)}, u32[]{:S(2)}, u32[]{:S(2)}) collective-permute-start(f32[3,64,128]{2,1,0:T(8,128)} %get-tuple-element.59), channel_id=1, source_target_pairs={{28,4},{29,5},{30,6},{31,7},{0,8},{1,9},{2,10},{3,11},{12,20},{13,... | collective-permute-start | bytes 294920 | tf_op jit(solution)/shard_map/ppermute | solution.py:536
  36.7 0.2 collective-permute-start.12
  37.0 0.9 %copy-done.5 = f32[3,64,128]{2,1,0:T(8,128)S(1)} copy-done((f32[3,64,128]{2,1,0:T(8,128)S(1)}, f32[3,64,128]{2,1,0:T(8,128)}, u32[]{:S(2)}) %copy-start.5) | copy-done | bytes 98328
  37.8 1.1 %copy-done.11 = f32[3,512,128]{2,1,0:T(8,128)S(1)} copy-done((f32[3,512,128]{2,1,0:T(8,128)S(1)}, f32[3,512,128]{2,1,0:T(8,128)}, u32[]{:S(2)}) %copy-start.11) | copy-done | bytes 786456
  39.0 3.0 %shard_map.86 = (f32[3,512,128]{2,1,0:T(8,128)S(1)}, f32[3,512,128]{2,1,0:T(8,128)S(1)}, f32[3,64,128]{2,1,0:T(8,128)S(1)}, f32[3,64,128]{2,1,0:T(8,128)S(1)}, f...) custom-call(f32[3,512,128]{2,1,0:T(8,128)S(1)} %get-tuple-element.34.moment_ref, ...), custom_call_target="tpu_custom_call" | custom-call | flops 20000000 | bytes 7356416 | tf_op jit(solution)/shard_map/pallas_call | solution.py:496
  42.0 0.0 copy-start.14
  42.0 0.8 %collective-permute-start.8 = (f32[3,64,128]{2,1,0:T(8,128)S(1)}, f32[3,64,128]{2,1,0:T(8,128)S(1)}, u32[]{:S(2)}, u32[]{:S(2)}) collective-permute-start(f32[3,64,128]{2,1,0:T(8,128)S(1)} %get-tuple-element.54), channel_id=1, source_target_pairs={{28,4},{29,5},{30,6},{31,7},{0,8},{1,9},{2,10},{3,11},{12,20},{13,... | collective-permute-start | bytes 294920 | tf_op jit(solution)/shard_map/ppermute | solution.py:536
  42.8 0.2 collective-permute-start.9
  43.0 1.0 %shard_map.88.refs_0_ = f32[3,64,128]{2,1,0:T(8,128)S(1)} custom-call(f32[3,64,128]{2,1,0:T(8,128)} %collective-permute-done.11.ie_ref.refs_1_, f32[3,64,128]{2,1,0:T(8,128)} %collective-permute-done.12.io_ref.refs_2_, f32[3,64,128]{2,1,0:T(8,128)S(1)} %copy-done.23), custom_call_target="tpu_custom_call" | custom-call | flops 24576 | bytes 393216 | tf_op jit(solution)/shard_map/pallas_call | solution.py:496
  44.0 2.5 %collective-permute-start.13 = (f32[3,64,128]{2,1,0:T(8,128)S(1)}, f32[3,64,128]{2,1,0:T(8,128)S(1)}, u32[]{:S(2)}, u32[]{:S(2)}) collective-permute-start(f32[3,64,128]{2,1,0:T(8,128)S(1)} %shard_map.88.refs_0_), channel_id=1, source_target_pairs={{29,30},{31,0},{1,2},{5,6},{7,8},{9,10},{13,14},{15,16},{17,18},{2... | collective-permute-start | bytes 294920 | tf_op jit(solution)/shard_map/ppermute | solution.py:536
  46.5 1.0 %shard_map.90 = f32[3,64,128]{2,1,0:T(8,128)S(1)} custom-call(f32[3,64,128]{2,1,0:T(8,128)} %collective-permute-done.11.ie_ref.refs_1_, f32[3,64,128]{2,1,0:T(8,128)} %collective-permute-done.12.io_ref.refs_2_, f32[3,64,128]{2,1,0:T(8,128)S(1)} %copy-done.25, f32[3,64,128]{2,1,0:T(8,128)S(1)} %shard_map.88.refs_0_), custom_call_target="tpu_custom_call" | custom-call | flops 24576 | bytes 491520 | tf_op jit(solution)/shard_map/pallas_call | solution.py:496
  47.5 0.1 collective-permute-start.14
  47.6 3.0 %collective-permute-start.10 = (f32[3,64,128]{2,1,0:T(8,128)S(1)}, f32[3,64,128]{2,1,0:T(8,128)S(1)}, u32[]{:S(2)}, u32[]{:S(2)}) collective-permute-start(f32[3,64,128]{2,1,0:T(8,128)S(1)} %shard_map.87.refs_0_), channel_id=1, source_target_pairs={{29,30},{31,0},{1,2},{5,6},{7,8},{9,10},{13,14},{15,16},{17,18},{2... | collective-permute-start | bytes 294920 | tf_op jit(solution)/shard_map/ppermute | solution.py:536
  50.7 0.1 collective-permute-start.15
  50.7 1.0 %collective-permute-done.13.refs_0_ = f32[3,64,128]{2,1,0:T(8,128)S(1)} collective-permute-done((f32[3,64,128]{2,1,0:T(8,128)S(1)}, f32[3,64,128]{2,1,0:T(8,128)S(1)}, u32[]{:S(2)}, u32[]{:S(2)}) %collective-permute-start.13) | collective-permute-done | bytes 98336 | tf_op jit(solution)/shard_map/ppermute | solution.py:536
  51.8 0.6 copy-done.20
  52.4 1.1 %copy-done.7 = f32[3,512,128]{2,1,0:T(8,128)S(1)} copy-done((f32[3,512,128]{2,1,0:T(8,128)S(1)}, f32[3,512,128]{2,1,0:T(8,128)}, u32[]{:S(2)}) %copy-start.7) | copy-done | bytes 786456
  53.5 1.1 %copy-done.9 = f32[3,512,128]{2,1,0:T(8,128)S(1)} copy-done((f32[3,512,128]{2,1,0:T(8,128)S(1)}, f32[3,512,128]{2,1,0:T(8,128)}, u32[]{:S(2)}) %copy-start.9) | copy-done | bytes 786456
  54.7 0.9 %copy-done.21 = f32[3,64,128]{2,1,0:T(8,128)S(1)} copy-done((f32[3,64,128]{2,1,0:T(8,128)S(1)}, f32[3,64,128]{2,1,0:T(8,128)}, u32[]{:S(2)}) %copy-start.21) | copy-done | bytes 98328
  55.6 3.7 %shard_map.91 = (f32[3,512,128]{2,1,0:T(8,128)}, f32[8,128]{1,0:T(8,128)S(1)}) custom-call(f32[3,512,128]{2,1,0:T(8,128)S(1)} %copy-done.7, f32[3,512,128]{2,1,0:T(8,128)S(1)} %get-tuple-element.35.carry_ref, f32[3,512,128]{2,1,0:T(8,128)S(1)} %get-tuple-element.36.weigh_ref, bf16[256,768]{1,0:T(8,128)(2,1)S(1)} %get-tuple-element.37.table_ref, ...), custom_call_target="tpu_custom_call" | custom-call | flops 20000000 | bytes 6180864 | tf_op jit(solution)/shard_map/pallas_call | solution.py:496
  59.2 0.6 copy-done.26
  59.8 0.6 copy-done.18
  60.5 1.1 %copy-done.15 = f32[3,512,128]{2,1,0:T(8,128)S(1)} copy-done((f32[3,512,128]{2,1,0:T(8,128)S(1)}, f32[3,512,128]{2,1,0:T(8,128)}, u32[]{:S(2)}) %copy-start.15) | copy-done | bytes 786456
  61.6 1.1 %copy-done.17 = f32[3,512,128]{2,1,0:T(8,128)S(1)} copy-done((f32[3,512,128]{2,1,0:T(8,128)S(1)}, f32[3,512,128]{2,1,0:T(8,128)}, u32[]{:S(2)}) %copy-start.17) | copy-done | bytes 786456
  62.7 0.9 %copy-done.19 = f32[3,64,128]{2,1,0:T(8,128)S(1)} copy-done((f32[3,64,128]{2,1,0:T(8,128)S(1)}, f32[3,64,128]{2,1,0:T(8,128)}, u32[]{:S(2)}) %copy-start.19) | copy-done | bytes 98328
  63.6 1.1 %shard_map.94 = f32[3,512,128]{2,1,0:T(8,128)} custom-call(f32[3,512,128]{2,1,0:T(8,128)S(1)} %copy-done.15, s32[4,8,128]{2,1,0:T(8,128)S(1)} %get-tuple-element.39.index_ref, f32[512,128]{1,0:T(8,128)S(1)} %copy-done.1, f32[3,512,128]{2,1,0:T(8,128)S(1)} %copy-done.17, f32[3,64,128]{2,1,0:T(8,128)S(1)} %collective-permute-done.8.ie_ref.gie_ref, ...), custom_call_target="tpu_custom_call" | custom-call | flops 1000000 | bytes 3031040 | tf_op jit(solution)/shard_map/pallas_call | solution.py:496
  (56 shorter events, 0.2 us)
Async XLA Ops:
  2.6 1.0 %copy-start.2 = (f32[4,512,128]{2,1,0:T(8,128)}, f32[4,512,128]{2,1,0:T(8,128)S(1)}, u32[]{:S(2)}) copy-start(f32[4,512,128]{2,1,0:T(8,128)S(1)} %get-tuple-element.41.joined_ref) | copy-start | bytes 3145732
  3.7 5.2 %copy-start.12 = (f32[3,512,128]{2,1,0:T(8,128)}, f32[3,512,128]{2,1,0:T(8,128)S(1)}, u32[]{:S(2)}) copy-start(f32[3,512,128]{2,1,0:T(8,128)S(1)} %get-tuple-element.40.state_ref) | copy-start | bytes 2359300
  3.7 8.4 %collective-permute-start = (f32[4,64,128]{2,1,0:T(8,128)S(1)}, f32[4,64,128]{2,1,0:T(8,128)S(1)}, u32[]{:S(2)}, u32[]{:S(2)}) collective-permute-start(f32[4,64,128]{2,1,0:T(8,128)S(1)} %get-tuple-element.42), channel_id=1, source_target_pairs={{28,4},{29,5},{30,6},{31,7},{0,8},{1,9},{2,10},{3,11},{12,20},{13,... | collective-permute-start | bytes 393224 | tf_op jit(solution)/shard_map/ppermute | solution.py:536
  6.7 5.4 %collective-permute-start.1 = (f32[4,64,128]{2,1,0:T(8,128)S(1)}, f32[4,64,128]{2,1,0:T(8,128)S(1)}, u32[]{:S(2)}, u32[]{:S(2)}) collective-permute-start(f32[4,64,128]{2,1,0:T(8,128)S(1)} %get-tuple-element.43), channel_id=1, source_target_pairs={{4,12},{5,13},{6,14},{7,15},{8,16},{9,17},{10,18},{11,19},{28,29},... | collective-permute-start | bytes 393224 | tf_op jit(solution)/shard_map/ppermute | solution.py:536
  8.8 9.4 %copy-start.10 = (f32[3,512,128]{2,1,0:T(8,128)}, f32[3,512,128]{2,1,0:T(8,128)S(1)}, u32[]{:S(2)}) copy-start(f32[3,512,128]{2,1,0:T(8,128)S(1)} %get-tuple-element.47.joined_ref) | copy-start | bytes 2359300
  8.8 8.7 %collective-permute-start.4 = (f32[3,64,128]{2,1,0:T(8,128)S(1)}, f32[3,64,128]{2,1,0:T(8,128)S(1)}, u32[]{:S(2)}, u32[]{:S(2)}) collective-permute-start(f32[3,64,128]{2,1,0:T(8,128)S(1)} %get-tuple-element.48), channel_id=1, source_target_pairs={{28,4},{29,5},{30,6},{31,7},{0,8},{1,9},{2,10},{3,11},{12,20},{13,... | collective-permute-start | bytes 294920 | tf_op jit(solution)/shard_map/ppermute | solution.py:536
  12.0 5.5 %collective-permute-start.5 = (f32[3,64,128]{2,1,0:T(8,128)S(1)}, f32[3,64,128]{2,1,0:T(8,128)S(1)}, u32[]{:S(2)}, u32[]{:S(2)}) collective-permute-start(f32[3,64,128]{2,1,0:T(8,128)S(1)} %get-tuple-element.49), channel_id=1, source_target_pairs={{4,12},{5,13},{6,14},{7,15},{8,16},{9,17},{10,18},{11,19},{28,29},... | collective-permute-start | bytes 294920 | tf_op jit(solution)/shard_map/ppermute | solution.py:536
  12.1 11.1 %collective-permute-start.2 = (f32[4,64,128]{2,1,0:T(8,128)S(1)}, f32[4,64,128]{2,1,0:T(8,128)}, u32[]{:S(2)}, u32[]{:S(2)}) collective-permute-start(f32[4,64,128]{2,1,0:T(8,128)S(1)} %shard_map.78.refs_0_), channel_id=1, source_target_pairs={{29,30},{31,0},{1,2},{5,6},{7,8},{9,10},{13,14},{15,16},{17,18},{2... | collective-permute-start | bytes 393224 | tf_op jit(solution)/shard_map/ppermute | solution.py:536
  17.5 5.7 %collective-permute-start.3 = (f32[4,64,128]{2,1,0:T(8,128)}, f32[4,64,128]{2,1,0:T(8,128)}, u32[]{:S(2)}, u32[]{:S(2)}) collective-permute-start(f32[4,64,128]{2,1,0:T(8,128)} %shard_map.80), channel_id=1, source_target_pairs={{28,29},{30,31},{0,1},{2,3},{4,5},{6,7},{8,9},{10,11},{12,13},{14,... | collective-permute-start | bytes 393224 | tf_op jit(solution)/shard_map/ppermute | solution.py:536
  17.5 4.1 %copy-start.4 = (f32[3,64,128]{2,1,0:T(8,128)}, f32[3,64,128]{2,1,0:T(8,128)S(1)}, u32[]{:S(2)}) copy-start(f32[3,64,128]{2,1,0:T(8,128)S(1)} %collective-permute-done.5.io_ref.gio_ref) | copy-start | bytes 294916
  18.2 18.7 %collective-permute-start.6 = (f32[3,64,128]{2,1,0:T(8,128)}, f32[3,64,128]{2,1,0:T(8,128)}, u32[]{:S(2)}, u32[]{:S(2)}) collective-permute-start(f32[3,64,128]{2,1,0:T(8,128)} %shard_map.83.refs_0_), channel_id=1, source_target_pairs={{29,30},{31,0},{1,2},{5,6},{7,8},{9,10},{13,14},{15,16},{17,18},{2... | collective-permute-start | bytes 294920 | tf_op jit(solution)/shard_map/ppermute | solution.py:536
  23.2 13.8 %collective-permute-start.7 = (f32[3,64,128]{2,1,0:T(8,128)}, f32[3,64,128]{2,1,0:T(8,128)}, u32[]{:S(2)}, u32[]{:S(2)}) collective-permute-start(f32[3,64,128]{2,1,0:T(8,128)} %shard_map.85), channel_id=1, source_target_pairs={{28,29},{30,31},{0,1},{2,3},{4,5},{6,7},{8,9},{10,11},{12,13},{14,... | collective-permute-start | bytes 294920 | tf_op jit(solution)/shard_map/ppermute | solution.py:536
  23.2 1.2 %copy-start.3 = (f32[4,512,128]{2,1,0:T(8,128)S(1)}, f32[4,512,128]{2,1,0:T(8,128)}, u32[]{:S(2)}) copy-start(f32[4,512,128]{2,1,0:T(8,128)} %copy-done.2) | copy-start | bytes 3145732
  24.4 1.1 %copy-start.13 = (f32[3,512,128]{2,1,0:T(8,128)S(1)}, f32[3,512,128]{2,1,0:T(8,128)}, u32[]{:S(2)}) copy-start(f32[3,512,128]{2,1,0:T(8,128)} %copy-done.12) | copy-start | bytes 2359300
  29.5 0.7 %copy-start = (f32[512,128]{1,0:T(8,128)}, f32[512,128]{1,0:T(8,128)S(1)}, u32[]{:S(2)}) copy-start(f32[512,128]{1,0:T(8,128)S(1)} %get-tuple-element.46.refs_1_.inverse_ref.refs_0_) | copy-start | bytes 786436
  30.2 0.9 %copy-start.6 = (f32[3,512,128]{2,1,0:T(8,128)}, f32[3,512,128]{2,1,0:T(8,128)S(1)}, u32[]{:S(2)}) copy-start(f32[3,512,128]{2,1,0:T(8,128)S(1)} %get-tuple-element.57.state_ref) | copy-start | bytes 2359300
  31.1 0.9 %copy-start.8 = (f32[3,512,128]{2,1,0:T(8,128)}, f32[3,512,128]{2,1,0:T(8,128)S(1)}, u32[]{:S(2)}) copy-start(f32[3,512,128]{2,1,0:T(8,128)S(1)} %get-tuple-element.58.joined_ref) | copy-start | bytes 2359300
  32.0 0.6 copy-start.22
  32.6 0.6 copy-start.24
  33.3 3.7 %copy-start.1 = (f32[512,128]{1,0:T(8,128)S(1)}, f32[512,128]{1,0:T(8,128)}, u32[]{:S(2)}) copy-start(f32[512,128]{1,0:T(8,128)} %copy-done) | copy-start | bytes 786436
  33.3 9.8 %collective-permute-start.11 = (f32[3,64,128]{2,1,0:T(8,128)}, f32[3,64,128]{2,1,0:T(8,128)}, u32[]{:S(2)}, u32[]{:S(2)}) collective-permute-start(f32[3,64,128]{2,1,0:T(8,128)} %get-tuple-element.59), channel_id=1, source_target_pairs={{28,4},{29,5},{30,6},{31,7},{0,8},{1,9},{2,10},{3,11},{12,20},{13,... | collective-permute-start | bytes 294920 | tf_op jit(solution)/shard_map/ppermute | solution.py:536
  36.7 6.3 %collective-permute-start.12 = (f32[3,64,128]{2,1,0:T(8,128)}, f32[3,64,128]{2,1,0:T(8,128)}, u32[]{:S(2)}, u32[]{:S(2)}) collective-permute-start(f32[3,64,128]{2,1,0:T(8,128)} %get-tuple-element.60), channel_id=1, source_target_pairs={{4,12},{5,13},{6,14},{7,15},{8,16},{9,17},{10,18},{11,19},{28,29},... | collective-permute-start | bytes 294920 | tf_op jit(solution)/shard_map/ppermute | solution.py:536
  36.9 0.9 %copy-start.5 = (f32[3,64,128]{2,1,0:T(8,128)S(1)}, f32[3,64,128]{2,1,0:T(8,128)}, u32[]{:S(2)}) copy-start(f32[3,64,128]{2,1,0:T(8,128)} %copy-done.4) | copy-start | bytes 294916
  37.8 1.1 %copy-start.11 = (f32[3,512,128]{2,1,0:T(8,128)S(1)}, f32[3,512,128]{2,1,0:T(8,128)}, u32[]{:S(2)}) copy-start(f32[3,512,128]{2,1,0:T(8,128)} %copy-done.10) | copy-start | bytes 2359300
  39.0 4.1 %copy-start.23 = (f32[3,64,128]{2,1,0:T(8,128)S(1)}, f32[3,64,128]{2,1,0:T(8,128)}, u32[]{:S(2)}) copy-start(f32[3,64,128]{2,1,0:T(8,128)} %copy-done.22) | copy-start | bytes 294916
  42.0 8.6 %copy-start.14 = (f32[3,512,128]{2,1,0:T(8,128)}, f32[3,512,128]{2,1,0:T(8,128)S(1)}, u32[]{:S(2)}) copy-start(f32[3,512,128]{2,1,0:T(8,128)S(1)} %get-tuple-element.52.moment_ref) | copy-start | bytes 2359300
  42.0 8.6 %copy-start.16 = (f32[3,512,128]{2,1,0:T(8,128)}, f32[3,512,128]{2,1,0:T(8,128)S(1)}, u32[]{:S(2)}) copy-start(f32[3,512,128]{2,1,0:T(8,128)S(1)} %get-tuple-element.53.joined_ref) | copy-start | bytes 2359300
  42.0 5.5 %collective-permute-start.8 = (f32[3,64,128]{2,1,0:T(8,128)S(1)}, f32[3,64,128]{2,1,0:T(8,128)S(1)}, u32[]{:S(2)}, u32[]{:S(2)}) collective-permute-start(f32[3,64,128]{2,1,0:T(8,128)S(1)} %get-tuple-element.54), channel_id=1, source_target_pairs={{28,4},{29,5},{30,6},{31,7},{0,8},{1,9},{2,10},{3,11},{12,20},{13,... | collective-permute-start | bytes 294920 | tf_op jit(solution)/shard_map/ppermute | solution.py:536
  42.8 4.8 %collective-permute-start.9 = (f32[3,64,128]{2,1,0:T(8,128)S(1)}, f32[3,64,128]{2,1,0:T(8,128)S(1)}, u32[]{:S(2)}, u32[]{:S(2)}) collective-permute-start(f32[3,64,128]{2,1,0:T(8,128)S(1)} %get-tuple-element.55), channel_id=1, source_target_pairs={{4,12},{5,13},{6,14},{7,15},{8,16},{9,17},{10,18},{11,19},{28,29},... | collective-permute-start | bytes 294920 | tf_op jit(solution)/shard_map/ppermute | solution.py:536
  43.0 3.5 %copy-start.25 = (f32[3,64,128]{2,1,0:T(8,128)S(1)}, f32[3,64,128]{2,1,0:T(8,128)}, u32[]{:S(2)}) copy-start(f32[3,64,128]{2,1,0:T(8,128)} %copy-done.24) | copy-start | bytes 294916
  44.0 7.7 %collective-permute-start.13 = (f32[3,64,128]{2,1,0:T(8,128)S(1)}, f32[3,64,128]{2,1,0:T(8,128)S(1)}, u32[]{:S(2)}, u32[]{:S(2)}) collective-permute-start(f32[3,64,128]{2,1,0:T(8,128)S(1)} %shard_map.88.refs_0_), channel_id=1, source_target_pairs={{29,30},{31,0},{1,2},{5,6},{7,8},{9,10},{13,14},{15,16},{17,18},{2... | collective-permute-start | bytes 294920 | tf_op jit(solution)/shard_map/ppermute | solution.py:536
  47.5 4.9 %collective-permute-start.14 = (f32[3,64,128]{2,1,0:T(8,128)S(1)}, f32[3,64,128]{2,1,0:T(8,128)}, u32[]{:S(2)}, u32[]{:S(2)}) collective-permute-start(f32[3,64,128]{2,1,0:T(8,128)S(1)} %shard_map.90), channel_id=1, source_target_pairs={{28,29},{30,31},{0,1},{2,3},{4,5},{6,7},{8,9},{10,11},{12,13},{14,... | collective-permute-start | bytes 294920 | tf_op jit(solution)/shard_map/ppermute | solution.py:536
  47.6 12.2 %collective-permute-start.10 = (f32[3,64,128]{2,1,0:T(8,128)S(1)}, f32[3,64,128]{2,1,0:T(8,128)S(1)}, u32[]{:S(2)}, u32[]{:S(2)}) collective-permute-start(f32[3,64,128]{2,1,0:T(8,128)S(1)} %shard_map.87.refs_0_), channel_id=1, source_target_pairs={{29,30},{31,0},{1,2},{5,6},{7,8},{9,10},{13,14},{15,16},{17,18},{2... | collective-permute-start | bytes 294920 | tf_op jit(solution)/shard_map/ppermute | solution.py:536
  50.7 9.8 %collective-permute-start.15 = (f32[3,64,128]{2,1,0:T(8,128)S(1)}, f32[3,64,128]{2,1,0:T(8,128)S(1)}, u32[]{:S(2)}, u32[]{:S(2)}) collective-permute-start(f32[3,64,128]{2,1,0:T(8,128)S(1)} %shard_map.93), channel_id=1, source_target_pairs={{28,29},{30,31},{0,1},{2,3},{4,5},{6,7},{8,9},{10,11},{12,13},{14,... | collective-permute-start | bytes 294920 | tf_op jit(solution)/shard_map/ppermute | solution.py:536
  51.7 0.6 copy-start.20
  52.4 1.1 %copy-start.7 = (f32[3,512,128]{2,1,0:T(8,128)S(1)}, f32[3,512,128]{2,1,0:T(8,128)}, u32[]{:S(2)}) copy-start(f32[3,512,128]{2,1,0:T(8,128)} %copy-done.6) | copy-start | bytes 2359300
  53.5 1.1 %copy-start.9 = (f32[3,512,128]{2,1,0:T(8,128)S(1)}, f32[3,512,128]{2,1,0:T(8,128)}, u32[]{:S(2)}) copy-start(f32[3,512,128]{2,1,0:T(8,128)} %copy-done.8) | copy-start | bytes 2359300
  54.7 0.9 %copy-start.21 = (f32[3,64,128]{2,1,0:T(8,128)S(1)}, f32[3,64,128]{2,1,0:T(8,128)}, u32[]{:S(2)}) copy-start(f32[3,64,128]{2,1,0:T(8,128)} %shard_map.89.refs_3_) | copy-start | bytes 294916
  59.2 0.6 copy-start.26
  59.8 0.6 copy-start.18
  60.5 1.1 %copy-start.15 = (f32[3,512,128]{2,1,0:T(8,128)S(1)}, f32[3,512,128]{2,1,0:T(8,128)}, u32[]{:S(2)}) copy-start(f32[3,512,128]{2,1,0:T(8,128)} %copy-done.14) | copy-start | bytes 2359300
  61.6 1.1 %copy-start.17 = (f32[3,512,128]{2,1,0:T(8,128)S(1)}, f32[3,512,128]{2,1,0:T(8,128)}, u32[]{:S(2)}) copy-start(f32[3,512,128]{2,1,0:T(8,128)} %copy-done.16) | copy-start | bytes 2359300
  62.7 0.9 %copy-start.19 = (f32[3,64,128]{2,1,0:T(8,128)S(1)}, f32[3,64,128]{2,1,0:T(8,128)}, u32[]{:S(2)}) copy-start(f32[3,64,128]{2,1,0:T(8,128)} %shard_map.92.gjo_ref) | copy-start | bytes 294916

commit v7 on v6

--- a/solution.py
+++ b/solution.py
@@ -543,6 +543,7 @@
             in_specs=[anywhere] * (1 + len(after)),
             out_specs=anywhere,
             input_output_aliases={0: 0},
+            compiler_params=pltpu.CompilerParams(vmem_limit_bytes=1024 * 1024),
         )(block, *after)
 
     def edge(count, way, *operands):

time: 65.4 us -> 43.2 us (0.66)
  the two profiles are of different devices: /device:TPU:0 before, /device:TPU:7 now
where the time goes in v7:
time: 43.2 us; the launch traced here: 43 us
  waiting for transfers between devices  20 us (46%)
  Pallas kernels  12.4 us (29%)
  starting transfers between devices  9.81 us (23%)
  between operations  0.78 us (2%)
    ppermute x16, waiting for transfers between devices, exchange(): return lax.ppermute(block, 'elem', pairs)  20 us
    pallas_call x14, Pallas kernels, call(): pl.pallas_call(kernel, out_shape=[jax.ShapeDtypeStruct(s, t) for s, t in...  12.4 us
    ppermute x16, starting transfers between devices, exchange(): return lax.ppermute(block, 'elem', pairs)  9.81 us
  transfers between devices with their start and end apart: 16, of which 9 were waited for; matrix products, arithmetic and copies ran while one was open for 0% of the time, Pallas kernels for 22%

profile of v7, /device:TPU:7, one launch (start us, length us, event | category | flops | bytes accessed | tf_op | source)
XLA Modules:
  0.0 43.0 jit_solution(2224165612260033715)
XLA Ops:
  0.6 2.0 %shard_map.77 = (f32[3,512,128]{2,1,0:T(8,128)S(1)}, f32[3,512,128]{2,1,0:T(8,128)S(1)}, f32[3,512,128]{2,1,0:T(8,128)S(1)}, f32[3,512,128]{2,1,0:T(8,128)S(1)},...) custom-call(f32[3,512,128]{2,1,0:T(8,128)} %moment_far.1, ...), custom_call_target="tpu_custom_call" | custom-call | flops 1000000 | bytes 8929804 | tf_op jit(solution)/shard_map/pallas_call | solution.py:496
  2.6 3.4 %collective-permute-start = (f32[4,64,128]{2,1,0:T(8,128)S(1)}, f32[4,64,128]{2,1,0:T(8,128)S(1)}, u32[]{:S(2)}, u32[]{:S(2)}) collective-permute-start(f32[4,64,128]{2,1,0:T(8,128)S(1)} %get-tuple-element.42), channel_id=1, source_target_pairs={{28,4},{29,5},{30,6},{31,7},{0,8},{1,9},{2,10},{3,11},{12,20},{13,... | collective-permute-start | bytes 393224 | tf_op jit(solution)/shard_map/ppermute | solution.py:536
  6.0 0.0 collective-permute-start.1
  6.0 2.1 %shard_map.82 = (f32[3,512,128]{2,1,0:T(8,128)S(1)}, f32[3,64,128]{2,1,0:T(8,128)S(1)}, f32[3,64,128]{2,1,0:T(8,128)S(1)}, f32[3,64,128]{2,1,0:T(8,128)S(1)}, f32[3,64,128]{2,1,0:T(8,128)S(1)}) custom-call(f32[3,512,128]{2,1,0:T(8,128)S(1)} %get-tuple-element.34.moment_ref, f32[3,512,128]{2,1,0:T(8,128)S(1)} %get-tuple-element.35.carry_ref, ...), custom_call_target="tpu_custom_call" | custom-call | flops 20000000 | bytes 5128192 | tf_op jit(solution)/shard_map/pallas_call | solution.py:496
  8.2 1.0 %collective-permute-start.4 = (f32[3,64,128]{2,1,0:T(8,128)S(1)}, f32[3,64,128]{2,1,0:T(8,128)S(1)}, u32[]{:S(2)}, u32[]{:S(2)}) collective-permute-start(f32[3,64,128]{2,1,0:T(8,128)S(1)} %get-tuple-element.48), channel_id=1, source_target_pairs={{28,4},{29,5},{30,6},{31,7},{0,8},{1,9},{2,10},{3,11},{12,20},{13,... | collective-permute-start | bytes 294920 | tf_op jit(solution)/shard_map/ppermute | solution.py:536
  9.1 0.6 %collective-permute-start.5 = (f32[3,64,128]{2,1,0:T(8,128)S(1)}, f32[3,64,128]{2,1,0:T(8,128)S(1)}, u32[]{:S(2)}, u32[]{:S(2)}) collective-permute-start(f32[3,64,128]{2,1,0:T(8,128)S(1)} %get-tuple-element.49), channel_id=1, source_target_pairs={{4,12},{5,13},{6,14},{7,15},{8,16},{9,17},{10,18},{11,19},{28,29},... | collective-permute-start | bytes 294920 | tf_op jit(solution)/shard_map/ppermute | solution.py:536
  9.8 0.0 collective-permute-done.ie_ref.refs_0_
  9.8 4.2 %collective-permute-done.1.io_ref.refs_1_ = f32[4,64,128]{2,1,0:T(8,128)S(1)} collective-permute-done((f32[4,64,128]{2,1,0:T(8,128)S(1)}, f32[4,64,128]{2,1,0:T(8,128)S(1)}, u32[]{:S(2)}, u32[]{:S(2)}) %collective-permute-start.1) | collective-permute-done | bytes 131104 | tf_op jit(solution)/shard_map/ppermute | solution.py:536
  14.0 0.1 collective-permute-start.2
  14.1 0.7 %collective-permute-start.3 = (f32[4,64,128]{2,1,0:T(8,128)S(1)}, f32[4,64,128]{2,1,0:T(8,128)S(1)}, u32[]{:S(2)}, u32[]{:S(2)}) collective-permute-start(f32[4,64,128]{2,1,0:T(8,128)S(1)} %shard_map.80), channel_id=1, source_target_pairs={{28,29},{30,31},{0,1},{2,3},{4,5},{6,7},{8,9},{10,11},{12,13},{14,... | collective-permute-start | bytes 393224 | tf_op jit(solution)/shard_map/ppermute | solution.py:536
  14.8 0.0 collective-permute-done.4.ie_ref.gie_ref
  14.8 3.7 %collective-permute-done.5.io_ref.gio_ref = f32[3,64,128]{2,1,0:T(8,128)S(1)} collective-permute-done((f32[3,64,128]{2,1,0:T(8,128)S(1)}, f32[3,64,128]{2,1,0:T(8,128)S(1)}, u32[]{:S(2)}, u32[]{:S(2)}) %collective-permute-start.5) | collective-permute-done | bytes 98336 | tf_op jit(solution)/shard_map/ppermute | solution.py:536
  18.5 0.1 collective-permute-start.6
  18.7 0.6 %collective-permute-start.7 = (f32[3,64,128]{2,1,0:T(8,128)S(1)}, f32[3,64,128]{2,1,0:T(8,128)S(1)}, u32[]{:S(2)}, u32[]{:S(2)}) collective-permute-start(f32[3,64,128]{2,1,0:T(8,128)S(1)} %shard_map.85), channel_id=1, source_target_pairs={{28,29},{30,31},{0,1},{2,3},{4,5},{6,7},{8,9},{10,11},{12,13},{14,... | collective-permute-start | bytes 294920 | tf_op jit(solution)/shard_map/ppermute | solution.py:536
  19.2 1.1 %collective-permute-done.2.refs_0_ = f32[4,64,128]{2,1,0:T(8,128)S(1)} collective-permute-done((f32[4,64,128]{2,1,0:T(8,128)S(1)}, f32[4,64,128]{2,1,0:T(8,128)S(1)}, u32[]{:S(2)}, u32[]{:S(2)}) %collective-permute-start.2) | collective-permute-done | bytes 131104 | tf_op jit(solution)/shard_map/ppermute | solution.py:536
  20.3 0.0 collective-permute-done.3.refs_3_
  20.4 2.3 %shard_map.81 = (f32[512,128]{1,0:T(8,128)S(1)}, f32[3,512,128]{2,1,0:T(8,128)S(1)}, f32[3,512,128]{2,1,0:T(8,128)S(1)}, f32[3,64,128]{2,1,0:T(8,128)S(1)}, f32[...) custom-call(f32[3,512,128]{2,1,0:T(8,128)S(1)} %get-tuple-element.40.state_ref, ...), custom_call_target="tpu_custom_call" | custom-call | flops 20000000 | bytes 7749632 | tf_op jit(solution)/shard_map/pallas_call | solution.py:496
  22.6 0.6 %collective-permute-start.11 = (f32[3,64,128]{2,1,0:T(8,128)S(1)}, f32[3,64,128]{2,1,0:T(8,128)S(1)}, u32[]{:S(2)}, u32[]{:S(2)}) collective-permute-start(f32[3,64,128]{2,1,0:T(8,128)S(1)} %get-tuple-element.59), channel_id=1, source_target_pairs={{28,4},{29,5},{30,6},{31,7},{0,8},{1,9},{2,10},{3,11},{12,20},{13,... | collective-permute-start | bytes 294920 | tf_op jit(solution)/shard_map/ppermute | solution.py:536
  23.3 0.0 collective-permute-start.12
  23.3 1.2 %collective-permute-done.6.refs_0_ = f32[3,64,128]{2,1,0:T(8,128)S(1)} collective-permute-done((f32[3,64,128]{2,1,0:T(8,128)S(1)}, f32[3,64,128]{2,1,0:T(8,128)S(1)}, u32[]{:S(2)}, u32[]{:S(2)}) %collective-permute-start.6) | collective-permute-done | bytes 98336 | tf_op jit(solution)/shard_map/ppermute | solution.py:536
  24.5 0.0 collective-permute-done.7.gje_ref
  24.5 2.1 %shard_map.86 = (f32[3,512,128]{2,1,0:T(8,128)S(1)}, f32[3,512,128]{2,1,0:T(8,128)S(1)}, f32[3,64,128]{2,1,0:T(8,128)S(1)}, f32[3,64,128]{2,1,0:T(8,128)S(1)}, f...) custom-call(f32[3,512,128]{2,1,0:T(8,128)S(1)} %get-tuple-element.34.moment_ref, ...), custom_call_target="tpu_custom_call" | custom-call | flops 20000000 | bytes 7356416 | tf_op jit(solution)/shard_map/pallas_call | solution.py:496
  26.5 1.6 %collective-permute-start.8 = (f32[3,64,128]{2,1,0:T(8,128)S(1)}, f32[3,64,128]{2,1,0:T(8,128)S(1)}, u32[]{:S(2)}, u32[]{:S(2)}) collective-permute-start(f32[3,64,128]{2,1,0:T(8,128)S(1)} %get-tuple-element.54), channel_id=1, source_target_pairs={{28,4},{29,5},{30,6},{31,7},{0,8},{1,9},{2,10},{3,11},{12,20},{13,... | collective-permute-start | bytes 294920 | tf_op jit(solution)/shard_map/ppermute | solution.py:536
  28.1 0.0 collective-permute-start.9
  28.1 0.7 %collective-permute-done.11.ie_ref.refs_1_ = f32[3,64,128]{2,1,0:T(8,128)S(1)} collective-permute-done((f32[3,64,128]{2,1,0:T(8,128)S(1)}, f32[3,64,128]{2,1,0:T(8,128)S(1)}, u32[]{:S(2)}, u32[]{:S(2)}) %collective-permute-start.11) | collective-permute-done | bytes 98336 | tf_op jit(solution)/shard_map/ppermute | solution.py:536
  28.8 1.1 %collective-permute-done.12.io_ref.refs_2_ = f32[3,64,128]{2,1,0:T(8,128)S(1)} collective-permute-done((f32[3,64,128]{2,1,0:T(8,128)S(1)}, f32[3,64,128]{2,1,0:T(8,128)S(1)}, u32[]{:S(2)}, u32[]{:S(2)}) %collective-permute-start.12) | collective-permute-done | bytes 98336 | tf_op jit(solution)/shard_map/ppermute | solution.py:536
  30.0 0.1 collective-permute-start.13
  30.1 0.5 %collective-permute-start.14 = (f32[3,64,128]{2,1,0:T(8,128)S(1)}, f32[3,64,128]{2,1,0:T(8,128)S(1)}, u32[]{:S(2)}, u32[]{:S(2)}) collective-permute-start(f32[3,64,128]{2,1,0:T(8,128)S(1)} %shard_map.90), channel_id=1, source_target_pairs={{28,29},{30,31},{0,1},{2,3},{4,5},{6,7},{8,9},{10,11},{12,13},{14,... | collective-permute-start | bytes 294920 | tf_op jit(solution)/shard_map/ppermute | solution.py:536
  30.6 2.2 %collective-permute-done.8.ie_ref.gie_ref = f32[3,64,128]{2,1,0:T(8,128)S(1)} collective-permute-done((f32[3,64,128]{2,1,0:T(8,128)S(1)}, f32[3,64,128]{2,1,0:T(8,128)S(1)}, u32[]{:S(2)}, u32[]{:S(2)}) %collective-permute-start.8) | collective-permute-done | bytes 98336 | tf_op jit(solution)/shard_map/ppermute | solution.py:536
  32.7 3.3 %collective-permute-done.9.io_ref.gio_ref = f32[3,64,128]{2,1,0:T(8,128)S(1)} collective-permute-done((f32[3,64,128]{2,1,0:T(8,128)S(1)}, f32[3,64,128]{2,1,0:T(8,128)S(1)}, u32[]{:S(2)}, u32[]{:S(2)}) %collective-permute-start.9) | collective-permute-done | bytes 98336 | tf_op jit(solution)/shard_map/ppermute | solution.py:536
  36.0 0.1 collective-permute-start.10
  36.1 0.6 %collective-permute-start.15 = (f32[3,64,128]{2,1,0:T(8,128)S(1)}, f32[3,64,128]{2,1,0:T(8,128)S(1)}, u32[]{:S(2)}, u32[]{:S(2)}) collective-permute-start(f32[3,64,128]{2,1,0:T(8,128)S(1)} %shard_map.93), channel_id=1, source_target_pairs={{28,29},{30,31},{0,1},{2,3},{4,5},{6,7},{8,9},{10,11},{12,13},{14,... | collective-permute-start | bytes 294920 | tf_op jit(solution)/shard_map/ppermute | solution.py:536
  36.7 0.0 collective-permute-done.13.refs_0_
  36.7 0.0 collective-permute-done.14.refs_4_
  36.7 2.7 %shard_map.91 = (f32[3,512,128]{2,1,0:T(8,128)}, f32[8,128]{1,0:T(8,128)S(1)}) custom-call(f32[3,512,128]{2,1,0:T(8,128)S(1)} %get-tuple-element.57.state_ref, f32[3,512,128]{2,1,0:T(8,128)S(1)} %get-tuple-element.35.carry_ref, f32[3,512,128]{2,1,0:T(8,128)S(1)} %get-tuple-element.36.weigh_ref, bf16[256,768]{1,0:T(8,128)(2,1)S(1)} %get-tuple-element.37.table_ref, ...), custom_call_target="tpu_custom_call" | custom-call | flops 20000000 | bytes 6180864 | tf_op jit(solution)/shard_map/pallas_call | solution.py:496
  39.4 2.5 %collective-permute-done.10.refs_0_ = f32[3,64,128]{2,1,0:T(8,128)S(1)} collective-permute-done((f32[3,64,128]{2,1,0:T(8,128)S(1)}, f32[3,64,128]{2,1,0:T(8,128)S(1)}, u32[]{:S(2)}, u32[]{:S(2)}) %collective-permute-start.10) | collective-permute-done | bytes 98336 | tf_op jit(solution)/shard_map/ppermute | solution.py:536
  41.9 0.0 collective-permute-done.15.gje_ref
  41.9 1.1 %shard_map.94 = f32[3,512,128]{2,1,0:T(8,128)} custom-call(f32[3,512,128]{2,1,0:T(8,128)S(1)} %get-tuple-element.52.moment_ref, s32[4,8,128]{2,1,0:T(8,128)S(1)} %get-tuple-element.39.index_ref, f32[512,128]{1,0:T(8,128)S(1)} %get-tuple-element.46.refs_1_.inverse_ref.refs_0_, f32[3,512,128]{2,1,0:T(8,128)S(1)} %get-tuple-element.53.joined_ref, ...), custom_call_target="tpu_custom_call" | custom-call | flops 1000000 | bytes 3031040 | tf_op jit(solution)/shard_map/pallas_call | solution.py:496
  (12 shorter events, 0.2 us)
Async XLA Ops:
  2.6 7.1 %collective-permute-start = (f32[4,64,128]{2,1,0:T(8,128)S(1)}, f32[4,64,128]{2,1,0:T(8,128)S(1)}, u32[]{:S(2)}, u32[]{:S(2)}) collective-permute-start(f32[4,64,128]{2,1,0:T(8,128)S(1)} %get-tuple-element.42), channel_id=1, source_target_pairs={{28,4},{29,5},{30,6},{31,7},{0,8},{1,9},{2,10},{3,11},{12,20},{13,... | collective-permute-start | bytes 393224 | tf_op jit(solution)/shard_map/ppermute | solution.py:536
  6.0 7.9 %collective-permute-start.1 = (f32[4,64,128]{2,1,0:T(8,128)S(1)}, f32[4,64,128]{2,1,0:T(8,128)S(1)}, u32[]{:S(2)}, u32[]{:S(2)}) collective-permute-start(f32[4,64,128]{2,1,0:T(8,128)S(1)} %get-tuple-element.43), channel_id=1, source_target_pairs={{4,12},{5,13},{6,14},{7,15},{8,16},{9,17},{10,18},{11,19},{28,29},... | collective-permute-start | bytes 393224 | tf_op jit(solution)/shard_map/ppermute | solution.py:536
  8.2 6.6 %collective-permute-start.4 = (f32[3,64,128]{2,1,0:T(8,128)S(1)}, f32[3,64,128]{2,1,0:T(8,128)S(1)}, u32[]{:S(2)}, u32[]{:S(2)}) collective-permute-start(f32[3,64,128]{2,1,0:T(8,128)S(1)} %get-tuple-element.48), channel_id=1, source_target_pairs={{28,4},{29,5},{30,6},{31,7},{0,8},{1,9},{2,10},{3,11},{12,20},{13,... | collective-permute-start | bytes 294920 | tf_op jit(solution)/shard_map/ppermute | solution.py:536
  9.1 9.4 %collective-permute-start.5 = (f32[3,64,128]{2,1,0:T(8,128)S(1)}, f32[3,64,128]{2,1,0:T(8,128)S(1)}, u32[]{:S(2)}, u32[]{:S(2)}) collective-permute-start(f32[3,64,128]{2,1,0:T(8,128)S(1)} %get-tuple-element.49), channel_id=1, source_target_pairs={{4,12},{5,13},{6,14},{7,15},{8,16},{9,17},{10,18},{11,19},{28,29},... | collective-permute-start | bytes 294920 | tf_op jit(solution)/shard_map/ppermute | solution.py:536
  14.0 6.4 %collective-permute-start.2 = (f32[4,64,128]{2,1,0:T(8,128)S(1)}, f32[4,64,128]{2,1,0:T(8,128)S(1)}, u32[]{:S(2)}, u32[]{:S(2)}) collective-permute-start(f32[4,64,128]{2,1,0:T(8,128)S(1)} %shard_map.78.refs_0_), channel_id=1, source_target_pairs={{29,30},{31,0},{1,2},{5,6},{7,8},{9,10},{13,14},{15,16},{17,18},{2... | collective-permute-start | bytes 393224 | tf_op jit(solution)/shard_map/ppermute | solution.py:536
  14.1 6.2 %collective-permute-start.3 = (f32[4,64,128]{2,1,0:T(8,128)S(1)}, f32[4,64,128]{2,1,0:T(8,128)S(1)}, u32[]{:S(2)}, u32[]{:S(2)}) collective-permute-start(f32[4,64,128]{2,1,0:T(8,128)S(1)} %shard_map.80), channel_id=1, source_target_pairs={{28,29},{30,31},{0,1},{2,3},{4,5},{6,7},{8,9},{10,11},{12,13},{14,... | collective-permute-start | bytes 393224 | tf_op jit(solution)/shard_map/ppermute | solution.py:536
  18.5 5.9 %collective-permute-start.6 = (f32[3,64,128]{2,1,0:T(8,128)S(1)}, f32[3,64,128]{2,1,0:T(8,128)S(1)}, u32[]{:S(2)}, u32[]{:S(2)}) collective-permute-start(f32[3,64,128]{2,1,0:T(8,128)S(1)} %shard_map.83.refs_0_), channel_id=1, source_target_pairs={{29,30},{31,0},{1,2},{5,6},{7,8},{9,10},{13,14},{15,16},{17,18},{2... | collective-permute-start | bytes 294920 | tf_op jit(solution)/shard_map/ppermute | solution.py:536
  18.7 5.8 %collective-permute-start.7 = (f32[3,64,128]{2,1,0:T(8,128)S(1)}, f32[3,64,128]{2,1,0:T(8,128)S(1)}, u32[]{:S(2)}, u32[]{:S(2)}) collective-permute-start(f32[3,64,128]{2,1,0:T(8,128)S(1)} %shard_map.85), channel_id=1, source_target_pairs={{28,29},{30,31},{0,1},{2,3},{4,5},{6,7},{8,9},{10,11},{12,13},{14,... | collective-permute-start | bytes 294920 | tf_op jit(solution)/shard_map/ppermute | solution.py:536
  22.6 6.2 %collective-permute-start.11 = (f32[3,64,128]{2,1,0:T(8,128)S(1)}, f32[3,64,128]{2,1,0:T(8,128)S(1)}, u32[]{:S(2)}, u32[]{:S(2)}) collective-permute-start(f32[3,64,128]{2,1,0:T(8,128)S(1)} %get-tuple-element.59), channel_id=1, source_target_pairs={{28,4},{29,5},{30,6},{31,7},{0,8},{1,9},{2,10},{3,11},{12,20},{13,... | collective-permute-start | bytes 294920 | tf_op jit(solution)/shard_map/ppermute | solution.py:536
  23.3 6.7 %collective-permute-start.12 = (f32[3,64,128]{2,1,0:T(8,128)S(1)}, f32[3,64,128]{2,1,0:T(8,128)S(1)}, u32[]{:S(2)}, u32[]{:S(2)}) collective-permute-start(f32[3,64,128]{2,1,0:T(8,128)S(1)} %get-tuple-element.60), channel_id=1, source_target_pairs={{4,12},{5,13},{6,14},{7,15},{8,16},{9,17},{10,18},{11,19},{28,29},... | collective-permute-start | bytes 294920 | tf_op jit(solution)/shard_map/ppermute | solution.py:536
  26.5 6.2 %collective-permute-start.8 = (f32[3,64,128]{2,1,0:T(8,128)S(1)}, f32[3,64,128]{2,1,0:T(8,128)S(1)}, u32[]{:S(2)}, u32[]{:S(2)}) collective-permute-start(f32[3,64,128]{2,1,0:T(8,128)S(1)} %get-tuple-element.54), channel_id=1, source_target_pairs={{28,4},{29,5},{30,6},{31,7},{0,8},{1,9},{2,10},{3,11},{12,20},{13,... | collective-permute-start | bytes 294920 | tf_op jit(solution)/shard_map/ppermute | solution.py:536
  28.1 7.9 %collective-permute-start.9 = (f32[3,64,128]{2,1,0:T(8,128)S(1)}, f32[3,64,128]{2,1,0:T(8,128)S(1)}, u32[]{:S(2)}, u32[]{:S(2)}) collective-permute-start(f32[3,64,128]{2,1,0:T(8,128)S(1)} %get-tuple-element.55), channel_id=1, source_target_pairs={{4,12},{5,13},{6,14},{7,15},{8,16},{9,17},{10,18},{11,19},{28,29},... | collective-permute-start | bytes 294920 | tf_op jit(solution)/shard_map/ppermute | solution.py:536
  30.0 6.7 %collective-permute-start.13 = (f32[3,64,128]{2,1,0:T(8,128)S(1)}, f32[3,64,128]{2,1,0:T(8,128)S(1)}, u32[]{:S(2)}, u32[]{:S(2)}) collective-permute-start(f32[3,64,128]{2,1,0:T(8,128)S(1)} %shard_map.88.refs_0_), channel_id=1, source_target_pairs={{29,30},{31,0},{1,2},{5,6},{7,8},{9,10},{13,14},{15,16},{17,18},{2... | collective-permute-start | bytes 294920 | tf_op jit(solution)/shard_map/ppermute | solution.py:536
  30.1 6.6 %collective-permute-start.14 = (f32[3,64,128]{2,1,0:T(8,128)S(1)}, f32[3,64,128]{2,1,0:T(8,128)S(1)}, u32[]{:S(2)}, u32[]{:S(2)}) collective-permute-start(f32[3,64,128]{2,1,0:T(8,128)S(1)} %shard_map.90), channel_id=1, source_target_pairs={{28,29},{30,31},{0,1},{2,3},{4,5},{6,7},{8,9},{10,11},{12,13},{14,... | collective-permute-start | bytes 294920 | tf_op jit(solution)/shard_map/ppermute | solution.py:536
  36.0 5.9 %collective-permute-start.10 = (f32[3,64,128]{2,1,0:T(8,128)S(1)}, f32[3,64,128]{2,1,0:T(8,128)S(1)}, u32[]{:S(2)}, u32[]{:S(2)}) collective-permute-start(f32[3,64,128]{2,1,0:T(8,128)S(1)} %shard_map.87.refs_0_), channel_id=1, source_target_pairs={{29,30},{31,0},{1,2},{5,6},{7,8},{9,10},{13,14},{15,16},{17,18},{2... | collective-permute-start | bytes 294920 | tf_op jit(solution)/shard_map/ppermute | solution.py:536
  36.1 5.8 %collective-permute-start.15 = (f32[3,64,128]{2,1,0:T(8,128)S(1)}, f32[3,64,128]{2,1,0:T(8,128)S(1)}, u32[]{:S(2)}, u32[]{:S(2)}) collective-permute-start(f32[3,64,128]{2,1,0:T(8,128)S(1)} %shard_map.93), channel_id=1, source_target_pairs={{28,29},{30,31},{0,1},{2,3},{4,5},{6,7},{8,9},{10,11},{12,13},{14,... | collective-permute-start | bytes 294920 | tf_op jit(solution)/shard_map/ppermute | solution.py:536

commit v8 on v7

--- a/solution.py
+++ b/solution.py
@@ -218,27 +218,47 @@
     ref[pl.ds(7, 64, stride=8)] = upper + jnp.where(tall < 127, lanes(lower, above), 0.0)
 
 
+def face_rows(ends, axis, way, k):
+    end = ends[axis][way]
+    return pl.ds(end * 8 + k, 8, stride=64) if axis else pl.ds(end * 64 + k, 8, stride=8)
+
+
+def tile(c, k):
+    return pl.ds((7 * c + k) * 8, 8)
+
+
+def top_tile(ref):
+    return pl.ds(ref.shape[0] - 8, 8)
+
+
 def send_faces(c, ref, index, ends, out):
     inverse = index[1]
-    for way in range(2):
-        i_face = ref[pl.ds(pl.multiple_of(ends[0][way] * 64, 64), 64)]
-        out[way][c] = lanes(i_face, inverse)
-        for i in range(8):
-            j_face = ref[pl.ds(pl.multiple_of(ends[1][way] * 8 + i * 64, 8), 8)]
-            out[2 + way][c, pl.ds(i * 8, 8)] = lanes(j_face, inverse)
+    top = jnp.broadcast_to(inverse[:, 127:], (8, 128))
+    lane = lax.broadcasted_iota(jnp.int32, (8, 128), 1)
+    for axis in range(2):
+        for way in range(2):
+            face = out[2 * axis + way]
+            for k in range(7):
+                face[tile(c, k)] = lanes(ref[face_rows(ends, axis, way, k)], inverse)
+            last = lanes(ref[face_rows(ends, axis, way, 7)], top)
+            others = face[top_tile(face)] if c else jnp.zeros((8, 128), F32)
+            face[top_tile(face)] = jnp.where(lane == c, last, others)
 
 
 def add_faces(c, ref, index, ends, got):
     height = index[0]
-    for way in range(2):
-        r = pl.ds(pl.multiple_of(ends[0][way] * 64, 64), 64)
-        part = lanes(got[way][c], height)
-        ref[r] = ref[r] + (part * ends[2][0] if way else part)
-    for way in range(2):
-        for i in range(8):
-            r = pl.ds(pl.multiple_of(ends[1][way] * 8 + i * 64, 8), 8)
-            part = lanes(got[3 - way][c, pl.ds(i * 8, 8)], height)
-            ref[r] = ref[r] + (part * ends[2][1] if way else part)
+    above = (height + 1) & 127
+    own = jnp.full((8, 128), c, jnp.int32)
+    for axis in range(2):
+        for way in range(2):
+            face = got[3 - way if axis else way]
+            last = jnp.where(
+                height < 127, lanes(face[tile(c, 0)], above), lanes(face[top_tile(face)], own)
+            )
+            parts = [lanes(face[tile(c, k)], height) for k in range(7)] + [last]
+            for k, part in enumerate(parts):
+                r = face_rows(ends, axis, way, k)
+                ref[r] = ref[r] + (part * ends[2][axis] if way else part)
 
 
 def ends_of(columns):
@@ -358,11 +378,12 @@
 def edge_kernel(columns, way, ie_ref, io_ref, face, *refs):
     ends, out = ends_of(columns), refs[-1]
     out[...] = face[...]
-    r = pl.ds(pl.multiple_of(ends[1][way] * 8, 8), 8)
+    tiles = face.shape[0] // 8
+    r = pl.ds(ends[1][way], tiles, stride=8)
     for other, got in enumerate((ie_ref, io_ref)):
-        w = pl.ds(pl.multiple_of(ends[0][other] * 8, 8), 8)
-        part = got[:, r]
-        out[:, w] = out[:, w] + (part * ends[2][0] if other else part)
+        w = pl.ds(ends[0][other], tiles, stride=8)
+        part = got[r]
+        out[w] = out[w] + (part * ends[2][0] if other else part)
 
 
 def state_kernel(
@@ -550,7 +571,7 @@
         return call(
             functools.partial(edge_kernel, columns, way),
             [VMEM] * len(operands),
-            [((count, 64, 128), F32)],
+            [(face_shape(count), F32)],
             [],
             count * 64 * 128,
             *operands,
@@ -568,8 +589,11 @@
     def far(array):
         return pltpu.with_memory_space_constraint(array, pltpu.HBM)
 
+    def face_shape(count):
+        return ((7 * count + 1) * 8, 128)
+
     def faces_shape(count):
-        return [((count, 64, 128), F32)] * 4
+        return [(face_shape(count), F32)] * 4
 
     moment, state, carry, weigh, table, turned, index, joined_state, *faces_state = call(
         functools.partial(index_kernel, columns),

time: 43.2 us -> 42.3 us (0.979)
  the two profiles are of different devices: /device:TPU:7 before, /device:TPU:0 now
where the time goes in v8:
time: 42.3 us; the launch traced here: 42.1 us
  starting transfers between devices  25.2 us (60%)
  Pallas kernels  14 us (33%)
  waiting for transfers between devices  2.2 us (5%)
  between operations  0.77 us (2%)
    ppermute x16, starting transfers between devices, exchange(): return lax.ppermute(block, 'elem', pairs)  25.2 us
    pallas_call x14, Pallas kernels, call(): pl.pallas_call(kernel, out_shape=[jax.ShapeDtypeStruct(s, t) for s, t in...  14 us
    ppermute x16, waiting for transfers between devices, exchange(): return lax.ppermute(block, 'elem', pairs)  2.2 us
  transfers between devices with their start and end apart: 16, of which 4 were waited for; matrix products, arithmetic and copies ran while one was open for 0% of the time, Pallas kernels for 25%

profile of v8, /device:TPU:0, one launch (start us, length us, event | category | flops | bytes accessed | tf_op | source)
XLA Modules:
  0.0 42.1 jit_solution(15901599008622576815)
XLA Ops:
  0.6 2.1 %shard_map.77 = (f32[3,512,128]{2,1,0:T(8,128)S(1)}, f32[3,512,128]{2,1,0:T(8,128)S(1)}, f32[3,512,128]{2,1,0:T(8,128)S(1)}, f32[3,512,128]{2,1,0:T(8,128)S(1)},...) custom-call(f32[3,512,128]{2,1,0:T(8,128)} %moment_far.1, ...), custom_call_target="tpu_custom_call" | custom-call | flops 1000000 | bytes 8880652 | tf_op jit(solution)/shard_map/pallas_call | solution.py:517
  2.8 3.1 %collective-permute-start = (f32[232,128]{1,0:T(8,128)S(1)}, f32[232,128]{1,0:T(8,128)S(1)}, u32[]{:S(2)}, u32[]{:S(2)}) collective-permute-start(f32[232,128]{1,0:T(8,128)S(1)} %get-tuple-element.42), channel_id=1, source_target_pairs={{28,4},{29,5},{30,6},{31,7},{0,8},{1,9},{2,10},{3,11},{12,20},{13,... | collective-permute-start | bytes 356360 | tf_op jit(solution)/shard_map/ppermute | solution.py:557
  5.8 0.0 collective-permute-start.1
  5.8 2.2 %shard_map.82 = (f32[3,512,128]{2,1,0:T(8,128)S(1)}, f32[176,128]{1,0:T(8,128)S(1)}, f32[176,128]{1,0:T(8,128)S(1)}, f32[176,128]{1,0:T(8,128)S(1)}, f32[176,128]{1,0:T(8,128)S(1)}) custom-call(f32[3,512,128]{2,1,0:T(8,128)S(1)} %get-tuple-element.34.moment_ref, f32[3,512,128]{2,1,0:T(8,128)S(1)} %get-tuple-element.35.carry_ref, ...), custom_call_target="tpu_custom_call" | custom-call | flops 20000000 | bytes 5095424 | tf_op jit(solution)/shard_map/pallas_call | solution.py:517
  8.1 3.2 %collective-permute-start.4 = (f32[176,128]{1,0:T(8,128)S(1)}, f32[176,128]{1,0:T(8,128)S(1)}, u32[]{:S(2)}, u32[]{:S(2)}) collective-permute-start(f32[176,128]{1,0:T(8,128)S(1)} %get-tuple-element.48), channel_id=1, source_target_pairs={{28,4},{29,5},{30,6},{31,7},{0,8},{1,9},{2,10},{3,11},{12,20},{13,... | collective-permute-start | bytes 270344 | tf_op jit(solution)/shard_map/ppermute | solution.py:557
  11.3 0.0 collective-permute-start.5
  11.3 0.0 collective-permute-done.ie_ref.refs_0_
  11.3 0.0 collective-permute-done.1.io_ref.refs_1_
  11.3 4.8 %collective-permute-start.2 = (f32[232,128]{1,0:T(8,128)S(1)}, f32[232,128]{1,0:T(8,128)S(1)}, u32[]{:S(2)}, u32[]{:S(2)}) collective-permute-start(f32[232,128]{1,0:T(8,128)S(1)} %shard_map.78.refs_0_), channel_id=1, source_target_pairs={{29,30},{31,0},{1,2},{5,6},{7,8},{9,10},{13,14},{15,16},{17,18},{2... | collective-permute-start | bytes 356360 | tf_op jit(solution)/shard_map/ppermute | solution.py:557
  16.1 0.1 collective-permute-start.3
  16.2 0.0 collective-permute-done.4.ie_ref.gie_ref
  16.2 0.0 collective-permute-done.5.io_ref.gio_ref
  16.2 3.2 %collective-permute-start.6 = (f32[176,128]{1,0:T(8,128)S(1)}, f32[176,128]{1,0:T(8,128)S(1)}, u32[]{:S(2)}, u32[]{:S(2)}) collective-permute-start(f32[176,128]{1,0:T(8,128)S(1)} %shard_map.83.refs_0_), channel_id=1, source_target_pairs={{29,30},{31,0},{1,2},{5,6},{7,8},{9,10},{13,14},{15,16},{17,18},{2... | collective-permute-start | bytes 270344 | tf_op jit(solution)/shard_map/ppermute | solution.py:557
  19.5 0.1 collective-permute-start.7
  19.6 0.2 collective-permute-done.2.refs_0_
  19.8 0.0 collective-permute-done.3.refs_3_
  19.8 2.7 %shard_map.81 = (f32[512,128]{1,0:T(8,128)S(1)}, f32[3,512,128]{2,1,0:T(8,128)S(1)}, f32[3,512,128]{2,1,0:T(8,128)S(1)}, f32[176,128]{1,0:T(8,128)S(1)}, f32[176...) custom-call(f32[3,512,128]{2,1,0:T(8,128)S(1)} %get-tuple-element.40.state_ref, ...), custom_call_target="tpu_custom_call" | custom-call | flops 20000000 | bytes 7667712 | tf_op jit(solution)/shard_map/pallas_call | solution.py:517
  22.5 2.8 %collective-permute-start.11 = (f32[176,128]{1,0:T(8,128)S(1)}, f32[176,128]{1,0:T(8,128)S(1)}, u32[]{:S(2)}, u32[]{:S(2)}) collective-permute-start(f32[176,128]{1,0:T(8,128)S(1)} %get-tuple-element.59), channel_id=1, source_target_pairs={{28,4},{29,5},{30,6},{31,7},{0,8},{1,9},{2,10},{3,11},{12,20},{13,... | collective-permute-start | bytes 270344 | tf_op jit(solution)/shard_map/ppermute | solution.py:557
  25.3 0.2 collective-permute-start.12
  25.5 0.0 collective-permute-done.6.refs_0_
  25.5 0.0 collective-permute-done.7.gje_ref
  25.5 2.5 %shard_map.86 = (f32[3,512,128]{2,1,0:T(8,128)S(1)}, f32[3,512,128]{2,1,0:T(8,128)S(1)}, f32[176,128]{1,0:T(8,128)S(1)}, f32[176,128]{1,0:T(8,128)S(1)}, f32[176,128]{1,0:T(8,128)S(1)}, /*index=5*/f32[176,128]{1,0:T(8,128)S(1)}) custom-call(f32[3,512,128]{2,1,0:T(8,128)S(1)} %get-tuple-element.34.moment_ref, f32[3,512,128]{2,1,0:T(8,128)S(1)} %get-tuple-element.35.carry_ref, ...), custom_call_target="tpu_custom_call" | custom-call | flops 20000000 | bytes 7290880 | tf_op jit(solution)/shard_map/pallas_call | solution.py:517
  28.0 0.1 collective-permute-start.8
  28.0 0.4 collective-permute-start.9
  28.4 0.1 collective-permute-done.11.ie_ref.refs_1_
  28.5 0.0 collective-permute-done.12.io_ref.refs_2_
  28.5 4.4 %collective-permute-start.13 = (f32[176,128]{1,0:T(8,128)S(1)}, f32[176,128]{1,0:T(8,128)S(1)}, u32[]{:S(2)}, u32[]{:S(2)}) collective-permute-start(f32[176,128]{1,0:T(8,128)S(1)} %shard_map.88.refs_0_), channel_id=1, source_target_pairs={{29,30},{31,0},{1,2},{5,6},{7,8},{9,10},{13,14},{15,16},{17,18},{2... | collective-permute-start | bytes 270344 | tf_op jit(solution)/shard_map/ppermute | solution.py:557
  33.0 0.1 collective-permute-start.14
  33.1 0.0 collective-permute-done.8.ie_ref.gie_ref
  33.1 0.0 collective-permute-done.9.io_ref.gio_ref
  33.1 2.8 %collective-permute-start.10 = (f32[176,128]{1,0:T(8,128)S(1)}, f32[176,128]{1,0:T(8,128)S(1)}, u32[]{:S(2)}, u32[]{:S(2)}) collective-permute-start(f32[176,128]{1,0:T(8,128)S(1)} %shard_map.87.refs_0_), channel_id=1, source_target_pairs={{29,30},{31,0},{1,2},{5,6},{7,8},{9,10},{13,14},{15,16},{17,18},{2... | collective-permute-start | bytes 270344 | tf_op jit(solution)/shard_map/ppermute | solution.py:557
  35.9 0.1 collective-permute-start.15
  36.0 0.9 %collective-permute-done.13.refs_0_ = f32[176,128]{1,0:T(8,128)S(1)} collective-permute-done((f32[176,128]{1,0:T(8,128)S(1)}, f32[176,128]{1,0:T(8,128)S(1)}, u32[]{:S(2)}, u32[]{:S(2)}) %collective-permute-start.13) | collective-permute-done | bytes 90144 | tf_op jit(solution)/shard_map/ppermute | solution.py:557
  36.9 0.0 collective-permute-done.14.refs_4_
  36.9 2.9 %shard_map.91 = (f32[3,512,128]{2,1,0:T(8,128)}, f32[8,128]{1,0:T(8,128)S(1)}) custom-call(f32[3,512,128]{2,1,0:T(8,128)S(1)} %get-tuple-element.57.state_ref, f32[3,512,128]{2,1,0:T(8,128)S(1)} %get-tuple-element.35.carry_ref, f32[3,512,128]{2,1,0:T(8,128)S(1)} %get-tuple-element.36.weigh_ref, bf16[256,768]{1,0:T(8,128)(2,1)S(1)} %get-tuple-element.37.table_ref, ...), custom_call_target="tpu_custom_call" | custom-call | flops 20000000 | bytes 6148096 | tf_op jit(solution)/shard_map/pallas_call | solution.py:517
  39.8 1.0 %collective-permute-done.10.refs_0_ = f32[176,128]{1,0:T(8,128)S(1)} collective-permute-done((f32[176,128]{1,0:T(8,128)S(1)}, f32[176,128]{1,0:T(8,128)S(1)}, u32[]{:S(2)}, u32[]{:S(2)}) %collective-permute-start.10) | collective-permute-done | bytes 90144 | tf_op jit(solution)/shard_map/ppermute | solution.py:557
  40.8 0.0 collective-permute-done.15.gje_ref
  40.8 1.3 %shard_map.94 = f32[3,512,128]{2,1,0:T(8,128)} custom-call(f32[3,512,128]{2,1,0:T(8,128)S(1)} %get-tuple-element.52.moment_ref, s32[4,8,128]{2,1,0:T(8,128)S(1)} %get-tuple-element.39.index_ref, f32[512,128]{1,0:T(8,128)S(1)} %get-tuple-element.46.refs_1_.inverse_ref.refs_0_, f32[3,512,128]{2,1,0:T(8,128)S(1)} %get-tuple-element.53.joined_ref, ...), custom_call_target="tpu_custom_call" | custom-call | flops 1000000 | bytes 2998272 | tf_op jit(solution)/shard_map/pallas_call | solution.py:517
  (12 shorter events, 0.3 us)
Async XLA Ops:
  2.8 8.5 %collective-permute-start = (f32[232,128]{1,0:T(8,128)S(1)}, f32[232,128]{1,0:T(8,128)S(1)}, u32[]{:S(2)}, u32[]{:S(2)}) collective-permute-start(f32[232,128]{1,0:T(8,128)S(1)} %get-tuple-element.42), channel_id=1, source_target_pairs={{28,4},{29,5},{30,6},{31,7},{0,8},{1,9},{2,10},{3,11},{12,20},{13,... | collective-permute-start | bytes 356360 | tf_op jit(solution)/shard_map/ppermute | solution.py:557
  5.8 5.4 %collective-permute-start.1 = (f32[232,128]{1,0:T(8,128)S(1)}, f32[232,128]{1,0:T(8,128)S(1)}, u32[]{:S(2)}, u32[]{:S(2)}) collective-permute-start(f32[232,128]{1,0:T(8,128)S(1)} %get-tuple-element.43), channel_id=1, source_target_pairs={{4,12},{5,13},{6,14},{7,15},{8,16},{9,17},{10,18},{11,19},{28,29},... | collective-permute-start | bytes 356360 | tf_op jit(solution)/shard_map/ppermute | solution.py:557
  8.1 8.1 %collective-permute-start.4 = (f32[176,128]{1,0:T(8,128)S(1)}, f32[176,128]{1,0:T(8,128)S(1)}, u32[]{:S(2)}, u32[]{:S(2)}) collective-permute-start(f32[176,128]{1,0:T(8,128)S(1)} %get-tuple-element.48), channel_id=1, source_target_pairs={{28,4},{29,5},{30,6},{31,7},{0,8},{1,9},{2,10},{3,11},{12,20},{13,... | collective-permute-start | bytes 270344 | tf_op jit(solution)/shard_map/ppermute | solution.py:557
  11.3 4.9 %collective-permute-start.5 = (f32[176,128]{1,0:T(8,128)S(1)}, f32[176,128]{1,0:T(8,128)S(1)}, u32[]{:S(2)}, u32[]{:S(2)}) collective-permute-start(f32[176,128]{1,0:T(8,128)S(1)} %get-tuple-element.49), channel_id=1, source_target_pairs={{4,12},{5,13},{6,14},{7,15},{8,16},{9,17},{10,18},{11,19},{28,29},... | collective-permute-start | bytes 270344 | tf_op jit(solution)/shard_map/ppermute | solution.py:557
  11.3 8.5 %collective-permute-start.2 = (f32[232,128]{1,0:T(8,128)S(1)}, f32[232,128]{1,0:T(8,128)S(1)}, u32[]{:S(2)}, u32[]{:S(2)}) collective-permute-start(f32[232,128]{1,0:T(8,128)S(1)} %shard_map.78.refs_0_), channel_id=1, source_target_pairs={{29,30},{31,0},{1,2},{5,6},{7,8},{9,10},{13,14},{15,16},{17,18},{2... | collective-permute-start | bytes 356360 | tf_op jit(solution)/shard_map/ppermute | solution.py:557
  16.1 3.7 %collective-permute-start.3 = (f32[232,128]{1,0:T(8,128)S(1)}, f32[232,128]{1,0:T(8,128)S(1)}, u32[]{:S(2)}, u32[]{:S(2)}) collective-permute-start(f32[232,128]{1,0:T(8,128)S(1)} %shard_map.80), channel_id=1, source_target_pairs={{28,29},{30,31},{0,1},{2,3},{4,5},{6,7},{8,9},{10,11},{12,13},{14,... | collective-permute-start | bytes 356360 | tf_op jit(solution)/shard_map/ppermute | solution.py:557
  16.2 9.2 %collective-permute-start.6 = (f32[176,128]{1,0:T(8,128)S(1)}, f32[176,128]{1,0:T(8,128)S(1)}, u32[]{:S(2)}, u32[]{:S(2)}) collective-permute-start(f32[176,128]{1,0:T(8,128)S(1)} %shard_map.83.refs_0_), channel_id=1, source_target_pairs={{29,30},{31,0},{1,2},{5,6},{7,8},{9,10},{13,14},{15,16},{17,18},{2... | collective-permute-start | bytes 270344 | tf_op jit(solution)/shard_map/ppermute | solution.py:557
  19.5 6.0 %collective-permute-start.7 = (f32[176,128]{1,0:T(8,128)S(1)}, f32[176,128]{1,0:T(8,128)S(1)}, u32[]{:S(2)}, u32[]{:S(2)}) collective-permute-start(f32[176,128]{1,0:T(8,128)S(1)} %shard_map.85), channel_id=1, source_target_pairs={{28,29},{30,31},{0,1},{2,3},{4,5},{6,7},{8,9},{10,11},{12,13},{14,... | collective-permute-start | bytes 270344 | tf_op jit(solution)/shard_map/ppermute | solution.py:557
  22.5 6.0 %collective-permute-start.11 = (f32[176,128]{1,0:T(8,128)S(1)}, f32[176,128]{1,0:T(8,128)S(1)}, u32[]{:S(2)}, u32[]{:S(2)}) collective-permute-start(f32[176,128]{1,0:T(8,128)S(1)} %get-tuple-element.59), channel_id=1, source_target_pairs={{28,4},{29,5},{30,6},{31,7},{0,8},{1,9},{2,10},{3,11},{12,20},{13,... | collective-permute-start | bytes 270344 | tf_op jit(solution)/shard_map/ppermute | solution.py:557
  25.3 3.2 %collective-permute-start.12 = (f32[176,128]{1,0:T(8,128)S(1)}, f32[176,128]{1,0:T(8,128)S(1)}, u32[]{:S(2)}, u32[]{:S(2)}) collective-permute-start(f32[176,128]{1,0:T(8,128)S(1)} %get-tuple-element.60), channel_id=1, source_target_pairs={{4,12},{5,13},{6,14},{7,15},{8,16},{9,17},{10,18},{11,19},{28,29},... | collective-permute-start | bytes 270344 | tf_op jit(solution)/shard_map/ppermute | solution.py:557
  28.0 5.1 %collective-permute-start.8 = (f32[176,128]{1,0:T(8,128)S(1)}, f32[176,128]{1,0:T(8,128)S(1)}, u32[]{:S(2)}, u32[]{:S(2)}) collective-permute-start(f32[176,128]{1,0:T(8,128)S(1)} %get-tuple-element.54), channel_id=1, source_target_pairs={{28,4},{29,5},{30,6},{31,7},{0,8},{1,9},{2,10},{3,11},{12,20},{13,... | collective-permute-start | bytes 270344 | tf_op jit(solution)/shard_map/ppermute | solution.py:557
  28.0 5.1 %collective-permute-start.9 = (f32[176,128]{1,0:T(8,128)S(1)}, f32[176,128]{1,0:T(8,128)S(1)}, u32[]{:S(2)}, u32[]{:S(2)}) collective-permute-start(f32[176,128]{1,0:T(8,128)S(1)} %get-tuple-element.55), channel_id=1, source_target_pairs={{4,12},{5,13},{6,14},{7,15},{8,16},{9,17},{10,18},{11,19},{28,29},... | collective-permute-start | bytes 270344 | tf_op jit(solution)/shard_map/ppermute | solution.py:557
  28.5 8.4 %collective-permute-start.13 = (f32[176,128]{1,0:T(8,128)S(1)}, f32[176,128]{1,0:T(8,128)S(1)}, u32[]{:S(2)}, u32[]{:S(2)}) collective-permute-start(f32[176,128]{1,0:T(8,128)S(1)} %shard_map.88.refs_0_), channel_id=1, source_target_pairs={{29,30},{31,0},{1,2},{5,6},{7,8},{9,10},{13,14},{15,16},{17,18},{2... | collective-permute-start | bytes 270344 | tf_op jit(solution)/shard_map/ppermute | solution.py:557
  33.0 3.9 %collective-permute-start.14 = (f32[176,128]{1,0:T(8,128)S(1)}, f32[176,128]{1,0:T(8,128)S(1)}, u32[]{:S(2)}, u32[]{:S(2)}) collective-permute-start(f32[176,128]{1,0:T(8,128)S(1)} %shard_map.90), channel_id=1, source_target_pairs={{28,29},{30,31},{0,1},{2,3},{4,5},{6,7},{8,9},{10,11},{12,13},{14,... | collective-permute-start | bytes 270344 | tf_op jit(solution)/shard_map/ppermute | solution.py:557
  33.1 7.7 %collective-permute-start.10 = (f32[176,128]{1,0:T(8,128)S(1)}, f32[176,128]{1,0:T(8,128)S(1)}, u32[]{:S(2)}, u32[]{:S(2)}) collective-permute-start(f32[176,128]{1,0:T(8,128)S(1)} %shard_map.87.refs_0_), channel_id=1, source_target_pairs={{29,30},{31,0},{1,2},{5,6},{7,8},{9,10},{13,14},{15,16},{17,18},{2... | collective-permute-start | bytes 270344 | tf_op jit(solution)/shard_map/ppermute | solution.py:557
  35.9 4.9 %collective-permute-start.15 = (f32[176,128]{1,0:T(8,128)S(1)}, f32[176,128]{1,0:T(8,128)S(1)}, u32[]{:S(2)}, u32[]{:S(2)}) collective-permute-start(f32[176,128]{1,0:T(8,128)S(1)} %shard_map.93), channel_id=1, source_target_pairs={{28,29},{30,31},{0,1},{2,3},{4,5},{6,7},{8,9},{10,11},{12,13},{14,... | collective-permute-start | bytes 270344 | tf_op jit(solution)/shard_map/ppermute | solution.py:557

commit v9 on v8

--- a/solution.py
+++ b/solution.py
@@ -245,7 +245,7 @@
             face[top_tile(face)] = jnp.where(lane == c, last, others)
 
 
-def add_faces(c, ref, index, ends, got):
+def take_faces(c, index, ends, got, spread_ref):
     height = index[0]
     above = (height + 1) & 127
     own = jnp.full((8, 128), c, jnp.int32)
@@ -256,9 +256,17 @@
                 height < 127, lanes(face[tile(c, 0)], above), lanes(face[top_tile(face)], own)
             )
             parts = [lanes(face[tile(c, k)], height) for k in range(7)] + [last]
+            slot = 2 * axis + jnp.minimum(ends[axis][way], 1)
             for k, part in enumerate(parts):
-                r = face_rows(ends, axis, way, k)
-                ref[r] = ref[r] + (part * ends[2][axis] if way else part)
+                spread_ref[c, slot, pl.ds(8 * k, 8)] = part * ends[2][axis] if way else part
+
+
+def assembled(c, i, j, joined, spread_ref):
+    total = joined[rows(i, j)]
+    for axis, (end, place) in enumerate(((i, j), (j, i))):
+        if end in (0, 7):
+            total = total + spread_ref[c, 2 * axis + end // 7, pl.ds(place, 8, stride=8)]
+    return total
 
 
 def ends_of(columns):
@@ -402,20 +410,21 @@
     index = index_of(index_ref)
     if first:
         got, (inverse_ref, state_out, joined_out), refs = refs[:4], refs[4:7], refs[7:]
-        out, (slope_ref, work_ref, hold_ref) = refs[:4], refs[4:]
-        held = hold_ref.at[0]
-        held[...] = joined_ref[3]
-        add_faces(3, held, index, ends, got)
-        inverse_ref[...] = 1.0 / held[...]
+        out, (slope_ref, work_ref, hold_ref, spread_ref) = refs[:4], refs[4:]
+        take_faces(3, index, ends, got, spread_ref)
+        for i in range(8):
+            for j in range(8):
+                inverse_ref[rows(i, j)] = 1.0 / assembled(3, i, j, joined_ref.at[3], spread_ref)
     else:
         inverse_ref, *got = refs[:5]
-        state_far, token_ref, slope_ref, work_ref, hold_ref, state_out, sent = refs[5:]
+        state_far, token_ref, slope_ref, work_ref, hold_ref, spread_ref, state_out, sent = refs[5:]
         token_ref[...] = jnp.zeros_like(token_ref)
     for f in range(3):
-        held = hold_ref.at[f]
-        held[...] = joined_ref[f]
-        add_faces(f, held, index, ends, got)
-        held[...] = held[...] * inverse_ref[...]
+        take_faces(f, index, ends, got, spread_ref)
+        for i in range(8):
+            for j in range(8):
+                total = assembled(f, i, j, joined_ref.at[f], spread_ref)
+                hold_ref[f, rows(i, j)] = total * inverse_ref[rows(i, j)]
 
     def finish(f):
         if first:
@@ -436,11 +445,13 @@
     return pltpu.make_async_copy(near.at[f], far.at[f], sent.at[f])
 
 
-def moment_step(f, ends, index, moment_ref, joined_ref, inverse_ref, got, hold_ref, moment_out):
-    held = hold_ref.at[f]
-    held[...] = joined_ref[f]
-    add_faces(f, held, index, ends, got)
-    moment_out[f] = moment_ref[f] - held[...] * inverse_ref[...]
+def moment_step(f, ends, index, moment_ref, joined_ref, inverse_ref, got, spread_ref, moment_out):
+    take_faces(f, index, ends, got, spread_ref)
+    for i in range(8):
+        for j in range(8):
+            r = rows(i, j)
+            total = assembled(f, i, j, joined_ref.at[f], spread_ref)
+            moment_out[f, r] = moment_ref[f, r] - total * inverse_ref[r]
 
 
 def middle_kernel(
@@ -465,14 +476,14 @@
     jo_ref,
     slope_ref,
     work_ref,
-    hold_ref,
+    spread_ref,
 ):
     ends = ends_of(columns)
     index = index_of(index_ref)
     out = (ie_ref, io_ref, je_ref, jo_ref)
     got = (gie_ref, gio_ref, gjo_ref, gje_ref)
     for f in range(3):
-        moment_step(f, ends, index, moment_ref, joined_ref, inverse_ref, got, hold_ref, moment_out)
+        moment_step(f, ends, index, moment_ref, joined_ref, inverse_ref, got, spread_ref, moment_out)
 
     def finish(f):
         join_heights(joined_out.at[f], index)
@@ -493,7 +504,7 @@
     gjo_ref,
     gje_ref,
     moment_far,
-    hold_ref,
+    spread_ref,
     moment_out,
     sent,
 ):
@@ -502,7 +513,7 @@
     got = (gie_ref, gio_ref, gjo_ref, gje_ref)
 
     for f in range(3):
-        moment_step(f, ends, index, moment_ref, joined_ref, inverse_ref, got, hold_ref, moment_out)
+        moment_step(f, ends, index, moment_ref, joined_ref, inverse_ref, got, spread_ref, moment_out)
         send_out(f, moment_out, moment_far, sent).start()
     for f in range(3):
         send_out(f, moment_out, moment_far, sent).wait()
@@ -552,6 +563,9 @@
     along_i, along_j = pairings(devices)
     whole, block = ((3, 512, 128), F32), ((512, 128), F32)
     work = pltpu.VMEM((3, 512, 128), F32)
+
+    def spread(count):
+        return pltpu.VMEM((count, 4, 64, 128), F32)
 
     def exchange(block, pairs):
         return lax.ppermute(block, "elem", pairs)
@@ -630,7 +644,7 @@
         functools.partial(state_kernel, columns, True),
         [VMEM] * 11,
         [block, whole, whole] + faces_shape(3),
-        [work] * 3,
+        [work] * 3 + [spread(4)],
         20_000_000,
         state,
         *tables,
@@ -642,7 +656,7 @@
         functools.partial(middle_kernel, columns),
         [VMEM] * 12,
         [whole, whole] + faces_shape(3),
-        [work] * 3,
+        [work] * 2 + [spread(3)],
         20_000_000,
         moment,
         *tables,
@@ -655,7 +669,7 @@
         functools.partial(state_kernel, columns, False),
         [VMEM] * 12,
         [whole, ((8, 128), F32)],
-        [work] * 4 + [pltpu.SemaphoreType.DMA((3,))],
+        [work] * 3 + [spread(3), work] + [pltpu.SemaphoreType.DMA((3,))],
         20_000_000,
         state,
         *tables,
@@ -668,7 +682,7 @@
         functools.partial(last_kernel, columns),
         [VMEM] * 8,
         [whole],
-        [work] * 2 + [pltpu.SemaphoreType.DMA((3,))],
+        [spread(3), work] + [pltpu.SemaphoreType.DMA((3,))],
         1_000_000,
         moment,
         index,

time: 42.3 us -> 41.7 us (0.986)
  Pallas kernels: 14 us -> 12.8 us
  waiting for transfers between devices: 2.2 us -> 3.02 us
    pallas_call x14, Pallas kernels: 14 us -> 12.8 us  [call(): pl.pallas_call(kernel, out_shape=[jax.ShapeDtypeStruct(s, t) for s, t in...]
    ppermute x16, waiting for transfers between devices: 2.2 us -> 3.02 us  [exchange(): return lax.ppermute(block, 'elem', pairs)]
  transfers between devices with their start and end apart: 16 -> 16, of which waited for: 4 -> 4; matrix products, arithmetic and copies ran while one was open for 0% -> 0% of each run, Pallas kernels for 25% -> 23%
where the time goes in v9:
time: 41.7 us; the launch traced here: 41.5 us
  starting transfers between devices  24.9 us (60%)
  Pallas kernels  12.8 us (31%)
  waiting for transfers between devices  3.02 us (7%)
  between operations  0.77 us (2%)
    ppermute x16, starting transfers between devices, exchange(): return lax.ppermute(block, 'elem', pairs)  24.9 us
    pallas_call x14, Pallas kernels, call(): pl.pallas_call(kernel, out_shape=[jax.ShapeDtypeStruct(s, t) for s, t in...  12.8 us
    ppermute x16, waiting for transfers between devices, exchange(): return lax.ppermute(block, 'elem', pairs)  3.02 us
  transfers between devices with their start and end apart: 16, of which 4 were waited for; matrix products, arithmetic and copies ran while one was open for 0% of the time, Pallas kernels for 23%

profile of v9, /device:TPU:0, one launch (start us, length us, event | category | flops | bytes accessed | tf_op | source)
XLA Modules:
  0.0 41.5 jit_solution(3931069153572552213)
XLA Ops:
  0.6 2.1 %shard_map.77 = (f32[3,512,128]{2,1,0:T(8,128)S(1)}, f32[3,512,128]{2,1,0:T(8,128)S(1)}, f32[3,512,128]{2,1,0:T(8,128)S(1)}, f32[3,512,128]{2,1,0:T(8,128)S(1)},...) custom-call(f32[3,512,128]{2,1,0:T(8,128)} %moment_far.1, ...), custom_call_target="tpu_custom_call" | custom-call | flops 1000000 | bytes 8880652 | tf_op jit(solution)/shard_map/pallas_call | solution.py:528
  2.8 3.1 %collective-permute-start = (f32[232,128]{1,0:T(8,128)S(1)}, f32[232,128]{1,0:T(8,128)S(1)}, u32[]{:S(2)}, u32[]{:S(2)}) collective-permute-start(f32[232,128]{1,0:T(8,128)S(1)} %get-tuple-element.42), channel_id=1, source_target_pairs={{28,4},{29,5},{30,6},{31,7},{0,8},{1,9},{2,10},{3,11},{12,20},{13,... | collective-permute-start | bytes 356360 | tf_op jit(solution)/shard_map/ppermute | solution.py:571
  5.8 0.0 collective-permute-start.1
  5.8 2.2 %shard_map.82 = (f32[3,512,128]{2,1,0:T(8,128)S(1)}, f32[176,128]{1,0:T(8,128)S(1)}, f32[176,128]{1,0:T(8,128)S(1)}, f32[176,128]{1,0:T(8,128)S(1)}, f32[176,128]{1,0:T(8,128)S(1)}) custom-call(f32[3,512,128]{2,1,0:T(8,128)S(1)} %get-tuple-element.34.moment_ref, f32[3,512,128]{2,1,0:T(8,128)S(1)} %get-tuple-element.35.carry_ref, ...), custom_call_target="tpu_custom_call" | custom-call | flops 20000000 | bytes 5095424 | tf_op jit(solution)/shard_map/pallas_call | solution.py:528
  8.1 3.2 %collective-permute-start.4 = (f32[176,128]{1,0:T(8,128)S(1)}, f32[176,128]{1,0:T(8,128)S(1)}, u32[]{:S(2)}, u32[]{:S(2)}) collective-permute-start(f32[176,128]{1,0:T(8,128)S(1)} %get-tuple-element.48), channel_id=1, source_target_pairs={{28,4},{29,5},{30,6},{31,7},{0,8},{1,9},{2,10},{3,11},{12,20},{13,... | collective-permute-start | bytes 270344 | tf_op jit(solution)/shard_map/ppermute | solution.py:571
  11.3 0.0 collective-permute-start.5
  11.3 0.0 collective-permute-done.ie_ref.refs_0_
  11.3 0.0 collective-permute-done.1.io_ref.refs_1_
  11.3 4.8 %collective-permute-start.2 = (f32[232,128]{1,0:T(8,128)S(1)}, f32[232,128]{1,0:T(8,128)S(1)}, u32[]{:S(2)}, u32[]{:S(2)}) collective-permute-start(f32[232,128]{1,0:T(8,128)S(1)} %shard_map.78.refs_0_), channel_id=1, source_target_pairs={{29,30},{31,0},{1,2},{5,6},{7,8},{9,10},{13,14},{15,16},{17,18},{2... | collective-permute-start | bytes 356360 | tf_op jit(solution)/shard_map/ppermute | solution.py:571
  16.1 0.1 collective-permute-start.3
  16.2 0.0 collective-permute-done.4.ie_ref.gie_ref
  16.2 0.0 collective-permute-done.5.io_ref.gio_ref
  16.2 3.2 %collective-permute-start.6 = (f32[176,128]{1,0:T(8,128)S(1)}, f32[176,128]{1,0:T(8,128)S(1)}, u32[]{:S(2)}, u32[]{:S(2)}) collective-permute-start(f32[176,128]{1,0:T(8,128)S(1)} %shard_map.83.refs_0_), channel_id=1, source_target_pairs={{29,30},{31,0},{1,2},{5,6},{7,8},{9,10},{13,14},{15,16},{17,18},{2... | collective-permute-start | bytes 270344 | tf_op jit(solution)/shard_map/ppermute | solution.py:571
  19.5 0.1 collective-permute-start.7
  19.6 0.2 collective-permute-done.2.refs_0_
  19.8 0.0 collective-permute-done.3.refs_3_
  19.8 2.3 %shard_map.81 = (f32[512,128]{1,0:T(8,128)S(1)}, f32[3,512,128]{2,1,0:T(8,128)S(1)}, f32[3,512,128]{2,1,0:T(8,128)S(1)}, f32[176,128]{1,0:T(8,128)S(1)}, f32[176...) custom-call(f32[3,512,128]{2,1,0:T(8,128)S(1)} %get-tuple-element.40.state_ref, ...), custom_call_target="tpu_custom_call" | custom-call | flops 20000000 | bytes 7667712 | tf_op jit(solution)/shard_map/pallas_call | solution.py:528
  22.1 2.8 %collective-permute-start.11 = (f32[176,128]{1,0:T(8,128)S(1)}, f32[176,128]{1,0:T(8,128)S(1)}, u32[]{:S(2)}, u32[]{:S(2)}) collective-permute-start(f32[176,128]{1,0:T(8,128)S(1)} %get-tuple-element.59), channel_id=1, source_target_pairs={{28,4},{29,5},{30,6},{31,7},{0,8},{1,9},{2,10},{3,11},{12,20},{13,... | collective-permute-start | bytes 270344 | tf_op jit(solution)/shard_map/ppermute | solution.py:571
  24.9 0.2 collective-permute-start.12
  25.1 0.0 collective-permute-done.6.refs_0_
  25.1 0.0 collective-permute-done.7.gje_ref
  25.1 2.3 %shard_map.86 = (f32[3,512,128]{2,1,0:T(8,128)S(1)}, f32[3,512,128]{2,1,0:T(8,128)S(1)}, f32[176,128]{1,0:T(8,128)S(1)}, f32[176,128]{1,0:T(8,128)S(1)}, f32[176,128]{1,0:T(8,128)S(1)}, /*index=5*/f32[176,128]{1,0:T(8,128)S(1)}) custom-call(f32[3,512,128]{2,1,0:T(8,128)S(1)} %get-tuple-element.34.moment_ref, f32[3,512,128]{2,1,0:T(8,128)S(1)} %get-tuple-element.35.carry_ref, ...), custom_call_target="tpu_custom_call" | custom-call | flops 20000000 | bytes 7290880 | tf_op jit(solution)/shard_map/pallas_call | solution.py:528
  27.3 0.1 collective-permute-start.8
  27.4 0.4 %collective-permute-start.9 = (f32[176,128]{1,0:T(8,128)S(1)}, f32[176,128]{1,0:T(8,128)S(1)}, u32[]{:S(2)}, u32[]{:S(2)}) collective-permute-start(f32[176,128]{1,0:T(8,128)S(1)} %get-tuple-element.55), channel_id=1, source_target_pairs={{4,12},{5,13},{6,14},{7,15},{8,16},{9,17},{10,18},{11,19},{28,29},... | collective-permute-start | bytes 270344 | tf_op jit(solution)/shard_map/ppermute | solution.py:571
  27.8 0.3 collective-permute-done.11.ie_ref.refs_1_
  28.1 0.0 collective-permute-done.12.io_ref.refs_2_
  28.1 4.4 %collective-permute-start.13 = (f32[176,128]{1,0:T(8,128)S(1)}, f32[176,128]{1,0:T(8,128)S(1)}, u32[]{:S(2)}, u32[]{:S(2)}) collective-permute-start(f32[176,128]{1,0:T(8,128)S(1)} %shard_map.88.refs_0_), channel_id=1, source_target_pairs={{29,30},{31,0},{1,2},{5,6},{7,8},{9,10},{13,14},{15,16},{17,18},{2... | collective-permute-start | bytes 270344 | tf_op jit(solution)/shard_map/ppermute | solution.py:571
  32.6 0.1 collective-permute-start.14
  32.6 0.0 collective-permute-done.8.ie_ref.gie_ref
  32.7 0.0 collective-permute-done.9.io_ref.gio_ref
  32.7 2.6 %collective-permute-start.10 = (f32[176,128]{1,0:T(8,128)S(1)}, f32[176,128]{1,0:T(8,128)S(1)}, u32[]{:S(2)}, u32[]{:S(2)}) collective-permute-start(f32[176,128]{1,0:T(8,128)S(1)} %shard_map.87.refs_0_), channel_id=1, source_target_pairs={{29,30},{31,0},{1,2},{5,6},{7,8},{9,10},{13,14},{15,16},{17,18},{2... | collective-permute-start | bytes 270344 | tf_op jit(solution)/shard_map/ppermute | solution.py:571
  35.3 0.1 collective-permute-start.15
  35.4 0.9 %collective-permute-done.13.refs_0_ = f32[176,128]{1,0:T(8,128)S(1)} collective-permute-done((f32[176,128]{1,0:T(8,128)S(1)}, f32[176,128]{1,0:T(8,128)S(1)}, u32[]{:S(2)}, u32[]{:S(2)}) %collective-permute-start.13) | collective-permute-done | bytes 90144 | tf_op jit(solution)/shard_map/ppermute | solution.py:571
  36.3 0.0 collective-permute-done.14.refs_4_
  36.3 2.6 %shard_map.91 = (f32[3,512,128]{2,1,0:T(8,128)}, f32[8,128]{1,0:T(8,128)S(1)}) custom-call(f32[3,512,128]{2,1,0:T(8,128)S(1)} %get-tuple-element.57.state_ref, f32[3,512,128]{2,1,0:T(8,128)S(1)} %get-tuple-element.35.carry_ref, f32[3,512,128]{2,1,0:T(8,128)S(1)} %get-tuple-element.36.weigh_ref, bf16[256,768]{1,0:T(8,128)(2,1)S(1)} %get-tuple-element.37.table_ref, ...), custom_call_target="tpu_custom_call" | custom-call | flops 20000000 | bytes 6148096 | tf_op jit(solution)/shard_map/pallas_call | solution.py:528
  38.9 1.6 %collective-permute-done.10.refs_0_ = f32[176,128]{1,0:T(8,128)S(1)} collective-permute-done((f32[176,128]{1,0:T(8,128)S(1)}, f32[176,128]{1,0:T(8,128)S(1)}, u32[]{:S(2)}, u32[]{:S(2)}) %collective-permute-start.10) | collective-permute-done | bytes 90144 | tf_op jit(solution)/shard_map/ppermute | solution.py:571
  40.4 0.0 collective-permute-done.15.gje_ref
  40.4 1.1 %shard_map.94 = f32[3,512,128]{2,1,0:T(8,128)} custom-call(f32[3,512,128]{2,1,0:T(8,128)S(1)} %get-tuple-element.52.moment_ref, s32[4,8,128]{2,1,0:T(8,128)S(1)} %get-tuple-element.39.index_ref, f32[512,128]{1,0:T(8,128)S(1)} %get-tuple-element.46.refs_1_.inverse_ref.refs_0_, f32[3,512,128]{2,1,0:T(8,128)S(1)} %get-tuple-element.53.joined_ref, ...), custom_call_target="tpu_custom_call" | custom-call | flops 1000000 | bytes 2998272 | tf_op jit(solution)/shard_map/pallas_call | solution.py:528
  (12 shorter events, 0.3 us)
Async XLA Ops:
  2.8 8.5 %collective-permute-start = (f32[232,128]{1,0:T(8,128)S(1)}, f32[232,128]{1,0:T(8,128)S(1)}, u32[]{:S(2)}, u32[]{:S(2)}) collective-permute-start(f32[232,128]{1,0:T(8,128)S(1)} %get-tuple-element.42), channel_id=1, source_target_pairs={{28,4},{29,5},{30,6},{31,7},{0,8},{1,9},{2,10},{3,11},{12,20},{13,... | collective-permute-start | bytes 356360 | tf_op jit(solution)/shard_map/ppermute | solution.py:571
  5.8 5.4 %collective-permute-start.1 = (f32[232,128]{1,0:T(8,128)S(1)}, f32[232,128]{1,0:T(8,128)S(1)}, u32[]{:S(2)}, u32[]{:S(2)}) collective-permute-start(f32[232,128]{1,0:T(8,128)S(1)} %get-tuple-element.43), channel_id=1, source_target_pairs={{4,12},{5,13},{6,14},{7,15},{8,16},{9,17},{10,18},{11,19},{28,29},... | collective-permute-start | bytes 356360 | tf_op jit(solution)/shard_map/ppermute | solution.py:571
  8.1 8.1 %collective-permute-start.4 = (f32[176,128]{1,0:T(8,128)S(1)}, f32[176,128]{1,0:T(8,128)S(1)}, u32[]{:S(2)}, u32[]{:S(2)}) collective-permute-start(f32[176,128]{1,0:T(8,128)S(1)} %get-tuple-element.48), channel_id=1, source_target_pairs={{28,4},{29,5},{30,6},{31,7},{0,8},{1,9},{2,10},{3,11},{12,20},{13,... | collective-permute-start | bytes 270344 | tf_op jit(solution)/shard_map/ppermute | solution.py:571
  11.3 4.9 %collective-permute-start.5 = (f32[176,128]{1,0:T(8,128)S(1)}, f32[176,128]{1,0:T(8,128)S(1)}, u32[]{:S(2)}, u32[]{:S(2)}) collective-permute-start(f32[176,128]{1,0:T(8,128)S(1)} %get-tuple-element.49), channel_id=1, source_target_pairs={{4,12},{5,13},{6,14},{7,15},{8,16},{9,17},{10,18},{11,19},{28,29},... | collective-permute-start | bytes 270344 | tf_op jit(solution)/shard_map/ppermute | solution.py:571
  11.3 8.5 %collective-permute-start.2 = (f32[232,128]{1,0:T(8,128)S(1)}, f32[232,128]{1,0:T(8,128)S(1)}, u32[]{:S(2)}, u32[]{:S(2)}) collective-permute-start(f32[232,128]{1,0:T(8,128)S(1)} %shard_map.78.refs_0_), channel_id=1, source_target_pairs={{29,30},{31,0},{1,2},{5,6},{7,8},{9,10},{13,14},{15,16},{17,18},{2... | collective-permute-start | bytes 356360 | tf_op jit(solution)/shard_map/ppermute | solution.py:571
  16.1 3.7 %collective-permute-start.3 = (f32[232,128]{1,0:T(8,128)S(1)}, f32[232,128]{1,0:T(8,128)S(1)}, u32[]{:S(2)}, u32[]{:S(2)}) collective-permute-start(f32[232,128]{1,0:T(8,128)S(1)} %shard_map.80), channel_id=1, source_target_pairs={{28,29},{30,31},{0,1},{2,3},{4,5},{6,7},{8,9},{10,11},{12,13},{14,... | collective-permute-start | bytes 356360 | tf_op jit(solution)/shard_map/ppermute | solution.py:571
  16.2 8.8 %collective-permute-start.6 = (f32[176,128]{1,0:T(8,128)S(1)}, f32[176,128]{1,0:T(8,128)S(1)}, u32[]{:S(2)}, u32[]{:S(2)}) collective-permute-start(f32[176,128]{1,0:T(8,128)S(1)} %shard_map.83.refs_0_), channel_id=1, source_target_pairs={{29,30},{31,0},{1,2},{5,6},{7,8},{9,10},{13,14},{15,16},{17,18},{2... | collective-permute-start | bytes 270344 | tf_op jit(solution)/shard_map/ppermute | solution.py:571
  19.5 5.6 %collective-permute-start.7 = (f32[176,128]{1,0:T(8,128)S(1)}, f32[176,128]{1,0:T(8,128)S(1)}, u32[]{:S(2)}, u32[]{:S(2)}) collective-permute-start(f32[176,128]{1,0:T(8,128)S(1)} %shard_map.85), channel_id=1, source_target_pairs={{28,29},{30,31},{0,1},{2,3},{4,5},{6,7},{8,9},{10,11},{12,13},{14,... | collective-permute-start | bytes 270344 | tf_op jit(solution)/shard_map/ppermute | solution.py:571
  22.1 6.0 %collective-permute-start.11 = (f32[176,128]{1,0:T(8,128)S(1)}, f32[176,128]{1,0:T(8,128)S(1)}, u32[]{:S(2)}, u32[]{:S(2)}) collective-permute-start(f32[176,128]{1,0:T(8,128)S(1)} %get-tuple-element.59), channel_id=1, source_target_pairs={{28,4},{29,5},{30,6},{31,7},{0,8},{1,9},{2,10},{3,11},{12,20},{13,... | collective-permute-start | bytes 270344 | tf_op jit(solution)/shard_map/ppermute | solution.py:571
  24.9 3.2 %collective-permute-start.12 = (f32[176,128]{1,0:T(8,128)S(1)}, f32[176,128]{1,0:T(8,128)S(1)}, u32[]{:S(2)}, u32[]{:S(2)}) collective-permute-start(f32[176,128]{1,0:T(8,128)S(1)} %get-tuple-element.60), channel_id=1, source_target_pairs={{4,12},{5,13},{6,14},{7,15},{8,16},{9,17},{10,18},{11,19},{28,29},... | collective-permute-start | bytes 270344 | tf_op jit(solution)/shard_map/ppermute | solution.py:571
  27.3 5.3 %collective-permute-start.8 = (f32[176,128]{1,0:T(8,128)S(1)}, f32[176,128]{1,0:T(8,128)S(1)}, u32[]{:S(2)}, u32[]{:S(2)}) collective-permute-start(f32[176,128]{1,0:T(8,128)S(1)} %get-tuple-element.54), channel_id=1, source_target_pairs={{28,4},{29,5},{30,6},{31,7},{0,8},{1,9},{2,10},{3,11},{12,20},{13,... | collective-permute-start | bytes 270344 | tf_op jit(solution)/shard_map/ppermute | solution.py:571
  27.4 5.3 %collective-permute-start.9 = (f32[176,128]{1,0:T(8,128)S(1)}, f32[176,128]{1,0:T(8,128)S(1)}, u32[]{:S(2)}, u32[]{:S(2)}) collective-permute-start(f32[176,128]{1,0:T(8,128)S(1)} %get-tuple-element.55), channel_id=1, source_target_pairs={{4,12},{5,13},{6,14},{7,15},{8,16},{9,17},{10,18},{11,19},{28,29},... | collective-permute-start | bytes 270344 | tf_op jit(solution)/shard_map/ppermute | solution.py:571
  28.1 8.1 %collective-permute-start.13 = (f32[176,128]{1,0:T(8,128)S(1)}, f32[176,128]{1,0:T(8,128)S(1)}, u32[]{:S(2)}, u32[]{:S(2)}) collective-permute-start(f32[176,128]{1,0:T(8,128)S(1)} %shard_map.88.refs_0_), channel_id=1, source_target_pairs={{29,30},{31,0},{1,2},{5,6},{7,8},{9,10},{13,14},{15,16},{17,18},{2... | collective-permute-start | bytes 270344 | tf_op jit(solution)/shard_map/ppermute | solution.py:571
  32.6 3.7 %collective-permute-start.14 = (f32[176,128]{1,0:T(8,128)S(1)}, f32[176,128]{1,0:T(8,128)S(1)}, u32[]{:S(2)}, u32[]{:S(2)}) collective-permute-start(f32[176,128]{1,0:T(8,128)S(1)} %shard_map.90), channel_id=1, source_target_pairs={{28,29},{30,31},{0,1},{2,3},{4,5},{6,7},{8,9},{10,11},{12,13},{14,... | collective-permute-start | bytes 270344 | tf_op jit(solution)/shard_map/ppermute | solution.py:571
  32.7 7.7 %collective-permute-start.10 = (f32[176,128]{1,0:T(8,128)S(1)}, f32[176,128]{1,0:T(8,128)S(1)}, u32[]{:S(2)}, u32[]{:S(2)}) collective-permute-start(f32[176,128]{1,0:T(8,128)S(1)} %shard_map.87.refs_0_), channel_id=1, source_target_pairs={{29,30},{31,0},{1,2},{5,6},{7,8},{9,10},{13,14},{15,16},{17,18},{2... | collective-permute-start | bytes 270344 | tf_op jit(solution)/shard_map/ppermute | solution.py:571
  35.3 5.1 %collective-permute-start.15 = (f32[176,128]{1,0:T(8,128)S(1)}, f32[176,128]{1,0:T(8,128)S(1)}, u32[]{:S(2)}, u32[]{:S(2)}) collective-permute-start(f32[176,128]{1,0:T(8,128)S(1)} %shard_map.93), channel_id=1, source_target_pairs={{28,29},{30,31},{0,1},{2,3},{4,5},{6,7},{8,9},{10,11},{12,13},{14,... | collective-permute-start | bytes 270344 | tf_op jit(solution)/shard_map/ppermute | solution.py:571

commit v10 on v9

--- a/solution.py
+++ b/solution.py
@@ -85,36 +85,62 @@
     return pl.ds((8 * i + j) * 8, 8)
 
 
-def along_k(table_ref, block):
+def split(block):
     wide = jnp.concatenate([block[:256], block[256:]], axis=1)
     high = wide.astype(BF16)
     low = (wide - high.astype(F32)).astype(BF16)
-    parts = jnp.concatenate([high, high, low], axis=0)
+    return [high, high, low]
+
+
+def tall(wide):
+    return jnp.concatenate([wide[:, :128], wide[:, 128:]], axis=0)
+
+
+def slopes_jk(table_ref, block):
+    parts = jnp.concatenate(split(block), axis=0)
     out = jnp.dot(table_ref[...], parts, preferred_element_type=F32)
-    return jnp.concatenate([out[:, :128], out[:, 128:]], axis=0)
-
-
-def write_table(table, table_ref):
+    return tall(out[:256]), tall(out[256:])
+
+
+def back_jk(turned_ref, flux_k, flux_j):
+    parts = jnp.concatenate(split(flux_k) + split(flux_j), axis=0)
+    return tall(jnp.dot(turned_ref[...], parts, preferred_element_type=F32))
+
+
+def write_table(table, axis, table_ref, start, column):
     sub = lax.broadcasted_iota(jnp.int32, (8, 128), 0)
     lane = lax.broadcasted_iota(jnp.int32, (8, 128), 1)
-    base = jnp.zeros((8, 128), F32)
-    for i in range(8):
-        one_row = jnp.zeros((8, 128), F32)
+    zero = jnp.zeros((8, 128), F32)
+    place = lax.shift_right_logical(lane, 3)
+    entry = place & 7 if axis else lane & 7
+    bases = []
+    for n in range(8):
+        one_row = zero
         for q in range(8):
-            one_row = jnp.where((lane & 7) == q, float(table[i, q]), one_row)
-        base = jnp.where(sub == i, one_row, base)
-    high = base.astype(BF16).astype(F32)
-    block = lax.shift_right_logical(lane, 3)
-    zero = jnp.zeros((8, 128), F32)
+            one_row = jnp.where(entry == q, float(table[n, q]), one_row)
+        bases.append(one_row)
+    if axis:
+        bases = [jnp.where((lane & 7) == sub, one_row, zero) for one_row in bases]
+        place = lax.shift_right_logical(lane, 6)
+    else:
+        base = zero
+        for n in range(8):
+            base = jnp.where(sub == n, bases[n], base)
+        bases = [base]
+    highs = [base.astype(BF16).astype(F32) for base in bases]
+    lows = [base - high for base, high in zip(bases, highs)]
     empty = jnp.zeros((16, 128), F32)
     for a in range(0, 32, 2):
         parts = []
-        for values in (high, base - high):
-            pair = [jnp.where(block == (a + n) % 16, values, zero) for n in range(2)]
+        for values in (highs, lows):
+            pair = []
+            for block in (a, a + 1):
+                own = place == (block // 8 % 2 if axis else block % 16)
+                pair.append(jnp.where(own, values[block % 8 if axis else 0], zero))
             pair = jnp.concatenate(pair, axis=0)
             parts.append([pair, empty] if a < 16 else [empty, pair])
         wide = jnp.concatenate(parts[0] + parts[1] + parts[0], axis=1)
-        table_ref[pl.ds(8 * a, 16)] = wide.astype(BF16)
+        table_ref[pl.ds(start + 8 * a, 16), column : column + 768] = wide.astype(BF16)
 
 
 def lanes(block, index):
@@ -133,79 +159,64 @@
             mass_ref[r] = weight_ref[r] * (along * float(WEIGHTS[i] * WEIGHTS[j]))
 
 
-def slope_k(source, table_ref, slope):
-    slope[...] = along_k(table_ref, source[...])
-
-
-def forward_k(carry_ref, weigh, turned_ref, slope, work):
-    work[...] = carry_ref[2] * slope[...] + along_k(turned_ref, weigh[...] * slope[...])
-
-
-def adjoint_k(source, carry_ref, weigh, turned_ref, slope, work):
-    work[...] = along_k(turned_ref, carry_ref[2] * source[...] + weigh[...] * slope[...])
-
-
-def forward_i(source, carry_ref, weigh, target):
+def forward_jk(carry_ref, weigh, turned_ref, slope, work):
+    fluxes = weigh[...] * slope[0], weigh[...] * slope[1]
+    carried = carry_ref[2] * slope[0] + carry_ref[1] * slope[1]
+    work[...] = carried + back_jk(turned_ref, *fluxes)
+
+
+def adjoint_jk(source, carry_ref, weigh, turned_ref, slope, work):
+    flux_k = carry_ref[2] * source[...] + weigh[...] * slope[0]
+    flux_j = carry_ref[1] * source[...] + weigh[...] * slope[1]
+    work[...] = back_jk(turned_ref, flux_k, flux_j)
+
+
+def forward_i(source, carry_ref, weigh, work, target):
     for j in range(8):
         slopes = line(DM, [source[rows(i, j)] for i in range(8)])
         back = line(DM.T, [weigh[rows(i, j)] * slopes[i] for i in range(8)])
         for i in range(8):
             r = rows(i, j)
-            target[r] = carry_ref[0, r] * slopes[i] + back[i]
-
-
-def forward_j(source, carry_ref, weigh, work, target):
-    for i in range(8):
-        slopes = line(DM, [source[rows(i, j)] for j in range(8)])
-        back = line(DM.T, [weigh[rows(i, j)] * slopes[j] for j in range(8)])
-        for j in range(8):
-            r = rows(i, j)
-            target[r] = target[r] + (carry_ref[1, r] * slopes[j] + (back[j] + work[r]))
-
-
-def adjoint_lines(d, source, carry_ref, weigh, line_rows):
-    for these in line_rows:
+            target[r] = work[r] + (carry_ref[0, r] * slopes[i] + back[i])
+
+
+def adjoint_i(source, base, carry_ref, weigh, work, target):
+    for j in range(8):
+        these = [rows(i, j) for i in range(8)]
         values = [source[r] for r in these]
         slopes = line(DM, values)
-        fluxes = [carry_ref[d, r] * v + weigh[r] * g for r, v, g in zip(these, values, slopes)]
-        yield from zip(these, line(DM.T, fluxes))
-
-
-def adjoint_i(source, base, carry_ref, weigh, target):
-    lines = [[rows(i, j) for i in range(8)] for j in range(8)]
-    for r, back in adjoint_lines(0, source, carry_ref, weigh, lines):
-        target[r] = base[r] - back
-
-
-def adjoint_j(source, carry_ref, weigh, work, target):
-    lines = [[rows(i, j) for j in range(8)] for i in range(8)]
-    for r, back in adjoint_lines(1, source, carry_ref, weigh, lines):
-        target[r] = target[r] - (back + work[r])
+        fluxes = [carry_ref[0, r] * v + weigh[r] * g for r, v, g in zip(these, values, slopes)]
+        for r, back in zip(these, line(DM.T, fluxes)):
+            target[r] = base[r] - (back + work[r])
+
+
+def set_slopes(source, table_ref, slope):
+    slope[0], slope[1] = slopes_jk(table_ref, source[...])
 
 
 def forward(sources, carry_ref, weigh_ref, table_ref, turned_ref, slope_ref, work_ref, target, finish):
-    slope_k(sources.at[0], table_ref, slope_ref.at[0])
+    for f in range(3):
+        set_slopes(sources.at[f], table_ref, slope_ref.at[f])
     for f in range(3):
         at = (carry_ref, weigh_ref.at[f])
-        forward_i(sources.at[f], *at, target.at[f])
-        forward_k(*at, turned_ref, slope_ref.at[f], work_ref.at[f])
-        if f < 2:
-            slope_k(sources.at[f + 1], table_ref, slope_ref.at[f + 1])
-        forward_j(sources.at[f], *at, work_ref.at[f], target.at[f])
+        forward_jk(*at, turned_ref, slope_ref.at[f], work_ref.at[f])
+    for f in range(3):
+        at = (carry_ref, weigh_ref.at[f])
+        forward_i(sources.at[f], *at, work_ref.at[f], target.at[f])
         finish(f)
 
 
 def adjoint(
     sources, base, carry_ref, weigh_ref, table_ref, turned_ref, slope_ref, work_ref, target, finish
 ):
-    slope_k(sources.at[0], table_ref, slope_ref.at[0])
+    for f in range(3):
+        set_slopes(sources.at[f], table_ref, slope_ref.at[f])
     for f in range(3):
         at = (carry_ref, weigh_ref.at[f])
-        adjoint_i(sources.at[f], base.at[f], *at, target.at[f])
-        adjoint_k(sources.at[f], *at, turned_ref, slope_ref.at[f], work_ref.at[f])
-        if f < 2:
-            slope_k(sources.at[f + 1], table_ref, slope_ref.at[f + 1])
-        adjoint_j(sources.at[f], *at, work_ref.at[f], target.at[f])
+        adjoint_jk(sources.at[f], *at, turned_ref, slope_ref.at[f], work_ref.at[f])
+    for f in range(3):
+        at = (carry_ref, weigh_ref.at[f])
+        adjoint_i(sources.at[f], base.at[f], *at, work_ref.at[f], target.at[f])
         finish(f)
 
 
@@ -251,7 +262,7 @@
     own = jnp.full((8, 128), c, jnp.int32)
     for axis in range(2):
         for way in range(2):
-            face = got[3 - way if axis else way]
+            face = got[2 * axis + way]
             last = jnp.where(
                 height < 127, lanes(face[tile(c, 0)], above), lanes(face[top_tile(face)], own)
             )
@@ -318,8 +329,9 @@
     copies = [pltpu.make_async_copy(a, b, arrived.at[n]) for n, (a, b) in enumerate(zip(far, near))]
     for copy in copies:
         copy.start()
-    write_table(DM, table_ref)
-    write_table(DM.T, turned_ref)
+    for axis in range(2):
+        write_table(DM, axis, table_ref, 256 * axis, 0)
+        write_table(DM.T, axis, turned_ref, 0, 768 * axis)
     ends = ends_of(columns)
     copies[0].wait()
     height = jnp.broadcast_to(numbers_ref[...] & 127, (8, 128))
@@ -383,15 +395,15 @@
     forward(moment_ref, *at, joined_ref, finish)
 
 
-def edge_kernel(columns, way, ie_ref, io_ref, face, *refs):
+def edge_kernel(columns, axis, way, e_ref, o_ref, face, *refs):
     ends, out = ends_of(columns), refs[-1]
     out[...] = face[...]
     tiles = face.shape[0] // 8
-    r = pl.ds(ends[1][way], tiles, stride=8)
-    for other, got in enumerate((ie_ref, io_ref)):
-        w = pl.ds(ends[0][other], tiles, stride=8)
+    r = pl.ds(ends[axis][way], tiles, stride=8)
+    for other, got in enumerate((e_ref, o_ref)):
+        w = pl.ds(ends[1 - axis][other], tiles, stride=8)
         part = got[r]
-        out[w] = out[w] + (part * ends[2][0] if other else part)
+        out[w] = out[w] + (part * ends[2][1 - axis] if other else part)
 
 
 def state_kernel(
@@ -417,8 +429,7 @@
                 inverse_ref[rows(i, j)] = 1.0 / assembled(3, i, j, joined_ref.at[3], spread_ref)
     else:
         inverse_ref, *got = refs[:5]
-        state_far, token_ref, slope_ref, work_ref, hold_ref, spread_ref, state_out, sent = refs[5:]
-        token_ref[...] = jnp.zeros_like(token_ref)
+        state_far, slope_ref, work_ref, hold_ref, spread_ref, state_out, sent = refs[5:]
     for f in range(3):
         take_faces(f, index, ends, got, spread_ref)
         for i in range(8):
@@ -466,8 +477,8 @@
     joined_ref,
     gie_ref,
     gio_ref,
+    gje_ref,
     gjo_ref,
-    gje_ref,
     moment_out,
     joined_out,
     ie_ref,
@@ -481,7 +492,7 @@
     ends = ends_of(columns)
     index = index_of(index_ref)
     out = (ie_ref, io_ref, je_ref, jo_ref)
-    got = (gie_ref, gio_ref, gjo_ref, gje_ref)
+    got = (gie_ref, gio_ref, gje_ref, gjo_ref)
     for f in range(3):
         moment_step(f, ends, index, moment_ref, joined_ref, inverse_ref, got, spread_ref, moment_out)
 
@@ -501,8 +512,8 @@
     joined_ref,
     gie_ref,
     gio_ref,
+    gje_ref,
     gjo_ref,
-    gje_ref,
     moment_far,
     spread_ref,
     moment_out,
@@ -510,7 +521,7 @@
 ):
     ends = ends_of(columns)
     index = index_of(index_ref)
-    got = (gie_ref, gio_ref, gjo_ref, gje_ref)
+    got = (gie_ref, gio_ref, gje_ref, gjo_ref)
 
     for f in range(3):
         moment_step(f, ends, index, moment_ref, joined_ref, inverse_ref, got, spread_ref, moment_out)
@@ -563,6 +574,7 @@
     along_i, along_j = pairings(devices)
     whole, block = ((3, 512, 128), F32), ((512, 128), F32)
     work = pltpu.VMEM((3, 512, 128), F32)
+    slopes = pltpu.VMEM((3, 2, 512, 128), F32)
 
     def spread(count):
         return pltpu.VMEM((count, 4, 64, 128), F32)
@@ -570,20 +582,20 @@
     def exchange(block, pairs):
         return lax.ppermute(block, "elem", pairs)
 
-    def settle(block, *after):
+    def settle(block):
         anywhere = pl.BlockSpec(memory_space=pl.ANY)
         return pl.pallas_call(
             lambda *refs: None,
             out_shape=jax.ShapeDtypeStruct(block.shape, block.dtype),
-            in_specs=[anywhere] * (1 + len(after)),
+            in_specs=[anywhere],
             out_specs=anywhere,
             input_output_aliases={0: 0},
             compiler_params=pltpu.CompilerParams(vmem_limit_bytes=1024 * 1024),
-        )(block, *after)
-
-    def edge(count, way, *operands):
+        )(block)
+
+    def edge(count, axis, way, *operands):
         return call(
-            functools.partial(edge_kernel, columns, way),
+            functools.partial(edge_kernel, columns, axis, way),
             [VMEM] * len(operands),
             [(face_shape(count), F32)],
             [],
@@ -591,14 +603,19 @@
             *operands,
         )[0]
 
-    def meet(count, faces):
-        got_i = [exchange(faces[way], along_i[way]) for way in range(2)]
-        far_face = edge(count, 1, *got_i, faces[3])
-        near_face = edge(count, 0, *got_i, faces[2], far_face)
-        return got_i + [exchange(far_face, along_j[1]), exchange(near_face, along_j[0])]
-
-    def settled(got, *after):
-        return got[:2] + [settle(got[2], *after), got[3]]
+    def meet_ij(count, faces):
+        got = [exchange(faces[way], along_i[way]) for way in range(2)]
+        far_face = edge(count, 1, 1, *got, faces[3])
+        near_face = edge(count, 1, 0, *got, faces[2], far_face)
+        far_face, near_face = exchange(far_face, along_j[1]), exchange(near_face, along_j[0])
+        return got + [near_face, settle(far_face)]
+
+    def meet_ji(count, faces):
+        got = [exchange(faces[2 + way], along_j[way]) for way in range(2)]
+        got[1] = settle(got[1])
+        face_e = edge(count, 0, 0, *got, faces[0])
+        face_o = edge(count, 0, 1, *got, faces[1])
+        return [exchange(face_e, along_i[0]), exchange(face_o, along_i[1])] + got
 
     def far(array):
         return pltpu.with_memory_space_constraint(array, pltpu.HBM)
@@ -613,7 +630,7 @@
         functools.partial(index_kernel, columns),
         [FAR] * 6,
         [whole] * 4
-        + [((256, 768), BF16)] * 2
+        + [((512, 768), BF16), ((256, 1536), BF16)]
         + [((4, 8, 128), jnp.int32), ((4, 512, 128), F32)]
         + faces_shape(4),
         [
@@ -629,53 +646,53 @@
         *map(far, (diffusivity, numbering.reshape(1, 128))),
     )
     tables = (carry, weigh, table, turned, index)
-    got_state = meet(4, faces_state)
+    got_state = meet_ij(4, faces_state)
     joined_moment, *faces_moment = call(
         functools.partial(moment_kernel, columns),
         [VMEM] * 6,
         [whole] + faces_shape(3),
-        [work] * 2,
+        [slopes, work],
         20_000_000,
         moment,
         *tables,
     )
-    got_moment = meet(3, faces_moment)
+    got_moment = meet_ji(3, faces_moment)
     inverse, state, joined_state, *faces_state = call(
         functools.partial(state_kernel, columns, True),
         [VMEM] * 11,
         [block, whole, whole] + faces_shape(3),
-        [work] * 3 + [spread(4)],
+        [slopes, work, work, spread(4)],
         20_000_000,
         state,
         *tables,
         joined_state,
-        *settled(got_state),
-    )
-    got_state = meet(3, faces_state)
+        *got_state,
+    )
+    got_state = meet_ij(3, faces_state)
     moment, joined_moment, *faces_moment = call(
         functools.partial(middle_kernel, columns),
         [VMEM] * 12,
         [whole, whole] + faces_shape(3),
-        [work] * 2 + [spread(3)],
+        [slopes, work, spread(3)],
         20_000_000,
         moment,
         *tables,
         inverse,
         joined_moment,
-        *settled(got_moment, inverse),
-    )
-    got_moment = meet(3, faces_moment)
-    state, token = call(
+        *got_moment,
+    )
+    got_moment = meet_ji(3, faces_moment)
+    (state,) = call(
         functools.partial(state_kernel, columns, False),
         [VMEM] * 12,
-        [whole, ((8, 128), F32)],
-        [work] * 3 + [spread(3), work] + [pltpu.SemaphoreType.DMA((3,))],
+        [whole],
+        [slopes, work, work, spread(3), work] + [pltpu.SemaphoreType.DMA((3,))],
         20_000_000,
         state,
         *tables,
         joined_state,
         inverse,
-        *settled(got_state),
+        *got_state,
         first_out=FAR,
     )
     (moment,) = call(
@@ -688,7 +705,7 @@
         index,
         inverse,
         joined_moment,
-        *settled(got_moment, token),
+        *got_moment,
         first_out=FAR,
     )
     return moment, state

time: 41.7 us -> 43.3 us (1.038)
  waiting for transfers between devices: 3.02 us -> 8.65 us
  starting transfers between devices: 24.9 us -> 21.1 us
    ppermute x16, waiting for transfers between devices: 3.02 us -> 8.65 us  [exchange(): return lax.ppermute(block, 'elem', pairs)]
    ppermute x16, starting transfers between devices: 24.9 us -> 21.1 us  [exchange(): return lax.ppermute(block, 'elem', pairs)]
  transfers between devices with their start and end apart: 16 -> 16, of which waited for: 4 -> 4; matrix products, arithmetic and copies ran while one was open for 0% -> 0% of each run, Pallas kernels for 23% -> 22%
where the time goes in v10:
time: 43.3 us; the launch traced here: 43.2 us
  starting transfers between devices  21.1 us (49%)
  Pallas kernels  12.8 us (30%)
  waiting for transfers between devices  8.65 us (20%)
  between operations  0.74 us (2%)
    ppermute x16, starting transfers between devices, exchange(): return lax.ppermute(block, 'elem', pairs)  21.1 us
    pallas_call x14, Pallas kernels, call(): pl.pallas_call(kernel, out_shape=[jax.ShapeDtypeStruct(s, t) for s, t in...  12.8 us
    ppermute x16, waiting for transfers between devices, exchange(): return lax.ppermute(block, 'elem', pairs)  8.65 us
  transfers between devices with their start and end apart: 16, of which 4 were waited for; matrix products, arithmetic and copies ran while one was open for 0% of the time, Pallas kernels for 22%

profile of v10, /device:TPU:0, one launch (start us, length us, event | category | flops | bytes accessed | tf_op | source)
XLA Modules:
  0.0 43.2 jit_solution(15836616816245077308)
XLA Ops:
  0.6 2.1 %shard_map.77 = (f32[3,512,128]{2,1,0:T(8,128)S(1)}, f32[3,512,128]{2,1,0:T(8,128)S(1)}, f32[3,512,128]{2,1,0:T(8,128)S(1)}, f32[3,512,128]{2,1,0:T(8,128)S(1)},...) custom-call(f32[3,512,128]{2,1,0:T(8,128)} %moment_far.1, ...), custom_call_target="tpu_custom_call" | custom-call | flops 1000000 | bytes 10453516 | tf_op jit(solution)/shard_map/pallas_call | solution.py:539
  2.8 3.1 %collective-permute-start = (f32[232,128]{1,0:T(8,128)S(1)}, f32[232,128]{1,0:T(8,128)S(1)}, u32[]{:S(2)}, u32[]{:S(2)}) collective-permute-start(f32[232,128]{1,0:T(8,128)S(1)} %get-tuple-element.40), channel_id=1, source_target_pairs={{28,4},{29,5},{30,6},{31,7},{0,8},{1,9},{2,10},{3,11},{12,20},{13,... | collective-permute-start | bytes 356360 | tf_op jit(solution)/shard_map/ppermute | solution.py:583
  5.8 0.0 collective-permute-start.1
  5.8 2.3 %shard_map.82 = (f32[3,512,128]{2,1,0:T(8,128)S(1)}, f32[176,128]{1,0:T(8,128)S(1)}, f32[176,128]{1,0:T(8,128)S(1)}, f32[176,128]{1,0:T(8,128)S(1)}, f32[176,128]{1,0:T(8,128)S(1)}) custom-call(f32[3,512,128]{2,1,0:T(8,128)S(1)} %get-tuple-element.32.moment_ref, f32[3,512,128]{2,1,0:T(8,128)S(1)} %get-tuple-element.33.carry_ref, ...), custom_call_target="tpu_custom_call" | custom-call | flops 20000000 | bytes 6668288 | tf_op jit(solution)/shard_map/pallas_call | solution.py:539
  8.1 4.3 %collective-permute-start.5 = (f32[176,128]{1,0:T(8,128)S(1)}, f32[176,128]{1,0:T(8,128)S(1)}, u32[]{:S(2)}, u32[]{:S(2)}) collective-permute-start(f32[176,128]{1,0:T(8,128)S(1)} %get-tuple-element.47), channel_id=1, source_target_pairs={{29,30},{31,0},{1,2},{5,6},{7,8},{9,10},{13,14},{15,16},{17,18},{2... | collective-permute-start | bytes 270344 | tf_op jit(solution)/shard_map/ppermute | solution.py:583
  12.4 0.0 collective-permute-start.4
  12.4 0.0 collective-permute-done.e_ref.refs_0_
  12.4 0.0 collective-permute-done.1.o_ref.refs_1_
  12.5 2.8 %collective-permute-start.3 = (f32[232,128]{1,0:T(8,128)S(1)}, f32[232,128]{1,0:T(8,128)S(1)}, u32[]{:S(2)}, u32[]{:S(2)}) collective-permute-start(f32[232,128]{1,0:T(8,128)S(1)} %shard_map.78.refs_0_), channel_id=1, source_target_pairs={{29,30},{31,0},{1,2},{5,6},{7,8},{9,10},{13,14},{15,16},{17,18},{2... | collective-permute-start | bytes 356360 | tf_op jit(solution)/shard_map/ppermute | solution.py:583
  15.3 0.1 collective-permute-start.2
  15.4 0.5 %collective-permute-done.5.refs_0_ = f32[176,128]{1,0:T(8,128)S(1)} collective-permute-done((f32[176,128]{1,0:T(8,128)S(1)}, f32[176,128]{1,0:T(8,128)S(1)}, u32[]{:S(2)}, u32[]{:S(2)}) %collective-permute-start.5) | collective-permute-done | bytes 90144 | tf_op jit(solution)/shard_map/ppermute | solution.py:583
  15.9 0.0 collective-permute-done.4.e_ref.gje_ref
  15.9 2.6 %collective-permute-start.6 = (f32[176,128]{1,0:T(8,128)S(1)}, f32[176,128]{1,0:T(8,128)S(1)}, u32[]{:S(2)}, u32[]{:S(2)}) collective-permute-start(f32[176,128]{1,0:T(8,128)S(1)} %shard_map.84), channel_id=1, source_target_pairs={{28,4},{29,5},{30,6},{31,7},{0,8},{1,9},{2,10},{3,11},{12,20},{13,... | collective-permute-start | bytes 270344 | tf_op jit(solution)/shard_map/ppermute | solution.py:583
  18.5 0.3 collective-permute-start.7
  18.8 1.7 %collective-permute-done.3.refs_0_ = f32[232,128]{1,0:T(8,128)S(1)} collective-permute-done((f32[232,128]{1,0:T(8,128)S(1)}, f32[232,128]{1,0:T(8,128)S(1)}, u32[]{:S(2)}, u32[]{:S(2)}) %collective-permute-start.3) | collective-permute-done | bytes 118816 | tf_op jit(solution)/shard_map/ppermute | solution.py:583
  20.5 0.0 collective-permute-done.2.refs_2_
  20.5 2.3 %shard_map.81 = (f32[512,128]{1,0:T(8,128)S(1)}, f32[3,512,128]{2,1,0:T(8,128)S(1)}, f32[3,512,128]{2,1,0:T(8,128)S(1)}, f32[176,128]{1,0:T(8,128)S(1)}, f32[176...) custom-call(f32[3,512,128]{2,1,0:T(8,128)S(1)} %get-tuple-element.38.state_ref, ...), custom_call_target="tpu_custom_call" | custom-call | flops 20000000 | bytes 9240576 | tf_op jit(solution)/shard_map/pallas_call | solution.py:539
  22.8 1.1 %collective-permute-start.12 = (f32[176,128]{1,0:T(8,128)S(1)}, f32[176,128]{1,0:T(8,128)S(1)}, u32[]{:S(2)}, u32[]{:S(2)}) collective-permute-start(f32[176,128]{1,0:T(8,128)S(1)} %get-tuple-element.58), channel_id=1, source_target_pairs={{28,4},{29,5},{30,6},{31,7},{0,8},{1,9},{2,10},{3,11},{12,20},{13,... | collective-permute-start | bytes 270344 | tf_op jit(solution)/shard_map/ppermute | solution.py:583
  23.9 0.0 collective-permute-start.13
  23.9 0.0 collective-permute-done.6.gie_ref
  23.9 0.0 collective-permute-done.7.gio_ref
  23.9 2.3 %shard_map.86 = (f32[3,512,128]{2,1,0:T(8,128)S(1)}, f32[3,512,128]{2,1,0:T(8,128)S(1)}, f32[176,128]{1,0:T(8,128)S(1)}, f32[176,128]{1,0:T(8,128)S(1)}, f32[176,128]{1,0:T(8,128)S(1)}, /*index=5*/f32[176,128]{1,0:T(8,128)S(1)}) custom-call(f32[3,512,128]{2,1,0:T(8,128)S(1)} %get-tuple-element.32.moment_ref, f32[3,512,128]{2,1,0:T(8,128)S(1)} %get-tuple-element.33.carry_ref, ...), custom_call_target="tpu_custom_call" | custom-call | flops 20000000 | bytes 8863744 | tf_op jit(solution)/shard_map/pallas_call | solution.py:539
  26.2 5.6 %collective-permute-start.9 = (f32[176,128]{1,0:T(8,128)S(1)}, f32[176,128]{1,0:T(8,128)S(1)}, u32[]{:S(2)}, u32[]{:S(2)}) collective-permute-start(f32[176,128]{1,0:T(8,128)S(1)} %get-tuple-element.53), channel_id=1, source_target_pairs={{29,30},{31,0},{1,2},{5,6},{7,8},{9,10},{13,14},{15,16},{17,18},{2... | collective-permute-start | bytes 270344 | tf_op jit(solution)/shard_map/ppermute | solution.py:583
  31.7 0.0 collective-permute-start.8
  31.7 0.0 collective-permute-done.12.e_ref.refs_1_
  31.7 0.0 collective-permute-done.13.o_ref.refs_2_
  31.8 0.6 %collective-permute-start.15 = (f32[176,128]{1,0:T(8,128)S(1)}, f32[176,128]{1,0:T(8,128)S(1)}, u32[]{:S(2)}, u32[]{:S(2)}) collective-permute-start(f32[176,128]{1,0:T(8,128)S(1)} %shard_map.91.refs_0_), channel_id=1, source_target_pairs={{29,30},{31,0},{1,2},{5,6},{7,8},{9,10},{13,14},{15,16},{17,18},{2... | collective-permute-start | bytes 270344 | tf_op jit(solution)/shard_map/ppermute | solution.py:583
  32.5 0.1 collective-permute-start.14
  32.5 1.4 %collective-permute-done.9.refs_0_ = f32[176,128]{1,0:T(8,128)S(1)} collective-permute-done((f32[176,128]{1,0:T(8,128)S(1)}, f32[176,128]{1,0:T(8,128)S(1)}, u32[]{:S(2)}, u32[]{:S(2)}) %collective-permute-start.9) | collective-permute-done | bytes 90144 | tf_op jit(solution)/shard_map/ppermute | solution.py:583
  33.9 0.0 collective-permute-done.8.e_ref.gje_ref
  34.0 0.3 collective-permute-start.10
  34.3 0.3 collective-permute-start.11
  34.5 5.0 %collective-permute-done.15.refs_0_ = f32[176,128]{1,0:T(8,128)S(1)} collective-permute-done((f32[176,128]{1,0:T(8,128)S(1)}, f32[176,128]{1,0:T(8,128)S(1)}, u32[]{:S(2)}, u32[]{:S(2)}) %collective-permute-start.15) | collective-permute-done | bytes 90144 | tf_op jit(solution)/shard_map/ppermute | solution.py:583
  39.6 0.0 collective-permute-done.14.refs_3_
  39.6 2.5 %shard_map.94 = f32[3,512,128]{2,1,0:T(8,128)} custom-call(f32[3,512,128]{2,1,0:T(8,128)S(1)} %get-tuple-element.56.state_ref, f32[3,512,128]{2,1,0:T(8,128)S(1)} %get-tuple-element.33.carry_ref, f32[3,512,128]{2,1,0:T(8,128)S(1)} %get-tuple-element.34.weigh_ref, bf16[512,768]{1,0:T(8,128)(2,1)S(1)} %get-tuple-element.35.table_ref, ...), custom_call_target="tpu_custom_call" | custom-call | flops 20000000 | bytes 7716864 | tf_op jit(solution)/shard_map/pallas_call | solution.py:539
  42.1 0.0 collective-permute-done.10.gie_ref
  42.1 0.0 collective-permute-done.11.gio_ref
  42.1 1.1 %shard_map.90 = f32[3,512,128]{2,1,0:T(8,128)} custom-call(f32[3,512,128]{2,1,0:T(8,128)S(1)} %get-tuple-element.50.moment_ref, s32[4,8,128]{2,1,0:T(8,128)S(1)} %get-tuple-element.37.index_ref, f32[512,128]{1,0:T(8,128)S(1)} %get-tuple-element.44.inverse_ref.refs_0_, f32[3,512,128]{2,1,0:T(8,128)S(1)} %get-tuple-element.51.joined_ref, ...), custom_call_target="tpu_custom_call" | custom-call | flops 1000000 | bytes 2998272 | tf_op jit(solution)/shard_map/pallas_call | solution.py:539
  (12 shorter events, 0.3 us)
Async XLA Ops:
  2.8 9.6 %collective-permute-start = (f32[232,128]{1,0:T(8,128)S(1)}, f32[232,128]{1,0:T(8,128)S(1)}, u32[]{:S(2)}, u32[]{:S(2)}) collective-permute-start(f32[232,128]{1,0:T(8,128)S(1)} %get-tuple-element.40), channel_id=1, source_target_pairs={{28,4},{29,5},{30,6},{31,7},{0,8},{1,9},{2,10},{3,11},{12,20},{13,... | collective-permute-start | bytes 356360 | tf_op jit(solution)/shard_map/ppermute | solution.py:583
  5.8 6.6 %collective-permute-start.1 = (f32[232,128]{1,0:T(8,128)S(1)}, f32[232,128]{1,0:T(8,128)S(1)}, u32[]{:S(2)}, u32[]{:S(2)}) collective-permute-start(f32[232,128]{1,0:T(8,128)S(1)} %get-tuple-element.41), channel_id=1, source_target_pairs={{4,12},{5,13},{6,14},{7,15},{8,16},{9,17},{10,18},{11,19},{28,29},... | collective-permute-start | bytes 356360 | tf_op jit(solution)/shard_map/ppermute | solution.py:583
  8.1 7.8 %collective-permute-start.5 = (f32[176,128]{1,0:T(8,128)S(1)}, f32[176,128]{1,0:T(8,128)S(1)}, u32[]{:S(2)}, u32[]{:S(2)}) collective-permute-start(f32[176,128]{1,0:T(8,128)S(1)} %get-tuple-element.47), channel_id=1, source_target_pairs={{29,30},{31,0},{1,2},{5,6},{7,8},{9,10},{13,14},{15,16},{17,18},{2... | collective-permute-start | bytes 270344 | tf_op jit(solution)/shard_map/ppermute | solution.py:583
  12.4 3.5 %collective-permute-start.4 = (f32[176,128]{1,0:T(8,128)S(1)}, f32[176,128]{1,0:T(8,128)S(1)}, u32[]{:S(2)}, u32[]{:S(2)}) collective-permute-start(f32[176,128]{1,0:T(8,128)S(1)} %get-tuple-element.46), channel_id=1, source_target_pairs={{28,29},{30,31},{0,1},{2,3},{4,5},{6,7},{8,9},{10,11},{12,13},{14,... | collective-permute-start | bytes 270344 | tf_op jit(solution)/shard_map/ppermute | solution.py:583
  12.5 8.0 %collective-permute-start.3 = (f32[232,128]{1,0:T(8,128)S(1)}, f32[232,128]{1,0:T(8,128)S(1)}, u32[]{:S(2)}, u32[]{:S(2)}) collective-permute-start(f32[232,128]{1,0:T(8,128)S(1)} %shard_map.78.refs_0_), channel_id=1, source_target_pairs={{29,30},{31,0},{1,2},{5,6},{7,8},{9,10},{13,14},{15,16},{17,18},{2... | collective-permute-start | bytes 356360 | tf_op jit(solution)/shard_map/ppermute | solution.py:583
  15.3 5.2 %collective-permute-start.2 = (f32[232,128]{1,0:T(8,128)S(1)}, f32[232,128]{1,0:T(8,128)S(1)}, u32[]{:S(2)}, u32[]{:S(2)}) collective-permute-start(f32[232,128]{1,0:T(8,128)S(1)} %shard_map.79), channel_id=1, source_target_pairs={{28,29},{30,31},{0,1},{2,3},{4,5},{6,7},{8,9},{10,11},{12,13},{14,... | collective-permute-start | bytes 356360 | tf_op jit(solution)/shard_map/ppermute | solution.py:583
  15.9 8.0 %collective-permute-start.6 = (f32[176,128]{1,0:T(8,128)S(1)}, f32[176,128]{1,0:T(8,128)S(1)}, u32[]{:S(2)}, u32[]{:S(2)}) collective-permute-start(f32[176,128]{1,0:T(8,128)S(1)} %shard_map.84), channel_id=1, source_target_pairs={{28,4},{29,5},{30,6},{31,7},{0,8},{1,9},{2,10},{3,11},{12,20},{13,... | collective-permute-start | bytes 270344 | tf_op jit(solution)/shard_map/ppermute | solution.py:583
  18.5 5.4 %collective-permute-start.7 = (f32[176,128]{1,0:T(8,128)S(1)}, f32[176,128]{1,0:T(8,128)S(1)}, u32[]{:S(2)}, u32[]{:S(2)}) collective-permute-start(f32[176,128]{1,0:T(8,128)S(1)} %shard_map.85), channel_id=1, source_target_pairs={{4,12},{5,13},{6,14},{7,15},{8,16},{9,17},{10,18},{11,19},{28,29},... | collective-permute-start | bytes 270344 | tf_op jit(solution)/shard_map/ppermute | solution.py:583
  22.8 8.9 %collective-permute-start.12 = (f32[176,128]{1,0:T(8,128)S(1)}, f32[176,128]{1,0:T(8,128)S(1)}, u32[]{:S(2)}, u32[]{:S(2)}) collective-permute-start(f32[176,128]{1,0:T(8,128)S(1)} %get-tuple-element.58), channel_id=1, source_target_pairs={{28,4},{29,5},{30,6},{31,7},{0,8},{1,9},{2,10},{3,11},{12,20},{13,... | collective-permute-start | bytes 270344 | tf_op jit(solution)/shard_map/ppermute | solution.py:583
  23.9 7.8 %collective-permute-start.13 = (f32[176,128]{1,0:T(8,128)S(1)}, f32[176,128]{1,0:T(8,128)S(1)}, u32[]{:S(2)}, u32[]{:S(2)}) collective-permute-start(f32[176,128]{1,0:T(8,128)S(1)} %get-tuple-element.59), channel_id=1, source_target_pairs={{4,12},{5,13},{6,14},{7,15},{8,16},{9,17},{10,18},{11,19},{28,29},... | collective-permute-start | bytes 270344 | tf_op jit(solution)/shard_map/ppermute | solution.py:583
  26.2 7.8 %collective-permute-start.9 = (f32[176,128]{1,0:T(8,128)S(1)}, f32[176,128]{1,0:T(8,128)S(1)}, u32[]{:S(2)}, u32[]{:S(2)}) collective-permute-start(f32[176,128]{1,0:T(8,128)S(1)} %get-tuple-element.53), channel_id=1, source_target_pairs={{29,30},{31,0},{1,2},{5,6},{7,8},{9,10},{13,14},{15,16},{17,18},{2... | collective-permute-start | bytes 270344 | tf_op jit(solution)/shard_map/ppermute | solution.py:583
  31.7 2.2 %collective-permute-start.8 = (f32[176,128]{1,0:T(8,128)S(1)}, f32[176,128]{1,0:T(8,128)S(1)}, u32[]{:S(2)}, u32[]{:S(2)}) collective-permute-start(f32[176,128]{1,0:T(8,128)S(1)} %get-tuple-element.52), channel_id=1, source_target_pairs={{28,29},{30,31},{0,1},{2,3},{4,5},{6,7},{8,9},{10,11},{12,13},{14,... | collective-permute-start | bytes 270344 | tf_op jit(solution)/shard_map/ppermute | solution.py:583
  31.8 7.8 %collective-permute-start.15 = (f32[176,128]{1,0:T(8,128)S(1)}, f32[176,128]{1,0:T(8,128)S(1)}, u32[]{:S(2)}, u32[]{:S(2)}) collective-permute-start(f32[176,128]{1,0:T(8,128)S(1)} %shard_map.91.refs_0_), channel_id=1, source_target_pairs={{29,30},{31,0},{1,2},{5,6},{7,8},{9,10},{13,14},{15,16},{17,18},{2... | collective-permute-start | bytes 270344 | tf_op jit(solution)/shard_map/ppermute | solution.py:583
  32.5 7.1 %collective-permute-start.14 = (f32[176,128]{1,0:T(8,128)S(1)}, f32[176,128]{1,0:T(8,128)S(1)}, u32[]{:S(2)}, u32[]{:S(2)}) collective-permute-start(f32[176,128]{1,0:T(8,128)S(1)} %shard_map.92), channel_id=1, source_target_pairs={{28,29},{30,31},{0,1},{2,3},{4,5},{6,7},{8,9},{10,11},{12,13},{14,... | collective-permute-start | bytes 270344 | tf_op jit(solution)/shard_map/ppermute | solution.py:583
  34.0 8.1 %collective-permute-start.10 = (f32[176,128]{1,0:T(8,128)S(1)}, f32[176,128]{1,0:T(8,128)S(1)}, u32[]{:S(2)}, u32[]{:S(2)}) collective-permute-start(f32[176,128]{1,0:T(8,128)S(1)} %shard_map.88), channel_id=1, source_target_pairs={{28,4},{29,5},{30,6},{31,7},{0,8},{1,9},{2,10},{3,11},{12,20},{13,... | collective-permute-start | bytes 270344 | tf_op jit(solution)/shard_map/ppermute | solution.py:583
  34.3 7.8 %collective-permute-start.11 = (f32[176,128]{1,0:T(8,128)S(1)}, f32[176,128]{1,0:T(8,128)S(1)}, u32[]{:S(2)}, u32[]{:S(2)}) collective-permute-start(f32[176,128]{1,0:T(8,128)S(1)} %shard_map.89), channel_id=1, source_target_pairs={{4,12},{5,13},{6,14},{7,15},{8,16},{9,17},{10,18},{11,19},{28,29},... | collective-permute-start | bytes 270344 | tf_op jit(solution)/shard_map/ppermute | solution.py:583

commit v11 on v10

--- a/solution.py
+++ b/solution.py
@@ -86,20 +86,20 @@
 
 
 def split(block):
-    wide = jnp.concatenate([block[:256], block[256:]], axis=1)
+    wide = jnp.concatenate([block[128 * n : 128 * (n + 1)] for n in range(4)], axis=1)
     high = wide.astype(BF16)
     low = (wide - high.astype(F32)).astype(BF16)
     return [high, high, low]
 
 
 def tall(wide):
-    return jnp.concatenate([wide[:, :128], wide[:, 128:]], axis=0)
+    return jnp.concatenate([wide[:, 128 * n : 128 * (n + 1)] for n in range(4)], axis=0)
 
 
 def slopes_jk(table_ref, block):
     parts = jnp.concatenate(split(block), axis=0)
     out = jnp.dot(table_ref[...], parts, preferred_element_type=F32)
-    return tall(out[:256]), tall(out[256:])
+    return tall(out[:128]), tall(out[128:])
 
 
 def back_jk(turned_ref, flux_k, flux_j):
@@ -129,18 +129,16 @@
         bases = [base]
     highs = [base.astype(BF16).astype(F32) for base in bases]
     lows = [base - high for base, high in zip(bases, highs)]
-    empty = jnp.zeros((16, 128), F32)
-    for a in range(0, 32, 2):
+    for a in range(0, 16, 2):
         parts = []
         for values in (highs, lows):
             pair = []
             for block in (a, a + 1):
-                own = place == (block // 8 % 2 if axis else block % 16)
+                own = place == (block // 8 if axis else block)
                 pair.append(jnp.where(own, values[block % 8 if axis else 0], zero))
-            pair = jnp.concatenate(pair, axis=0)
-            parts.append([pair, empty] if a < 16 else [empty, pair])
-        wide = jnp.concatenate(parts[0] + parts[1] + parts[0], axis=1)
-        table_ref[pl.ds(start + 8 * a, 16), column : column + 768] = wide.astype(BF16)
+            parts.append(jnp.concatenate(pair, axis=0))
+        wide = jnp.concatenate([parts[0], parts[1], parts[0]], axis=1)
+        table_ref[pl.ds(start + 8 * a, 16), column : column + 384] = wide.astype(BF16)
 
 
 def lanes(block, index):
@@ -262,7 +260,7 @@
     own = jnp.full((8, 128), c, jnp.int32)
     for axis in range(2):
         for way in range(2):
-            face = got[2 * axis + way]
+            face = got[3 - way if axis else way]
             last = jnp.where(
                 height < 127, lanes(face[tile(c, 0)], above), lanes(face[top_tile(face)], own)
             )
@@ -330,8 +328,8 @@
     for copy in copies:
         copy.start()
     for axis in range(2):
-        write_table(DM, axis, table_ref, 256 * axis, 0)
-        write_table(DM.T, axis, turned_ref, 0, 768 * axis)
+        write_table(DM, axis, table_ref, 128 * axis, 0)
+        write_table(DM.T, axis, turned_ref, 0, 384 * axis)
     ends = ends_of(columns)
     copies[0].wait()
     height = jnp.broadcast_to(numbers_ref[...] & 127, (8, 128))
@@ -395,15 +393,15 @@
     forward(moment_ref, *at, joined_ref, finish)
 
 
-def edge_kernel(columns, axis, way, e_ref, o_ref, face, *refs):
+def edge_kernel(columns, way, ie_ref, io_ref, face, *refs):
     ends, out = ends_of(columns), refs[-1]
     out[...] = face[...]
     tiles = face.shape[0] // 8
-    r = pl.ds(ends[axis][way], tiles, stride=8)
-    for other, got in enumerate((e_ref, o_ref)):
-        w = pl.ds(ends[1 - axis][other], tiles, stride=8)
+    r = pl.ds(ends[1][way], tiles, stride=8)
+    for other, got in enumerate((ie_ref, io_ref)):
+        w = pl.ds(ends[0][other], tiles, stride=8)
         part = got[r]
-        out[w] = out[w] + (part * ends[2][1 - axis] if other else part)
+        out[w] = out[w] + (part * ends[2][0] if other else part)
 
 
 def state_kernel(
@@ -429,7 +427,8 @@
                 inverse_ref[rows(i, j)] = 1.0 / assembled(3, i, j, joined_ref.at[3], spread_ref)
     else:
         inverse_ref, *got = refs[:5]
-        state_far, slope_ref, work_ref, hold_ref, spread_ref, state_out, sent = refs[5:]
+        state_far, token_ref, slope_ref, work_ref, hold_ref, spread_ref, state_out, sent = refs[5:]
+        token_ref[...] = jnp.zeros_like(token_ref)
     for f in range(3):
         take_faces(f, index, ends, got, spread_ref)
         for i in range(8):
@@ -477,8 +476,8 @@
     joined_ref,
     gie_ref,
     gio_ref,
+    gjo_ref,
     gje_ref,
-    gjo_ref,
     moment_out,
     joined_out,
     ie_ref,
@@ -492,7 +491,7 @@
     ends = ends_of(columns)
     index = index_of(index_ref)
     out = (ie_ref, io_ref, je_ref, jo_ref)
-    got = (gie_ref, gio_ref, gje_ref, gjo_ref)
+    got = (gie_ref, gio_ref, gjo_ref, gje_ref)
     for f in range(3):
         moment_step(f, ends, index, moment_ref, joined_ref, inverse_ref, got, spread_ref, moment_out)
 
@@ -512,8 +511,8 @@
     joined_ref,
     gie_ref,
     gio_ref,
+    gjo_ref,
     gje_ref,
-    gjo_ref,
     moment_far,
     spread_ref,
     moment_out,
@@ -521,7 +520,7 @@
 ):
     ends = ends_of(columns)
     index = index_of(index_ref)
-    got = (gie_ref, gio_ref, gje_ref, gjo_ref)
+    got = (gie_ref, gio_ref, gjo_ref, gje_ref)
 
     for f in range(3):
         moment_step(f, ends, index, moment_ref, joined_ref, inverse_ref, got, spread_ref, moment_out)
@@ -582,20 +581,20 @@
     def exchange(block, pairs):
         return lax.ppermute(block, "elem", pairs)
 
-    def settle(block):
+    def settle(block, *after):
         anywhere = pl.BlockSpec(memory_space=pl.ANY)
         return pl.pallas_call(
             lambda *refs: None,
             out_shape=jax.ShapeDtypeStruct(block.shape, block.dtype),
-            in_specs=[anywhere],
+            in_specs=[anywhere] * (1 + len(after)),
             out_specs=anywhere,
             input_output_aliases={0: 0},
             compiler_params=pltpu.CompilerParams(vmem_limit_bytes=1024 * 1024),
-        )(block)
-
-    def edge(count, axis, way, *operands):
+        )(block, *after)
+
+    def edge(count, way, *operands):
         return call(
-            functools.partial(edge_kernel, columns, axis, way),
+            functools.partial(edge_kernel, columns, way),
             [VMEM] * len(operands),
             [(face_shape(count), F32)],
             [],
@@ -603,19 +602,14 @@
             *operands,
         )[0]
 
-    def meet_ij(count, faces):
-        got = [exchange(faces[way], along_i[way]) for way in range(2)]
-        far_face = edge(count, 1, 1, *got, faces[3])
-        near_face = edge(count, 1, 0, *got, faces[2], far_face)
-        far_face, near_face = exchange(far_face, along_j[1]), exchange(near_face, along_j[0])
-        return got + [near_face, settle(far_face)]
-
-    def meet_ji(count, faces):
-        got = [exchange(faces[2 + way], along_j[way]) for way in range(2)]
-        got[1] = settle(got[1])
-        face_e = edge(count, 0, 0, *got, faces[0])
-        face_o = edge(count, 0, 1, *got, faces[1])
-        return [exchange(face_e, along_i[0]), exchange(face_o, along_i[1])] + got
+    def meet(count, faces):
+        got_i = [exchange(faces[way], along_i[way]) for way in range(2)]
+        far_face = edge(count, 1, *got_i, faces[3])
+        near_face = edge(count, 0, *got_i, faces[2], far_face)
+        return got_i + [exchange(far_face, along_j[1]), exchange(near_face, along_j[0])]
+
+    def settled(got, *after):
+        return got[:2] + [settle(got[2], *after), got[3]]
 
     def far(array):
         return pltpu.with_memory_space_constraint(array, pltpu.HBM)
@@ -630,7 +624,7 @@
         functools.partial(index_kernel, columns),
         [FAR] * 6,
         [whole] * 4
-        + [((512, 768), BF16), ((256, 1536), BF16)]
+        + [((256, 384), BF16), ((128, 768), BF16)]
         + [((4, 8, 128), jnp.int32), ((4, 512, 128), F32)]
         + faces_shape(4),
         [
@@ -646,7 +640,7 @@
         *map(far, (diffusivity, numbering.reshape(1, 128))),
     )
     tables = (carry, weigh, table, turned, index)
-    got_state = meet_ij(4, faces_state)
+    got_state = meet(4, faces_state)
     joined_moment, *faces_moment = call(
         functools.partial(moment_kernel, columns),
         [VMEM] * 6,
@@ -656,7 +650,7 @@
         moment,
         *tables,
     )
-    got_moment = meet_ji(3, faces_moment)
+    got_moment = meet(3, faces_moment)
     inverse, state, joined_state, *faces_state = call(
         functools.partial(state_kernel, columns, True),
         [VMEM] * 11,
@@ -666,9 +660,9 @@
         state,
         *tables,
         joined_state,
-        *got_state,
-    )
-    got_state = meet_ij(3, faces_state)
+        *settled(got_state),
+    )
+    got_state = meet(3, faces_state)
     moment, joined_moment, *faces_moment = call(
         functools.partial(middle_kernel, columns),
         [VMEM] * 12,
@@ -679,20 +673,20 @@
         *tables,
         inverse,
         joined_moment,
-        *got_moment,
-    )
-    got_moment = meet_ji(3, faces_moment)
-    (state,) = call(
+        *settled(got_moment, inverse),
+    )
+    got_moment = meet(3, faces_moment)
+    state, token = call(
         functools.partial(state_kernel, columns, False),
         [VMEM] * 12,
-        [whole],
+        [whole, ((8, 128), F32)],
         [slopes, work, work, spread(3), work] + [pltpu.SemaphoreType.DMA((3,))],
         20_000_000,
         state,
         *tables,
         joined_state,
         inverse,
-        *got_state,
+        *settled(got_state),
         first_out=FAR,
     )
     (moment,) = call(
@@ -705,7 +699,7 @@
         index,
         inverse,
         joined_moment,
-        *got_moment,
+        *settled(got_moment, token),
         first_out=FAR,
     )
     return moment, state

time: 43.3 us -> 41.2 us (0.952)
  waiting for transfers between devices: 8.65 us -> 2.24 us
  starting transfers between devices: 21.1 us -> 26.3 us
  Pallas kernels: 12.8 us -> 11.7 us
    ppermute x16, waiting for transfers between devices: 8.65 us -> 2.24 us  [exchange(): return lax.ppermute(block, 'elem', pairs)]
    ppermute x16, starting transfers between devices: 21.1 us -> 26.3 us  [exchange(): return lax.ppermute(block, 'elem', pairs)]
    pallas_call x14, Pallas kernels: 12.8 us -> 11.7 us  [call(): pl.pallas_call(kernel, out_shape=[jax.ShapeDtypeStruct(s, t) for s, t in...]
  transfers between devices with their start and end apart: 16 -> 16, of which waited for: 4 -> 2; matrix products, arithmetic and copies ran while one was open for 0% -> 0% of each run, Pallas kernels for 22% -> 21%
where the time goes in v11:
time: 41.2 us; the launch traced here: 41 us
  starting transfers between devices  26.3 us (64%)
  Pallas kernels  11.7 us (28%)
  waiting for transfers between devices  2.24 us (5%)
  between operations  0.82 us (2%)
    ppermute x16, starting transfers between devices, exchange(): return lax.ppermute(block, 'elem', pairs)  26.3 us
    pallas_call x14, Pallas kernels, call(): pl.pallas_call(kernel, out_shape=[jax.ShapeDtypeStruct(s, t) for s, t in...  11.7 us
    ppermute x16, waiting for transfers between devices, exchange(): return lax.ppermute(block, 'elem', pairs)  2.24 us
  transfers between devices with their start and end apart: 16, of which 2 were waited for; matrix products, arithmetic and copies ran while one was open for 0% of the time, Pallas kernels for 21%

profile of v11, /device:TPU:0, one launch (start us, length us, event | category | flops | bytes accessed | tf_op | source)
XLA Modules:
  0.0 41.0 jit_solution(3606558872102460485)
XLA Ops:
  0.6 2.1 %shard_map.77 = (f32[3,512,128]{2,1,0:T(8,128)S(1)}, f32[3,512,128]{2,1,0:T(8,128)S(1)}, f32[3,512,128]{2,1,0:T(8,128)S(1)}, f32[3,512,128]{2,1,0:T(8,128)S(1)},...) custom-call(f32[3,512,128]{2,1,0:T(8,128)} %moment_far.1, ...), custom_call_target="tpu_custom_call" | custom-call | flops 1000000 | bytes 8094220 | tf_op jit(solution)/shard_map/pallas_call | solution.py:538
  2.8 3.1 %collective-permute-start = (f32[232,128]{1,0:T(8,128)S(1)}, f32[232,128]{1,0:T(8,128)S(1)}, u32[]{:S(2)}, u32[]{:S(2)}) collective-permute-start(f32[232,128]{1,0:T(8,128)S(1)} %get-tuple-element.42), channel_id=1, source_target_pairs={{28,4},{29,5},{30,6},{31,7},{0,8},{1,9},{2,10},{3,11},{12,20},{13,... | collective-permute-start | bytes 356360 | tf_op jit(solution)/shard_map/ppermute | solution.py:582
  5.8 0.0 collective-permute-start.1
  5.8 1.9 %shard_map.82 = (f32[3,512,128]{2,1,0:T(8,128)S(1)}, f32[176,128]{1,0:T(8,128)S(1)}, f32[176,128]{1,0:T(8,128)S(1)}, f32[176,128]{1,0:T(8,128)S(1)}, f32[176,128]{1,0:T(8,128)S(1)}) custom-call(f32[3,512,128]{2,1,0:T(8,128)S(1)} %get-tuple-element.34.moment_ref, f32[3,512,128]{2,1,0:T(8,128)S(1)} %get-tuple-element.35.carry_ref, ...), custom_call_target="tpu_custom_call" | custom-call | flops 20000000 | bytes 4308992 | tf_op jit(solution)/shard_map/pallas_call | solution.py:538
  7.7 3.2 %collective-permute-start.4 = (f32[176,128]{1,0:T(8,128)S(1)}, f32[176,128]{1,0:T(8,128)S(1)}, u32[]{:S(2)}, u32[]{:S(2)}) collective-permute-start(f32[176,128]{1,0:T(8,128)S(1)} %get-tuple-element.48), channel_id=1, source_target_pairs={{28,4},{29,5},{30,6},{31,7},{0,8},{1,9},{2,10},{3,11},{12,20},{13,... | collective-permute-start | bytes 270344 | tf_op jit(solution)/shard_map/ppermute | solution.py:582
  10.9 0.0 collective-permute-start.5
  10.9 0.0 collective-permute-done.ie_ref.refs_0_
  10.9 0.0 collective-permute-done.1.io_ref.refs_1_
  11.0 4.8 %collective-permute-start.2 = (f32[232,128]{1,0:T(8,128)S(1)}, f32[232,128]{1,0:T(8,128)S(1)}, u32[]{:S(2)}, u32[]{:S(2)}) collective-permute-start(f32[232,128]{1,0:T(8,128)S(1)} %shard_map.78.refs_0_), channel_id=1, source_target_pairs={{29,30},{31,0},{1,2},{5,6},{7,8},{9,10},{13,14},{15,16},{17,18},{2... | collective-permute-start | bytes 356360 | tf_op jit(solution)/shard_map/ppermute | solution.py:582
  15.8 0.1 collective-permute-start.3
  15.9 0.0 collective-permute-done.4.ie_ref.gie_ref
  15.9 0.0 collective-permute-done.5.io_ref.gio_ref
  15.9 3.5 %collective-permute-start.6 = (f32[176,128]{1,0:T(8,128)S(1)}, f32[176,128]{1,0:T(8,128)S(1)}, u32[]{:S(2)}, u32[]{:S(2)}) collective-permute-start(f32[176,128]{1,0:T(8,128)S(1)} %shard_map.83.refs_0_), channel_id=1, source_target_pairs={{29,30},{31,0},{1,2},{5,6},{7,8},{9,10},{13,14},{15,16},{17,18},{2... | collective-permute-start | bytes 270344 | tf_op jit(solution)/shard_map/ppermute | solution.py:582
  19.5 0.1 collective-permute-start.7
  19.6 0.0 collective-permute-done.2.refs_0_
  19.6 0.0 collective-permute-done.3.refs_3_
  19.6 2.1 %shard_map.81 = (f32[512,128]{1,0:T(8,128)S(1)}, f32[3,512,128]{2,1,0:T(8,128)S(1)}, f32[3,512,128]{2,1,0:T(8,128)S(1)}, f32[176,128]{1,0:T(8,128)S(1)}, f32[176...) custom-call(f32[3,512,128]{2,1,0:T(8,128)S(1)} %get-tuple-element.40.state_ref, ...), custom_call_target="tpu_custom_call" | custom-call | flops 20000000 | bytes 6881280 | tf_op jit(solution)/shard_map/pallas_call | solution.py:538
  21.7 3.0 %collective-permute-start.11 = (f32[176,128]{1,0:T(8,128)S(1)}, f32[176,128]{1,0:T(8,128)S(1)}, u32[]{:S(2)}, u32[]{:S(2)}) collective-permute-start(f32[176,128]{1,0:T(8,128)S(1)} %get-tuple-element.59), channel_id=1, source_target_pairs={{28,4},{29,5},{30,6},{31,7},{0,8},{1,9},{2,10},{3,11},{12,20},{13,... | collective-permute-start | bytes 270344 | tf_op jit(solution)/shard_map/ppermute | solution.py:582
  24.7 0.2 collective-permute-start.12
  24.8 0.0 collective-permute-done.6.refs_0_
  24.8 0.0 collective-permute-done.7.gje_ref
  24.8 2.0 %shard_map.86 = (f32[3,512,128]{2,1,0:T(8,128)S(1)}, f32[3,512,128]{2,1,0:T(8,128)S(1)}, f32[176,128]{1,0:T(8,128)S(1)}, f32[176,128]{1,0:T(8,128)S(1)}, f32[176,128]{1,0:T(8,128)S(1)}, /*index=5*/f32[176,128]{1,0:T(8,128)S(1)}) custom-call(f32[3,512,128]{2,1,0:T(8,128)S(1)} %get-tuple-element.34.moment_ref, f32[3,512,128]{2,1,0:T(8,128)S(1)} %get-tuple-element.35.carry_ref, ...), custom_call_target="tpu_custom_call" | custom-call | flops 20000000 | bytes 6504448 | tf_op jit(solution)/shard_map/pallas_call | solution.py:538
  26.8 0.1 collective-permute-start.8
  26.9 0.4 %collective-permute-start.9 = (f32[176,128]{1,0:T(8,128)S(1)}, f32[176,128]{1,0:T(8,128)S(1)}, u32[]{:S(2)}, u32[]{:S(2)}) collective-permute-start(f32[176,128]{1,0:T(8,128)S(1)} %get-tuple-element.55), channel_id=1, source_target_pairs={{4,12},{5,13},{6,14},{7,15},{8,16},{9,17},{10,18},{11,19},{28,29},... | collective-permute-start | bytes 270344 | tf_op jit(solution)/shard_map/ppermute | solution.py:582
  27.3 0.6 %collective-permute-done.11.ie_ref.refs_1_ = f32[176,128]{1,0:T(8,128)S(1)} collective-permute-done((f32[176,128]{1,0:T(8,128)S(1)}, f32[176,128]{1,0:T(8,128)S(1)}, u32[]{:S(2)}, u32[]{:S(2)}) %collective-permute-start.11) | collective-permute-done | bytes 90144 | tf_op jit(solution)/shard_map/ppermute | solution.py:582
  27.9 0.0 collective-permute-done.12.io_ref.refs_2_
  27.9 4.2 %collective-permute-start.13 = (f32[176,128]{1,0:T(8,128)S(1)}, f32[176,128]{1,0:T(8,128)S(1)}, u32[]{:S(2)}, u32[]{:S(2)}) collective-permute-start(f32[176,128]{1,0:T(8,128)S(1)} %shard_map.88.refs_0_), channel_id=1, source_target_pairs={{29,30},{31,0},{1,2},{5,6},{7,8},{9,10},{13,14},{15,16},{17,18},{2... | collective-permute-start | bytes 270344 | tf_op jit(solution)/shard_map/ppermute | solution.py:582
  32.1 0.1 collective-permute-start.14
  32.2 0.0 collective-permute-done.8.ie_ref.gie_ref
  32.2 0.0 collective-permute-done.9.io_ref.gio_ref
  32.3 3.6 %collective-permute-start.10 = (f32[176,128]{1,0:T(8,128)S(1)}, f32[176,128]{1,0:T(8,128)S(1)}, u32[]{:S(2)}, u32[]{:S(2)}) collective-permute-start(f32[176,128]{1,0:T(8,128)S(1)} %shard_map.87.refs_0_), channel_id=1, source_target_pairs={{29,30},{31,0},{1,2},{5,6},{7,8},{9,10},{13,14},{15,16},{17,18},{2... | collective-permute-start | bytes 270344 | tf_op jit(solution)/shard_map/ppermute | solution.py:582
  35.9 0.1 collective-permute-start.15
  36.0 0.0 collective-permute-done.13.refs_0_
  36.0 0.0 collective-permute-done.14.refs_4_
  36.0 2.3 %shard_map.91 = (f32[3,512,128]{2,1,0:T(8,128)}, f32[8,128]{1,0:T(8,128)S(1)}) custom-call(f32[3,512,128]{2,1,0:T(8,128)S(1)} %get-tuple-element.57.state_ref, f32[3,512,128]{2,1,0:T(8,128)S(1)} %get-tuple-element.35.carry_ref, f32[3,512,128]{2,1,0:T(8,128)S(1)} %get-tuple-element.36.weigh_ref, bf16[256,384]{1,0:T(8,128)(2,1)S(1)} %get-tuple-element.37.table_ref, ...), custom_call_target="tpu_custom_call" | custom-call | flops 20000000 | bytes 5361664 | tf_op jit(solution)/shard_map/pallas_call | solution.py:538
  38.3 1.6 %collective-permute-done.10.refs_0_ = f32[176,128]{1,0:T(8,128)S(1)} collective-permute-done((f32[176,128]{1,0:T(8,128)S(1)}, f32[176,128]{1,0:T(8,128)S(1)}, u32[]{:S(2)}, u32[]{:S(2)}) %collective-permute-start.10) | collective-permute-done | bytes 90144 | tf_op jit(solution)/shard_map/ppermute | solution.py:582
  39.9 0.0 collective-permute-done.15.gje_ref
  39.9 1.1 %shard_map.94 = f32[3,512,128]{2,1,0:T(8,128)} custom-call(f32[3,512,128]{2,1,0:T(8,128)S(1)} %get-tuple-element.52.moment_ref, s32[4,8,128]{2,1,0:T(8,128)S(1)} %get-tuple-element.39.index_ref, f32[512,128]{1,0:T(8,128)S(1)} %get-tuple-element.46.refs_1_.inverse_ref.refs_0_, f32[3,512,128]{2,1,0:T(8,128)S(1)} %get-tuple-element.53.joined_ref, ...), custom_call_target="tpu_custom_call" | custom-call | flops 1000000 | bytes 2998272 | tf_op jit(solution)/shard_map/pallas_call | solution.py:538
  (12 shorter events, 0.3 us)
Async XLA Ops:
  2.8 8.2 %collective-permute-start = (f32[232,128]{1,0:T(8,128)S(1)}, f32[232,128]{1,0:T(8,128)S(1)}, u32[]{:S(2)}, u32[]{:S(2)}) collective-permute-start(f32[232,128]{1,0:T(8,128)S(1)} %get-tuple-element.42), channel_id=1, source_target_pairs={{28,4},{29,5},{30,6},{31,7},{0,8},{1,9},{2,10},{3,11},{12,20},{13,... | collective-permute-start | bytes 356360 | tf_op jit(solution)/shard_map/ppermute | solution.py:582
  5.8 5.1 %collective-permute-start.1 = (f32[232,128]{1,0:T(8,128)S(1)}, f32[232,128]{1,0:T(8,128)S(1)}, u32[]{:S(2)}, u32[]{:S(2)}) collective-permute-start(f32[232,128]{1,0:T(8,128)S(1)} %get-tuple-element.43), channel_id=1, source_target_pairs={{4,12},{5,13},{6,14},{7,15},{8,16},{9,17},{10,18},{11,19},{28,29},... | collective-permute-start | bytes 356360 | tf_op jit(solution)/shard_map/ppermute | solution.py:582
  7.7 8.1 %collective-permute-start.4 = (f32[176,128]{1,0:T(8,128)S(1)}, f32[176,128]{1,0:T(8,128)S(1)}, u32[]{:S(2)}, u32[]{:S(2)}) collective-permute-start(f32[176,128]{1,0:T(8,128)S(1)} %get-tuple-element.48), channel_id=1, source_target_pairs={{28,4},{29,5},{30,6},{31,7},{0,8},{1,9},{2,10},{3,11},{12,20},{13,... | collective-permute-start | bytes 270344 | tf_op jit(solution)/shard_map/ppermute | solution.py:582
  10.9 4.9 %collective-permute-start.5 = (f32[176,128]{1,0:T(8,128)S(1)}, f32[176,128]{1,0:T(8,128)S(1)}, u32[]{:S(2)}, u32[]{:S(2)}) collective-permute-start(f32[176,128]{1,0:T(8,128)S(1)} %get-tuple-element.49), channel_id=1, source_target_pairs={{4,12},{5,13},{6,14},{7,15},{8,16},{9,17},{10,18},{11,19},{28,29},... | collective-permute-start | bytes 270344 | tf_op jit(solution)/shard_map/ppermute | solution.py:582
  11.0 8.6 %collective-permute-start.2 = (f32[232,128]{1,0:T(8,128)S(1)}, f32[232,128]{1,0:T(8,128)S(1)}, u32[]{:S(2)}, u32[]{:S(2)}) collective-permute-start(f32[232,128]{1,0:T(8,128)S(1)} %shard_map.78.refs_0_), channel_id=1, source_target_pairs={{29,30},{31,0},{1,2},{5,6},{7,8},{9,10},{13,14},{15,16},{17,18},{2... | collective-permute-start | bytes 356360 | tf_op jit(solution)/shard_map/ppermute | solution.py:582
  15.8 3.8 %collective-permute-start.3 = (f32[232,128]{1,0:T(8,128)S(1)}, f32[232,128]{1,0:T(8,128)S(1)}, u32[]{:S(2)}, u32[]{:S(2)}) collective-permute-start(f32[232,128]{1,0:T(8,128)S(1)} %shard_map.80), channel_id=1, source_target_pairs={{28,29},{30,31},{0,1},{2,3},{4,5},{6,7},{8,9},{10,11},{12,13},{14,... | collective-permute-start | bytes 356360 | tf_op jit(solution)/shard_map/ppermute | solution.py:582
  15.9 8.9 %collective-permute-start.6 = (f32[176,128]{1,0:T(8,128)S(1)}, f32[176,128]{1,0:T(8,128)S(1)}, u32[]{:S(2)}, u32[]{:S(2)}) collective-permute-start(f32[176,128]{1,0:T(8,128)S(1)} %shard_map.83.refs_0_), channel_id=1, source_target_pairs={{29,30},{31,0},{1,2},{5,6},{7,8},{9,10},{13,14},{15,16},{17,18},{2... | collective-permute-start | bytes 270344 | tf_op jit(solution)/shard_map/ppermute | solution.py:582
  19.5 5.3 %collective-permute-start.7 = (f32[176,128]{1,0:T(8,128)S(1)}, f32[176,128]{1,0:T(8,128)S(1)}, u32[]{:S(2)}, u32[]{:S(2)}) collective-permute-start(f32[176,128]{1,0:T(8,128)S(1)} %shard_map.85), channel_id=1, source_target_pairs={{28,29},{30,31},{0,1},{2,3},{4,5},{6,7},{8,9},{10,11},{12,13},{14,... | collective-permute-start | bytes 270344 | tf_op jit(solution)/shard_map/ppermute | solution.py:582
  21.7 6.2 %collective-permute-start.11 = (f32[176,128]{1,0:T(8,128)S(1)}, f32[176,128]{1,0:T(8,128)S(1)}, u32[]{:S(2)}, u32[]{:S(2)}) collective-permute-start(f32[176,128]{1,0:T(8,128)S(1)} %get-tuple-element.59), channel_id=1, source_target_pairs={{28,4},{29,5},{30,6},{31,7},{0,8},{1,9},{2,10},{3,11},{12,20},{13,... | collective-permute-start | bytes 270344 | tf_op jit(solution)/shard_map/ppermute | solution.py:582
  24.7 3.2 %collective-permute-start.12 = (f32[176,128]{1,0:T(8,128)S(1)}, f32[176,128]{1,0:T(8,128)S(1)}, u32[]{:S(2)}, u32[]{:S(2)}) collective-permute-start(f32[176,128]{1,0:T(8,128)S(1)} %get-tuple-element.60), channel_id=1, source_target_pairs={{4,12},{5,13},{6,14},{7,15},{8,16},{9,17},{10,18},{11,19},{28,29},... | collective-permute-start | bytes 270344 | tf_op jit(solution)/shard_map/ppermute | solution.py:582
  26.8 5.4 %collective-permute-start.8 = (f32[176,128]{1,0:T(8,128)S(1)}, f32[176,128]{1,0:T(8,128)S(1)}, u32[]{:S(2)}, u32[]{:S(2)}) collective-permute-start(f32[176,128]{1,0:T(8,128)S(1)} %get-tuple-element.54), channel_id=1, source_target_pairs={{28,4},{29,5},{30,6},{31,7},{0,8},{1,9},{2,10},{3,11},{12,20},{13,... | collective-permute-start | bytes 270344 | tf_op jit(solution)/shard_map/ppermute | solution.py:582
  26.9 5.3 %collective-permute-start.9 = (f32[176,128]{1,0:T(8,128)S(1)}, f32[176,128]{1,0:T(8,128)S(1)}, u32[]{:S(2)}, u32[]{:S(2)}) collective-permute-start(f32[176,128]{1,0:T(8,128)S(1)} %get-tuple-element.55), channel_id=1, source_target_pairs={{4,12},{5,13},{6,14},{7,15},{8,16},{9,17},{10,18},{11,19},{28,29},... | collective-permute-start | bytes 270344 | tf_op jit(solution)/shard_map/ppermute | solution.py:582
  27.9 8.0 %collective-permute-start.13 = (f32[176,128]{1,0:T(8,128)S(1)}, f32[176,128]{1,0:T(8,128)S(1)}, u32[]{:S(2)}, u32[]{:S(2)}) collective-permute-start(f32[176,128]{1,0:T(8,128)S(1)} %shard_map.88.refs_0_), channel_id=1, source_target_pairs={{29,30},{31,0},{1,2},{5,6},{7,8},{9,10},{13,14},{15,16},{17,18},{2... | collective-permute-start | bytes 270344 | tf_op jit(solution)/shard_map/ppermute | solution.py:582
  32.1 3.9 %collective-permute-start.14 = (f32[176,128]{1,0:T(8,128)S(1)}, f32[176,128]{1,0:T(8,128)S(1)}, u32[]{:S(2)}, u32[]{:S(2)}) collective-permute-start(f32[176,128]{1,0:T(8,128)S(1)} %shard_map.90), channel_id=1, source_target_pairs={{28,29},{30,31},{0,1},{2,3},{4,5},{6,7},{8,9},{10,11},{12,13},{14,... | collective-permute-start | bytes 270344 | tf_op jit(solution)/shard_map/ppermute | solution.py:582
  32.3 7.7 %collective-permute-start.10 = (f32[176,128]{1,0:T(8,128)S(1)}, f32[176,128]{1,0:T(8,128)S(1)}, u32[]{:S(2)}, u32[]{:S(2)}) collective-permute-start(f32[176,128]{1,0:T(8,128)S(1)} %shard_map.87.refs_0_), channel_id=1, source_target_pairs={{29,30},{31,0},{1,2},{5,6},{7,8},{9,10},{13,14},{15,16},{17,18},{2... | collective-permute-start | bytes 270344 | tf_op jit(solution)/shard_map/ppermute | solution.py:582
  35.9 4.1 %collective-permute-start.15 = (f32[176,128]{1,0:T(8,128)S(1)}, f32[176,128]{1,0:T(8,128)S(1)}, u32[]{:S(2)}, u32[]{:S(2)}) collective-permute-start(f32[176,128]{1,0:T(8,128)S(1)} %shard_map.93), channel_id=1, source_target_pairs={{28,29},{30,31},{0,1},{2,3},{4,5},{6,7},{8,9},{10,11},{12,13},{14,... | collective-permute-start | bytes 270344 | tf_op jit(solution)/shard_map/ppermute | solution.py:582

commit v12 on v11

--- a/solution.py
+++ b/solution.py
@@ -157,64 +157,60 @@
             mass_ref[r] = weight_ref[r] * (along * float(WEIGHTS[i] * WEIGHTS[j]))
 
 
-def forward_jk(carry_ref, weigh, turned_ref, slope, work):
-    fluxes = weigh[...] * slope[0], weigh[...] * slope[1]
-    carried = carry_ref[2] * slope[0] + carry_ref[1] * slope[1]
-    work[...] = carried + back_jk(turned_ref, *fluxes)
-
-
-def adjoint_jk(source, carry_ref, weigh, turned_ref, slope, work):
-    flux_k = carry_ref[2] * source[...] + weigh[...] * slope[0]
-    flux_j = carry_ref[1] * source[...] + weigh[...] * slope[1]
-    work[...] = back_jk(turned_ref, flux_k, flux_j)
-
-
-def forward_i(source, carry_ref, weigh, work, target):
+def set_slopes(source, table_ref, slope):
+    slope[0], slope[1] = slopes_jk(table_ref, source[...])
+
+
+def forward_i(source, carry_ref, weigh, target):
     for j in range(8):
         slopes = line(DM, [source[rows(i, j)] for i in range(8)])
         back = line(DM.T, [weigh[rows(i, j)] * slopes[i] for i in range(8)])
         for i in range(8):
             r = rows(i, j)
-            target[r] = work[r] + (carry_ref[0, r] * slopes[i] + back[i])
-
-
-def adjoint_i(source, base, carry_ref, weigh, work, target):
+            target[r] = carry_ref[0, r] * slopes[i] + back[i]
+
+
+def forward_jk(carry_ref, weigh, turned_ref, slope, target):
+    fluxes = weigh[...] * slope[0], weigh[...] * slope[1]
+    carried = carry_ref[2] * slope[0] + carry_ref[1] * slope[1]
+    target[...] = target[...] + (carried + back_jk(turned_ref, *fluxes))
+
+
+def adjoint_i(source, base, carry_ref, weigh, target):
     for j in range(8):
         these = [rows(i, j) for i in range(8)]
         values = [source[r] for r in these]
         slopes = line(DM, values)
         fluxes = [carry_ref[0, r] * v + weigh[r] * g for r, v, g in zip(these, values, slopes)]
         for r, back in zip(these, line(DM.T, fluxes)):
-            target[r] = base[r] - (back + work[r])
-
-
-def set_slopes(source, table_ref, slope):
-    slope[0], slope[1] = slopes_jk(table_ref, source[...])
-
-
-def forward(sources, carry_ref, weigh_ref, table_ref, turned_ref, slope_ref, work_ref, target, finish):
-    for f in range(3):
-        set_slopes(sources.at[f], table_ref, slope_ref.at[f])
+            target[r] = base[r] - back
+
+
+def adjoint_jk(source, carry_ref, weigh, turned_ref, slope, target):
+    flux_k = carry_ref[2] * source[...] + weigh[...] * slope[0]
+    flux_j = carry_ref[1] * source[...] + weigh[...] * slope[1]
+    target[...] = target[...] - back_jk(turned_ref, flux_k, flux_j)
+
+
+def forward(sources, carry_ref, weigh_ref, table_ref, turned_ref, slope_ref, target, finish):
+    set_slopes(sources.at[0], table_ref, slope_ref.at[0])
     for f in range(3):
         at = (carry_ref, weigh_ref.at[f])
-        forward_jk(*at, turned_ref, slope_ref.at[f], work_ref.at[f])
+        forward_i(sources.at[f], *at, target.at[f])
+        if f < 2:
+            set_slopes(sources.at[f + 1], table_ref, slope_ref.at[f + 1])
+        forward_jk(*at, turned_ref, slope_ref.at[f], target.at[f])
+        finish(f)
+
+
+def adjoint(sources, base, carry_ref, weigh_ref, table_ref, turned_ref, slope_ref, target, finish):
+    set_slopes(sources.at[0], table_ref, slope_ref.at[0])
     for f in range(3):
         at = (carry_ref, weigh_ref.at[f])
-        forward_i(sources.at[f], *at, work_ref.at[f], target.at[f])
-        finish(f)
-
-
-def adjoint(
-    sources, base, carry_ref, weigh_ref, table_ref, turned_ref, slope_ref, work_ref, target, finish
-):
-    for f in range(3):
-        set_slopes(sources.at[f], table_ref, slope_ref.at[f])
-    for f in range(3):
-        at = (carry_ref, weigh_ref.at[f])
-        adjoint_jk(sources.at[f], *at, turned_ref, slope_ref.at[f], work_ref.at[f])
-    for f in range(3):
-        at = (carry_ref, weigh_ref.at[f])
-        adjoint_i(sources.at[f], base.at[f], *at, work_ref.at[f], target.at[f])
+        adjoint_i(sources.at[f], base.at[f], *at, target.at[f])
+        if f < 2:
+            set_slopes(sources.at[f + 1], table_ref, slope_ref.at[f + 1])
+        adjoint_jk(sources.at[f], *at, turned_ref, slope_ref.at[f], target.at[f])
         finish(f)
 
 
@@ -254,11 +250,11 @@
             face[top_tile(face)] = jnp.where(lane == c, last, others)
 
 
-def take_faces(c, index, ends, got, spread_ref):
+def take_faces(c, index, ends, got, spread_ref, axes=(0, 1)):
     height = index[0]
     above = (height + 1) & 127
     own = jnp.full((8, 128), c, jnp.int32)
-    for axis in range(2):
+    for axis in axes:
         for way in range(2):
             face = got[3 - way if axis else way]
             last = jnp.where(
@@ -270,10 +266,10 @@
                 spread_ref[c, slot, pl.ds(8 * k, 8)] = part * ends[2][axis] if way else part
 
 
-def assembled(c, i, j, joined, spread_ref):
+def assembled(c, i, j, joined, spread_ref, axes=(0, 1)):
     total = joined[rows(i, j)]
     for axis, (end, place) in enumerate(((i, j), (j, i))):
-        if end in (0, 7):
+        if end in (0, 7) and axis in axes:
             total = total + spread_ref[c, 2 * axis + end // 7, pl.ds(place, 8, stride=8)]
     return total
 
@@ -379,7 +375,6 @@
     je_ref,
     jo_ref,
     slope_ref,
-    work_ref,
 ):
     ends = ends_of(columns)
     index = index_of(index_ref)
@@ -389,7 +384,7 @@
         join_heights(joined_ref.at[f], index)
         send_faces(f, joined_ref.at[f], index, ends, out)
 
-    at = (carry_ref, weigh_ref, table_ref, turned_ref, slope_ref, work_ref)
+    at = (carry_ref, weigh_ref, table_ref, turned_ref, slope_ref)
     forward(moment_ref, *at, joined_ref, finish)
 
 
@@ -420,14 +415,14 @@
     index = index_of(index_ref)
     if first:
         got, (inverse_ref, state_out, joined_out), refs = refs[:4], refs[4:7], refs[7:]
-        out, (slope_ref, work_ref, hold_ref, spread_ref) = refs[:4], refs[4:]
+        out, (slope_ref, hold_ref, spread_ref) = refs[:4], refs[4:]
         take_faces(3, index, ends, got, spread_ref)
         for i in range(8):
             for j in range(8):
                 inverse_ref[rows(i, j)] = 1.0 / assembled(3, i, j, joined_ref.at[3], spread_ref)
     else:
         inverse_ref, *got = refs[:5]
-        state_far, token_ref, slope_ref, work_ref, hold_ref, spread_ref, state_out, sent = refs[5:]
+        state_far, token_ref, slope_ref, hold_ref, spread_ref, state_out, sent = refs[5:]
         token_ref[...] = jnp.zeros_like(token_ref)
     for f in range(3):
         take_faces(f, index, ends, got, spread_ref)
@@ -444,7 +439,7 @@
         else:
             send_out(f, state_out, state_far, sent).start()
 
-    at = (carry_ref, weigh_ref, table_ref, turned_ref, slope_ref, work_ref)
+    at = (carry_ref, weigh_ref, table_ref, turned_ref, slope_ref)
     adjoint(hold_ref, state_ref, *at, state_out, finish)
     if not first:
         for f in range(3):
@@ -485,7 +480,6 @@
     je_ref,
     jo_ref,
     slope_ref,
-    work_ref,
     spread_ref,
 ):
     ends = ends_of(columns)
@@ -499,11 +493,11 @@
         join_heights(joined_out.at[f], index)
         send_faces(f, joined_out.at[f], index, ends, out)
 
-    at = (carry_ref, weigh_ref, table_ref, turned_ref, slope_ref, work_ref)
+    at = (carry_ref, weigh_ref, table_ref, turned_ref, slope_ref)
     forward(moment_out, *at, joined_out, finish)
 
 
-def last_kernel(
+def inner_kernel(
     columns,
     moment_ref,
     index_ref,
@@ -511,29 +505,64 @@
     joined_ref,
     gie_ref,
     gio_ref,
+    token_ref,
+    moment_far,
+    moment_out,
+    spread_ref,
+    sent,
+):
+    ends = ends_of(columns)
+    index = index_of(index_ref)
+    for f in range(3):
+        take_faces(f, index, ends, (gie_ref, gio_ref), spread_ref, (0,))
+        for i in range(8):
+            for j in range(8):
+                r = rows(i, j)
+                total = assembled(f, i, j, joined_ref.at[f], spread_ref, (0,))
+                moment_out[f, i, j] = moment_ref[f, r] - total * inverse_ref[r]
+        send_out(f, moment_out, moment_far, sent).start()
+    for f in range(3):
+        send_out(f, moment_out, moment_far, sent).wait()
+
+
+def outer_kernel(
+    columns,
+    inner_far,
+    moment_ref,
+    index_ref,
+    inverse_ref,
     gjo_ref,
     gje_ref,
     moment_far,
     spread_ref,
-    moment_out,
+    rows_ref,
     sent,
 ):
     ends = ends_of(columns)
     index = index_of(index_ref)
-    got = (gie_ref, gio_ref, gjo_ref, gje_ref)
-
+    got = (None, None, gjo_ref, gje_ref)
+    copies = []
     for f in range(3):
-        moment_step(f, ends, index, moment_ref, joined_ref, inverse_ref, got, spread_ref, moment_out)
-        send_out(f, moment_out, moment_far, sent).start()
-    for f in range(3):
-        send_out(f, moment_out, moment_far, sent).wait()
+        take_faces(f, index, ends, got, spread_ref, (1,))
+        for end in range(2):
+            for i in range(8):
+                part = spread_ref[f, 2 + end, pl.ds(i, 8, stride=8)]
+                kept = moment_ref[f, i, 7 * end]
+                rows_ref[f, end, i] = kept - part * inverse_ref[rows(i, 7 * end)]
+            copy = pltpu.make_async_copy(
+                rows_ref.at[f, end], moment_far.at[f, :, 7 * end], sent.at[2 * f + end]
+            )
+            copy.start()
+            copies.append(copy)
+    for copy in copies:
+        copy.wait()
 
 
 VMEM = pl.BlockSpec(memory_space=pltpu.VMEM)
 FAR = pl.BlockSpec(memory_space=pltpu.HBM)
 
 
-def call(kernel, specs, shapes, scratch, flops, *operands, first_out=VMEM):
+def call(kernel, specs, shapes, scratch, flops, *operands, first_out=VMEM, aliases={}):
     moved = sum(o.size * 4 for o in operands) + sum(int(np.prod(s)) * 4 for s, _ in shapes)
     return pl.pallas_call(
         kernel,
@@ -541,6 +570,7 @@
         in_specs=specs,
         out_specs=[first_out] + [VMEM] * (len(shapes) - 1),
         scratch_shapes=scratch,
+        input_output_aliases=aliases,
         compiler_params=pltpu.CompilerParams(vmem_limit_bytes=32 * 1024 * 1024),
         cost_estimate=pl.CostEstimate(flops=flops, bytes_accessed=moved, transcendentals=0),
     )(*operands)
@@ -645,7 +675,7 @@
         functools.partial(moment_kernel, columns),
         [VMEM] * 6,
         [whole] + faces_shape(3),
-        [slopes, work],
+        [slopes],
         20_000_000,
         moment,
         *tables,
@@ -655,7 +685,7 @@
         functools.partial(state_kernel, columns, True),
         [VMEM] * 11,
         [block, whole, whole] + faces_shape(3),
-        [slopes, work, work, spread(4)],
+        [slopes, work, spread(4)],
         20_000_000,
         state,
         *tables,
@@ -667,7 +697,7 @@
         functools.partial(middle_kernel, columns),
         [VMEM] * 12,
         [whole, whole] + faces_shape(3),
-        [slopes, work, spread(3)],
+        [slopes, spread(3)],
         20_000_000,
         moment,
         *tables,
@@ -680,7 +710,7 @@
         functools.partial(state_kernel, columns, False),
         [VMEM] * 12,
         [whole, ((8, 128), F32)],
-        [slopes, work, work, spread(3), work] + [pltpu.SemaphoreType.DMA((3,))],
+        [slopes, work, spread(3), work] + [pltpu.SemaphoreType.DMA((3,))],
         20_000_000,
         state,
         *tables,
@@ -689,19 +719,42 @@
         *settled(got_state),
         first_out=FAR,
     )
-    (moment,) = call(
-        functools.partial(last_kernel, columns),
-        [VMEM] * 8,
-        [whole],
-        [spread(3), work] + [pltpu.SemaphoreType.DMA((3,))],
+    cube = ((3, 8, 8, 8, 128), F32)
+    inner, kept = call(
+        functools.partial(inner_kernel, columns),
+        [VMEM] * 7,
+        [cube, cube],
+        [spread(3), pltpu.SemaphoreType.DMA((3,))],
         1_000_000,
         moment,
         index,
         inverse,
         joined_moment,
-        *settled(got_moment, token),
+        *got_moment[:2],
+        token,
         first_out=FAR,
     )
+    far_face, near_face = got_moment[2:]
+    (moment,) = call(
+        functools.partial(outer_kernel, columns),
+        [FAR] + [VMEM] * 5,
+        [cube],
+        [
+            spread(3),
+            pltpu.VMEM((3, 2, 8, 8, 128), F32),
+            pltpu.SemaphoreType.DMA((6,)),
+        ],
+        1_000_000,
+        far(inner),
+        kept,
+        index,
+        inverse,
+        settle(far_face, kept),
+        near_face,
+        first_out=FAR,
+        aliases={0: 0},
+    )
+    moment = moment.reshape(whole[0])
     return moment, state
 
 

time: 41.2 us -> 40.8 us (level)
  waiting for transfers between devices: 2.24 us -> 1.25 us
  Pallas kernels: 11.7 us -> 12.3 us
    ppermute x16, waiting for transfers between devices: 2.24 us -> 1.25 us  [exchange(): return lax.ppermute(block, 'elem', pairs)]
    pallas_call x14 -> x15, Pallas kernels: 11.7 us -> 12.3 us  [call(): pl.pallas_call(kernel, out_shape=[jax.ShapeDtypeStruct(s, t) for s, t in...]
  transfers between devices with their start and end apart: 16 -> 16, of which waited for: 2 -> 2; matrix products, arithmetic and copies ran while one was open for 0% -> 0% of each run, Pallas kernels for 21% -> 23%
where the time goes in v12:
time: 40.8 us; the launch traced here: 40.7 us
  starting transfers between devices  26.3 us (64%)
  Pallas kernels  12.3 us (30%)
  waiting for transfers between devices  1.25 us (3%)
  between operations  0.83 us (2%)
    ppermute x16, starting transfers between devices, exchange(): return lax.ppermute(block, 'elem', pairs)  26.3 us
    pallas_call x15, Pallas kernels, call(): pl.pallas_call(kernel, out_shape=[jax.ShapeDtypeStruct(s, t) for s, t in...  12.3 us
    ppermute x16, waiting for transfers between devices, exchange(): return lax.ppermute(block, 'elem', pairs)  1.25 us
  transfers between devices with their start and end apart: 16, of which 2 were waited for; matrix products, arithmetic and copies ran while one was open for 0% of the time, Pallas kernels for 23%

profile of v12, /device:TPU:0, one launch (start us, length us, event | category | flops | bytes accessed | tf_op | source)
XLA Modules:
  0.0 40.7 jit_solution(31430902101836152)
XLA Ops:
  0.6 2.1 %shard_map.77 = (f32[3,512,128]{2,1,0:T(8,128)S(1)}, f32[3,512,128]{2,1,0:T(8,128)S(1)}, f32[3,512,128]{2,1,0:T(8,128)S(1)}, f32[3,512,128]{2,1,0:T(8,128)S(1)},...) custom-call(f32[3,512,128]{2,1,0:T(8,128)} %moment_far.1, ...), custom_call_target="tpu_custom_call" | custom-call | flops 1000000 | bytes 8094220 | tf_op jit(solution)/shard_map/pallas_call | solution.py:567
  2.8 3.1 %collective-permute-start = (f32[232,128]{1,0:T(8,128)S(1)}, f32[232,128]{1,0:T(8,128)S(1)}, u32[]{:S(2)}, u32[]{:S(2)}) collective-permute-start(f32[232,128]{1,0:T(8,128)S(1)} %get-tuple-element.44), channel_id=1, source_target_pairs={{28,4},{29,5},{30,6},{31,7},{0,8},{1,9},{2,10},{3,11},{12,20},{13,... | collective-permute-start | bytes 356360 | tf_op jit(solution)/shard_map/ppermute | solution.py:612
  5.8 0.0 collective-permute-start.1
  5.8 1.8 %shard_map.82 = (f32[3,512,128]{2,1,0:T(8,128)S(1)}, f32[176,128]{1,0:T(8,128)S(1)}, f32[176,128]{1,0:T(8,128)S(1)}, f32[176,128]{1,0:T(8,128)S(1)}, f32[176,128]{1,0:T(8,128)S(1)}) custom-call(f32[3,512,128]{2,1,0:T(8,128)S(1)} %get-tuple-element.36.moment_ref, f32[3,512,128]{2,1,0:T(8,128)S(1)} %get-tuple-element.37.carry_ref, ...), custom_call_target="tpu_custom_call" | custom-call | flops 20000000 | bytes 4308992 | tf_op jit(solution)/shard_map/pallas_call | solution.py:567
  7.7 3.2 %collective-permute-start.4 = (f32[176,128]{1,0:T(8,128)S(1)}, f32[176,128]{1,0:T(8,128)S(1)}, u32[]{:S(2)}, u32[]{:S(2)}) collective-permute-start(f32[176,128]{1,0:T(8,128)S(1)} %get-tuple-element.50), channel_id=1, source_target_pairs={{28,4},{29,5},{30,6},{31,7},{0,8},{1,9},{2,10},{3,11},{12,20},{13,... | collective-permute-start | bytes 270344 | tf_op jit(solution)/shard_map/ppermute | solution.py:612
  10.9 0.0 collective-permute-start.5
  10.9 0.0 collective-permute-done.ie_ref.refs_0_
  10.9 0.0 collective-permute-done.1.io_ref.refs_1_
  11.0 4.8 %collective-permute-start.2 = (f32[232,128]{1,0:T(8,128)S(1)}, f32[232,128]{1,0:T(8,128)S(1)}, u32[]{:S(2)}, u32[]{:S(2)}) collective-permute-start(f32[232,128]{1,0:T(8,128)S(1)} %shard_map.78.refs_0_), channel_id=1, source_target_pairs={{29,30},{31,0},{1,2},{5,6},{7,8},{9,10},{13,14},{15,16},{17,18},{2... | collective-permute-start | bytes 356360 | tf_op jit(solution)/shard_map/ppermute | solution.py:612
  15.8 0.1 collective-permute-start.3
  15.8 0.0 collective-permute-done.4.ie_ref.gie_ref
  15.8 0.0 collective-permute-done.5.io_ref.gio_ref
  15.9 3.6 %collective-permute-start.6 = (f32[176,128]{1,0:T(8,128)S(1)}, f32[176,128]{1,0:T(8,128)S(1)}, u32[]{:S(2)}, u32[]{:S(2)}) collective-permute-start(f32[176,128]{1,0:T(8,128)S(1)} %shard_map.83.refs_0_), channel_id=1, source_target_pairs={{29,30},{31,0},{1,2},{5,6},{7,8},{9,10},{13,14},{15,16},{17,18},{2... | collective-permute-start | bytes 270344 | tf_op jit(solution)/shard_map/ppermute | solution.py:612
  19.5 0.1 collective-permute-start.7
  19.6 0.0 collective-permute-done.2.refs_0_
  19.6 0.0 collective-permute-done.3.refs_3_
  19.6 2.0 %shard_map.81 = (f32[512,128]{1,0:T(8,128)S(1)}, f32[3,512,128]{2,1,0:T(8,128)S(1)}, f32[3,512,128]{2,1,0:T(8,128)S(1)}, f32[176,128]{1,0:T(8,128)S(1)}, f32[176...) custom-call(f32[3,512,128]{2,1,0:T(8,128)S(1)} %get-tuple-element.42.state_ref, ...), custom_call_target="tpu_custom_call" | custom-call | flops 20000000 | bytes 6881280 | tf_op jit(solution)/shard_map/pallas_call | solution.py:567
  21.6 3.0 %collective-permute-start.10 = (f32[176,128]{1,0:T(8,128)S(1)}, f32[176,128]{1,0:T(8,128)S(1)}, u32[]{:S(2)}, u32[]{:S(2)}) collective-permute-start(f32[176,128]{1,0:T(8,128)S(1)} %get-tuple-element.60), channel_id=1, source_target_pairs={{28,4},{29,5},{30,6},{31,7},{0,8},{1,9},{2,10},{3,11},{12,20},{13,... | collective-permute-start | bytes 270344 | tf_op jit(solution)/shard_map/ppermute | solution.py:612
  24.6 0.1 collective-permute-start.11
  24.8 0.0 collective-permute-done.6.refs_0_
  24.8 0.0 collective-permute-done.7.gje_ref
  24.8 1.9 %shard_map.86 = (f32[3,512,128]{2,1,0:T(8,128)S(1)}, f32[3,512,128]{2,1,0:T(8,128)S(1)}, f32[176,128]{1,0:T(8,128)S(1)}, f32[176,128]{1,0:T(8,128)S(1)}, f32[176,128]{1,0:T(8,128)S(1)}, /*index=5*/f32[176,128]{1,0:T(8,128)S(1)}) custom-call(f32[3,512,128]{2,1,0:T(8,128)S(1)} %get-tuple-element.36.moment_ref, f32[3,512,128]{2,1,0:T(8,128)S(1)} %get-tuple-element.37.carry_ref, ...), custom_call_target="tpu_custom_call" | custom-call | flops 20000000 | bytes 6504448 | tf_op jit(solution)/shard_map/pallas_call | solution.py:567
  26.7 0.1 collective-permute-start.8
  26.8 0.4 %collective-permute-start.9 = (f32[176,128]{1,0:T(8,128)S(1)}, f32[176,128]{1,0:T(8,128)S(1)}, u32[]{:S(2)}, u32[]{:S(2)}) collective-permute-start(f32[176,128]{1,0:T(8,128)S(1)} %get-tuple-element.57), channel_id=1, source_target_pairs={{4,12},{5,13},{6,14},{7,15},{8,16},{9,17},{10,18},{11,19},{28,29},... | collective-permute-start | bytes 270344 | tf_op jit(solution)/shard_map/ppermute | solution.py:612
  27.2 0.6 %collective-permute-done.10.ie_ref.refs_1_ = f32[176,128]{1,0:T(8,128)S(1)} collective-permute-done((f32[176,128]{1,0:T(8,128)S(1)}, f32[176,128]{1,0:T(8,128)S(1)}, u32[]{:S(2)}, u32[]{:S(2)}) %collective-permute-start.10) | collective-permute-done | bytes 90144 | tf_op jit(solution)/shard_map/ppermute | solution.py:612
  27.8 0.0 collective-permute-done.11.io_ref.refs_2_
  27.8 4.1 %collective-permute-start.12 = (f32[176,128]{1,0:T(8,128)S(1)}, f32[176,128]{1,0:T(8,128)S(1)}, u32[]{:S(2)}, u32[]{:S(2)}) collective-permute-start(f32[176,128]{1,0:T(8,128)S(1)} %shard_map.87.refs_0_), channel_id=1, source_target_pairs={{29,30},{31,0},{1,2},{5,6},{7,8},{9,10},{13,14},{15,16},{17,18},{2... | collective-permute-start | bytes 270344 | tf_op jit(solution)/shard_map/ppermute | solution.py:612
  32.0 0.1 collective-permute-start.13
  32.1 0.0 collective-permute-done.8.gie_ref.ie_ref
  32.1 0.0 collective-permute-done.9.gio_ref.io_ref
  32.1 3.6 %collective-permute-start.14 = (f32[176,128]{1,0:T(8,128)S(1)}, f32[176,128]{1,0:T(8,128)S(1)}, u32[]{:S(2)}, u32[]{:S(2)}) collective-permute-start(f32[176,128]{1,0:T(8,128)S(1)} %shard_map.92.refs_0_), channel_id=1, source_target_pairs={{29,30},{31,0},{1,2},{5,6},{7,8},{9,10},{13,14},{15,16},{17,18},{2... | collective-permute-start | bytes 270344 | tf_op jit(solution)/shard_map/ppermute | solution.py:612
  35.8 0.1 collective-permute-start.15
  35.8 0.0 collective-permute-done.12.refs_0_
  35.9 0.0 collective-permute-done.13.refs_4_
  35.9 2.3 %shard_map.90 = (f32[3,512,128]{2,1,0:T(8,128)}, f32[8,128]{1,0:T(8,128)S(1)}) custom-call(f32[3,512,128]{2,1,0:T(8,128)S(1)} %get-tuple-element.58.state_ref, f32[3,512,128]{2,1,0:T(8,128)S(1)} %get-tuple-element.37.carry_ref, f32[3,512,128]{2,1,0:T(8,128)S(1)} %get-tuple-element.38.weigh_ref, bf16[256,384]{1,0:T(8,128)(2,1)S(1)} %get-tuple-element.39.table_ref, ...), custom_call_target="tpu_custom_call" | custom-call | flops 20000000 | bytes 5361664 | tf_op jit(solution)/shard_map/pallas_call | solution.py:567
  38.1 1.0 %shard_map.91 = (f32[3,8,8,8,128]{4,3,2,1,0:T(8,128)}, f32[3,8,8,8,128]{4,3,2,1,0:T(8,128)S(1)}) custom-call(f32[3,512,128]{2,1,0:T(8,128)S(1)} %get-tuple-element.54.moment_ref, s32[4,8,128]{2,1,0:T(8,128)S(1)} %get-tuple-element.41.index_ref, f32[512,128]{1,0:T(8,128)S(1)} %get-tuple-element.48.refs_1_.inverse_ref.refs_0_, ...), custom_call_target="tpu_custom_call" | custom-call | flops 1000000 | bytes 3608576 | tf_op jit(solution)/shard_map/pallas_call | solution.py:567
  39.2 0.6 %collective-permute-done.14.refs_0_ = f32[176,128]{1,0:T(8,128)S(1)} collective-permute-done((f32[176,128]{1,0:T(8,128)S(1)}, f32[176,128]{1,0:T(8,128)S(1)}, u32[]{:S(2)}, u32[]{:S(2)}) %collective-permute-start.14) | collective-permute-done | bytes 90144 | tf_op jit(solution)/shard_map/ppermute | solution.py:612
  39.8 0.0 collective-permute-done.15.gje_ref
  39.8 0.9 %shard_map.95 = f32[3,8,8,8,128]{4,3,2,1,0:T(8,128)} custom-call(f32[3,8,8,8,128]{4,3,2,1,0:T(8,128)} %get-tuple-element.65.inner_far, f32[3,8,8,8,128]{4,3,2,1,0:T(8,128)S(1)} %get-tuple-element.66.refs_1_.moment_ref, s32[4,8,128]{2,1,0:T(8,128)S(1)} %get-tuple-element.41.index_ref, ...), custom_call_target="tpu_custom_call", output_to_operand_aliasing={{}: (0, {})} | custom-call | flops 1000000 | bytes 2818048 | tf_op jit(solution)/shard_map/pallas_call | solution.py:567
  (12 shorter events, 0.3 us)
Async XLA Ops:
  2.8 8.2 %collective-permute-start = (f32[232,128]{1,0:T(8,128)S(1)}, f32[232,128]{1,0:T(8,128)S(1)}, u32[]{:S(2)}, u32[]{:S(2)}) collective-permute-start(f32[232,128]{1,0:T(8,128)S(1)} %get-tuple-element.44), channel_id=1, source_target_pairs={{28,4},{29,5},{30,6},{31,7},{0,8},{1,9},{2,10},{3,11},{12,20},{13,... | collective-permute-start | bytes 356360 | tf_op jit(solution)/shard_map/ppermute | solution.py:612
  5.8 5.1 %collective-permute-start.1 = (f32[232,128]{1,0:T(8,128)S(1)}, f32[232,128]{1,0:T(8,128)S(1)}, u32[]{:S(2)}, u32[]{:S(2)}) collective-permute-start(f32[232,128]{1,0:T(8,128)S(1)} %get-tuple-element.45), channel_id=1, source_target_pairs={{4,12},{5,13},{6,14},{7,15},{8,16},{9,17},{10,18},{11,19},{28,29},... | collective-permute-start | bytes 356360 | tf_op jit(solution)/shard_map/ppermute | solution.py:612
  7.7 8.1 %collective-permute-start.4 = (f32[176,128]{1,0:T(8,128)S(1)}, f32[176,128]{1,0:T(8,128)S(1)}, u32[]{:S(2)}, u32[]{:S(2)}) collective-permute-start(f32[176,128]{1,0:T(8,128)S(1)} %get-tuple-element.50), channel_id=1, source_target_pairs={{28,4},{29,5},{30,6},{31,7},{0,8},{1,9},{2,10},{3,11},{12,20},{13,... | collective-permute-start | bytes 270344 | tf_op jit(solution)/shard_map/ppermute | solution.py:612
  10.9 4.9 %collective-permute-start.5 = (f32[176,128]{1,0:T(8,128)S(1)}, f32[176,128]{1,0:T(8,128)S(1)}, u32[]{:S(2)}, u32[]{:S(2)}) collective-permute-start(f32[176,128]{1,0:T(8,128)S(1)} %get-tuple-element.51), channel_id=1, source_target_pairs={{4,12},{5,13},{6,14},{7,15},{8,16},{9,17},{10,18},{11,19},{28,29},... | collective-permute-start | bytes 270344 | tf_op jit(solution)/shard_map/ppermute | solution.py:612
  11.0 8.6 %collective-permute-start.2 = (f32[232,128]{1,0:T(8,128)S(1)}, f32[232,128]{1,0:T(8,128)S(1)}, u32[]{:S(2)}, u32[]{:S(2)}) collective-permute-start(f32[232,128]{1,0:T(8,128)S(1)} %shard_map.78.refs_0_), channel_id=1, source_target_pairs={{29,30},{31,0},{1,2},{5,6},{7,8},{9,10},{13,14},{15,16},{17,18},{2... | collective-permute-start | bytes 356360 | tf_op jit(solution)/shard_map/ppermute | solution.py:612
  15.8 3.8 %collective-permute-start.3 = (f32[232,128]{1,0:T(8,128)S(1)}, f32[232,128]{1,0:T(8,128)S(1)}, u32[]{:S(2)}, u32[]{:S(2)}) collective-permute-start(f32[232,128]{1,0:T(8,128)S(1)} %shard_map.80), channel_id=1, source_target_pairs={{28,29},{30,31},{0,1},{2,3},{4,5},{6,7},{8,9},{10,11},{12,13},{14,... | collective-permute-start | bytes 356360 | tf_op jit(solution)/shard_map/ppermute | solution.py:612
  15.9 8.9 %collective-permute-start.6 = (f32[176,128]{1,0:T(8,128)S(1)}, f32[176,128]{1,0:T(8,128)S(1)}, u32[]{:S(2)}, u32[]{:S(2)}) collective-permute-start(f32[176,128]{1,0:T(8,128)S(1)} %shard_map.83.refs_0_), channel_id=1, source_target_pairs={{29,30},{31,0},{1,2},{5,6},{7,8},{9,10},{13,14},{15,16},{17,18},{2... | collective-permute-start | bytes 270344 | tf_op jit(solution)/shard_map/ppermute | solution.py:612
  19.5 5.3 %collective-permute-start.7 = (f32[176,128]{1,0:T(8,128)S(1)}, f32[176,128]{1,0:T(8,128)S(1)}, u32[]{:S(2)}, u32[]{:S(2)}) collective-permute-start(f32[176,128]{1,0:T(8,128)S(1)} %shard_map.85), channel_id=1, source_target_pairs={{28,29},{30,31},{0,1},{2,3},{4,5},{6,7},{8,9},{10,11},{12,13},{14,... | collective-permute-start | bytes 270344 | tf_op jit(solution)/shard_map/ppermute | solution.py:612
  21.6 6.2 %collective-permute-start.10 = (f32[176,128]{1,0:T(8,128)S(1)}, f32[176,128]{1,0:T(8,128)S(1)}, u32[]{:S(2)}, u32[]{:S(2)}) collective-permute-start(f32[176,128]{1,0:T(8,128)S(1)} %get-tuple-element.60), channel_id=1, source_target_pairs={{28,4},{29,5},{30,6},{31,7},{0,8},{1,9},{2,10},{3,11},{12,20},{13,... | collective-permute-start | bytes 270344 | tf_op jit(solution)/shard_map/ppermute | solution.py:612
  24.6 3.2 %collective-permute-start.11 = (f32[176,128]{1,0:T(8,128)S(1)}, f32[176,128]{1,0:T(8,128)S(1)}, u32[]{:S(2)}, u32[]{:S(2)}) collective-permute-start(f32[176,128]{1,0:T(8,128)S(1)} %get-tuple-element.61), channel_id=1, source_target_pairs={{4,12},{5,13},{6,14},{7,15},{8,16},{9,17},{10,18},{11,19},{28,29},... | collective-permute-start | bytes 270344 | tf_op jit(solution)/shard_map/ppermute | solution.py:612
  26.7 5.4 %collective-permute-start.8 = (f32[176,128]{1,0:T(8,128)S(1)}, f32[176,128]{1,0:T(8,128)S(1)}, u32[]{:S(2)}, u32[]{:S(2)}) collective-permute-start(f32[176,128]{1,0:T(8,128)S(1)} %get-tuple-element.56), channel_id=1, source_target_pairs={{28,4},{29,5},{30,6},{31,7},{0,8},{1,9},{2,10},{3,11},{12,20},{13,... | collective-permute-start | bytes 270344 | tf_op jit(solution)/shard_map/ppermute | solution.py:612
  26.8 5.3 %collective-permute-start.9 = (f32[176,128]{1,0:T(8,128)S(1)}, f32[176,128]{1,0:T(8,128)S(1)}, u32[]{:S(2)}, u32[]{:S(2)}) collective-permute-start(f32[176,128]{1,0:T(8,128)S(1)} %get-tuple-element.57), channel_id=1, source_target_pairs={{4,12},{5,13},{6,14},{7,15},{8,16},{9,17},{10,18},{11,19},{28,29},... | collective-permute-start | bytes 270344 | tf_op jit(solution)/shard_map/ppermute | solution.py:612
  27.8 8.0 %collective-permute-start.12 = (f32[176,128]{1,0:T(8,128)S(1)}, f32[176,128]{1,0:T(8,128)S(1)}, u32[]{:S(2)}, u32[]{:S(2)}) collective-permute-start(f32[176,128]{1,0:T(8,128)S(1)} %shard_map.87.refs_0_), channel_id=1, source_target_pairs={{29,30},{31,0},{1,2},{5,6},{7,8},{9,10},{13,14},{15,16},{17,18},{2... | collective-permute-start | bytes 270344 | tf_op jit(solution)/shard_map/ppermute | solution.py:612
  32.0 3.9 %collective-permute-start.13 = (f32[176,128]{1,0:T(8,128)S(1)}, f32[176,128]{1,0:T(8,128)S(1)}, u32[]{:S(2)}, u32[]{:S(2)}) collective-permute-start(f32[176,128]{1,0:T(8,128)S(1)} %shard_map.89), channel_id=1, source_target_pairs={{28,29},{30,31},{0,1},{2,3},{4,5},{6,7},{8,9},{10,11},{12,13},{14,... | collective-permute-start | bytes 270344 | tf_op jit(solution)/shard_map/ppermute | solution.py:612
  32.1 7.7 %collective-permute-start.14 = (f32[176,128]{1,0:T(8,128)S(1)}, f32[176,128]{1,0:T(8,128)S(1)}, u32[]{:S(2)}, u32[]{:S(2)}) collective-permute-start(f32[176,128]{1,0:T(8,128)S(1)} %shard_map.92.refs_0_), channel_id=1, source_target_pairs={{29,30},{31,0},{1,2},{5,6},{7,8},{9,10},{13,14},{15,16},{17,18},{2... | collective-permute-start | bytes 270344 | tf_op jit(solution)/shard_map/ppermute | solution.py:612
  35.8 4.0 %collective-permute-start.15 = (f32[176,128]{1,0:T(8,128)S(1)}, f32[176,128]{1,0:T(8,128)S(1)}, u32[]{:S(2)}, u32[]{:S(2)}) collective-permute-start(f32[176,128]{1,0:T(8,128)S(1)} %shard_map.94), channel_id=1, source_target_pairs={{28,29},{30,31},{0,1},{2,3},{4,5},{6,7},{8,9},{10,11},{12,13},{14,... | collective-permute-start | bytes 270344 | tf_op jit(solution)/shard_map/ppermute | solution.py:612

commit v13 on v12

--- a/solution.py
+++ b/solution.py
@@ -295,13 +295,12 @@
     columns,
     moment_far,
     state_far,
-    flow_far,
     weight_far,
     diff_far,
     numbers_far,
     moment_ref,
     state_ref,
-    carry_ref,
+    mass_ref,
     weigh_ref,
     table_ref,
     turned_ref,
@@ -312,14 +311,12 @@
     je_ref,
     jo_ref,
     weight_ref,
-    mass_ref,
-    flow_ref,
     numbers_ref,
     diff_ref,
     arrived,
 ):
-    far = (numbers_far, weight_far, state_far, diff_far, moment_far, flow_far)
-    near = (numbers_ref, weight_ref, state_ref, diff_ref, moment_ref, flow_ref)
+    far = (numbers_far, weight_far, state_far, diff_far, moment_far)
+    near = (numbers_ref, weight_ref, state_ref, diff_ref, moment_ref)
     copies = [pltpu.make_async_copy(a, b, arrived.at[n]) for n, (a, b) in enumerate(zip(far, near))]
     for copy in copies:
         copy.start()
@@ -355,20 +352,19 @@
     copies[3].wait()
     for f in range(3):
         weigh_ref[f] = mass_ref[...] * (DT * diff_ref[f])
-    copies[5].wait()
-    for d in range(3):
-        carry_ref[d] = mass_ref[...] * (DT * flow_ref[d])
     copies[4].wait()
 
 
 def moment_kernel(
     columns,
     moment_ref,
-    carry_ref,
+    flow_ref,
+    mass_ref,
     weigh_ref,
     table_ref,
     turned_ref,
     index_ref,
+    carry_ref,
     joined_ref,
     ie_ref,
     io_ref,
@@ -379,6 +375,8 @@
     ends = ends_of(columns)
     index = index_of(index_ref)
     out = (ie_ref, io_ref, je_ref, jo_ref)
+    for d in range(3):
+        carry_ref[d] = mass_ref[...] * (DT * flow_ref[d])
 
     def finish(f):
         join_heights(joined_ref.at[f], index)
@@ -650,36 +648,39 @@
     def faces_shape(count):
         return [(face_shape(count), F32)] * 4
 
-    moment, state, carry, weigh, table, turned, index, joined_state, *faces_state = call(
+    moment, state, mass, weigh, table, turned, index, joined_state, *faces_state = call(
         functools.partial(index_kernel, columns),
-        [FAR] * 6,
-        [whole] * 4
+        [FAR] * 5,
+        [whole, whole, block, whole]
         + [((256, 384), BF16), ((128, 768), BF16)]
         + [((4, 8, 128), jnp.int32), ((4, 512, 128), F32)]
         + faces_shape(4),
         [
             pltpu.VMEM((512, 128), F32),
-            pltpu.VMEM((512, 128), F32),
-            work,
             pltpu.VMEM((1, 128), jnp.int32),
             pltpu.SMEM((3,), F32),
-            pltpu.SemaphoreType.DMA((6,)),
+            pltpu.SemaphoreType.DMA((5,)),
         ],
         1_000_000,
-        *map(far, (moment_fields, adjoint_fields, velocity, mass_weights)),
-        *map(far, (diffusivity, numbering.reshape(1, 128))),
-    )
-    tables = (carry, weigh, table, turned, index)
+        *map(far, (moment_fields, adjoint_fields, mass_weights, diffusivity)),
+        far(numbering.reshape(1, 128)),
+    )
     got_state = meet(4, faces_state)
-    joined_moment, *faces_moment = call(
+    carry, joined_moment, *faces_moment = call(
         functools.partial(moment_kernel, columns),
-        [VMEM] * 6,
-        [whole] + faces_shape(3),
+        [VMEM] * 7,
+        [whole, whole] + faces_shape(3),
         [slopes],
         20_000_000,
         moment,
-        *tables,
-    )
+        velocity,
+        mass,
+        weigh,
+        table,
+        turned,
+        index,
+    )
+    tables = (carry, weigh, table, turned, index)
     got_moment = meet(3, faces_moment)
     inverse, state, joined_state, *faces_state = call(
         functools.partial(state_kernel, columns, True),

time: 40.8 us -> 40.8 us (level)
  no operation moved by 1% of the time
where the time goes in v13:
time: 40.8 us; the launch traced here: 40.7 us
  starting transfers between devices  26.3 us (64%)
  Pallas kernels  12.3 us (30%)
  waiting for transfers between devices  1.3 us (3%)
  between operations  0.83 us (2%)
    ppermute x16, starting transfers between devices, exchange(): return lax.ppermute(block, 'elem', pairs)  26.3 us
    pallas_call x15, Pallas kernels, call(): pl.pallas_call(kernel, out_shape=[jax.ShapeDtypeStruct(s, t) for s, t in...  12.3 us
    ppermute x16, waiting for transfers between devices, exchange(): return lax.ppermute(block, 'elem', pairs)  1.3 us
  transfers between devices with their start and end apart: 16, of which 2 were waited for; matrix products, arithmetic and copies ran while one was open for 0% of the time, Pallas kernels for 23%

profile of v13, /device:TPU:0, one launch (start us, length us, event | category | flops | bytes accessed | tf_op | source)
XLA Modules:
  0.0 40.7 jit_solution(7715414285454253930)
XLA Ops:
  0.6 0.0 copy-start
  0.6 2.1 %shard_map.77 = (f32[3,512,128]{2,1,0:T(8,128)S(1)}, f32[3,512,128]{2,1,0:T(8,128)S(1)}, f32[512,128]{1,0:T(8,128)S(1)}, f32[3,512,128]{2,1,0:T(8,128)S(1)}, bf1...) custom-call(f32[3,512,128]{2,1,0:T(8,128)} %moment_far.1, ...), custom_call_target="tpu_custom_call" | custom-call | flops 1000000 | bytes 6783500 | tf_op jit(solution)/shard_map/pallas_call | solution.py:565
  2.7 3.1 %collective-permute-start = (f32[232,128]{1,0:T(8,128)S(1)}, f32[232,128]{1,0:T(8,128)S(1)}, u32[]{:S(2)}, u32[]{:S(2)}) collective-permute-start(f32[232,128]{1,0:T(8,128)S(1)} %get-tuple-element.46), channel_id=1, source_target_pairs={{28,4},{29,5},{30,6},{31,7},{0,8},{1,9},{2,10},{3,11},{12,20},{13,... | collective-permute-start | bytes 356360 | tf_op jit(solution)/shard_map/ppermute | solution.py:610
  5.8 0.0 collective-permute-start.1
  5.8 0.0 copy-done
  5.8 1.9 %shard_map.78 = (f32[3,512,128]{2,1,0:T(8,128)S(1)}, f32[3,512,128]{2,1,0:T(8,128)S(1)}, f32[176,128]{1,0:T(8,128)S(1)}, f32[176,128]{1,0:T(8,128)S(1)}, f32[176,128]{1,0:T(8,128)S(1)}, /*index=5*/f32[176,128]{1,0:T(8,128)S(1)}) custom-call(f32[3,512,128]{2,1,0:T(8,128)S(1)} %get-tuple-element.37.moment_ref, f32[3,512,128]{2,1,0:T(8,128)S(1)} %copy-done, ...), custom_call_target="tpu_custom_call" | custom-call | flops 20000000 | bytes 5357568 | tf_op jit(solution)/shard_map/pallas_call | solution.py:565
  7.7 3.2 %collective-permute-start.4 = (f32[176,128]{1,0:T(8,128)S(1)}, f32[176,128]{1,0:T(8,128)S(1)}, u32[]{:S(2)}, u32[]{:S(2)}) collective-permute-start(f32[176,128]{1,0:T(8,128)S(1)} %get-tuple-element.52), channel_id=1, source_target_pairs={{28,4},{29,5},{30,6},{31,7},{0,8},{1,9},{2,10},{3,11},{12,20},{13,... | collective-permute-start | bytes 270344 | tf_op jit(solution)/shard_map/ppermute | solution.py:610
  10.9 0.0 collective-permute-start.5
  10.9 0.0 collective-permute-done.ie_ref.refs_0_
  10.9 0.0 collective-permute-done.1.io_ref.refs_1_
  11.0 4.8 %collective-permute-start.2 = (f32[232,128]{1,0:T(8,128)S(1)}, f32[232,128]{1,0:T(8,128)S(1)}, u32[]{:S(2)}, u32[]{:S(2)}) collective-permute-start(f32[232,128]{1,0:T(8,128)S(1)} %shard_map.79.refs_0_), channel_id=1, source_target_pairs={{29,30},{31,0},{1,2},{5,6},{7,8},{9,10},{13,14},{15,16},{17,18},{2... | collective-permute-start | bytes 356360 | tf_op jit(solution)/shard_map/ppermute | solution.py:610
  15.8 0.1 collective-permute-start.3
  15.9 0.0 collective-permute-done.4.ie_ref.gie_ref
  15.9 0.0 collective-permute-done.5.io_ref.gio_ref
  15.9 3.5 %collective-permute-start.6 = (f32[176,128]{1,0:T(8,128)S(1)}, f32[176,128]{1,0:T(8,128)S(1)}, u32[]{:S(2)}, u32[]{:S(2)}) collective-permute-start(f32[176,128]{1,0:T(8,128)S(1)} %shard_map.83.refs_0_), channel_id=1, source_target_pairs={{29,30},{31,0},{1,2},{5,6},{7,8},{9,10},{13,14},{15,16},{17,18},{2... | collective-permute-start | bytes 270344 | tf_op jit(solution)/shard_map/ppermute | solution.py:610
  19.5 0.1 collective-permute-start.7
  19.6 0.0 collective-permute-done.2.refs_0_
  19.6 0.0 collective-permute-done.3.refs_3_
  19.6 2.0 %shard_map.82 = (f32[512,128]{1,0:T(8,128)S(1)}, f32[3,512,128]{2,1,0:T(8,128)S(1)}, f32[3,512,128]{2,1,0:T(8,128)S(1)}, f32[176,128]{1,0:T(8,128)S(1)}, f32[176...) custom-call(f32[3,512,128]{2,1,0:T(8,128)S(1)} %get-tuple-element.44.state_ref, ...), custom_call_target="tpu_custom_call" | custom-call | flops 20000000 | bytes 6881280 | tf_op jit(solution)/shard_map/pallas_call | solution.py:565
  21.6 3.0 %collective-permute-start.10 = (f32[176,128]{1,0:T(8,128)S(1)}, f32[176,128]{1,0:T(8,128)S(1)}, u32[]{:S(2)}, u32[]{:S(2)}) collective-permute-start(f32[176,128]{1,0:T(8,128)S(1)} %get-tuple-element.62), channel_id=1, source_target_pairs={{28,4},{29,5},{30,6},{31,7},{0,8},{1,9},{2,10},{3,11},{12,20},{13,... | collective-permute-start | bytes 270344 | tf_op jit(solution)/shard_map/ppermute | solution.py:610
  24.6 0.1 collective-permute-start.11
  24.7 0.0 collective-permute-done.6.refs_0_
  24.7 0.0 collective-permute-done.7.gje_ref
  24.7 1.9 %shard_map.86 = (f32[3,512,128]{2,1,0:T(8,128)S(1)}, f32[3,512,128]{2,1,0:T(8,128)S(1)}, f32[176,128]{1,0:T(8,128)S(1)}, f32[176,128]{1,0:T(8,128)S(1)}, f32[176,128]{1,0:T(8,128)S(1)}, /*index=5*/f32[176,128]{1,0:T(8,128)S(1)}) custom-call(f32[3,512,128]{2,1,0:T(8,128)S(1)} %get-tuple-element.37.moment_ref, f32[3,512,128]{2,1,0:T(8,128)S(1)} %get-tuple-element.43.carry_ref, ...), custom_call_target="tpu_custom_call" | custom-call | flops 20000000 | bytes 6504448 | tf_op jit(solution)/shard_map/pallas_call | solution.py:565
  26.7 0.1 collective-permute-start.8
  26.8 0.4 %collective-permute-start.9 = (f32[176,128]{1,0:T(8,128)S(1)}, f32[176,128]{1,0:T(8,128)S(1)}, u32[]{:S(2)}, u32[]{:S(2)}) collective-permute-start(f32[176,128]{1,0:T(8,128)S(1)} %get-tuple-element.59), channel_id=1, source_target_pairs={{4,12},{5,13},{6,14},{7,15},{8,16},{9,17},{10,18},{11,19},{28,29},... | collective-permute-start | bytes 270344 | tf_op jit(solution)/shard_map/ppermute | solution.py:610
  27.2 0.6 %collective-permute-done.10.ie_ref.refs_1_ = f32[176,128]{1,0:T(8,128)S(1)} collective-permute-done((f32[176,128]{1,0:T(8,128)S(1)}, f32[176,128]{1,0:T(8,128)S(1)}, u32[]{:S(2)}, u32[]{:S(2)}) %collective-permute-start.10) | collective-permute-done | bytes 90144 | tf_op jit(solution)/shard_map/ppermute | solution.py:610
  27.8 0.0 collective-permute-done.11.io_ref.refs_2_
  27.8 4.2 %collective-permute-start.12 = (f32[176,128]{1,0:T(8,128)S(1)}, f32[176,128]{1,0:T(8,128)S(1)}, u32[]{:S(2)}, u32[]{:S(2)}) collective-permute-start(f32[176,128]{1,0:T(8,128)S(1)} %shard_map.87.refs_0_), channel_id=1, source_target_pairs={{29,30},{31,0},{1,2},{5,6},{7,8},{9,10},{13,14},{15,16},{17,18},{2... | collective-permute-start | bytes 270344 | tf_op jit(solution)/shard_map/ppermute | solution.py:610
  32.0 0.1 collective-permute-start.13
  32.1 0.0 collective-permute-done.8.gie_ref.ie_ref
  32.1 0.0 collective-permute-done.9.gio_ref.io_ref
  32.1 3.6 %collective-permute-start.14 = (f32[176,128]{1,0:T(8,128)S(1)}, f32[176,128]{1,0:T(8,128)S(1)}, u32[]{:S(2)}, u32[]{:S(2)}) collective-permute-start(f32[176,128]{1,0:T(8,128)S(1)} %shard_map.92.refs_0_), channel_id=1, source_target_pairs={{29,30},{31,0},{1,2},{5,6},{7,8},{9,10},{13,14},{15,16},{17,18},{2... | collective-permute-start | bytes 270344 | tf_op jit(solution)/shard_map/ppermute | solution.py:610
  35.7 0.1 collective-permute-start.15
  35.8 0.0 collective-permute-done.12.refs_0_
  35.8 0.0 collective-permute-done.13.refs_4_
  35.8 2.2 %shard_map.90 = (f32[3,512,128]{2,1,0:T(8,128)}, f32[8,128]{1,0:T(8,128)S(1)}) custom-call(f32[3,512,128]{2,1,0:T(8,128)S(1)} %get-tuple-element.60.state_ref, f32[3,512,128]{2,1,0:T(8,128)S(1)} %get-tuple-element.43.carry_ref, f32[3,512,128]{2,1,0:T(8,128)S(1)} %get-tuple-element.39.weigh_ref, bf16[256,384]{1,0:T(8,128)(2,1)S(1)} %get-tuple-element.40.table_ref, ...), custom_call_target="tpu_custom_call" | custom-call | flops 20000000 | bytes 5361664 | tf_op jit(solution)/shard_map/pallas_call | solution.py:565
  38.1 1.0 %shard_map.91 = (f32[3,8,8,8,128]{4,3,2,1,0:T(8,128)}, f32[3,8,8,8,128]{4,3,2,1,0:T(8,128)S(1)}) custom-call(f32[3,512,128]{2,1,0:T(8,128)S(1)} %get-tuple-element.56.moment_ref, s32[4,8,128]{2,1,0:T(8,128)S(1)} %get-tuple-element.42.index_ref, f32[512,128]{1,0:T(8,128)S(1)} %get-tuple-element.50.refs_1_.inverse_ref.refs_0_, ...), custom_call_target="tpu_custom_call" | custom-call | flops 1000000 | bytes 3608576 | tf_op jit(solution)/shard_map/pallas_call | solution.py:565
  39.1 0.7 %collective-permute-done.14.refs_0_ = f32[176,128]{1,0:T(8,128)S(1)} collective-permute-done((f32[176,128]{1,0:T(8,128)S(1)}, f32[176,128]{1,0:T(8,128)S(1)}, u32[]{:S(2)}, u32[]{:S(2)}) %collective-permute-start.14) | collective-permute-done | bytes 90144 | tf_op jit(solution)/shard_map/ppermute | solution.py:610
  39.8 0.0 collective-permute-done.15.gje_ref
  39.8 0.9 %shard_map.95 = f32[3,8,8,8,128]{4,3,2,1,0:T(8,128)} custom-call(f32[3,8,8,8,128]{4,3,2,1,0:T(8,128)} %get-tuple-element.67.inner_far, f32[3,8,8,8,128]{4,3,2,1,0:T(8,128)S(1)} %get-tuple-element.68.refs_1_.moment_ref, s32[4,8,128]{2,1,0:T(8,128)S(1)} %get-tuple-element.42.index_ref, ...), custom_call_target="tpu_custom_call", output_to_operand_aliasing={{}: (0, {})} | custom-call | flops 1000000 | bytes 2818048 | tf_op jit(solution)/shard_map/pallas_call | solution.py:565
  (12 shorter events, 0.3 us)
Async XLA Ops:
  0.6 5.2 %copy-start = (f32[3,512,128]{2,1,0:T(8,128)S(1)}, f32[3,512,128]{2,1,0:T(8,128)}, u32[]{:S(2)}) copy-start(f32[3,512,128]{2,1,0:T(8,128)} %flow_ref.1) | copy-start | bytes 2359300
  2.7 8.2 %collective-permute-start = (f32[232,128]{1,0:T(8,128)S(1)}, f32[232,128]{1,0:T(8,128)S(1)}, u32[]{:S(2)}, u32[]{:S(2)}) collective-permute-start(f32[232,128]{1,0:T(8,128)S(1)} %get-tuple-element.46), channel_id=1, source_target_pairs={{28,4},{29,5},{30,6},{31,7},{0,8},{1,9},{2,10},{3,11},{12,20},{13,... | collective-permute-start | bytes 356360 | tf_op jit(solution)/shard_map/ppermute | solution.py:610
  5.8 5.1 %collective-permute-start.1 = (f32[232,128]{1,0:T(8,128)S(1)}, f32[232,128]{1,0:T(8,128)S(1)}, u32[]{:S(2)}, u32[]{:S(2)}) collective-permute-start(f32[232,128]{1,0:T(8,128)S(1)} %get-tuple-element.47), channel_id=1, source_target_pairs={{4,12},{5,13},{6,14},{7,15},{8,16},{9,17},{10,18},{11,19},{28,29},... | collective-permute-start | bytes 356360 | tf_op jit(solution)/shard_map/ppermute | solution.py:610
  7.7 8.1 %collective-permute-start.4 = (f32[176,128]{1,0:T(8,128)S(1)}, f32[176,128]{1,0:T(8,128)S(1)}, u32[]{:S(2)}, u32[]{:S(2)}) collective-permute-start(f32[176,128]{1,0:T(8,128)S(1)} %get-tuple-element.52), channel_id=1, source_target_pairs={{28,4},{29,5},{30,6},{31,7},{0,8},{1,9},{2,10},{3,11},{12,20},{13,... | collective-permute-start | bytes 270344 | tf_op jit(solution)/shard_map/ppermute | solution.py:610
  10.9 4.9 %collective-permute-start.5 = (f32[176,128]{1,0:T(8,128)S(1)}, f32[176,128]{1,0:T(8,128)S(1)}, u32[]{:S(2)}, u32[]{:S(2)}) collective-permute-start(f32[176,128]{1,0:T(8,128)S(1)} %get-tuple-element.53), channel_id=1, source_target_pairs={{4,12},{5,13},{6,14},{7,15},{8,16},{9,17},{10,18},{11,19},{28,29},... | collective-permute-start | bytes 270344 | tf_op jit(solution)/shard_map/ppermute | solution.py:610
  11.0 8.6 %collective-permute-start.2 = (f32[232,128]{1,0:T(8,128)S(1)}, f32[232,128]{1,0:T(8,128)S(1)}, u32[]{:S(2)}, u32[]{:S(2)}) collective-permute-start(f32[232,128]{1,0:T(8,128)S(1)} %shard_map.79.refs_0_), channel_id=1, source_target_pairs={{29,30},{31,0},{1,2},{5,6},{7,8},{9,10},{13,14},{15,16},{17,18},{2... | collective-permute-start | bytes 356360 | tf_op jit(solution)/shard_map/ppermute | solution.py:610
  15.8 3.8 %collective-permute-start.3 = (f32[232,128]{1,0:T(8,128)S(1)}, f32[232,128]{1,0:T(8,128)S(1)}, u32[]{:S(2)}, u32[]{:S(2)}) collective-permute-start(f32[232,128]{1,0:T(8,128)S(1)} %shard_map.81), channel_id=1, source_target_pairs={{28,29},{30,31},{0,1},{2,3},{4,5},{6,7},{8,9},{10,11},{12,13},{14,... | collective-permute-start | bytes 356360 | tf_op jit(solution)/shard_map/ppermute | solution.py:610
  15.9 8.8 %collective-permute-start.6 = (f32[176,128]{1,0:T(8,128)S(1)}, f32[176,128]{1,0:T(8,128)S(1)}, u32[]{:S(2)}, u32[]{:S(2)}) collective-permute-start(f32[176,128]{1,0:T(8,128)S(1)} %shard_map.83.refs_0_), channel_id=1, source_target_pairs={{29,30},{31,0},{1,2},{5,6},{7,8},{9,10},{13,14},{15,16},{17,18},{2... | collective-permute-start | bytes 270344 | tf_op jit(solution)/shard_map/ppermute | solution.py:610
  19.5 5.3 %collective-permute-start.7 = (f32[176,128]{1,0:T(8,128)S(1)}, f32[176,128]{1,0:T(8,128)S(1)}, u32[]{:S(2)}, u32[]{:S(2)}) collective-permute-start(f32[176,128]{1,0:T(8,128)S(1)} %shard_map.85), channel_id=1, source_target_pairs={{28,29},{30,31},{0,1},{2,3},{4,5},{6,7},{8,9},{10,11},{12,13},{14,... | collective-permute-start | bytes 270344 | tf_op jit(solution)/shard_map/ppermute | solution.py:610
  21.6 6.2 %collective-permute-start.10 = (f32[176,128]{1,0:T(8,128)S(1)}, f32[176,128]{1,0:T(8,128)S(1)}, u32[]{:S(2)}, u32[]{:S(2)}) collective-permute-start(f32[176,128]{1,0:T(8,128)S(1)} %get-tuple-element.62), channel_id=1, source_target_pairs={{28,4},{29,5},{30,6},{31,7},{0,8},{1,9},{2,10},{3,11},{12,20},{13,... | collective-permute-start | bytes 270344 | tf_op jit(solution)/shard_map/ppermute | solution.py:610
  24.6 3.2 %collective-permute-start.11 = (f32[176,128]{1,0:T(8,128)S(1)}, f32[176,128]{1,0:T(8,128)S(1)}, u32[]{:S(2)}, u32[]{:S(2)}) collective-permute-start(f32[176,128]{1,0:T(8,128)S(1)} %get-tuple-element.63), channel_id=1, source_target_pairs={{4,12},{5,13},{6,14},{7,15},{8,16},{9,17},{10,18},{11,19},{28,29},... | collective-permute-start | bytes 270344 | tf_op jit(solution)/shard_map/ppermute | solution.py:610
  26.7 5.4 %collective-permute-start.8 = (f32[176,128]{1,0:T(8,128)S(1)}, f32[176,128]{1,0:T(8,128)S(1)}, u32[]{:S(2)}, u32[]{:S(2)}) collective-permute-start(f32[176,128]{1,0:T(8,128)S(1)} %get-tuple-element.58), channel_id=1, source_target_pairs={{28,4},{29,5},{30,6},{31,7},{0,8},{1,9},{2,10},{3,11},{12,20},{13,... | collective-permute-start | bytes 270344 | tf_op jit(solution)/shard_map/ppermute | solution.py:610
  26.8 5.3 %collective-permute-start.9 = (f32[176,128]{1,0:T(8,128)S(1)}, f32[176,128]{1,0:T(8,128)S(1)}, u32[]{:S(2)}, u32[]{:S(2)}) collective-permute-start(f32[176,128]{1,0:T(8,128)S(1)} %get-tuple-element.59), channel_id=1, source_target_pairs={{4,12},{5,13},{6,14},{7,15},{8,16},{9,17},{10,18},{11,19},{28,29},... | collective-permute-start | bytes 270344 | tf_op jit(solution)/shard_map/ppermute | solution.py:610
  27.8 8.0 %collective-permute-start.12 = (f32[176,128]{1,0:T(8,128)S(1)}, f32[176,128]{1,0:T(8,128)S(1)}, u32[]{:S(2)}, u32[]{:S(2)}) collective-permute-start(f32[176,128]{1,0:T(8,128)S(1)} %shard_map.87.refs_0_), channel_id=1, source_target_pairs={{29,30},{31,0},{1,2},{5,6},{7,8},{9,10},{13,14},{15,16},{17,18},{2... | collective-permute-start | bytes 270344 | tf_op jit(solution)/shard_map/ppermute | solution.py:610
  32.0 3.8 %collective-permute-start.13 = (f32[176,128]{1,0:T(8,128)S(1)}, f32[176,128]{1,0:T(8,128)S(1)}, u32[]{:S(2)}, u32[]{:S(2)}) collective-permute-start(f32[176,128]{1,0:T(8,128)S(1)} %shard_map.89), channel_id=1, source_target_pairs={{28,29},{30,31},{0,1},{2,3},{4,5},{6,7},{8,9},{10,11},{12,13},{14,... | collective-permute-start | bytes 270344 | tf_op jit(solution)/shard_map/ppermute | solution.py:610
  32.1 7.7 %collective-permute-start.14 = (f32[176,128]{1,0:T(8,128)S(1)}, f32[176,128]{1,0:T(8,128)S(1)}, u32[]{:S(2)}, u32[]{:S(2)}) collective-permute-start(f32[176,128]{1,0:T(8,128)S(1)} %shard_map.92.refs_0_), channel_id=1, source_target_pairs={{29,30},{31,0},{1,2},{5,6},{7,8},{9,10},{13,14},{15,16},{17,18},{2... | collective-permute-start | bytes 270344 | tf_op jit(solution)/shard_map/ppermute | solution.py:610
  35.7 4.1 %collective-permute-start.15 = (f32[176,128]{1,0:T(8,128)S(1)}, f32[176,128]{1,0:T(8,128)S(1)}, u32[]{:S(2)}, u32[]{:S(2)}) collective-permute-start(f32[176,128]{1,0:T(8,128)S(1)} %shard_map.94), channel_id=1, source_target_pairs={{28,29},{30,31},{0,1},{2,3},{4,5},{6,7},{8,9},{10,11},{12,13},{14,... | collective-permute-start | bytes 270344 | tf_op jit(solution)/shard_map/ppermute | solution.py:610

commit v14 on v13

--- a/solution.py
+++ b/solution.py
@@ -236,7 +236,7 @@
     return pl.ds(ref.shape[0] - 8, 8)
 
 
-def send_faces(c, ref, index, ends, out):
+def send_faces(c, ref, index, ends, out, fresh):
     inverse = index[1]
     top = jnp.broadcast_to(inverse[:, 127:], (8, 128))
     lane = lax.broadcasted_iota(jnp.int32, (8, 128), 1)
@@ -246,7 +246,7 @@
             for k in range(7):
                 face[tile(c, k)] = lanes(ref[face_rows(ends, axis, way, k)], inverse)
             last = lanes(ref[face_rows(ends, axis, way, 7)], top)
-            others = face[top_tile(face)] if c else jnp.zeros((8, 128), F32)
+            others = jnp.zeros((8, 128), F32) if fresh else face[top_tile(face)]
             face[top_tile(face)] = jnp.where(lane == c, last, others)
 
 
@@ -315,8 +315,9 @@
     diff_ref,
     arrived,
 ):
-    far = (numbers_far, weight_far, state_far, diff_far, moment_far)
-    near = (numbers_ref, weight_ref, state_ref, diff_ref, moment_ref)
+    joined_state = joined_ref.at[pl.ds(0, 3)]
+    far = (numbers_far, weight_far, diff_far, state_far, moment_far, state_far)
+    near = (numbers_ref, weight_ref, diff_ref, joined_state, moment_ref, state_ref)
     copies = [pltpu.make_async_copy(a, b, arrived.at[n]) for n, (a, b) in enumerate(zip(far, near))]
     for copy in copies:
         copy.start()
@@ -342,17 +343,18 @@
     copies[1].wait()
     set_mass(weight_ref, mass_ref)
     joined_ref[3] = mass_ref[...]
+    out = (ie_ref, io_ref, je_ref, jo_ref)
+    join_heights(joined_ref.at[3], index)
+    send_faces(3, joined_ref.at[3], index, ends, out, True)
     copies[2].wait()
-    out = (ie_ref, io_ref, je_ref, jo_ref)
-    for c in range(3):
-        joined_ref[c] = state_ref[c]
-    for c in range(4):
-        join_heights(joined_ref.at[c], index)
-        send_faces(c, joined_ref.at[c], index, ends, out)
-    copies[3].wait()
     for f in range(3):
         weigh_ref[f] = mass_ref[...] * (DT * diff_ref[f])
+    copies[3].wait()
+    for c in range(3):
+        join_heights(joined_ref.at[c], index)
+        send_faces(c, joined_ref.at[c], index, ends, out, False)
     copies[4].wait()
+    copies[5].wait()
 
 
 def moment_kernel(
@@ -380,7 +382,7 @@
 
     def finish(f):
         join_heights(joined_ref.at[f], index)
-        send_faces(f, joined_ref.at[f], index, ends, out)
+        send_faces(f, joined_ref.at[f], index, ends, out, f == 0)
 
     at = (carry_ref, weigh_ref, table_ref, turned_ref, slope_ref)
     forward(moment_ref, *at, joined_ref, finish)
@@ -433,7 +435,7 @@
         if first:
             joined_out[f] = state_out[f]
             join_heights(joined_out.at[f], index)
-            send_faces(f, joined_out.at[f], index, ends, out)
+            send_faces(f, joined_out.at[f], index, ends, out, f == 0)
         else:
             send_out(f, state_out, state_far, sent).start()
 
@@ -489,7 +491,7 @@
 
     def finish(f):
         join_heights(joined_out.at[f], index)
-        send_faces(f, joined_out.at[f], index, ends, out)
+        send_faces(f, joined_out.at[f], index, ends, out, f == 0)
 
     at = (carry_ref, weigh_ref, table_ref, turned_ref, slope_ref)
     forward(moment_out, *at, joined_out, finish)
@@ -659,7 +661,7 @@
             pltpu.VMEM((512, 128), F32),
             pltpu.VMEM((1, 128), jnp.int32),
             pltpu.SMEM((3,), F32),
-            pltpu.SemaphoreType.DMA((5,)),
+            pltpu.SemaphoreType.DMA((6,)),
         ],
         1_000_000,
         *map(far, (moment_fields, adjoint_fields, mass_weights, diffusivity)),

time: 40.8 us -> 40.6 us (level)
  no operation moved by 1% of the time
where the time goes in v14:
time: 40.6 us; the launch traced here: 40.4 us
  starting transfers between devices  26.2 us (65%)
  Pallas kernels  12 us (30%)
  waiting for transfers between devices  1.32 us (3%)
  between operations  0.83 us (2%)
    ppermute x16, starting transfers between devices, exchange(): return lax.ppermute(block, 'elem', pairs)  26.2 us
    pallas_call x15, Pallas kernels, call(): pl.pallas_call(kernel, out_shape=[jax.ShapeDtypeStruct(s, t) for s, t in...  12 us
    ppermute x16, waiting for transfers between devices, exchange(): return lax.ppermute(block, 'elem', pairs)  1.32 us
  transfers between devices with their start and end apart: 16, of which 2 were waited for; matrix products, arithmetic and copies ran while one was open for 0% of the time, Pallas kernels for 23%

profile of v14, /device:TPU:0, one launch (start us, length us, event | category | flops | bytes accessed | tf_op | source)
XLA Modules:
  0.0 40.4 jit_solution(4270688568847860137)
XLA Ops:
  0.6 0.0 copy-start
  0.6 1.9 %shard_map.77 = (f32[3,512,128]{2,1,0:T(8,128)S(1)}, f32[3,512,128]{2,1,0:T(8,128)S(1)}, f32[512,128]{1,0:T(8,128)S(1)}, f32[3,512,128]{2,1,0:T(8,128)S(1)}, bf1...) custom-call(f32[3,512,128]{2,1,0:T(8,128)} %moment_far.1, ...), custom_call_target="tpu_custom_call" | custom-call | flops 1000000 | bytes 6783500 | tf_op jit(solution)/shard_map/pallas_call | solution.py:567
  2.5 3.1 %collective-permute-start = (f32[232,128]{1,0:T(8,128)S(1)}, f32[232,128]{1,0:T(8,128)S(1)}, u32[]{:S(2)}, u32[]{:S(2)}) collective-permute-start(f32[232,128]{1,0:T(8,128)S(1)} %get-tuple-element.46), channel_id=1, source_target_pairs={{28,4},{29,5},{30,6},{31,7},{0,8},{1,9},{2,10},{3,11},{12,20},{13,... | collective-permute-start | bytes 356360 | tf_op jit(solution)/shard_map/ppermute | solution.py:612
  5.6 0.0 collective-permute-start.1
  5.6 0.0 copy-done
  5.6 1.9 %shard_map.78 = (f32[3,512,128]{2,1,0:T(8,128)S(1)}, f32[3,512,128]{2,1,0:T(8,128)S(1)}, f32[176,128]{1,0:T(8,128)S(1)}, f32[176,128]{1,0:T(8,128)S(1)}, f32[176,128]{1,0:T(8,128)S(1)}, /*index=5*/f32[176,128]{1,0:T(8,128)S(1)}) custom-call(f32[3,512,128]{2,1,0:T(8,128)S(1)} %get-tuple-element.37.moment_ref, f32[3,512,128]{2,1,0:T(8,128)S(1)} %copy-done, ...), custom_call_target="tpu_custom_call" | custom-call | flops 20000000 | bytes 5357568 | tf_op jit(solution)/shard_map/pallas_call | solution.py:567
  7.5 3.2 %collective-permute-start.4 = (f32[176,128]{1,0:T(8,128)S(1)}, f32[176,128]{1,0:T(8,128)S(1)}, u32[]{:S(2)}, u32[]{:S(2)}) collective-permute-start(f32[176,128]{1,0:T(8,128)S(1)} %get-tuple-element.52), channel_id=1, source_target_pairs={{28,4},{29,5},{30,6},{31,7},{0,8},{1,9},{2,10},{3,11},{12,20},{13,... | collective-permute-start | bytes 270344 | tf_op jit(solution)/shard_map/ppermute | solution.py:612
  10.7 0.0 collective-permute-start.5
  10.7 0.0 collective-permute-done.ie_ref.refs_0_
  10.7 0.0 collective-permute-done.1.io_ref.refs_1_
  10.8 4.8 %collective-permute-start.2 = (f32[232,128]{1,0:T(8,128)S(1)}, f32[232,128]{1,0:T(8,128)S(1)}, u32[]{:S(2)}, u32[]{:S(2)}) collective-permute-start(f32[232,128]{1,0:T(8,128)S(1)} %shard_map.79.refs_0_), channel_id=1, source_target_pairs={{29,30},{31,0},{1,2},{5,6},{7,8},{9,10},{13,14},{15,16},{17,18},{2... | collective-permute-start | bytes 356360 | tf_op jit(solution)/shard_map/ppermute | solution.py:612
  15.6 0.1 collective-permute-start.3
  15.6 0.0 collective-permute-done.4.ie_ref.gie_ref
  15.6 0.0 collective-permute-done.5.io_ref.gio_ref
  15.7 3.5 %collective-permute-start.6 = (f32[176,128]{1,0:T(8,128)S(1)}, f32[176,128]{1,0:T(8,128)S(1)}, u32[]{:S(2)}, u32[]{:S(2)}) collective-permute-start(f32[176,128]{1,0:T(8,128)S(1)} %shard_map.83.refs_0_), channel_id=1, source_target_pairs={{29,30},{31,0},{1,2},{5,6},{7,8},{9,10},{13,14},{15,16},{17,18},{2... | collective-permute-start | bytes 270344 | tf_op jit(solution)/shard_map/ppermute | solution.py:612
  19.3 0.1 collective-permute-start.7
  19.3 0.0 collective-permute-done.2.refs_0_
  19.4 0.0 collective-permute-done.3.refs_3_
  19.4 2.0 %shard_map.82 = (f32[512,128]{1,0:T(8,128)S(1)}, f32[3,512,128]{2,1,0:T(8,128)S(1)}, f32[3,512,128]{2,1,0:T(8,128)S(1)}, f32[176,128]{1,0:T(8,128)S(1)}, f32[176...) custom-call(f32[3,512,128]{2,1,0:T(8,128)S(1)} %get-tuple-element.44.state_ref, ...), custom_call_target="tpu_custom_call" | custom-call | flops 20000000 | bytes 6881280 | tf_op jit(solution)/shard_map/pallas_call | solution.py:567
  21.3 3.0 %collective-permute-start.10 = (f32[176,128]{1,0:T(8,128)S(1)}, f32[176,128]{1,0:T(8,128)S(1)}, u32[]{:S(2)}, u32[]{:S(2)}) collective-permute-start(f32[176,128]{1,0:T(8,128)S(1)} %get-tuple-element.62), channel_id=1, source_target_pairs={{28,4},{29,5},{30,6},{31,7},{0,8},{1,9},{2,10},{3,11},{12,20},{13,... | collective-permute-start | bytes 270344 | tf_op jit(solution)/shard_map/ppermute | solution.py:612
  24.3 0.1 collective-permute-start.11
  24.5 0.0 collective-permute-done.6.refs_0_
  24.5 0.0 collective-permute-done.7.gje_ref
  24.5 1.9 %shard_map.86 = (f32[3,512,128]{2,1,0:T(8,128)S(1)}, f32[3,512,128]{2,1,0:T(8,128)S(1)}, f32[176,128]{1,0:T(8,128)S(1)}, f32[176,128]{1,0:T(8,128)S(1)}, f32[176,128]{1,0:T(8,128)S(1)}, /*index=5*/f32[176,128]{1,0:T(8,128)S(1)}) custom-call(f32[3,512,128]{2,1,0:T(8,128)S(1)} %get-tuple-element.37.moment_ref, f32[3,512,128]{2,1,0:T(8,128)S(1)} %get-tuple-element.43.carry_ref, ...), custom_call_target="tpu_custom_call" | custom-call | flops 20000000 | bytes 6504448 | tf_op jit(solution)/shard_map/pallas_call | solution.py:567
  26.4 0.1 collective-permute-start.8
  26.5 0.4 %collective-permute-start.9 = (f32[176,128]{1,0:T(8,128)S(1)}, f32[176,128]{1,0:T(8,128)S(1)}, u32[]{:S(2)}, u32[]{:S(2)}) collective-permute-start(f32[176,128]{1,0:T(8,128)S(1)} %get-tuple-element.59), channel_id=1, source_target_pairs={{4,12},{5,13},{6,14},{7,15},{8,16},{9,17},{10,18},{11,19},{28,29},... | collective-permute-start | bytes 270344 | tf_op jit(solution)/shard_map/ppermute | solution.py:612
  26.9 0.6 %collective-permute-done.10.ie_ref.refs_1_ = f32[176,128]{1,0:T(8,128)S(1)} collective-permute-done((f32[176,128]{1,0:T(8,128)S(1)}, f32[176,128]{1,0:T(8,128)S(1)}, u32[]{:S(2)}, u32[]{:S(2)}) %collective-permute-start.10) | collective-permute-done | bytes 90144 | tf_op jit(solution)/shard_map/ppermute | solution.py:612
  27.5 0.0 collective-permute-done.11.io_ref.refs_2_
  27.6 4.2 %collective-permute-start.12 = (f32[176,128]{1,0:T(8,128)S(1)}, f32[176,128]{1,0:T(8,128)S(1)}, u32[]{:S(2)}, u32[]{:S(2)}) collective-permute-start(f32[176,128]{1,0:T(8,128)S(1)} %shard_map.87.refs_0_), channel_id=1, source_target_pairs={{29,30},{31,0},{1,2},{5,6},{7,8},{9,10},{13,14},{15,16},{17,18},{2... | collective-permute-start | bytes 270344 | tf_op jit(solution)/shard_map/ppermute | solution.py:612
  31.8 0.1 collective-permute-start.13
  31.8 0.0 collective-permute-done.8.gie_ref.ie_ref
  31.9 0.0 collective-permute-done.9.gio_ref.io_ref
  31.9 3.6 %collective-permute-start.14 = (f32[176,128]{1,0:T(8,128)S(1)}, f32[176,128]{1,0:T(8,128)S(1)}, u32[]{:S(2)}, u32[]{:S(2)}) collective-permute-start(f32[176,128]{1,0:T(8,128)S(1)} %shard_map.92.refs_0_), channel_id=1, source_target_pairs={{29,30},{31,0},{1,2},{5,6},{7,8},{9,10},{13,14},{15,16},{17,18},{2... | collective-permute-start | bytes 270344 | tf_op jit(solution)/shard_map/ppermute | solution.py:612
  35.5 0.1 collective-permute-start.15
  35.6 0.0 collective-permute-done.12.refs_0_
  35.6 0.0 collective-permute-done.13.refs_4_
  35.6 2.2 %shard_map.90 = (f32[3,512,128]{2,1,0:T(8,128)}, f32[8,128]{1,0:T(8,128)S(1)}) custom-call(f32[3,512,128]{2,1,0:T(8,128)S(1)} %get-tuple-element.60.state_ref, f32[3,512,128]{2,1,0:T(8,128)S(1)} %get-tuple-element.43.carry_ref, f32[3,512,128]{2,1,0:T(8,128)S(1)} %get-tuple-element.39.weigh_ref, bf16[256,384]{1,0:T(8,128)(2,1)S(1)} %get-tuple-element.40.table_ref, ...), custom_call_target="tpu_custom_call" | custom-call | flops 20000000 | bytes 5361664 | tf_op jit(solution)/shard_map/pallas_call | solution.py:567
  37.9 1.0 %shard_map.91 = (f32[3,8,8,8,128]{4,3,2,1,0:T(8,128)}, f32[3,8,8,8,128]{4,3,2,1,0:T(8,128)S(1)}) custom-call(f32[3,512,128]{2,1,0:T(8,128)S(1)} %get-tuple-element.56.moment_ref, s32[4,8,128]{2,1,0:T(8,128)S(1)} %get-tuple-element.42.index_ref, f32[512,128]{1,0:T(8,128)S(1)} %get-tuple-element.50.refs_1_.inverse_ref.refs_0_, ...), custom_call_target="tpu_custom_call" | custom-call | flops 1000000 | bytes 3608576 | tf_op jit(solution)/shard_map/pallas_call | solution.py:567
  38.9 0.7 %collective-permute-done.14.refs_0_ = f32[176,128]{1,0:T(8,128)S(1)} collective-permute-done((f32[176,128]{1,0:T(8,128)S(1)}, f32[176,128]{1,0:T(8,128)S(1)}, u32[]{:S(2)}, u32[]{:S(2)}) %collective-permute-start.14) | collective-permute-done | bytes 90144 | tf_op jit(solution)/shard_map/ppermute | solution.py:612
  39.6 0.0 collective-permute-done.15.gje_ref
  39.6 0.9 %shard_map.95 = f32[3,8,8,8,128]{4,3,2,1,0:T(8,128)} custom-call(f32[3,8,8,8,128]{4,3,2,1,0:T(8,128)} %get-tuple-element.67.inner_far, f32[3,8,8,8,128]{4,3,2,1,0:T(8,128)S(1)} %get-tuple-element.68.refs_1_.moment_ref, s32[4,8,128]{2,1,0:T(8,128)S(1)} %get-tuple-element.42.index_ref, ...), custom_call_target="tpu_custom_call", output_to_operand_aliasing={{}: (0, {})} | custom-call | flops 1000000 | bytes 2818048 | tf_op jit(solution)/shard_map/pallas_call | solution.py:567
  (12 shorter events, 0.3 us)
Async XLA Ops:
  0.6 5.0 %copy-start = (f32[3,512,128]{2,1,0:T(8,128)S(1)}, f32[3,512,128]{2,1,0:T(8,128)}, u32[]{:S(2)}) copy-start(f32[3,512,128]{2,1,0:T(8,128)} %flow_ref.1) | copy-start | bytes 2359300
  2.5 8.2 %collective-permute-start = (f32[232,128]{1,0:T(8,128)S(1)}, f32[232,128]{1,0:T(8,128)S(1)}, u32[]{:S(2)}, u32[]{:S(2)}) collective-permute-start(f32[232,128]{1,0:T(8,128)S(1)} %get-tuple-element.46), channel_id=1, source_target_pairs={{28,4},{29,5},{30,6},{31,7},{0,8},{1,9},{2,10},{3,11},{12,20},{13,... | collective-permute-start | bytes 356360 | tf_op jit(solution)/shard_map/ppermute | solution.py:612
  5.6 5.1 %collective-permute-start.1 = (f32[232,128]{1,0:T(8,128)S(1)}, f32[232,128]{1,0:T(8,128)S(1)}, u32[]{:S(2)}, u32[]{:S(2)}) collective-permute-start(f32[232,128]{1,0:T(8,128)S(1)} %get-tuple-element.47), channel_id=1, source_target_pairs={{4,12},{5,13},{6,14},{7,15},{8,16},{9,17},{10,18},{11,19},{28,29},... | collective-permute-start | bytes 356360 | tf_op jit(solution)/shard_map/ppermute | solution.py:612
  7.5 8.1 %collective-permute-start.4 = (f32[176,128]{1,0:T(8,128)S(1)}, f32[176,128]{1,0:T(8,128)S(1)}, u32[]{:S(2)}, u32[]{:S(2)}) collective-permute-start(f32[176,128]{1,0:T(8,128)S(1)} %get-tuple-element.52), channel_id=1, source_target_pairs={{28,4},{29,5},{30,6},{31,7},{0,8},{1,9},{2,10},{3,11},{12,20},{13,... | collective-permute-start | bytes 270344 | tf_op jit(solution)/shard_map/ppermute | solution.py:612
  10.7 4.9 %collective-permute-start.5 = (f32[176,128]{1,0:T(8,128)S(1)}, f32[176,128]{1,0:T(8,128)S(1)}, u32[]{:S(2)}, u32[]{:S(2)}) collective-permute-start(f32[176,128]{1,0:T(8,128)S(1)} %get-tuple-element.53), channel_id=1, source_target_pairs={{4,12},{5,13},{6,14},{7,15},{8,16},{9,17},{10,18},{11,19},{28,29},... | collective-permute-start | bytes 270344 | tf_op jit(solution)/shard_map/ppermute | solution.py:612
  10.8 8.6 %collective-permute-start.2 = (f32[232,128]{1,0:T(8,128)S(1)}, f32[232,128]{1,0:T(8,128)S(1)}, u32[]{:S(2)}, u32[]{:S(2)}) collective-permute-start(f32[232,128]{1,0:T(8,128)S(1)} %shard_map.79.refs_0_), channel_id=1, source_target_pairs={{29,30},{31,0},{1,2},{5,6},{7,8},{9,10},{13,14},{15,16},{17,18},{2... | collective-permute-start | bytes 356360 | tf_op jit(solution)/shard_map/ppermute | solution.py:612
  15.6 3.8 %collective-permute-start.3 = (f32[232,128]{1,0:T(8,128)S(1)}, f32[232,128]{1,0:T(8,128)S(1)}, u32[]{:S(2)}, u32[]{:S(2)}) collective-permute-start(f32[232,128]{1,0:T(8,128)S(1)} %shard_map.81), channel_id=1, source_target_pairs={{28,29},{30,31},{0,1},{2,3},{4,5},{6,7},{8,9},{10,11},{12,13},{14,... | collective-permute-start | bytes 356360 | tf_op jit(solution)/shard_map/ppermute | solution.py:612
  15.7 8.8 %collective-permute-start.6 = (f32[176,128]{1,0:T(8,128)S(1)}, f32[176,128]{1,0:T(8,128)S(1)}, u32[]{:S(2)}, u32[]{:S(2)}) collective-permute-start(f32[176,128]{1,0:T(8,128)S(1)} %shard_map.83.refs_0_), channel_id=1, source_target_pairs={{29,30},{31,0},{1,2},{5,6},{7,8},{9,10},{13,14},{15,16},{17,18},{2... | collective-permute-start | bytes 270344 | tf_op jit(solution)/shard_map/ppermute | solution.py:612
  19.3 5.2 %collective-permute-start.7 = (f32[176,128]{1,0:T(8,128)S(1)}, f32[176,128]{1,0:T(8,128)S(1)}, u32[]{:S(2)}, u32[]{:S(2)}) collective-permute-start(f32[176,128]{1,0:T(8,128)S(1)} %shard_map.85), channel_id=1, source_target_pairs={{28,29},{30,31},{0,1},{2,3},{4,5},{6,7},{8,9},{10,11},{12,13},{14,... | collective-permute-start | bytes 270344 | tf_op jit(solution)/shard_map/ppermute | solution.py:612
  21.3 6.2 %collective-permute-start.10 = (f32[176,128]{1,0:T(8,128)S(1)}, f32[176,128]{1,0:T(8,128)S(1)}, u32[]{:S(2)}, u32[]{:S(2)}) collective-permute-start(f32[176,128]{1,0:T(8,128)S(1)} %get-tuple-element.62), channel_id=1, source_target_pairs={{28,4},{29,5},{30,6},{31,7},{0,8},{1,9},{2,10},{3,11},{12,20},{13,... | collective-permute-start | bytes 270344 | tf_op jit(solution)/shard_map/ppermute | solution.py:612
  24.3 3.2 %collective-permute-start.11 = (f32[176,128]{1,0:T(8,128)S(1)}, f32[176,128]{1,0:T(8,128)S(1)}, u32[]{:S(2)}, u32[]{:S(2)}) collective-permute-start(f32[176,128]{1,0:T(8,128)S(1)} %get-tuple-element.63), channel_id=1, source_target_pairs={{4,12},{5,13},{6,14},{7,15},{8,16},{9,17},{10,18},{11,19},{28,29},... | collective-permute-start | bytes 270344 | tf_op jit(solution)/shard_map/ppermute | solution.py:612
  26.4 5.4 %collective-permute-start.8 = (f32[176,128]{1,0:T(8,128)S(1)}, f32[176,128]{1,0:T(8,128)S(1)}, u32[]{:S(2)}, u32[]{:S(2)}) collective-permute-start(f32[176,128]{1,0:T(8,128)S(1)} %get-tuple-element.58), channel_id=1, source_target_pairs={{28,4},{29,5},{30,6},{31,7},{0,8},{1,9},{2,10},{3,11},{12,20},{13,... | collective-permute-start | bytes 270344 | tf_op jit(solution)/shard_map/ppermute | solution.py:612
  26.5 5.3 %collective-permute-start.9 = (f32[176,128]{1,0:T(8,128)S(1)}, f32[176,128]{1,0:T(8,128)S(1)}, u32[]{:S(2)}, u32[]{:S(2)}) collective-permute-start(f32[176,128]{1,0:T(8,128)S(1)} %get-tuple-element.59), channel_id=1, source_target_pairs={{4,12},{5,13},{6,14},{7,15},{8,16},{9,17},{10,18},{11,19},{28,29},... | collective-permute-start | bytes 270344 | tf_op jit(solution)/shard_map/ppermute | solution.py:612
  27.6 8.0 %collective-permute-start.12 = (f32[176,128]{1,0:T(8,128)S(1)}, f32[176,128]{1,0:T(8,128)S(1)}, u32[]{:S(2)}, u32[]{:S(2)}) collective-permute-start(f32[176,128]{1,0:T(8,128)S(1)} %shard_map.87.refs_0_), channel_id=1, source_target_pairs={{29,30},{31,0},{1,2},{5,6},{7,8},{9,10},{13,14},{15,16},{17,18},{2... | collective-permute-start | bytes 270344 | tf_op jit(solution)/shard_map/ppermute | solution.py:612
  31.8 3.8 %collective-permute-start.13 = (f32[176,128]{1,0:T(8,128)S(1)}, f32[176,128]{1,0:T(8,128)S(1)}, u32[]{:S(2)}, u32[]{:S(2)}) collective-permute-start(f32[176,128]{1,0:T(8,128)S(1)} %shard_map.89), channel_id=1, source_target_pairs={{28,29},{30,31},{0,1},{2,3},{4,5},{6,7},{8,9},{10,11},{12,13},{14,... | collective-permute-start | bytes 270344 | tf_op jit(solution)/shard_map/ppermute | solution.py:612
  31.9 7.7 %collective-permute-start.14 = (f32[176,128]{1,0:T(8,128)S(1)}, f32[176,128]{1,0:T(8,128)S(1)}, u32[]{:S(2)}, u32[]{:S(2)}) collective-permute-start(f32[176,128]{1,0:T(8,128)S(1)} %shard_map.92.refs_0_), channel_id=1, source_target_pairs={{29,30},{31,0},{1,2},{5,6},{7,8},{9,10},{13,14},{15,16},{17,18},{2... | collective-permute-start | bytes 270344 | tf_op jit(solution)/shard_map/ppermute | solution.py:612
  35.5 4.1 %collective-permute-start.15 = (f32[176,128]{1,0:T(8,128)S(1)}, f32[176,128]{1,0:T(8,128)S(1)}, u32[]{:S(2)}, u32[]{:S(2)}) collective-permute-start(f32[176,128]{1,0:T(8,128)S(1)} %shard_map.94), channel_id=1, source_target_pairs={{28,29},{30,31},{0,1},{2,3},{4,5},{6,7},{8,9},{10,11},{12,13},{14,... | collective-permute-start | bytes 270344 | tf_op jit(solution)/shard_map/ppermute | solution.py:612

commit v15 on v14

--- a/solution.py
+++ b/solution.py
@@ -319,13 +319,15 @@
     far = (numbers_far, weight_far, diff_far, state_far, moment_far, state_far)
     near = (numbers_ref, weight_ref, diff_ref, joined_state, moment_ref, state_ref)
     copies = [pltpu.make_async_copy(a, b, arrived.at[n]) for n, (a, b) in enumerate(zip(far, near))]
-    for copy in copies:
+    for copy in copies[:4]:
         copy.start()
     for axis in range(2):
         write_table(DM, axis, table_ref, 128 * axis, 0)
         write_table(DM.T, axis, turned_ref, 0, 384 * axis)
     ends = ends_of(columns)
     copies[0].wait()
+    for copy in copies[4:]:
+        copy.start()
     height = jnp.broadcast_to(numbers_ref[...] & 127, (8, 128))
     square = jnp.broadcast_to(height[:1].astype(F32), (128, 128)).T
     lane = lax.broadcasted_iota(jnp.int32, (128, 128), 1).astype(F32)

time: 40.6 us -> 40.9 us (level)
  no operation moved by 1% of the time
where the time goes in v15:
time: 40.9 us; the launch traced here: 40.8 us
  starting transfers between devices  26.3 us (64%)
  Pallas kernels  12.4 us (30%)
  waiting for transfers between devices  1.31 us (3%)
  between operations  0.83 us (2%)
    ppermute x16, starting transfers between devices, exchange(): return lax.ppermute(block, 'elem', pairs)  26.3 us
    pallas_call x15, Pallas kernels, call(): pl.pallas_call(kernel, out_shape=[jax.ShapeDtypeStruct(s, t) for s, t in...  12.4 us
    ppermute x16, waiting for transfers between devices, exchange(): return lax.ppermute(block, 'elem', pairs)  1.31 us
  transfers between devices with their start and end apart: 16, of which 2 were waited for; matrix products, arithmetic and copies ran while one was open for 0% of the time, Pallas kernels for 23%

profile of v15, /device:TPU:0, one launch (start us, length us, event | category | flops | bytes accessed | tf_op | source)
XLA Modules:
  0.0 40.8 jit_solution(2764996791601862539)
XLA Ops:
  0.6 0.0 copy-start
  0.6 2.2 %shard_map.77 = (f32[3,512,128]{2,1,0:T(8,128)S(1)}, f32[3,512,128]{2,1,0:T(8,128)S(1)}, f32[512,128]{1,0:T(8,128)S(1)}, f32[3,512,128]{2,1,0:T(8,128)S(1)}, bf1...) custom-call(f32[3,512,128]{2,1,0:T(8,128)} %moment_far.1, ...), custom_call_target="tpu_custom_call" | custom-call | flops 1000000 | bytes 6783500 | tf_op jit(solution)/shard_map/pallas_call | solution.py:569
  2.9 3.1 %collective-permute-start = (f32[232,128]{1,0:T(8,128)S(1)}, f32[232,128]{1,0:T(8,128)S(1)}, u32[]{:S(2)}, u32[]{:S(2)}) collective-permute-start(f32[232,128]{1,0:T(8,128)S(1)} %get-tuple-element.46), channel_id=1, source_target_pairs={{28,4},{29,5},{30,6},{31,7},{0,8},{1,9},{2,10},{3,11},{12,20},{13,... | collective-permute-start | bytes 356360 | tf_op jit(solution)/shard_map/ppermute | solution.py:614
  6.0 0.0 collective-permute-start.1
  6.0 0.0 copy-done
  6.0 1.9 %shard_map.78 = (f32[3,512,128]{2,1,0:T(8,128)S(1)}, f32[3,512,128]{2,1,0:T(8,128)S(1)}, f32[176,128]{1,0:T(8,128)S(1)}, f32[176,128]{1,0:T(8,128)S(1)}, f32[176,128]{1,0:T(8,128)S(1)}, /*index=5*/f32[176,128]{1,0:T(8,128)S(1)}) custom-call(f32[3,512,128]{2,1,0:T(8,128)S(1)} %get-tuple-element.37.moment_ref, f32[3,512,128]{2,1,0:T(8,128)S(1)} %copy-done, ...), custom_call_target="tpu_custom_call" | custom-call | flops 20000000 | bytes 5357568 | tf_op jit(solution)/shard_map/pallas_call | solution.py:569
  7.9 3.2 %collective-permute-start.4 = (f32[176,128]{1,0:T(8,128)S(1)}, f32[176,128]{1,0:T(8,128)S(1)}, u32[]{:S(2)}, u32[]{:S(2)}) collective-permute-start(f32[176,128]{1,0:T(8,128)S(1)} %get-tuple-element.52), channel_id=1, source_target_pairs={{28,4},{29,5},{30,6},{31,7},{0,8},{1,9},{2,10},{3,11},{12,20},{13,... | collective-permute-start | bytes 270344 | tf_op jit(solution)/shard_map/ppermute | solution.py:614
  11.1 0.0 collective-permute-start.5
  11.1 0.0 collective-permute-done.ie_ref.refs_0_
  11.1 0.0 collective-permute-done.1.io_ref.refs_1_
  11.1 4.8 %collective-permute-start.2 = (f32[232,128]{1,0:T(8,128)S(1)}, f32[232,128]{1,0:T(8,128)S(1)}, u32[]{:S(2)}, u32[]{:S(2)}) collective-permute-start(f32[232,128]{1,0:T(8,128)S(1)} %shard_map.79.refs_0_), channel_id=1, source_target_pairs={{29,30},{31,0},{1,2},{5,6},{7,8},{9,10},{13,14},{15,16},{17,18},{2... | collective-permute-start | bytes 356360 | tf_op jit(solution)/shard_map/ppermute | solution.py:614
  15.9 0.1 collective-permute-start.3
  16.0 0.0 collective-permute-done.4.ie_ref.gie_ref
  16.0 0.0 collective-permute-done.5.io_ref.gio_ref
  16.1 3.5 %collective-permute-start.6 = (f32[176,128]{1,0:T(8,128)S(1)}, f32[176,128]{1,0:T(8,128)S(1)}, u32[]{:S(2)}, u32[]{:S(2)}) collective-permute-start(f32[176,128]{1,0:T(8,128)S(1)} %shard_map.83.refs_0_), channel_id=1, source_target_pairs={{29,30},{31,0},{1,2},{5,6},{7,8},{9,10},{13,14},{15,16},{17,18},{2... | collective-permute-start | bytes 270344 | tf_op jit(solution)/shard_map/ppermute | solution.py:614
  19.6 0.1 collective-permute-start.7
  19.7 0.0 collective-permute-done.2.refs_0_
  19.7 0.0 collective-permute-done.3.refs_3_
  19.7 2.0 %shard_map.82 = (f32[512,128]{1,0:T(8,128)S(1)}, f32[3,512,128]{2,1,0:T(8,128)S(1)}, f32[3,512,128]{2,1,0:T(8,128)S(1)}, f32[176,128]{1,0:T(8,128)S(1)}, f32[176...) custom-call(f32[3,512,128]{2,1,0:T(8,128)S(1)} %get-tuple-element.44.state_ref, ...), custom_call_target="tpu_custom_call" | custom-call | flops 20000000 | bytes 6881280 | tf_op jit(solution)/shard_map/pallas_call | solution.py:569
  21.7 3.0 %collective-permute-start.10 = (f32[176,128]{1,0:T(8,128)S(1)}, f32[176,128]{1,0:T(8,128)S(1)}, u32[]{:S(2)}, u32[]{:S(2)}) collective-permute-start(f32[176,128]{1,0:T(8,128)S(1)} %get-tuple-element.62), channel_id=1, source_target_pairs={{28,4},{29,5},{30,6},{31,7},{0,8},{1,9},{2,10},{3,11},{12,20},{13,... | collective-permute-start | bytes 270344 | tf_op jit(solution)/shard_map/ppermute | solution.py:614
  24.7 0.1 collective-permute-start.11
  24.9 0.0 collective-permute-done.6.refs_0_
  24.9 0.0 collective-permute-done.7.gje_ref
  24.9 1.9 %shard_map.86 = (f32[3,512,128]{2,1,0:T(8,128)S(1)}, f32[3,512,128]{2,1,0:T(8,128)S(1)}, f32[176,128]{1,0:T(8,128)S(1)}, f32[176,128]{1,0:T(8,128)S(1)}, f32[176,128]{1,0:T(8,128)S(1)}, /*index=5*/f32[176,128]{1,0:T(8,128)S(1)}) custom-call(f32[3,512,128]{2,1,0:T(8,128)S(1)} %get-tuple-element.37.moment_ref, f32[3,512,128]{2,1,0:T(8,128)S(1)} %get-tuple-element.43.carry_ref, ...), custom_call_target="tpu_custom_call" | custom-call | flops 20000000 | bytes 6504448 | tf_op jit(solution)/shard_map/pallas_call | solution.py:569
  26.8 0.1 collective-permute-start.8
  26.9 0.4 %collective-permute-start.9 = (f32[176,128]{1,0:T(8,128)S(1)}, f32[176,128]{1,0:T(8,128)S(1)}, u32[]{:S(2)}, u32[]{:S(2)}) collective-permute-start(f32[176,128]{1,0:T(8,128)S(1)} %get-tuple-element.59), channel_id=1, source_target_pairs={{4,12},{5,13},{6,14},{7,15},{8,16},{9,17},{10,18},{11,19},{28,29},... | collective-permute-start | bytes 270344 | tf_op jit(solution)/shard_map/ppermute | solution.py:614
  27.3 0.6 %collective-permute-done.10.ie_ref.refs_1_ = f32[176,128]{1,0:T(8,128)S(1)} collective-permute-done((f32[176,128]{1,0:T(8,128)S(1)}, f32[176,128]{1,0:T(8,128)S(1)}, u32[]{:S(2)}, u32[]{:S(2)}) %collective-permute-start.10) | collective-permute-done | bytes 90144 | tf_op jit(solution)/shard_map/ppermute | solution.py:614
  27.9 0.0 collective-permute-done.11.io_ref.refs_2_
  28.0 4.1 %collective-permute-start.12 = (f32[176,128]{1,0:T(8,128)S(1)}, f32[176,128]{1,0:T(8,128)S(1)}, u32[]{:S(2)}, u32[]{:S(2)}) collective-permute-start(f32[176,128]{1,0:T(8,128)S(1)} %shard_map.87.refs_0_), channel_id=1, source_target_pairs={{29,30},{31,0},{1,2},{5,6},{7,8},{9,10},{13,14},{15,16},{17,18},{2... | collective-permute-start | bytes 270344 | tf_op jit(solution)/shard_map/ppermute | solution.py:614
  32.1 0.1 collective-permute-start.13
  32.2 0.0 collective-permute-done.8.gie_ref.ie_ref
  32.2 0.0 collective-permute-done.9.gio_ref.io_ref
  32.3 3.6 %collective-permute-start.14 = (f32[176,128]{1,0:T(8,128)S(1)}, f32[176,128]{1,0:T(8,128)S(1)}, u32[]{:S(2)}, u32[]{:S(2)}) collective-permute-start(f32[176,128]{1,0:T(8,128)S(1)} %shard_map.92.refs_0_), channel_id=1, source_target_pairs={{29,30},{31,0},{1,2},{5,6},{7,8},{9,10},{13,14},{15,16},{17,18},{2... | collective-permute-start | bytes 270344 | tf_op jit(solution)/shard_map/ppermute | solution.py:614
  35.9 0.1 collective-permute-start.15
  36.0 0.0 collective-permute-done.12.refs_0_
  36.0 0.0 collective-permute-done.13.refs_4_
  36.0 2.2 %shard_map.90 = (f32[3,512,128]{2,1,0:T(8,128)}, f32[8,128]{1,0:T(8,128)S(1)}) custom-call(f32[3,512,128]{2,1,0:T(8,128)S(1)} %get-tuple-element.60.state_ref, f32[3,512,128]{2,1,0:T(8,128)S(1)} %get-tuple-element.43.carry_ref, f32[3,512,128]{2,1,0:T(8,128)S(1)} %get-tuple-element.39.weigh_ref, bf16[256,384]{1,0:T(8,128)(2,1)S(1)} %get-tuple-element.40.table_ref, ...), custom_call_target="tpu_custom_call" | custom-call | flops 20000000 | bytes 5361664 | tf_op jit(solution)/shard_map/pallas_call | solution.py:569
  38.2 1.0 %shard_map.91 = (f32[3,8,8,8,128]{4,3,2,1,0:T(8,128)}, f32[3,8,8,8,128]{4,3,2,1,0:T(8,128)S(1)}) custom-call(f32[3,512,128]{2,1,0:T(8,128)S(1)} %get-tuple-element.56.moment_ref, s32[4,8,128]{2,1,0:T(8,128)S(1)} %get-tuple-element.42.index_ref, f32[512,128]{1,0:T(8,128)S(1)} %get-tuple-element.50.refs_1_.inverse_ref.refs_0_, ...), custom_call_target="tpu_custom_call" | custom-call | flops 1000000 | bytes 3608576 | tf_op jit(solution)/shard_map/pallas_call | solution.py:569
  39.3 0.7 %collective-permute-done.14.refs_0_ = f32[176,128]{1,0:T(8,128)S(1)} collective-permute-done((f32[176,128]{1,0:T(8,128)S(1)}, f32[176,128]{1,0:T(8,128)S(1)}, u32[]{:S(2)}, u32[]{:S(2)}) %collective-permute-start.14) | collective-permute-done | bytes 90144 | tf_op jit(solution)/shard_map/ppermute | solution.py:614
  39.9 0.0 collective-permute-done.15.gje_ref
  39.9 0.9 %shard_map.95 = f32[3,8,8,8,128]{4,3,2,1,0:T(8,128)} custom-call(f32[3,8,8,8,128]{4,3,2,1,0:T(8,128)} %get-tuple-element.67.inner_far, f32[3,8,8,8,128]{4,3,2,1,0:T(8,128)S(1)} %get-tuple-element.68.refs_1_.moment_ref, s32[4,8,128]{2,1,0:T(8,128)S(1)} %get-tuple-element.42.index_ref, ...), custom_call_target="tpu_custom_call", output_to_operand_aliasing={{}: (0, {})} | custom-call | flops 1000000 | bytes 2818048 | tf_op jit(solution)/shard_map/pallas_call | solution.py:569
  (12 shorter events, 0.3 us)
Async XLA Ops:
  0.6 5.3 %copy-start = (f32[3,512,128]{2,1,0:T(8,128)S(1)}, f32[3,512,128]{2,1,0:T(8,128)}, u32[]{:S(2)}) copy-start(f32[3,512,128]{2,1,0:T(8,128)} %flow_ref.1) | copy-start | bytes 2359300
  2.9 8.2 %collective-permute-start = (f32[232,128]{1,0:T(8,128)S(1)}, f32[232,128]{1,0:T(8,128)S(1)}, u32[]{:S(2)}, u32[]{:S(2)}) collective-permute-start(f32[232,128]{1,0:T(8,128)S(1)} %get-tuple-element.46), channel_id=1, source_target_pairs={{28,4},{29,5},{30,6},{31,7},{0,8},{1,9},{2,10},{3,11},{12,20},{13,... | collective-permute-start | bytes 356360 | tf_op jit(solution)/shard_map/ppermute | solution.py:614
  6.0 5.1 %collective-permute-start.1 = (f32[232,128]{1,0:T(8,128)S(1)}, f32[232,128]{1,0:T(8,128)S(1)}, u32[]{:S(2)}, u32[]{:S(2)}) collective-permute-start(f32[232,128]{1,0:T(8,128)S(1)} %get-tuple-element.47), channel_id=1, source_target_pairs={{4,12},{5,13},{6,14},{7,15},{8,16},{9,17},{10,18},{11,19},{28,29},... | collective-permute-start | bytes 356360 | tf_op jit(solution)/shard_map/ppermute | solution.py:614
  7.9 8.1 %collective-permute-start.4 = (f32[176,128]{1,0:T(8,128)S(1)}, f32[176,128]{1,0:T(8,128)S(1)}, u32[]{:S(2)}, u32[]{:S(2)}) collective-permute-start(f32[176,128]{1,0:T(8,128)S(1)} %get-tuple-element.52), channel_id=1, source_target_pairs={{28,4},{29,5},{30,6},{31,7},{0,8},{1,9},{2,10},{3,11},{12,20},{13,... | collective-permute-start | bytes 270344 | tf_op jit(solution)/shard_map/ppermute | solution.py:614
  11.1 4.9 %collective-permute-start.5 = (f32[176,128]{1,0:T(8,128)S(1)}, f32[176,128]{1,0:T(8,128)S(1)}, u32[]{:S(2)}, u32[]{:S(2)}) collective-permute-start(f32[176,128]{1,0:T(8,128)S(1)} %get-tuple-element.53), channel_id=1, source_target_pairs={{4,12},{5,13},{6,14},{7,15},{8,16},{9,17},{10,18},{11,19},{28,29},... | collective-permute-start | bytes 270344 | tf_op jit(solution)/shard_map/ppermute | solution.py:614
  11.1 8.6 %collective-permute-start.2 = (f32[232,128]{1,0:T(8,128)S(1)}, f32[232,128]{1,0:T(8,128)S(1)}, u32[]{:S(2)}, u32[]{:S(2)}) collective-permute-start(f32[232,128]{1,0:T(8,128)S(1)} %shard_map.79.refs_0_), channel_id=1, source_target_pairs={{29,30},{31,0},{1,2},{5,6},{7,8},{9,10},{13,14},{15,16},{17,18},{2... | collective-permute-start | bytes 356360 | tf_op jit(solution)/shard_map/ppermute | solution.py:614
  15.9 3.8 %collective-permute-start.3 = (f32[232,128]{1,0:T(8,128)S(1)}, f32[232,128]{1,0:T(8,128)S(1)}, u32[]{:S(2)}, u32[]{:S(2)}) collective-permute-start(f32[232,128]{1,0:T(8,128)S(1)} %shard_map.81), channel_id=1, source_target_pairs={{28,29},{30,31},{0,1},{2,3},{4,5},{6,7},{8,9},{10,11},{12,13},{14,... | collective-permute-start | bytes 356360 | tf_op jit(solution)/shard_map/ppermute | solution.py:614
  16.1 8.8 %collective-permute-start.6 = (f32[176,128]{1,0:T(8,128)S(1)}, f32[176,128]{1,0:T(8,128)S(1)}, u32[]{:S(2)}, u32[]{:S(2)}) collective-permute-start(f32[176,128]{1,0:T(8,128)S(1)} %shard_map.83.refs_0_), channel_id=1, source_target_pairs={{29,30},{31,0},{1,2},{5,6},{7,8},{9,10},{13,14},{15,16},{17,18},{2... | collective-permute-start | bytes 270344 | tf_op jit(solution)/shard_map/ppermute | solution.py:614
  19.6 5.3 %collective-permute-start.7 = (f32[176,128]{1,0:T(8,128)S(1)}, f32[176,128]{1,0:T(8,128)S(1)}, u32[]{:S(2)}, u32[]{:S(2)}) collective-permute-start(f32[176,128]{1,0:T(8,128)S(1)} %shard_map.85), channel_id=1, source_target_pairs={{28,29},{30,31},{0,1},{2,3},{4,5},{6,7},{8,9},{10,11},{12,13},{14,... | collective-permute-start | bytes 270344 | tf_op jit(solution)/shard_map/ppermute | solution.py:614
  21.7 6.2 %collective-permute-start.10 = (f32[176,128]{1,0:T(8,128)S(1)}, f32[176,128]{1,0:T(8,128)S(1)}, u32[]{:S(2)}, u32[]{:S(2)}) collective-permute-start(f32[176,128]{1,0:T(8,128)S(1)} %get-tuple-element.62), channel_id=1, source_target_pairs={{28,4},{29,5},{30,6},{31,7},{0,8},{1,9},{2,10},{3,11},{12,20},{13,... | collective-permute-start | bytes 270344 | tf_op jit(solution)/shard_map/ppermute | solution.py:614
  24.7 3.2 %collective-permute-start.11 = (f32[176,128]{1,0:T(8,128)S(1)}, f32[176,128]{1,0:T(8,128)S(1)}, u32[]{:S(2)}, u32[]{:S(2)}) collective-permute-start(f32[176,128]{1,0:T(8,128)S(1)} %get-tuple-element.63), channel_id=1, source_target_pairs={{4,12},{5,13},{6,14},{7,15},{8,16},{9,17},{10,18},{11,19},{28,29},... | collective-permute-start | bytes 270344 | tf_op jit(solution)/shard_map/ppermute | solution.py:614
  26.8 5.4 %collective-permute-start.8 = (f32[176,128]{1,0:T(8,128)S(1)}, f32[176,128]{1,0:T(8,128)S(1)}, u32[]{:S(2)}, u32[]{:S(2)}) collective-permute-start(f32[176,128]{1,0:T(8,128)S(1)} %get-tuple-element.58), channel_id=1, source_target_pairs={{28,4},{29,5},{30,6},{31,7},{0,8},{1,9},{2,10},{3,11},{12,20},{13,... | collective-permute-start | bytes 270344 | tf_op jit(solution)/shard_map/ppermute | solution.py:614
  26.9 5.3 %collective-permute-start.9 = (f32[176,128]{1,0:T(8,128)S(1)}, f32[176,128]{1,0:T(8,128)S(1)}, u32[]{:S(2)}, u32[]{:S(2)}) collective-permute-start(f32[176,128]{1,0:T(8,128)S(1)} %get-tuple-element.59), channel_id=1, source_target_pairs={{4,12},{5,13},{6,14},{7,15},{8,16},{9,17},{10,18},{11,19},{28,29},... | collective-permute-start | bytes 270344 | tf_op jit(solution)/shard_map/ppermute | solution.py:614
  28.0 8.0 %collective-permute-start.12 = (f32[176,128]{1,0:T(8,128)S(1)}, f32[176,128]{1,0:T(8,128)S(1)}, u32[]{:S(2)}, u32[]{:S(2)}) collective-permute-start(f32[176,128]{1,0:T(8,128)S(1)} %shard_map.87.refs_0_), channel_id=1, source_target_pairs={{29,30},{31,0},{1,2},{5,6},{7,8},{9,10},{13,14},{15,16},{17,18},{2... | collective-permute-start | bytes 270344 | tf_op jit(solution)/shard_map/ppermute | solution.py:614
  32.1 3.8 %collective-permute-start.13 = (f32[176,128]{1,0:T(8,128)S(1)}, f32[176,128]{1,0:T(8,128)S(1)}, u32[]{:S(2)}, u32[]{:S(2)}) collective-permute-start(f32[176,128]{1,0:T(8,128)S(1)} %shard_map.89), channel_id=1, source_target_pairs={{28,29},{30,31},{0,1},{2,3},{4,5},{6,7},{8,9},{10,11},{12,13},{14,... | collective-permute-start | bytes 270344 | tf_op jit(solution)/shard_map/ppermute | solution.py:614
  32.3 7.7 %collective-permute-start.14 = (f32[176,128]{1,0:T(8,128)S(1)}, f32[176,128]{1,0:T(8,128)S(1)}, u32[]{:S(2)}, u32[]{:S(2)}) collective-permute-start(f32[176,128]{1,0:T(8,128)S(1)} %shard_map.92.refs_0_), channel_id=1, source_target_pairs={{29,30},{31,0},{1,2},{5,6},{7,8},{9,10},{13,14},{15,16},{17,18},{2... | collective-permute-start | bytes 270344 | tf_op jit(solution)/shard_map/ppermute | solution.py:614
  35.9 4.1 %collective-permute-start.15 = (f32[176,128]{1,0:T(8,128)S(1)}, f32[176,128]{1,0:T(8,128)S(1)}, u32[]{:S(2)}, u32[]{:S(2)}) collective-permute-start(f32[176,128]{1,0:T(8,128)S(1)} %shard_map.94), channel_id=1, source_target_pairs={{28,29},{30,31},{0,1},{2,3},{4,5},{6,7},{8,9},{10,11},{12,13},{14,... | collective-permute-start | bytes 270344 | tf_op jit(solution)/shard_map/ppermute | solution.py:614
